TPU v7x, 32 devices: a whole 2x2x4 slice. The times are simulated.
32 devices in a mesh: ep: 16 (over z, y, x), tp: 2 (over core).
Axes of the slice: x: 2, y: 2, z: 4, core: 2. Of those that a mesh axis runs over, the one named last changes fastest.
Arguments:
- tokens: bfloat16 [2, 8192, 1024], P(None, ('ep', 'tp')), may hold values from -6 to 6
- gain_attn: bfloat16 [1024], P('ep'), may hold values from 0.5 to 1.5
- w_query: bfloat16 [1024, 1024], P('ep', 'tp'), may hold values from -0.1875 to 0.1875
- w_key: bfloat16 [1024, 512], P('ep', 'tp'), may hold values from -0.1875 to 0.1875
- w_value: bfloat16 [1024, 512], P('ep', 'tp'), may hold values from -0.1875 to 0.1875
- w_output: bfloat16 [1024, 1024], P('tp', 'ep'), may hold values from -3 to 3
- gain_moe: bfloat16 [1024], P('ep'), may hold values from 0.5 to 1.5
- w_router: bfloat16 [1024, 16], P('ep'), may hold values from -0.09375 to 0.09375
- w_gate: bfloat16 [16, 1024, 512], P('ep'), may hold values from -0.1875 to 0.1875
- w_up: bfloat16 [16, 1024, 512], P('ep'), may hold values from -0.1875 to 0.1875
- w_down: bfloat16 [16, 512, 1024], P('ep'), may hold values from -0.75 to 0.75
- routes: int32 [2, 8192, 8], P(None, ('ep', 'tp')), may hold values from 0 to 15, all different within a row; in each aligned block of 256 rows (0 to 255, 256 to 511, ..., all dimensions but the last counted through in order) at most 192 rows name the same one
- piece_starts: int32 [2, 16], replicated, may hold values from 0 to 7936, as said below
- cotangent: bfloat16 [2, 8192, 1024], P(None, ('ep', 'tp')), may hold values from -6 to 6
Outputs:
- mixed: bfloat16 [2, 8192, 1024], P(None, ('ep', 'tp'))
- grad_tokens: float32 [2, 8192, 1024], P(None, ('ep', 'tp'))
- grad_gain_attn: float32 [1024], P(('ep', 'tp'))
- grad_w_query: float32 [1024, 1024], P('ep', 'tp')
- grad_w_key: float32 [1024, 512], P('ep', 'tp')
- grad_w_value: float32 [1024, 512], P('ep', 'tp')
- grad_w_output: float32 [1024, 1024], P('tp', 'ep')
- grad_gain_moe: float32 [1024], P(('ep', 'tp'))
- grad_w_router: float32 [1024, 16], P(('ep', 'tp'))
- grad_w_gate: float32 [16, 1024, 512], P('ep', 'tp')
- grad_w_up: float32 [16, 1024, 512], P('ep', 'tp')
- grad_w_down: float32 [16, 512, 1024], P('ep', None, 'tp')
Inputs may be any that keep to these rules, and one draw needn't show every extreme that they name: `routes`: each token names 8 different experts. Within the rows of one device (aligned blocks of 256 positions of a micro-batch) no expert is named more than 192 times, a bound that some block reaches. `piece_starts`: in each sequence the 16 picture pieces [start, start + 256) rise and do not intersect.
All inputs are finite; a program needn't handle non-finite values.
Results may differ from a plain program's by a relative error of at most 0.03.
Values may be sent and summed in bfloat16 or wider, within the bound.
No kernel may reach another device: no remote copies, remote signals or barrier semaphores. Data moves between devices by JAX's collectives and lax.ppermute only.
A program may use at most 256 MiB of HBM per device.

v0:
```python
import math

import jax
import jax.numpy as jnp
from jax import lax
from jax.sharding import PartitionSpec as P

HEAD_DIM = 64
PIECE = 256


EPS = 1e-06
THETA = 10000.0
NEG = -1e30


def rms_scale(values):
    return lax.rsqrt(jnp.mean(values * values, -1, keepdims=True) + EPS)


def angle_tables(positions):
    halves = jnp.arange(HEAD_DIM // 2, dtype=jnp.float32)
    freqs = THETA ** (-2.0 * halves / HEAD_DIM)
    angles = positions.astype(jnp.float32)[:, None] * freqs[None, :]
    return (jnp.cos(angles)[:, None, :], jnp.sin(angles)[:, None, :])


def rotate(values, cosine, sine):
    half_dim = values.shape[-1] // 2
    first_half = values[..., :half_dim]
    second_half = values[..., half_dim:]
    return jnp.concatenate(
        [first_half * cosine - second_half * sine, second_half * cosine + first_half * sine], -1
    )


def piece_index(starts, positions):
    inside = (positions[:, None] >= starts[None, :]) & (
        positions[:, None] < starts[None, :] + PIECE
    )
    numbers = jnp.arange(1, starts.shape[0] + 1, dtype=jnp.int32)
    return jnp.sum(jnp.where(inside, numbers[None, :], 0), -1) - 1


def allowed_mask(query_pos, query_piece, key_pos, key_piece):
    return (key_pos[None, :] <= query_pos[:, None]) | (
        key_piece[None, :] == query_piece[:, None]
    ) & (query_piece[:, None] >= 0)


def to_groups(rows, kv_here, group_size):
    row_total = rows.shape[0]
    return (
        rows.reshape(row_total, kv_here, group_size, HEAD_DIM)
        .transpose(1, 2, 0, 3)
        .reshape(kv_here, group_size * row_total, HEAD_DIM)
    )


def from_groups(grouped, row_total):
    kv_here = grouped.shape[0]
    return (
        grouped.reshape(kv_here, -1, row_total, HEAD_DIM)
        .transpose(2, 0, 1, 3)
        .reshape(row_total, -1)
    )


def tp_major(values, ep_count, tp_count):
    leading = values.shape[0]
    shaped = values.reshape(
        (ep_count, tp_count, leading // (ep_count * tp_count)) + values.shape[1:]
    )
    return jnp.swapaxes(shaped, 0, 1).reshape(values.shape)


def add_all(left_parts, right_parts):
    return tuple((left_part + right_part for left_part, right_part in zip(left_parts, right_parts)))


def reduce_grads(parts, ep_count, tp_count):
    (
        grad_gate_w,
        grad_up_w,
        grad_down_w,
        grad_gain_one,
        grad_gain_two,
        grad_route,
        grad_proj,
        grad_outw,
    ) = parts
    tp_sums = (
        lax.psum_scatter(
            grad_gate_w.astype(jnp.bfloat16), "tp", scatter_dimension=1, tiled=True
        ).astype(jnp.float32),
        lax.psum_scatter(
            grad_up_w.astype(jnp.bfloat16), "tp", scatter_dimension=1, tiled=True
        ).astype(jnp.float32),
        lax.psum_scatter(
            grad_down_w.astype(jnp.bfloat16), "tp", scatter_dimension=2, tiled=True
        ).astype(jnp.float32),
        lax.psum_scatter(
            tp_major(grad_gain_one, ep_count, tp_count).astype(jnp.bfloat16),
            "tp",
            scatter_dimension=0,
            tiled=True,
        ).astype(jnp.float32),
        lax.psum_scatter(
            tp_major(grad_gain_two, ep_count, tp_count).astype(jnp.bfloat16),
            "tp",
            scatter_dimension=0,
            tiled=True,
        ).astype(jnp.float32),
        lax.psum_scatter(
            tp_major(grad_route, ep_count, tp_count).astype(jnp.bfloat16),
            "tp",
            scatter_dimension=0,
            tiled=True,
        ).astype(jnp.float32),
    )
    ep_sums = (
        lax.psum_scatter(
            grad_proj.astype(jnp.bfloat16), "ep", scatter_dimension=0, tiled=True
        ).astype(jnp.float32),
        lax.psum_scatter(
            grad_outw.astype(jnp.bfloat16), "ep", scatter_dimension=1, tiled=True
        ).astype(jnp.float32),
        lax.psum_scatter(
            tp_sums[3].astype(jnp.bfloat16), "ep", scatter_dimension=0, tiled=True
        ).astype(jnp.float32),
        lax.psum_scatter(
            tp_sums[4].astype(jnp.bfloat16), "ep", scatter_dimension=0, tiled=True
        ).astype(jnp.float32),
        lax.psum_scatter(
            tp_sums[5].astype(jnp.bfloat16), "ep", scatter_dimension=0, tiled=True
        ).astype(jnp.float32),
    )
    return (
        tp_sums[0],
        tp_sums[1],
        tp_sums[2],
        ep_sums[2],
        ep_sums[3],
        ep_sums[4],
        ep_sums[0],
        ep_sums[1],
    )


def on_device(
    tokens,
    gain_attn,
    w_query,
    w_key,
    w_value,
    w_output,
    gain_moe,
    w_router,
    w_gate,
    w_up,
    w_down,
    routes,
    piece_starts,
    cotangent,
):
    ep_count = lax.axis_size("ep")
    tp_count = lax.axis_size("tp")
    micro_count, slice_rows, width = tokens.shape
    span_rows = slice_rows * tp_count
    seq_len = span_rows * ep_count
    q_cols = w_query.shape[1]
    kv_cols = w_key.shape[1]
    kv_here = kv_cols // HEAD_DIM
    group_size = q_cols // kv_cols
    query_rows = group_size * span_rows
    experts_here = w_gate.shape[0]
    experts_all = experts_here * ep_count
    top_count = routes.shape[2]
    capacity = max(2, slice_rows * top_count * 3 // (2 * experts_all))
    expert_rows = ep_count * capacity
    score_scale = HEAD_DIM ** (-0.5)
    key_block = math.gcd(seq_len, 512)
    block_count = seq_len // key_block
    local_pos = lax.axis_index("ep") * span_rows + jnp.arange(span_rows, dtype=jnp.int32)
    all_pos = jnp.arange(seq_len, dtype=jnp.int32)
    row_pos = jnp.tile(local_pos, group_size)
    cosine, sine = angle_tables(local_pos)
    slot_ids = jnp.arange(experts_all * capacity, dtype=jnp.int32)
    expert_ids = jnp.arange(experts_all, dtype=jnp.int32)
    gathered = (
        lax.all_gather(gain_attn, "ep", axis=0, tiled=True),
        lax.all_gather(w_query, "ep", axis=0, tiled=True),
        lax.all_gather(w_key, "ep", axis=0, tiled=True),
        lax.all_gather(w_value, "ep", axis=0, tiled=True),
        lax.all_gather(w_output, "ep", axis=1, tiled=True),
        lax.all_gather(gain_moe, "ep", axis=0, tiled=True),
        lax.all_gather(w_router, "ep", axis=0, tiled=True),
    )
    gain_one = gathered[0].astype(jnp.float32)
    w_proj = jnp.concatenate([gathered[1], gathered[2], gathered[3]], 1)
    w_out_full = gathered[4]
    gain_two = gathered[5].astype(jnp.float32)
    w_route_full = gathered[6]
    totals = None
    mixed_rows = []
    grad_rows = []
    for micro_index in range(micro_count):
        starts = piece_starts[micro_index]
        key_pieces = piece_index(starts, all_pos)
        row_piece = jnp.tile(piece_index(starts, local_pos), group_size)
        x_rows = tokens[micro_index].astype(jnp.float32)
        scale_one = rms_scale(x_rows)
        normed = (x_rows * scale_one * gain_one).astype(jnp.bfloat16)
        normed_all = lax.all_gather(normed, "tp", axis=0, tiled=True)
        projected = jnp.dot(normed_all, w_proj, preferred_element_type=jnp.float32)
        queries = rotate(
            projected[:, :q_cols].reshape(span_rows, -1, HEAD_DIM), cosine, sine
        ).astype(jnp.bfloat16)
        q_grouped = to_groups(queries.reshape(span_rows, q_cols), kv_here, group_size)
        keys_own = (
            rotate(
                projected[:, q_cols : q_cols + kv_cols].reshape(span_rows, kv_here, HEAD_DIM),
                cosine,
                sine,
            )
            .astype(jnp.bfloat16)
            .reshape(span_rows, kv_cols)
        )
        values_own = projected[:, q_cols + kv_cols :].astype(jnp.bfloat16)
        keys_all, values_all = (
            lax.all_gather(keys_own, "ep", axis=0, tiled=True),
            lax.all_gather(values_own, "ep", axis=0, tiled=True),
        )

        def block_scores(first_row, block_size):
            key_blk = lax.dynamic_slice_in_dim(keys_all, first_row, block_size, 0).reshape(
                block_size, kv_here, HEAD_DIM
            )
            value_blk = lax.dynamic_slice_in_dim(values_all, first_row, block_size, 0).reshape(
                block_size, kv_here, HEAD_DIM
            )
            key_pos = first_row + jnp.arange(block_size, dtype=jnp.int32)
            piece_blk = lax.dynamic_slice_in_dim(key_pieces, first_row, block_size, 0)
            allowed = allowed_mask(row_pos, row_piece, key_pos, piece_blk)[None]
            scores = (
                jnp.einsum("hrd,khd->hrk", q_grouped, key_blk, preferred_element_type=jnp.float32)
                * score_scale
            )
            return (scores, allowed, key_blk, value_blk)

        def forward_step(block_index, running):
            run_max, run_sum, run_acc = running
            scores, allowed, key_blk, value_blk = block_scores(block_index * key_block, key_block)
            scores = jnp.where(allowed, scores, NEG)
            new_max = jnp.maximum(run_max, jnp.max(scores, -1))
            weights = jnp.where(allowed, jnp.exp(scores - new_max[..., None]), 0.0)
            factor = jnp.exp(run_max - new_max)
            run_sum = run_sum * factor + jnp.sum(weights, -1)
            run_acc = run_acc * factor[..., None] + jnp.einsum(
                "hrk,khd->hrd",
                weights.astype(jnp.bfloat16),
                value_blk,
                preferred_element_type=jnp.float32,
            )
            return (new_max, run_sum, run_acc)

        start_state = (
            jnp.full((kv_here, query_rows), NEG, jnp.float32),
            jnp.zeros((kv_here, query_rows), jnp.float32),
            jnp.zeros((kv_here, query_rows, HEAD_DIM), jnp.float32),
        )
        run_max, run_sum, run_acc = lax.fori_loop(0, block_count, forward_step, start_state)
        log_total = run_max + jnp.log(run_sum)
        attended_f = run_acc / run_sum[..., None]
        attended = from_groups(attended_f.astype(jnp.bfloat16), span_rows)
        partial_attn = jnp.dot(attended, w_out_full, preferred_element_type=jnp.float32)
        attn_rows = lax.psum_scatter(
            partial_attn.astype(jnp.bfloat16), "tp", scatter_dimension=0, tiled=True
        ).astype(jnp.float32)
        resid = x_rows + attn_rows
        scale_two = rms_scale(resid)
        normed_two = (resid * scale_two * gain_two).astype(jnp.bfloat16)
        logits = jnp.dot(normed_two, w_route_full, preferred_element_type=jnp.float32)
        route_rows = routes[micro_index]
        route_hot = (route_rows[:, :, None] == expert_ids[None, None, :]).astype(jnp.float32)
        picked = jnp.sum(route_hot * logits[:, None, :], -1)
        highest = jnp.max(picked, -1, keepdims=True)
        raised = jnp.exp(picked - highest)
        gates = raised / jnp.sum(raised, -1, keepdims=True)
        flat_hot = route_hot.reshape(-1, experts_all)
        earlier = jnp.cumsum(flat_hot, 0) - flat_hot
        slot_of = jnp.sum(earlier * flat_hot, -1).astype(jnp.int32)
        target = route_rows.reshape(-1) * capacity + slot_of
        place_pairs = slot_ids[:, None] == target[None, :]
        place_pairs_b = place_pairs.astype(jnp.bfloat16)
        place_tokens = jnp.any(place_pairs.reshape(-1, slice_rows, top_count), -1).astype(
            jnp.bfloat16
        )
        send_rows = (
            jnp.dot(place_tokens, normed_two, preferred_element_type=jnp.float32)
            .astype(jnp.bfloat16)
            .reshape(ep_count, experts_here, capacity, width)
        )
        received = lax.all_to_all(send_rows, "ep", split_axis=0, concat_axis=0, tiled=True)
        expert_in = jnp.swapaxes(received, 0, 1).reshape(experts_here, expert_rows, width)
        gate_pre = jnp.einsum("erd,edf->erf", expert_in, w_gate, preferred_element_type=jnp.float32)
        up_pre = jnp.einsum("erd,edf->erf", expert_in, w_up, preferred_element_type=jnp.float32)
        sigmoid_val = jax.nn.sigmoid(gate_pre)
        silu_val = gate_pre * sigmoid_val
        hidden = (silu_val * up_pre).astype(jnp.bfloat16)
        expert_out = jnp.einsum(
            "erf,efd->erd", hidden, w_down, preferred_element_type=jnp.float32
        ).astype(jnp.bfloat16)
        returned = lax.all_to_all(
            jnp.swapaxes(expert_out.reshape(experts_here, ep_count, capacity, width), 0, 1),
            "ep",
            split_axis=0,
            concat_axis=0,
            tiled=True,
        )
        slot_rows = returned.reshape(-1, width)
        picked_rows = jnp.einsum(
            "sn,sd->nd", place_pairs_b, slot_rows, preferred_element_type=jnp.float32
        ).reshape(slice_rows, top_count, width)
        mixture = jnp.einsum("tk,tkd->td", gates, picked_rows)
        mixed_rows.append((resid + mixture).astype(jnp.bfloat16))
        grad_out = cotangent[micro_index].astype(jnp.float32)
        grad_gates = jnp.einsum("tkd,td->tk", picked_rows, grad_out)
        weighted = (
            (gates[:, :, None] * grad_out[:, None, :]).astype(jnp.bfloat16).reshape(-1, width)
        )
        grad_slots = (
            jnp.dot(place_pairs_b, weighted, preferred_element_type=jnp.float32)
            .astype(jnp.bfloat16)
            .reshape(ep_count, experts_here, capacity, width)
        )
        grad_recv = lax.all_to_all(grad_slots, "ep", split_axis=0, concat_axis=0, tiled=True)
        grad_expert = jnp.swapaxes(grad_recv, 0, 1).reshape(experts_here, expert_rows, width)
        grad_hidden = jnp.einsum(
            "erd,efd->erf", grad_expert, w_down, preferred_element_type=jnp.float32
        )
        grad_down_w = jnp.einsum(
            "erf,erd->efd", hidden, grad_expert, preferred_element_type=jnp.float32
        )
        silu_slope = sigmoid_val * (1.0 + gate_pre * (1.0 - sigmoid_val))
        grad_gate_pre = (grad_hidden * up_pre * silu_slope).astype(jnp.bfloat16)
        grad_up_pre = (grad_hidden * silu_val).astype(jnp.bfloat16)
        grad_gate_w = jnp.einsum(
            "erd,erf->edf", expert_in, grad_gate_pre, preferred_element_type=jnp.float32
        )
        grad_up_w = jnp.einsum(
            "erd,erf->edf", expert_in, grad_up_pre, preferred_element_type=jnp.float32
        )
        grad_copy = (
            jnp.einsum("erf,edf->erd", grad_gate_pre, w_gate, preferred_element_type=jnp.float32)
            + jnp.einsum("erf,edf->erd", grad_up_pre, w_up, preferred_element_type=jnp.float32)
        ).astype(jnp.bfloat16)
        grad_back = lax.all_to_all(
            jnp.swapaxes(grad_copy.reshape(experts_here, ep_count, capacity, width), 0, 1),
            "ep",
            split_axis=0,
            concat_axis=0,
            tiled=True,
        ).reshape(-1, width)
        grad_spread = gates * (grad_gates - jnp.sum(gates * grad_gates, -1, keepdims=True))
        grad_logits = jnp.einsum("tk,tke->te", grad_spread, route_hot).astype(jnp.bfloat16)
        grad_normed_two = jnp.einsum(
            "st,sd->td", place_tokens, grad_back, preferred_element_type=jnp.float32
        ) + jnp.einsum("te,de->td", grad_logits, w_route_full, preferred_element_type=jnp.float32)
        grad_route = jnp.einsum(
            "td,te->de", normed_two, grad_logits, preferred_element_type=jnp.float32
        )
        gained_two = grad_normed_two * gain_two
        grad_gain_two = jnp.sum(grad_normed_two * resid * scale_two, 0)
        grad_resid = (
            grad_out
            + scale_two * gained_two
            - resid * scale_two**3 * jnp.mean(resid * gained_two, -1, keepdims=True)
        )
        grad_attn = lax.all_gather(grad_resid.astype(jnp.bfloat16), "tp", axis=0, tiled=True)
        grad_outw = jnp.einsum("cq,cd->qd", attended, grad_attn, preferred_element_type=jnp.float32)
        grad_att_rows = jnp.einsum(
            "cd,qd->cq", grad_attn, w_out_full, preferred_element_type=jnp.float32
        ).astype(jnp.bfloat16)
        grad_grouped = to_groups(grad_att_rows, kv_here, group_size)
        delta = jnp.sum(grad_grouped.astype(jnp.float32) * attended_f, -1)

        def block_grads(first_row, block_size):
            scores, allowed, key_blk, value_blk = block_scores(first_row, block_size)
            probs = jnp.where(allowed, jnp.exp(scores - log_total[..., None]), 0.0)
            grad_probs = jnp.einsum(
                "hrd,khd->hrk", grad_grouped, value_blk, preferred_element_type=jnp.float32
            )
            grad_scores = (probs * (grad_probs - delta[..., None])).astype(jnp.bfloat16)
            return (probs, grad_scores, key_blk)

        def key_side(first_row, block_size):
            probs, grad_scores, key_blk = block_grads(first_row, block_size)
            grad_keys = (
                jnp.einsum(
                    "hrk,hrd->khd", grad_scores, q_grouped, preferred_element_type=jnp.float32
                ).reshape(block_size, kv_cols)
                * score_scale
            )
            grad_values = jnp.einsum(
                "hrk,hrd->khd",
                probs.astype(jnp.bfloat16),
                grad_grouped,
                preferred_element_type=jnp.float32,
            ).reshape(block_size, kv_cols)
            return (jnp.concatenate([grad_keys, grad_values], 1), grad_scores, key_blk)

        query_zero = jnp.zeros((kv_here, query_rows, HEAD_DIM), jnp.float32)

        def backward_step(block_index, running):
            grad_query, grad_kv = running
            first_row = block_index * key_block
            kv_terms, grad_scores, key_blk = key_side(first_row, key_block)
            grad_query = grad_query + jnp.einsum(
                "hrk,khd->hrd", grad_scores, key_blk, preferred_element_type=jnp.float32
            )
            grad_kv = lax.dynamic_update_slice_in_dim(grad_kv, kv_terms, first_row, 0)
            return (grad_query, grad_kv)

        grad_query, grad_kv = lax.fori_loop(
            0,
            block_count,
            backward_step,
            (query_zero, jnp.zeros((seq_len, 2 * kv_cols), jnp.float32)),
        )
        grad_kv_own = lax.psum_scatter(
            grad_kv.astype(jnp.bfloat16), "ep", scatter_dimension=0, tiled=True
        ).astype(jnp.float32)
        grad_query_rows = from_groups(grad_query * score_scale, span_rows).reshape(
            span_rows, -1, HEAD_DIM
        )
        grad_query_raw = (
            rotate(grad_query_rows, cosine, -sine).astype(jnp.bfloat16).reshape(span_rows, q_cols)
        )
        grad_key_raw = (
            rotate(grad_kv_own[:, :kv_cols].reshape(span_rows, kv_here, HEAD_DIM), cosine, -sine)
            .astype(jnp.bfloat16)
            .reshape(span_rows, kv_cols)
        )
        grad_value_raw = grad_kv_own[:, kv_cols:].astype(jnp.bfloat16)
        grad_proj_rows = jnp.concatenate([grad_query_raw, grad_key_raw, grad_value_raw], 1)
        grad_proj = jnp.einsum(
            "cd,cp->dp", normed_all, grad_proj_rows, preferred_element_type=jnp.float32
        )
        grad_normed_part = jnp.einsum(
            "cp,dp->cd", grad_proj_rows, w_proj, preferred_element_type=jnp.float32
        )
        grad_normed = lax.psum_scatter(
            grad_normed_part.astype(jnp.bfloat16), "tp", scatter_dimension=0, tiled=True
        ).astype(jnp.float32)
        gained_one = grad_normed * gain_one
        grad_gain_one = jnp.sum(grad_normed * x_rows * scale_one, 0)
        grad_rows.append(
            grad_resid
            + scale_one * gained_one
            - x_rows * scale_one**3 * jnp.mean(x_rows * gained_one, -1, keepdims=True)
        )
        parts = (
            grad_gate_w,
            grad_up_w,
            grad_down_w,
            grad_gain_one,
            grad_gain_two,
            grad_route,
            grad_proj,
            grad_outw,
        )
        reduced = reduce_grads(parts, ep_count, tp_count)
        totals = reduced if totals is None else add_all(totals, reduced)
    grad_qkv = totals[6]
    return (
        jnp.stack(mixed_rows),
        jnp.stack(grad_rows),
        totals[3],
        grad_qkv[:, :q_cols],
        grad_qkv[:, q_cols : q_cols + kv_cols],
        grad_qkv[:, q_cols + kv_cols :],
        totals[7],
        totals[4],
        totals[5],
        totals[0],
        totals[1],
        totals[2],
    )


def solution(mesh):
    in_specs = (
        P(None, ("ep", "tp"), None),
        P("ep"),
        P("ep", "tp"),
        P("ep", "tp"),
        P("ep", "tp"),
        P("tp", "ep"),
        P("ep"),
        P("ep", None),
        P("ep", None, None),
        P("ep", None, None),
        P("ep", None, None),
        P(None, ("ep", "tp"), None),
        P(),
        P(None, ("ep", "tp"), None),
    )
    out_specs = (
        P(None, ("ep", "tp"), None),
        P(None, ("ep", "tp"), None),
        P(("ep", "tp")),
        P("ep", "tp"),
        P("ep", "tp"),
        P("ep", "tp"),
        P("tp", "ep"),
        P(("ep", "tp")),
        P(("ep", "tp"), None),
        P("ep", "tp", None),
        P("ep", "tp", None),
        P("ep", None, "tp"),
    )
    return jax.shard_map(
        on_device, mesh=mesh, in_specs=in_specs, out_specs=out_specs, check_vma=False
    )
```

profile of v0, /device:TPU:14, one launch (start us, length us, event | category | flops | bytes accessed | tf_op | source)
XLA Modules:
  0.0 3476.8 jit_solution(13076654242886167718)
XLA Ops:
  11.7 29.2 all-reduce.11
  46.2 42.6 %all_gather.48 = bf16[1024,256]{1,0:T(8,128)(2,1)S(1)} all-gather(bf16[64,256]{1,0:T(8,128)(2,1)} %param.25), channel_id=1, replica_groups=mesh['ep'=16,'tp'=2] {'ep'}, dimensions={0}, use_global_device_ids=true | all-gather | bytes 557056 | tf_op jit(solution)/shard_map/all_gather | solution.py:193
  88.9 39.1 %all_gather.49 = bf16[1024,256]{1,0:T(8,128)(2,1)S(1)} all-gather(bf16[64,256]{1,0:T(8,128)(2,1)} %param.26), channel_id=1, replica_groups=mesh['ep'=16,'tp'=2] {'ep'}, dimensions={0}, use_global_device_ids=true | all-gather | bytes 557056 | tf_op jit(solution)/shard_map/all_gather | solution.py:194
  156.4 63.1 %all-gather.18.cloned.1.call-done = bf16[8192,256]{1,0:T(8,128)(2,1)} async-done(((bf16[512,256]{1,0:T(8,128)(2,1)}), bf16[8192,256]{1,0:T(8,128)(2,1)}) %all-gather.18.cloned.1.call-update) | async-done | bytes 4194320 | tf_op jit(solution)/shard_map/all_gather | solution.py:232
  225.9 74.7 %all-gather.16.cloned.1.call-done = bf16[8192,256]{0,1:T(8,128)(2,1)} async-done(((bf16[512,256]{0,1:T(8,128)(2,1)}), bf16[8192,256]{0,1:T(8,128)(2,1)}) %all-gather.16.cloned.1.call-update) | async-done | bytes 4194320 | tf_op jit(solution)/shard_map/all_gather | solution.py:231
  300.7 271.1 %while.68 = (s32[]{:T(128)}, f32[4,1024]{1,0:T(4,128)S(1)}, f32[4,1024]{1,0:T(4,128)S(1)}, f32[4,1024,64]{1,2,0:T(8,128)}, s32[8192]{0:T(1024)S(1)}, /*index=5*/...) while((s32[]{:T(128)}, f32[4,1024]{1,0:T(4,128)S(1)}, ...), condition=%wide.region_6.7_spmd.clone, body=%wide.region_3.6_spmd.clone.sunk | while | flops 567039488 | bytes 65327332 | solution.py:272
  583.8 269.9 %while.69 = (s32[]{:T(128)}, f32[4,1024]{1,0:T(4,128)S(1)}, f32[4,1024]{1,0:T(4,128)S(1)}, f32[4,1024,64]{1,2,0:T(8,128)}, s32[8192]{0:T(1024)S(1)}, /*index=5*/...) while((s32[]{:T(128)}, f32[4,1024]{1,0:T(4,128)S(1)}, ...), condition=%wide.region_22.23_spmd.clone, body=%wide.region_19.22_spmd.clone.sunk | while | flops 567039488 | bytes 65327332 | solution.py:272
  867.0 29.2 fusion.59
  906.7 8.2 all-to-all-start.2
  920.6 28.0 fusion.57
  953.9 103.9 %all-to-all-done.2 = bf16[16,1,192,1024]{3,2,1,0:T(8,128)(2,1)} async-done(((bf16[16,1,192,1024]{3,2,1,0:T(8,128)(2,1)}), bf16[16,1,192,1024]{3,2,1,0:T(8,128)(2,1)}, u32[]{:S(2)}, u32[]{:S(2)}) %all-to-all-start.2) | async-done | bytes 6291488 | tf_op jit(solution)/shard_map/all_to_all | solution.py:304
  1069.6 11.1 multiply_convert_fusion.4
  1087.6 115.2 %all-to-all-done = bf16[16,1,192,1024]{3,2,1,0:T(8,128)(2,1)} async-done(((bf16[16,1,192,1024]{3,2,1,0:T(8,128)(2,1)}), bf16[16,1,192,1024]{3,2,1,0:T(8,128)(2,1)}, u32[]{:S(2)}, u32[]{:S(2)}) %all-to-all-start) | async-done | bytes 6291488 | tf_op jit(solution)/shard_map/all_to_all | solution.py:304
  1213.7 11.1 multiply_convert_fusion.5
  1231.7 116.2 %all-to-all-done.3 = bf16[16,1,192,1024]{3,2,1,0:T(8,128)(2,1)} async-done(((bf16[16,1,192,1024]{3,2,1,0:T(8,128)(2,1)}), bf16[16,1,192,1024]{3,2,1,0:T(8,128)(2,1)}, u32[]{:S(2)}, u32[]{:S(2)}) %all-to-all-start.3) | async-done | bytes 6291488 | tf_op jit(solution)/shard_map/all_to_all | solution.py:314
  1353.1 162.1 %all-gather = bf16[16,64,16]{1,2,0:T(8,128)(2,1)S(1)} all-gather(bf16[1,64,16]{1,2,0:T(8,128)(2,1)S(1)} %bitcast.701), channel_id=1, replica_groups=mesh['ep'=16,'tp'=2] {'ep'}, dimensions={0}, use_global_device_ids=true | all-gather | bytes 34816 | tf_op jit(solution)/shard_map/all_gather | solution.py:197
  1525.4 17.4 fusion.62
  1548.8 15.1 fusion.80
  1578.4 17.4 fusion.64
  1601.3 15.3 fusion.81
  1616.6 85.5 %all-to-all-done.6 = bf16[16,1,192,1024]{3,2,1,0:T(8,128)(2,1)} async-done(((bf16[16,1,192,1024]{3,2,1,0:T(8,128)(2,1)}), bf16[16,1,192,1024]{3,2,1,0:T(8,128)(2,1)}, u32[]{:S(2)}, u32[]{:S(2)}) %all-to-all-start.6) | async-done | bytes 6291488 | tf_op jit(solution)/shard_map/all_to_all | solution.py:337
  1707.2 11.3 multiply_convert_fusion
  1729.7 117.3 %all-to-all-done.4 = bf16[16,1,192,1024]{3,2,1,0:T(8,128)(2,1)} async-done(((bf16[16,1,192,1024]{3,2,1,0:T(8,128)(2,1)}), bf16[16,1,192,1024]{3,2,1,0:T(8,128)(2,1)}, u32[]{:S(2)}, u32[]{:S(2)}) %all-to-all-start.4) | async-done | bytes 6291488 | tf_op jit(solution)/shard_map/all_to_all | solution.py:337
  1852.6 11.3 multiply_convert_fusion.2
  1875.0 117.2 %all-to-all-done.7 = bf16[16,1,192,1024]{3,2,1,0:T(8,128)(2,1)} async-done(((bf16[16,1,192,1024]{3,2,1,0:T(8,128)(2,1)}), bf16[16,1,192,1024]{3,2,1,0:T(8,128)(2,1)}, u32[]{:S(2)}, u32[]{:S(2)}) %all-to-all-start.7) | async-done | bytes 6291488 | tf_op jit(solution)/shard_map/all_to_all | solution.py:358
  2014.1 123.1 %all-to-all-done.5 = bf16[16,1,192,1024]{3,2,1,0:T(8,128)(2,1)} async-done(((bf16[16,1,192,1024]{3,2,1,0:T(8,128)(2,1)}), bf16[16,1,192,1024]{3,2,1,0:T(8,128)(2,1)}, u32[]{:S(2)}, u32[]{:S(2)}) %all-to-all-start.5) | async-done | bytes 6291488 | tf_op jit(solution)/shard_map/all_to_all | solution.py:358
  2164.5 298.0 %while.71 = (s32[]{:T(128)}, f32[4,1024,64]{1,2,0:T(8,128)S(1)}, bf16[8192,512]{0,1:T(8,128)(2,1)}, s32[8192]{0:T(1024)}, bf16[8192,256]{0,1:T(8,128)(2,1)}, /*i...) while((s32[]{:T(128)}, f32[4,1024,64]{1,2,0:T(8,128)S(1)}, ...), condition=%wide.region_44.45_spmd.clone, body=%wide.region_43.44_spmd.clone.sunk | while | flops 1367082496 | bytes 63803636 | solution.py:425
  2471.4 264.0 %while.70 = (s32[]{:T(128)}, f32[4,1024,64]{1,2,0:T(8,128)S(1)}, bf16[8192,512]{0,1:T(8,128)(2,1)}, s32[8192]{0:T(1024)}, bf16[8192,256]{0,1:T(8,128)(2,1)}, /*i...) while((s32[]{:T(128)}, f32[4,1024,64]{1,2,0:T(8,128)S(1)}, ...), condition=%wide.region_36.37_spmd.clone, body=%wide.region_35.36_spmd.clone.sunk | while | flops 1367082496 | bytes 65900820 | solution.py:425
  2747.1 8.3 fusion.92
  2763.6 8.2 fusion.90
  2771.8 8.2 fusion.89
  2780.3 8.2 fusion.88
  2796.6 118.9 %reduce-scatter.29.cloned.1.call-done = bf16[512,512]{0,1:T(8,128)(2,1)} async-done(((bf16[8192,512]{0,1:T(8,128)(2,1)}), bf16[512,512]{0,1:T(8,128)(2,1)}) %reduce-scatter.29.cloned.1.call-update) | async-done | bytes 524304 | tf_op jit(solution)/shard_map/reduce_scatter | solution.py:431
  2935.8 45.1 %reduce-scatter.63.cloned.1.call-done = bf16[32,16]{1,0:T(8,128)(2,1)} async-done(((bf16[512,16]{1,0:T(8,128)(2,1)}), bf16[32,16]{1,0:T(8,128)(2,1)}) %reduce-scatter.63.cloned.1.call-update) | async-done | bytes 1040
  2981.7 74.4 %reduce-scatter.61.cloned.1.call-done = bf16[32,16]{1,0:T(8,128)(2,1)} async-done(((bf16[512,16]{1,0:T(8,128)(2,1)}), bf16[32,16]{1,0:T(8,128)(2,1)}) %reduce-scatter.61.cloned.1.call-update) | async-done | bytes 1040
  3057.4 21.1 reduce-scatter.59.cloned.1.call-done
  3078.5 11.9 reduce-scatter.57.cloned.1.call-done
  3092.7 10.2 reduce-scatter.55.cloned.1.call-done
  3102.9 12.1 reduce-scatter.53.cloned.1.call-done
  3117.3 10.2 reduce-scatter.51.cloned.1.call-done
  3127.6 12.5 reduce-scatter.49.cloned.1.call-done
  3143.8 62.8 %reduce-scatter.41.cloned.1.call-done = bf16[512,64]{0,1:T(8,128)(2,1)} async-done(((bf16[512,1024]{0,1:T(8,128)(2,1)}), bf16[512,64]{0,1:T(8,128)(2,1)}) %reduce-scatter.41.cloned.1.call-update) | async-done | bytes 65552 | tf_op jit(solution)/shard_map/reduce_scatter | solution.py:125
  3206.6 76.5 %reduce-scatter.43.cloned.1.call-done = bf16[512,64]{0,1:T(8,128)(2,1)} async-done(((bf16[512,1024]{0,1:T(8,128)(2,1)}), bf16[512,64]{0,1:T(8,128)(2,1)}) %reduce-scatter.43.cloned.1.call-update) | async-done | bytes 65552 | tf_op jit(solution)/shard_map/reduce_scatter | solution.py:125
  3284.6 20.0 reduce-scatter.35.cloned.1.call-done
  3304.6 12.1 reduce-scatter.31.cloned.1.call-done
  3322.0 29.5 all-reduce.10
  3356.3 31.2 reduce-scatter.37.cloned.1.call-done
  3387.4 79.9 %reduce-scatter.39.cloned.1.call-done = bf16[64,1024]{1,0:T(8,128)(2,1)} async-done(((bf16[1024,1024]{1,0:T(8,128)(2,1)}), bf16[64,1024]{1,0:T(8,128)(2,1)}) %reduce-scatter.39.cloned.1.call-update) | async-done | bytes 131088 | tf_op jit(solution)/shard_map/reduce_scatter | solution.py:122
  (1561 shorter events, 1428.5 us)
Async XLA Ops:
  7.2 1075.2 %copy-start = (bf16[1,512,1024]{2,1,0:T(8,128)(2,1)S(1)}, bf16[1,512,1024]{2,1,0:T(8,128)(2,1)}, u32[]{:S(2)}) copy-start(bf16[1,512,1024]{2,1,0:T(8,128)(2,1)} %param.32) | copy-start | bytes 3145732
  7.2 120.7 %all-gather.14.cloned.1.call-start = ((), (), s32[]{:S(2)}) async-start(), calls=%async_computation.29 | async-start | bytes 1114112 | tf_op jit(solution)/shard_map/all_gather | solution.py:192
  7.9 123.9 %all-gather.12.cloned.1.call-start = ((), (), s32[]{:S(2)}) async-start(), calls=%async_computation.28 | async-start | bytes 1572864 | tf_op jit(solution)/shard_map/all_gather | solution.py:214
  45.5 93.9 %all-gather.22.cloned.1.call-start = ((), (), s32[]{:S(2)}) async-start(), calls=%async_computation.34 | async-start | bytes 1572864 | tf_op jit(solution)/shard_map/all_gather | solution.py:214
  46.2 173.3 %all-gather.18.cloned.1.call-start = ((), (), s32[]{:S(2)}) async-start(), calls=%async_computation.31 | async-start | bytes 4456448 | tf_op jit(solution)/shard_map/all_gather | solution.py:232
  137.2 163.5 %all-gather.16.cloned.1.call-start = ((), (), s32[]{:S(2)}) async-start(), calls=%async_computation.30 | async-start | bytes 4456448 | tf_op jit(solution)/shard_map/all_gather | solution.py:231
  145.9 427.8 %all-gather.20.cloned.1.call-start = ((), (), s32[]{:S(2)}) async-start(), calls=%async_computation.32 | async-start | bytes 1114112 | tf_op jit(solution)/shard_map/all_gather | solution.py:195
  146.5 430.7 %all-gather.26.cloned.1.call-start = ((), (), s32[]{:S(2)}) async-start(), calls=%async_computation.36 | async-start | bytes 4456448 | tf_op jit(solution)/shard_map/all_gather | solution.py:232
  148.4 435.4 %all-gather.24.cloned.1.call-start = ((), (), s32[]{:S(2)}) async-start(), calls=%async_computation.35 | async-start | bytes 4456448 | tf_op jit(solution)/shard_map/all_gather | solution.py:231
  156.2 740.0 %reduce-scatter.25.cloned.1.call-start = ((), (), s32[]{:S(2)}) async-start(), calls=%async_computation.33 | async-start | bytes 1572864 | tf_op jit(solution)/shard_map/reduce_scatter | solution.py:277
  576.9 319.3 %reduce-scatter.27.cloned.1.call-start = ((), (), s32[]{:S(2)}) async-start(), calls=%async_computation.37 | async-start | bytes 1572864 | tf_op jit(solution)/shard_map/reduce_scatter | solution.py:277
  861.3 663.9 %copy-start.67 = (s32[256,8]{0,1:T(8,128)}, s32[256,8]{0,1:T(8,128)S(1)}, u32[]{:S(2)}) copy-start(s32[256,8]{0,1:T(8,128)S(1)} %get-tuple-element.1351) | copy-start | bytes 24580
  900.7 624.3 %copy-start.16 = (bf16[256,1024]{1,0:T(8,128)(2,1)}, bf16[256,1024]{1,0:T(8,128)(2,1)S(1)}, u32[]{:S(2)}) copy-start(bf16[256,1024]{1,0:T(8,128)(2,1)S(1)} %get-tuple-element.1321) | copy-start | bytes 1572868
  900.7 677.3 %copy-start.15 = (bf16[256,1024]{1,0:T(8,128)(2,1)}, bf16[256,1024]{1,0:T(8,128)(2,1)S(1)}, u32[]{:S(2)}) copy-start(bf16[256,1024]{1,0:T(8,128)(2,1)S(1)} %get-tuple-element.1320) | copy-start | bytes 1572868
  906.7 151.1 %all-to-all-start.2 = ((bf16[16,1,192,1024]{3,2,1,0:T(8,128)(2,1)}), bf16[16,1,192,1024]{3,2,1,0:T(8,128)(2,1)}, u32[]{:S(2)}, u32[]{:S(2)}) async-start(bf16[16,1,192,1024]{3,2,1,0:T(8,128)(2,1)} %bitcast.638), calls=%async_computation.4 | async-start | bytes 12582912 | tf_op jit(solution)/shard_map/all_to_all | solution.py:304
  1057.8 145.1 %all-to-all-start = ((bf16[16,1,192,1024]{3,2,1,0:T(8,128)(2,1)}), bf16[16,1,192,1024]{3,2,1,0:T(8,128)(2,1)}, u32[]{:S(2)}, u32[]{:S(2)}) async-start(bf16[16,1,192,1024]{3,2,1,0:T(8,128)(2,1)} %bitcast.641), calls=%async_computation.1 | async-start | bytes 12582912 | tf_op jit(solution)/shard_map/all_to_all | solution.py:304
  1202.9 145.0 %all-to-all-start.3 = ((bf16[16,1,192,1024]{3,2,1,0:T(8,128)(2,1)}), bf16[16,1,192,1024]{3,2,1,0:T(8,128)(2,1)}, u32[]{:S(2)}, u32[]{:S(2)}) async-start(bf16[16,1,192,1024]{3,2,1,0:T(8,128)(2,1)} %bitcast.642), calls=%async_computation.5 | async-start | bytes 12582912 | tf_op jit(solution)/shard_map/all_to_all | solution.py:314
  1347.8 216.0 %all-to-all-start.1 = ((bf16[16,1,192,1024]{3,2,1,0:T(8,128)(2,1)}), bf16[16,1,192,1024]{3,2,1,0:T(8,128)(2,1)}, u32[]{:S(2)}, u32[]{:S(2)}) async-start(bf16[16,1,192,1024]{3,2,1,0:T(8,128)(2,1)} %bitcast.635), calls=%async_computation.2 | async-start | bytes 12582912 | tf_op jit(solution)/shard_map/all_to_all | solution.py:314
  1563.9 138.2 %all-to-all-start.6 = ((bf16[16,1,192,1024]{3,2,1,0:T(8,128)(2,1)}), bf16[16,1,192,1024]{3,2,1,0:T(8,128)(2,1)}, u32[]{:S(2)}, u32[]{:S(2)}) async-start(bf16[16,1,192,1024]{3,2,1,0:T(8,128)(2,1)} %bitcast.636), calls=%async_computation.10 | async-start | bytes 12582912 | tf_op jit(solution)/shard_map/all_to_all | solution.py:337
  1702.1 144.9 %all-to-all-start.4 = ((bf16[16,1,192,1024]{3,2,1,0:T(8,128)(2,1)}), bf16[16,1,192,1024]{3,2,1,0:T(8,128)(2,1)}, u32[]{:S(2)}, u32[]{:S(2)}) async-start(bf16[16,1,192,1024]{3,2,1,0:T(8,128)(2,1)} %bitcast.639), calls=%async_computation.6 | async-start | bytes 12582912 | tf_op jit(solution)/shard_map/all_to_all | solution.py:337
  1846.9 145.3 %all-to-all-start.7 = ((bf16[16,1,192,1024]{3,2,1,0:T(8,128)(2,1)}), bf16[16,1,192,1024]{3,2,1,0:T(8,128)(2,1)}, u32[]{:S(2)}, u32[]{:S(2)}) async-start(bf16[16,1,192,1024]{3,2,1,0:T(8,128)(2,1)} %bitcast.640), calls=%async_computation.11 | async-start | bytes 12582912 | tf_op jit(solution)/shard_map/all_to_all | solution.py:358
  1992.2 145.1 %all-to-all-start.5 = ((bf16[16,1,192,1024]{3,2,1,0:T(8,128)(2,1)}), bf16[16,1,192,1024]{3,2,1,0:T(8,128)(2,1)}, u32[]{:S(2)}, u32[]{:S(2)}) async-start(bf16[16,1,192,1024]{3,2,1,0:T(8,128)(2,1)} %bitcast.637), calls=%async_computation.7 | async-start | bytes 12582912 | tf_op jit(solution)/shard_map/all_to_all | solution.py:358
  1997.5 157.9 %all-gather.30.cloned.1.call-start = ((), (), s32[]{:S(2)}) async-start(), calls=%async_computation.41 | async-start | bytes 1572864 | tf_op jit(solution)/shard_map/all_gather | solution.py:380
  2146.9 315.7 %all-gather.28.cloned.1.call-start = ((), (), s32[]{:S(2)}) async-start(), calls=%async_computation.38 | async-start | bytes 1572864 | tf_op jit(solution)/shard_map/all_gather | solution.py:380
  2147.5 588.1 %reduce-scatter.47.cloned.1.call-start = ((), (), s32[]{:S(2)}) async-start(), calls=%async_computation.49 | async-start | bytes 49152 | tf_op jit(solution)/shard_map/reduce_scatter | solution.py:114
  2149.9 587.2 %reduce-scatter.45.cloned.1.call-start = ((), (), s32[]{:S(2)}) async-start(), calls=%async_computation.48 | async-start | bytes 49152 | tf_op jit(solution)/shard_map/reduce_scatter | solution.py:114
  2152.4 643.1 %reduce-scatter.33.cloned.1.call-start = ((), (), s32[]{:S(2)}) async-start(), calls=%async_computation.42 | async-start | bytes 8912896 | tf_op jit(solution)/shard_map/reduce_scatter | solution.py:431
  2466.6 448.9 %reduce-scatter.29.cloned.1.call-start = ((), (), s32[]{:S(2)}) async-start(), calls=%async_computation.39 | async-start | bytes 8912896 | tf_op jit(solution)/shard_map/reduce_scatter | solution.py:431
  2735.5 245.4 %reduce-scatter.63.cloned.1.call-start = ((), (), s32[]{:S(2)}) async-start(), calls=%async_computation.57 | async-start | bytes 139264
  2737.1 319.0 %reduce-scatter.61.cloned.1.call-start = ((), (), s32[]{:S(2)}) async-start(), calls=%async_computation.56 | async-start | bytes 139264
  2738.6 339.8 %reduce-scatter.59.cloned.1.call-start = ((), (), s32[]{:S(2)}) async-start(), calls=%async_computation.55 | async-start | bytes 1572864 | tf_op jit(solution)/shard_map/reduce_scatter | solution.py:99
  2746.8 343.5 %reduce-scatter.57.cloned.1.call-start = ((), (), s32[]{:S(2)}) async-start(), calls=%async_computation.54 | async-start | bytes 1572864 | tf_op jit(solution)/shard_map/reduce_scatter | solution.py:99
  2755.4 347.6 %reduce-scatter.55.cloned.1.call-start = ((), (), s32[]{:S(2)}) async-start(), calls=%async_computation.53 | async-start | bytes 1572864 | tf_op jit(solution)/shard_map/reduce_scatter | solution.py:96
  2763.6 351.4 %reduce-scatter.53.cloned.1.call-start = ((), (), s32[]{:S(2)}) async-start(), calls=%async_computation.52 | async-start | bytes 1572864 | tf_op jit(solution)/shard_map/reduce_scatter | solution.py:96
  2771.8 355.8 %reduce-scatter.51.cloned.1.call-start = ((), (), s32[]{:S(2)}) async-start(), calls=%async_computation.51 | async-start | bytes 1572864 | tf_op jit(solution)/shard_map/reduce_scatter | solution.py:93
  2780.1 360.0 %reduce-scatter.49.cloned.1.call-start = ((), (), s32[]{:S(2)}) async-start(), calls=%async_computation.50 | async-start | bytes 1572864 | tf_op jit(solution)/shard_map/reduce_scatter | solution.py:93
  2788.5 418.1 %reduce-scatter.41.cloned.1.call-start = ((), (), s32[]{:S(2)}) async-start(), calls=%async_computation.46 | async-start | bytes 1114112 | tf_op jit(solution)/shard_map/reduce_scatter | solution.py:125
  2791.6 491.5 %reduce-scatter.43.cloned.1.call-start = ((), (), s32[]{:S(2)}) async-start(), calls=%async_computation.47 | async-start | bytes 1114112 | tf_op jit(solution)/shard_map/reduce_scatter | solution.py:125
  2794.6 510.0 %reduce-scatter.35.cloned.1.call-start = ((), (), s32[]{:S(2)}) async-start(), calls=%async_computation.43 | async-start | bytes 1572864 | tf_op jit(solution)/shard_map/reduce_scatter | solution.py:453
  2921.6 395.1 %reduce-scatter.31.cloned.1.call-start = ((), (), s32[]{:S(2)}) async-start(), calls=%async_computation.40 | async-start | bytes 1572864 | tf_op jit(solution)/shard_map/reduce_scatter | solution.py:453
  2925.6 461.8 %reduce-scatter.37.cloned.1.call-start = ((), (), s32[]{:S(2)}) async-start(), calls=%async_computation.44 | async-start | bytes 2228224 | tf_op jit(solution)/shard_map/reduce_scatter | solution.py:122
  2929.7 537.7 %reduce-scatter.39.cloned.1.call-start = ((), (), s32[]{:S(2)}) async-start(), calls=%async_computation.45 | async-start | bytes 2228224 | tf_op jit(solution)/shard_map/reduce_scatter | solution.py:122
  2933.9 382.8 %copy-start.70 = (f32[1024]{0:T(1024)S(1)}, f32[1024]{0:T(1024)}, u32[]{:S(2)}) copy-start(f32[1024]{0:T(1024)} %copy-done.69) | copy-start | bytes 12292
  2933.9 382.8 %copy-start.74 = (f32[256]{0:T(256)S(1)}, f32[256]{0:T(256)}, u32[]{:S(2)}) copy-start(f32[256]{0:T(256)} %copy-done.73) | copy-start | bytes 3076
  2933.9 382.8 %copy-start.76 = (f32[256]{0:T(256)S(1)}, f32[256]{0:T(256)}, u32[]{:S(2)}) copy-start(f32[256]{0:T(256)} %copy-done.75) | copy-start | bytes 3076
  2933.9 418.8 %copy-start.21 = (f32[256,1024]{1,0:T(8,128)S(1)}, f32[256,1024]{1,0:T(8,128)}, u32[]{:S(2)}) copy-start(f32[256,1024]{1,0:T(8,128)} %get-tuple-element.1275) | copy-start | bytes 3145732
  2933.9 418.8 %copy-start.84 = (f32[256]{0:T(256)S(1)}, f32[256]{0:T(256)}, u32[]{:S(2)}) copy-start(f32[256]{0:T(256)} %get-tuple-element.1359) | copy-start | bytes 3076
  2933.9 418.8 %copy-start.85 = (f32[256]{0:T(256)S(1)}, f32[256]{0:T(256)}, u32[]{:S(2)}) copy-start(f32[256]{0:T(256)} %get-tuple-element.1377) | copy-start | bytes 3076
  (170 other events, 2852.0 us)
Sparse Core Ops, SparseCore 0:
  10.8 55.2 all-gather.13
  68.2 9.9 all-gather.11
  80.4 10.1 all-gather.21
  137.3 82.1 all-gather.17
  222.7 77.9 all-gather.15
  303.3 54.5 all-gather.19
  360.6 75.6 all-gather.25
  439.6 77.9 all-gather.23
  577.1 9.7 reduce-scatter.24
  861.4 9.7 reduce-scatter.26
  2147.0 8.3 all-gather.29
  2157.4 10.1 all-gather.27
  2170.4 8.5 reduce-scatter.46
  2181.0 8.5 reduce-scatter.44
  2466.7 180.0 reduce-scatter.32
  2735.6 179.9 reduce-scatter.28
  2918.2 62.6 reduce-scatter.62
  2983.6 72.3 reduce-scatter.60
  3058.8 19.6 reduce-scatter.58
  3080.7 9.6 reduce-scatter.56
  3093.2 9.6 reduce-scatter.54
  3105.3 9.6 reduce-scatter.52
  3117.8 9.6 reduce-scatter.50
  3130.3 9.6 reduce-scatter.48
  3142.3 64.2 reduce-scatter.40
  3208.8 74.1 reduce-scatter.42
  3285.2 19.4 reduce-scatter.34
  3306.9 9.6 reduce-scatter.30
  3319.0 68.4 reduce-scatter.36
  3389.6 77.7 reduce-scatter.38
where the time goes:
time: 3500 us; the launch traced here: 3480 us
  waiting for transfers between devices  1520 us (43%)
  matrix products  964 us (28%)
  other arithmetic  346 us (10%)
  blocking collectives  305 us (9%)
  local copies, waits for them, and re-layouts  268 us (8%)
  starting transfers between devices  50.2 us (1%)
    all_to_all x2, waiting for transfers between devices, on_device(): lax.all_to_all(jnp.swapaxes(grad_copy.reshape(experts_here, ep_count, cap...  240 us
    all_to_all x2, waiting for transfers between devices, on_device(): lax.all_to_all(send_rows, 'ep', split_axis=0, concat_axis=0, tiled=True)  219 us
    all_to_all x2, waiting for transfers between devices, on_device(): lax.all_to_all(grad_slots, 'ep', split_axis=0, concat_axis=0, tiled=True)  203 us
    dot_general x64, matrix products, block_scores(): jnp.einsum('hrd,khd->hrk', q_grouped, key_blk, preferred_element_type=jnp...  198 us
    all_gather x1, blocking collectives, on_device(): lax.all_gather(w_router, 'ep', axis=0, tiled=True)  162 us
    reduce_sum x32, other arithmetic, forward_step(): run_sum = run_sum * factor + jnp.sum(weights, -1)  150 us
    reduce_scatter x2, waiting for transfers between devices, reduce_grads(): lax.psum_scatter(grad_outw.astype(jnp.bfloat16), 'ep', scatter_dimension=...  139 us
    dot_general x32, matrix products, forward_step(): jnp.einsum('hrk,khd->hrd', weights.astype(jnp.bfloat16), value_blk, prefe...  138 us
  transfers between devices with their start and end apart: 38, of which 25 were waited for; matrix products, arithmetic and copies ran while one was open for 41% of the time, Pallas kernels for 0%

commit v1 on v0

--- a/solution.py
+++ b/solution.py
@@ -1,17 +1,24 @@
+import functools
 import math
 
 import jax
 import jax.numpy as jnp
 from jax import lax
+from jax.experimental import pallas as pl
+from jax.experimental.pallas import tpu as pltpu
 from jax.sharding import PartitionSpec as P
 
 HEAD_DIM = 64
 PIECE = 256
+PLANE = 4
+LANES = 128
+MIB = 1 << 20
 
 
 EPS = 1e-06
 THETA = 10000.0
 NEG = -1e30
+EXP_SCALE = HEAD_DIM ** (-0.5) * math.log2(math.e)
 
 
 def rms_scale(values):
@@ -147,7 +154,7 @@
     )
 
 
-def on_device(
+def on_device_general(
     tokens,
     gain_attn,
     w_query,
@@ -489,6 +496,768 @@
     )
 
 
+def dot_f32(left, right, left_dim, right_dim):
+    return lax.dot_general(
+        left, right, (((left_dim,), (right_dim,)), ((), ())), preferred_element_type=jnp.float32
+    )
+
+
+def at_rows(first_row, count):
+    return pl.ds(pl.multiple_of(first_row, count), count)
+
+
+def whole_vmem():
+    return pl.BlockSpec(memory_space=pltpu.VMEM)
+
+
+def attend_kernel(
+    tp_ref, own_ref, other_ref, limit_ref, out_ref, out_f_ref, log_ref, keys, queries, values,
+    *, query_block, key_block
+):
+    core = tp_ref[0]
+    blocks, _, rows = own_ref.shape
+    seq_len = blocks * rows
+
+    def fill(block, _):
+        cols = at_rows(block * rows, rows)
+        first, second = own_ref[block, HEAD_DIM:, :], other_ref[block]
+        key_rows = jnp.where(core == 0, first, second)
+        queries[:, cols] = own_ref[block, :HEAD_DIM, :]
+        values[:HEAD_DIM, cols] = jnp.where(core == 0, second, first)
+        values[HEAD_DIM:, cols] = jnp.ones((16, rows), jnp.bfloat16)
+        keys[cols, :] = key_rows.astype(jnp.float32).T.astype(jnp.bfloat16)
+        return 0
+
+    lax.fori_loop(0, blocks, fill, 0)
+
+    def update(scores, value_cols, carry):
+        highest, total = carry
+        new_highest = jnp.maximum(highest, jnp.max(scores, 0, keepdims=True) * EXP_SCALE)
+        weights = jnp.exp2(scores * EXP_SCALE - new_highest).astype(jnp.bfloat16)
+        factor = jnp.exp2(highest - new_highest)
+        return (new_highest, total * factor + dot_f32(value_cols, weights, 1, 0))
+
+    def query_step(index, _):
+        first = index * query_block
+        cols = at_rows(first, query_block)
+        query = queries[:, cols]
+        limit = limit_ref[:, cols]
+
+        def full_step(step, carry):
+            key_cols = at_rows(step * key_block, key_block)
+            return update(
+                dot_f32(keys[key_cols, :], query, 1, 0), values[:, key_cols], carry
+            )
+
+        carry = lax.fori_loop(
+            0,
+            first // key_block,
+            full_step,
+            (
+                jnp.full((1, query_block), NEG, jnp.float32),
+                jnp.zeros((HEAD_DIM + 16, query_block), jnp.float32),
+            ),
+        )
+        scores = dot_f32(keys[cols, :], query, 1, 0)
+        key_pos = first + lax.broadcasted_iota(jnp.int32, scores.shape, 0)
+        highest, total = update(
+            jnp.where(key_pos <= limit, scores, NEG), values[:, cols], carry
+        )
+        last = query_block - rows
+        after = at_rows(jnp.minimum(first + query_block, seq_len - rows), rows)
+        scores = dot_f32(keys[after, :], query[:, last:], 1, 0)
+        key_pos = first + query_block + lax.broadcasted_iota(jnp.int32, scores.shape, 0)
+        tail_highest, tail_total = update(
+            jnp.where(key_pos <= limit[:, last:], scores, NEG),
+            values[:, after],
+            (highest[:, last:], total[:, last:]),
+        )
+        per_step = query_block // rows
+        for piece in range(per_step):
+            here = slice(piece * rows, (piece + 1) * rows)
+            high, both = highest[:, here], total[:, here]
+            if piece == per_step - 1:
+                high, both = tail_highest, tail_total
+            row_sum = both[HEAD_DIM : HEAD_DIM + 1, :]
+            result = both[:HEAD_DIM, :] / row_sum
+            block = index * per_step + piece
+            out_ref[block] = result.astype(jnp.bfloat16)
+            out_f_ref[block] = result
+            log_ref[:, at_rows(first + piece * rows, rows)] = high + jnp.log2(row_sum)
+        return 0
+
+    lax.fori_loop(0, seq_len // query_block, query_step, 0)
+
+
+def attend(core, own, other, limit):
+    blocks, _, rows = own.shape
+    seq_len = blocks * rows
+    query_block = math.gcd(seq_len, 2048)
+    key_block = math.gcd(query_block, 1024)
+    block_shape = (blocks, HEAD_DIM, rows)
+    return pl.pallas_call(
+        functools.partial(attend_kernel, query_block=query_block, key_block=key_block),
+        out_shape=(
+            jax.ShapeDtypeStruct(block_shape, jnp.bfloat16),
+            jax.ShapeDtypeStruct(block_shape, jnp.float32),
+            jax.ShapeDtypeStruct((1, seq_len), jnp.float32),
+        ),
+        in_specs=[pl.BlockSpec(memory_space=pltpu.SMEM)] + [whole_vmem()] * 3,
+        out_specs=(whole_vmem(),) * 3,
+        scratch_shapes=[
+            pltpu.VMEM((seq_len, HEAD_DIM), jnp.bfloat16),
+            pltpu.VMEM((HEAD_DIM, seq_len), jnp.bfloat16),
+            pltpu.VMEM((HEAD_DIM + 16, seq_len), jnp.bfloat16),
+        ],
+        cost_estimate=pl.CostEstimate(
+            flops=seq_len * seq_len * 512, bytes_accessed=8 * MIB, transcendentals=0
+        ),
+        compiler_params=pltpu.CompilerParams(vmem_limit_bytes=56 * MIB),
+        name="attend",
+    )(core, own, other, limit)
+
+
+def three_parts(values):
+    high = values.astype(jnp.bfloat16).astype(jnp.float32)
+    middle = (values - high).astype(jnp.bfloat16).astype(jnp.float32)
+    low = values - high - middle
+    row = lax.broadcasted_iota(jnp.int32, (16, values.shape[1]), 0)
+    parts = jnp.where(
+        row == 0, high, jnp.where(row == 1, middle, jnp.where(row == 2, low, 0.0))
+    )
+    return parts.astype(jnp.bfloat16)
+
+
+def attend_back_kernel(
+    tp_ref, own_ref, other_ref, limit_ref, out_f_ref, log_ref, grad_ref,
+    grad_q_ref, keep_ref, send_ref,
+    keys, keys_t, queries_t, queries, values, grads_t, grads, grad_k, grad_v,
+    *, query_block, key_block
+):
+    core = tp_ref[0]
+    blocks, _, rows = own_ref.shape
+    seq_len = blocks * rows
+
+    def fill(block, _):
+        cols = at_rows(block * rows, rows)
+        first, second = own_ref[block, HEAD_DIM:, :], other_ref[block]
+        key_rows = jnp.where(core == 0, first, second)
+        value_rows = jnp.where(core == 0, second, first)
+        query, grad = own_ref[block, :HEAD_DIM, :], grad_ref[block]
+        grad_f = grad.astype(jnp.float32)
+        delta = jnp.sum(grad_f * out_f_ref[block], 0, keepdims=True)
+        ones = jnp.ones((16, rows), jnp.float32)
+        queries_t[:HEAD_DIM, cols] = query
+        queries_t[HEAD_DIM:, cols] = three_parts(log_ref[:, cols] * (-1.0 / EXP_SCALE))
+        queries[cols, :] = query.astype(jnp.float32).T.astype(jnp.bfloat16)
+        keys_t[:, cols] = key_rows
+        keys[cols, :] = (
+            jnp.concatenate([key_rows.astype(jnp.float32), ones], 0).T.astype(jnp.bfloat16)
+        )
+        values[cols, :] = (
+            jnp.concatenate([value_rows.astype(jnp.float32), ones], 0).T.astype(jnp.bfloat16)
+        )
+        grads_t[:HEAD_DIM, cols] = grad
+        grads_t[HEAD_DIM:, cols] = three_parts(-delta)
+        grads[cols, :] = grad_f.T.astype(jnp.bfloat16)
+        grad_k[cols, :] = jnp.zeros((rows, HEAD_DIM), jnp.float32)
+        grad_v[cols, :] = jnp.zeros((rows, HEAD_DIM), jnp.float32)
+        return 0
+
+    lax.fori_loop(0, blocks, fill, 0)
+
+    def tile(operands, key_cols, allowed):
+        query_t, query, grad_t, grad = operands
+        probs = jnp.exp2(dot_f32(keys[key_cols, :], query_t, 1, 0) * EXP_SCALE)
+        if allowed is not None:
+            probs = jnp.where(allowed, probs, 0.0)
+        grad_scores = (probs * dot_f32(values[key_cols, :], grad_t, 1, 0)).astype(jnp.bfloat16)
+        grad_v[key_cols, :] += dot_f32(probs.astype(jnp.bfloat16), grad, 1, 0)
+        grad_k[key_cols, :] += dot_f32(grad_scores, query, 1, 0)
+        return dot_f32(keys_t[:, key_cols], grad_scores, 1, 0)
+
+    def query_step(index, _):
+        first = index * query_block
+        cols = at_rows(first, query_block)
+        limit = limit_ref[:, cols]
+        operands = (queries_t[:, cols], queries[cols, :], grads_t[:, cols], grads[cols, :])
+
+        def full_step(step, total):
+            return total + tile(operands, at_rows(step * key_block, key_block), None)
+
+        total = lax.fori_loop(
+            0, first // key_block, full_step, jnp.zeros((HEAD_DIM, query_block), jnp.float32)
+        )
+        key_pos = first + lax.broadcasted_iota(jnp.int32, (query_block, query_block), 0)
+        total = total + tile(operands, cols, key_pos <= limit)
+        last = query_block - rows
+        after = at_rows(jnp.minimum(first + query_block, seq_len - rows), rows)
+        key_pos = first + query_block + lax.broadcasted_iota(jnp.int32, (rows, rows), 0)
+        query_t, query, grad_t, grad = operands
+        extra = tile(
+            (query_t[:, last:], query[last:], grad_t[:, last:], grad[last:]),
+            after,
+            key_pos <= limit[:, last:],
+        )
+        per_step = query_block // rows
+        for piece in range(per_step):
+            here = total[:, piece * rows : (piece + 1) * rows]
+            if piece == per_step - 1:
+                here = here + extra
+            grad_q_ref[index * per_step + piece] = (here * HEAD_DIM ** (-0.5)).astype(
+                jnp.bfloat16
+            )
+        return 0
+
+    lax.fori_loop(0, seq_len // query_block, query_step, 0)
+
+    def finish(block, _):
+        cols = at_rows(block * rows, rows)
+        key_part = (grad_k[cols, :] * HEAD_DIM ** (-0.5)).T
+        value_part = grad_v[cols, :].T
+        keep_ref[block] = jnp.where(core == 0, key_part, value_part)
+        send_ref[block] = jnp.where(core == 0, value_part, key_part).astype(jnp.bfloat16)
+        return 0
+
+    lax.fori_loop(0, blocks, finish, 0)
+
+
+def attend_back(core, own, other, limit, out_f, log_total, grad):
+    blocks, _, rows = own.shape
+    seq_len = blocks * rows
+    query_block = math.gcd(seq_len, 1024)
+    key_block = math.gcd(query_block, 1024)
+    block_shape = (blocks, HEAD_DIM, rows)
+    wide = HEAD_DIM + 16
+    return pl.pallas_call(
+        functools.partial(attend_back_kernel, query_block=query_block, key_block=key_block),
+        out_shape=(
+            jax.ShapeDtypeStruct(block_shape, jnp.bfloat16),
+            jax.ShapeDtypeStruct(block_shape, jnp.float32),
+            jax.ShapeDtypeStruct(block_shape, jnp.bfloat16),
+        ),
+        in_specs=[pl.BlockSpec(memory_space=pltpu.SMEM)] + [whole_vmem()] * 6,
+        out_specs=(whole_vmem(),) * 3,
+        scratch_shapes=[
+            pltpu.VMEM((seq_len, wide), jnp.bfloat16),
+            pltpu.VMEM((HEAD_DIM, seq_len), jnp.bfloat16),
+            pltpu.VMEM((wide, seq_len), jnp.bfloat16),
+            pltpu.VMEM((seq_len, HEAD_DIM), jnp.bfloat16),
+            pltpu.VMEM((seq_len, wide), jnp.bfloat16),
+            pltpu.VMEM((wide, seq_len), jnp.bfloat16),
+            pltpu.VMEM((seq_len, HEAD_DIM), jnp.bfloat16),
+            pltpu.VMEM((seq_len, HEAD_DIM), jnp.float32),
+            pltpu.VMEM((seq_len, HEAD_DIM), jnp.float32),
+        ],
+        cost_estimate=pl.CostEstimate(
+            flops=seq_len * seq_len * 1024, bytes_accessed=12 * MIB, transcendentals=0
+        ),
+        compiler_params=pltpu.CompilerParams(vmem_limit_bytes=60 * MIB),
+        name="attend_back",
+    )(core, own, other, limit, out_f, log_total, grad)
+
+
+def experts_kernel(
+    tp_ref, x_ref, dy_ref, gate_ref, w_gate_ref, w_up_ref, w_down_ref, keep_in_ref, send_in_ref,
+    mix_ref, grad_x_ref, grad_gate_ref, keep_ref, send_ref,
+    x_t, dy_t, mix_sum, grad_x_sum, grad_w,
+    *, tile_rows, first_call
+):
+    expert, expert_count = pl.program_id(0), pl.num_programs(0)
+    rows, width = x_ref.shape
+    half = width // 2
+    core = tp_ref[0]
+    tiles = rows // tile_rows
+
+    @pl.when(expert == 0)
+    def _():
+        def turn(index, _):
+            here = at_rows(index * tile_rows, tile_rows)
+            x_t[:, here] = x_ref[here, :].T
+            dy_t[:, here] = dy_ref[here, :].T
+            mix_sum[here, :] = jnp.zeros((tile_rows, width), jnp.float32)
+            grad_x_sum[here, :] = jnp.zeros((tile_rows, width), jnp.float32)
+            return 0
+
+        lax.fori_loop(0, tiles, turn, 0)
+
+    if first_call:
+        grad_w[...] = jnp.zeros_like(grad_w)
+    else:
+        for part in range(2):
+            grad_w[part] = jnp.where(core == part, keep_in_ref[0], send_in_ref[0]).astype(
+                jnp.float32
+            )
+    w_gate, w_up, w_down = w_gate_ref[0], w_up_ref[0], w_down_ref[0]
+
+    def tile(index, _):
+        here = at_rows(index * tile_rows, tile_rows)
+        x = x_ref[here, :]
+        dy = dy_ref[here, :].astype(jnp.float32)
+        gate = gate_ref[0, here, :]
+        gate_pre = dot_f32(x, w_gate, 1, 0)
+        up_pre = dot_f32(x, w_up, 1, 0)
+        sigmoid_val = 1.0 / (1.0 + jnp.exp(-gate_pre))
+        silu_val = gate_pre * sigmoid_val
+        hidden = (silu_val * up_pre).astype(jnp.bfloat16)
+        out = dot_f32(hidden, w_down, 1, 0).astype(jnp.bfloat16).astype(jnp.float32)
+        grad_gate_ref[0, here, :] = jnp.sum(out * dy, 1, keepdims=True)
+        mix_sum[here, :] += gate * out
+        grad_out = (gate * dy).astype(jnp.bfloat16)
+        grad_hidden = dot_f32(grad_out, w_down, 1, 1)
+        slope = sigmoid_val * (1.0 + gate_pre * (1.0 - sigmoid_val))
+        grad_gate_pre = (grad_hidden * up_pre * slope).astype(jnp.bfloat16)
+        grad_up_pre = (grad_hidden * silu_val).astype(jnp.bfloat16)
+        grad_copy = dot_f32(grad_gate_pre, w_gate, 1, 1) + dot_f32(grad_up_pre, w_up, 1, 1)
+        grad_x_sum[here, :] += grad_copy.astype(jnp.bfloat16).astype(jnp.float32)
+        grad_out_t = (dy_t[:, here].astype(jnp.float32) * gate.T).astype(jnp.bfloat16)
+        for part in range(2):
+            cut = slice(part * half, (part + 1) * half)
+            turned = x_t[cut, here]
+            grad_w[part, 0] += dot_f32(turned, grad_gate_pre, 1, 0)
+            grad_w[part, 1] += dot_f32(turned, grad_up_pre, 1, 0)
+            grad_w[part, 2] += dot_f32(grad_out_t[cut], hidden, 1, 0)
+        return 0
+
+    lax.fori_loop(0, tiles, tile, 0)
+    keep_ref[0] = grad_w[core].astype(jnp.bfloat16)
+    send_ref[0] = grad_w[1 - core].astype(jnp.bfloat16)
+
+    @pl.when(expert == expert_count - 1)
+    def _():
+        mix_ref[...] = mix_sum[...].astype(jnp.bfloat16)
+        grad_x_ref[...] = grad_x_sum[...].astype(jnp.bfloat16)
+
+
+def experts(core, x, dy, gates, w_gate, w_up, w_down, before):
+    count, width, hidden_width = w_gate.shape
+    rows = x.shape[0]
+    half = width // 2
+    first_call = before is None
+    if first_call:
+        before = (jnp.zeros((1, 3, 16, hidden_width), jnp.bfloat16),) * 2
+        before_spec = pl.BlockSpec((1, 3, 16, hidden_width), lambda expert: (0, 0, 0, 0))
+    else:
+        before_spec = pl.BlockSpec((1, 3, half, hidden_width), lambda expert: (expert, 0, 0, 0))
+    row_spec = pl.BlockSpec((rows, width), lambda expert: (0, 0))
+    gate_spec = pl.BlockSpec((1, rows, 1), lambda expert: (expert, 0, 0))
+    grad_spec = pl.BlockSpec((1, 3, half, hidden_width), lambda expert: (expert, 0, 0, 0))
+    in_spec = pl.BlockSpec((1, width, hidden_width), lambda expert: (expert, 0, 0))
+    out_spec = pl.BlockSpec((1, hidden_width, width), lambda expert: (expert, 0, 0))
+    grad_shape = jax.ShapeDtypeStruct((count, 3, half, hidden_width), jnp.bfloat16)
+    row_shape = jax.ShapeDtypeStruct((rows, width), jnp.bfloat16)
+    return pl.pallas_call(
+        functools.partial(
+            experts_kernel, tile_rows=math.gcd(rows, 512), first_call=first_call
+        ),
+        grid=(count,),
+        out_shape=(
+            row_shape,
+            row_shape,
+            jax.ShapeDtypeStruct((count, rows, 1), jnp.float32),
+            grad_shape,
+            grad_shape,
+        ),
+        in_specs=[
+            pl.BlockSpec(memory_space=pltpu.SMEM),
+            row_spec,
+            row_spec,
+            gate_spec,
+            in_spec,
+            in_spec,
+            out_spec,
+            before_spec,
+            before_spec,
+        ],
+        out_specs=(row_spec, row_spec, gate_spec, grad_spec, grad_spec),
+        scratch_shapes=[
+            pltpu.VMEM((width, rows), jnp.bfloat16),
+            pltpu.VMEM((width, rows), jnp.bfloat16),
+            pltpu.VMEM((rows, width), jnp.float32),
+            pltpu.VMEM((rows, width), jnp.float32),
+            pltpu.VMEM((2, 3, half, hidden_width), jnp.float32),
+        ],
+        cost_estimate=pl.CostEstimate(
+            flops=count * rows * width * hidden_width * 18,
+            bytes_accessed=count * width * hidden_width * 12,
+            transcendentals=0,
+        ),
+        compiler_params=pltpu.CompilerParams(
+            vmem_limit_bytes=60 * MIB, dimension_semantics=("arbitrary",)
+        ),
+        name="experts",
+    )(core, x, dy, gates, w_gate, w_up, w_down, *before)
+
+
+def flip(values, bits):
+    count = lax.axis_size("ep")
+    return lax.ppermute(values, "ep", [(index, index ^ bits) for index in range(count)])
+
+
+def swap_cores(values):
+    return lax.ppermute(values, "tp", [(0, 1), (1, 0)])
+
+
+def every_device(values):
+    return lax.all_to_all(values, ("ep", "tp"), 0, 0, tiled=True)
+
+
+def head_tables(first_pos, rows):
+    positions = first_pos + jnp.arange(rows, dtype=jnp.int32)
+    halves = jnp.arange(HEAD_DIM // 2, dtype=jnp.float32)
+    freqs = THETA ** (-2.0 * halves / HEAD_DIM)
+    angles = freqs[:, None] * positions.astype(jnp.float32)[None, :]
+    turned = jnp.array([[True, True], [True, False]])[:, :, None, None]
+    cosine = jnp.where(turned, jnp.cos(angles), 1.0)
+    sine = jnp.where(turned, jnp.sin(angles), 0.0)
+    return cosine, sine
+
+
+def rotate_heads(heads, cosine, sine):
+    first_half, second_half = heads[..., 0, :, :], heads[..., 1, :, :]
+    return jnp.stack(
+        [first_half * cosine - second_half * sine, second_half * cosine + first_half * sine], -3
+    )
+
+
+def paired_layout(ep_count, tp_count, micro_count, slice_rows, width, q_cols, kv_cols, experts_here):
+    group = q_cols // kv_cols
+    kv_heads = kv_cols * tp_count // HEAD_DIM
+    return (
+        tp_count == 2
+        and group == 2
+        and ep_count == micro_count * kv_heads
+        and ep_count == PLANE * PLANE
+        and experts_here == 1
+        and slice_rows >= PIECE
+        and slice_rows % PIECE == 0
+        and width % (2 * LANES) == 0
+    )
+
+
+def on_device_paired(
+    tokens,
+    gain_attn,
+    w_query,
+    w_key,
+    w_value,
+    w_output,
+    gain_moe,
+    w_router,
+    w_gate,
+    w_up,
+    w_down,
+    routes,
+    piece_starts,
+    cotangent,
+):
+    ep_count = lax.axis_size("ep")
+    tp_count = lax.axis_size("tp")
+    ep_index, tp_index = lax.axis_index("ep"), lax.axis_index("tp")
+    micro_count, rows, width = tokens.shape
+    devices = ep_count * tp_count
+    seq_len = rows * devices
+    all_rows = micro_count * rows
+    shard = gain_attn.shape[0]
+    q_cols, kv_cols = w_query.shape[1], w_key.shape[1]
+    kv_here = kv_cols // HEAD_DIM
+    half_cols = q_cols + 2 * kv_cols
+    out_cols = w_output.shape[0]
+    columns = ep_count // PLANE
+    experts_all = ep_count
+    core = tp_index.astype(jnp.int32).reshape(1)
+
+    head_cols = jnp.stack(
+        [
+            w_query.reshape(shard, kv_here, 2, HEAD_DIM),
+            jnp.stack(
+                [
+                    w_key.reshape(shard, kv_here, HEAD_DIM),
+                    w_value.reshape(shard, kv_here, HEAD_DIM),
+                ],
+                2,
+            ),
+        ],
+        3,
+    ).reshape(shard, half_cols)
+    small = jnp.concatenate([w_router, gain_attn[:, None], gain_moe[:, None]], 1)
+    small = jnp.pad(small, ((0, 0), (0, LANES - small.shape[1])))
+    packed = jnp.concatenate([head_cols, w_output.T, small], 1)
+    gathered = lax.all_gather(packed, ("ep", "tp"), axis=0, tiled=False).reshape(
+        ep_count, tp_count, shard, -1
+    )
+    w_heads = [gathered[:, part, :, :half_cols].reshape(width, half_cols) for part in range(2)]
+    w_out_t = jnp.concatenate(
+        [
+            gathered[:, part, :, half_cols : half_cols + out_cols].reshape(width, out_cols)
+            for part in range(2)
+        ],
+        1,
+    )
+    small_all = gathered[:, 0, :, half_cols + out_cols :].reshape(width, LANES)
+    w_route_full = small_all[:, :experts_all]
+    gain_one = small_all[:, experts_all].astype(jnp.float32)
+    gain_two = small_all[:, experts_all + 1].astype(jnp.float32)
+
+    half = width // 2
+    expert_half = jnp.where(
+        tp_index == 0,
+        jnp.concatenate([w_gate[0, :half], w_up[0, :half], w_down[0, :, :half].T], 0),
+        jnp.concatenate([w_gate[0, half:], w_up[0, half:], w_down[0, :, half:].T], 0),
+    )
+    column_halves = jnp.stack([flip(expert_half, PLANE * step) for step in range(1, columns)])
+    column_others = swap_cores(column_halves)
+    low = jnp.where(tp_index == 0, column_halves, column_others)
+    high = jnp.where(tp_index == 0, column_others, column_halves)
+    hidden_width = w_gate.shape[2]
+    low = low.reshape(columns - 1, 3, half, hidden_width)
+    high = high.reshape(columns - 1, 3, half, hidden_width)
+    gate_cols = jnp.concatenate([w_gate, jnp.concatenate([low[:, 0], high[:, 0]], 1)], 0)
+    up_cols = jnp.concatenate([w_up, jnp.concatenate([low[:, 1], high[:, 1]], 1)], 0)
+    down_cols = jnp.concatenate(
+        [
+            w_down,
+            jnp.concatenate([jnp.swapaxes(low[:, 2], 1, 2), jnp.swapaxes(high[:, 2], 1, 2)], 2),
+        ],
+        0,
+    )
+
+    dy_plane = [
+        jnp.concatenate(
+            [cotangent[micro]] + [flip(cotangent[micro], step) for step in range(1, PLANE)], 0
+        )
+        for micro in range(micro_count)
+    ]
+
+    x_rows = tokens.reshape(all_rows, width).astype(jnp.float32)
+    scale_one = rms_scale(x_rows)
+    normed = (x_rows * scale_one * gain_one).astype(jnp.bfloat16)
+    device_index = ep_index * tp_count + tp_index
+    cosine, sine = head_tables(device_index * rows, rows)
+    sent = []
+    for micro in range(micro_count):
+        here = normed[micro * rows : (micro + 1) * rows]
+        for part in range(tp_count):
+            heads = dot_f32(w_heads[part], here, 0, 1).reshape(
+                kv_here, 2, 2, 2, HEAD_DIM // 2, rows
+            )
+            sent.append(
+                rotate_heads(heads, cosine, sine)
+                .astype(jnp.bfloat16)
+                .reshape(kv_here * 2, 2 * HEAD_DIM, rows)
+            )
+    own = every_device(jnp.concatenate(sent, 0))
+    other = swap_cores(own[:, HEAD_DIM:, :])
+
+    micro_here = ep_index // (ep_count // micro_count)
+    starts = lax.dynamic_index_in_dim(piece_starts, micro_here, 0, keepdims=False)
+    all_pos = jnp.arange(seq_len, dtype=jnp.int32)[None, :]
+    inside = (all_pos >= starts[:, None]) & (all_pos < starts[:, None] + PIECE)
+    piece_last = jnp.max(jnp.where(inside, starts[:, None] + (PIECE - 1), -1), 0, keepdims=True)
+    limit = jnp.maximum(all_pos, piece_last).astype(jnp.int32)
+    out_b, out_f, log_total = attend(core, own, other, limit)
+    attended_t = every_device(out_b).reshape(micro_count, out_cols * tp_count, rows)
+
+    attn_rows = jnp.concatenate(
+        [dot_f32(attended_t[micro], w_out_t, 0, 1) for micro in range(micro_count)], 0
+    )
+    resid = x_rows + attn_rows
+    scale_two = rms_scale(resid)
+    normed_two = (resid * scale_two * gain_two).astype(jnp.bfloat16)
+    plane_x = [
+        jnp.concatenate(
+            [normed_two[micro * rows : (micro + 1) * rows]]
+            + [
+                flip(normed_two[micro * rows : (micro + 1) * rows], step)
+                for step in range(1, PLANE)
+            ],
+            0,
+        )
+        for micro in range(micro_count)
+    ]
+    logits = jnp.dot(normed_two, w_route_full, preferred_element_type=jnp.float32)
+    route_rows = routes.reshape(all_rows, -1)
+    expert_ids = jnp.arange(experts_all, dtype=jnp.int32)
+    route_hot = (route_rows[:, :, None] == expert_ids[None, None, :]).astype(jnp.float32)
+    picked = jnp.sum(route_hot * logits[:, None, :], -1)
+    highest = jnp.max(picked, -1, keepdims=True)
+    raised = jnp.exp(picked - highest)
+    gates = raised / jnp.sum(raised, -1, keepdims=True)
+
+    level, spot = ep_index // PLANE, ep_index % PLANE
+    slot_ids = jnp.stack(
+        [
+            jnp.stack([(level ^ up) * PLANE + (spot ^ step) for up in range(columns)])
+            for step in range(PLANE)
+        ]
+    )
+    slot_hot = (route_rows[None, None, :, :] == slot_ids[:, :, None, None]).astype(jnp.float32)
+    slot_gates = jnp.sum(slot_hot * gates[None, None], -1)
+    plane_gates = jnp.stack(
+        [slot_gates[0]] + [flip(slot_gates[step], step) for step in range(1, PLANE)], 1
+    ).reshape(columns, PLANE, micro_count, rows)
+
+    before = None
+    mixes, grads_x, grads_gate = [], [], []
+    for micro in range(micro_count):
+        mix, grad_x, grad_gate, *before = experts(
+            core,
+            plane_x[micro],
+            dy_plane[micro],
+            plane_gates[:, :, micro].reshape(columns, PLANE * rows, 1),
+            gate_cols,
+            up_cols,
+            down_cols,
+            before,
+        )
+
+        def back_home(parts):
+            parts = parts.reshape(PLANE, rows, width)
+            total = parts[0].astype(jnp.float32)
+            for step in range(1, PLANE):
+                total = total + flip(parts[step], step).astype(jnp.float32)
+            return total
+
+        mixes.append(back_home(mix))
+        grads_x.append(back_home(grad_x))
+        grad_gate = grad_gate.reshape(columns, PLANE, rows)
+        grads_gate.append(
+            jnp.stack(
+                [grad_gate[:, 0]]
+                + [flip(grad_gate[:, step], step) for step in range(1, PLANE)]
+            )
+        )
+    keep_w, send_w = before
+    column_w = (keep_w.astype(jnp.float32) + swap_cores(send_w).astype(jnp.float32)).astype(
+        jnp.bfloat16
+    )
+    grad_expert_w = column_w[0].astype(jnp.float32)
+    for step in range(1, columns):
+        grad_expert_w = grad_expert_w + flip(column_w[step], PLANE * step).astype(jnp.float32)
+
+    mixed = (resid + jnp.concatenate(mixes, 0)).astype(jnp.bfloat16)
+    grad_out = cotangent.reshape(all_rows, width).astype(jnp.float32)
+    slot_grads = jnp.concatenate(grads_gate, 2)
+    grad_gates = jnp.sum(slot_hot * slot_grads[:, :, :, None], (0, 1))
+    grad_spread = gates * (grad_gates - jnp.sum(gates * grad_gates, -1, keepdims=True))
+    grad_logits = jnp.sum(grad_spread[:, :, None] * route_hot, 1).astype(jnp.bfloat16)
+    grad_normed_two = jnp.concatenate(grads_x, 0) + dot_f32(grad_logits, w_route_full, 1, 1)
+    grad_route = dot_f32(normed_two, grad_logits, 0, 0)
+    gained_two = grad_normed_two * gain_two
+    grad_gain_two = jnp.sum(grad_normed_two * resid * scale_two, 0)
+    grad_resid = (
+        grad_out
+        + scale_two * gained_two
+        - resid * scale_two**3 * jnp.mean(resid * gained_two, -1, keepdims=True)
+    )
+    grad_branch = grad_resid.astype(jnp.bfloat16)
+    grad_att = jnp.concatenate(
+        [
+            dot_f32(w_out_t, grad_branch[micro * rows : (micro + 1) * rows], 0, 1).astype(
+                jnp.bfloat16
+            )
+            for micro in range(micro_count)
+        ],
+        0,
+    ).reshape(devices, HEAD_DIM, rows)
+    grad_heads = every_device(grad_att)
+    grad_outw = sum(
+        dot_f32(grad_branch[micro * rows : (micro + 1) * rows], attended_t[micro], 0, 1)
+        for micro in range(micro_count)
+    )
+
+    grad_q, keep_kv, send_kv = attend_back(
+        core, own, other, limit, out_f, log_total, grad_heads
+    )
+    grad_kv = (keep_kv + swap_cores(send_kv).astype(jnp.float32)).astype(jnp.bfloat16)
+    grad_own = every_device(jnp.concatenate([grad_q, grad_kv], 1)).astype(jnp.float32)
+    grad_proj_t = (
+        rotate_heads(
+            grad_own.reshape(
+                micro_count, tp_count * kv_here, 2, 2, 2, HEAD_DIM // 2, rows
+            ),
+            cosine,
+            -sine,
+        )
+        .astype(jnp.bfloat16)
+        .reshape(micro_count, tp_count, half_cols, rows)
+    )
+    grad_normed = jnp.concatenate(
+        [
+            sum(dot_f32(grad_proj_t[micro, part], w_heads[part], 0, 1) for part in range(2))
+            for micro in range(micro_count)
+        ],
+        0,
+    )
+    grad_proj = [
+        sum(
+            dot_f32(normed[micro * rows : (micro + 1) * rows], grad_proj_t[micro, part], 0, 1)
+            for micro in range(micro_count)
+        ).astype(jnp.bfloat16)
+        for part in range(2)
+    ]
+    gained_one = grad_normed * gain_one
+    grad_gain_one = jnp.sum(grad_normed * x_rows * scale_one, 0)
+    grad_tokens = (
+        grad_resid
+        + scale_one * gained_one
+        - x_rows * scale_one**3 * jnp.mean(x_rows * gained_one, -1, keepdims=True)
+    )
+
+    small_grads = jnp.concatenate([grad_route, grad_gain_one[:, None], grad_gain_two[:, None]], 1)
+    small_grads = jnp.pad(small_grads, ((0, 0), (0, LANES - small_grads.shape[1]))).astype(
+        jnp.bfloat16
+    )
+    grad_outw = grad_outw.astype(jnp.bfloat16)
+    parts = [
+        jnp.concatenate(
+            [grad_proj[part], grad_outw[:, part * out_cols : (part + 1) * out_cols], small_grads],
+            1,
+        )
+        for part in range(2)
+    ]
+    kept = jnp.where(tp_index == 0, parts[0], parts[1])
+    given = jnp.where(tp_index == 0, parts[1], parts[0])
+    core_sum = (kept.astype(jnp.float32) + swap_cores(given).astype(jnp.float32)).astype(
+        jnp.bfloat16
+    )
+    shares = lax.all_to_all(
+        core_sum.reshape(ep_count, shard, -1), "ep", split_axis=0, concat_axis=0, tiled=True
+    )
+    own_share = jnp.sum(shares.astype(jnp.float32), 0)
+    head_grads = own_share[:, :half_cols].reshape(shard, kv_here, 2, 2, HEAD_DIM)
+    small_share = lax.dynamic_slice_in_dim(
+        own_share[:, half_cols + out_cols :], tp_index * (shard // 2), shard // 2, 0
+    )
+    return (
+        mixed.reshape(micro_count, rows, width),
+        grad_tokens.reshape(micro_count, rows, width),
+        small_share[:, experts_all],
+        head_grads[:, :, :, 0].reshape(shard, q_cols),
+        head_grads[:, :, 0, 1].reshape(shard, kv_cols),
+        head_grads[:, :, 1, 1].reshape(shard, kv_cols),
+        own_share[:, half_cols : half_cols + out_cols].T,
+        small_share[:, experts_all + 1],
+        small_share[:, :experts_all],
+        grad_expert_w[0][None],
+        grad_expert_w[1][None],
+        grad_expert_w[2].T[None],
+    )
+
+
+def on_device(*args):
+    tokens, w_query, w_key, w_gate = args[0], args[2], args[3], args[8]
+    paired = paired_layout(
+        lax.axis_size("ep"),
+        lax.axis_size("tp"),
+        *tokens.shape,
+        w_query.shape[1],
+        w_key.shape[1],
+        w_gate.shape[0],
+    )
+    return (on_device_paired if paired else on_device_general)(*args)
+
+
 def solution(mesh):
     in_specs = (
         P(None, ("ep", "tp"), None),

time: 3500 us -> 1200 us (0.34)
  matrix products: 964 us -> 18.7 us
  waiting for transfers between devices: 1520 us -> 584 us
  Pallas kernels: 0 us -> 296 us
  blocking collectives: 305 us -> 30.1 us
  other arithmetic: 346 us -> 85.7 us
  local copies, waits for them, and re-layouts: 268 us -> 84.6 us
    dot_general x272 -> x21, matrix products: 964 us -> 18.7 us  [the longest x20 18.4 us: dot_f32(): lax.dot_general(left, right, (((left_dim,), (right_dim,)), ((), ())), pre...]
    all_to_all x8 -> x4, waiting for transfers between devices: 778 us -> 0.01 us  [the longest x3 0.01 us: every_device(): return lax.all_to_all(values, ('ep', 'tp'), 0, 0, tiled=True)]
    ppermute x0 -> x44, waiting for transfers between devices: none -> 514 us  [the longest x39 501 us: flip(): lax.ppermute(values, 'ep', [(index, index ^ bits) for index in range(coun...]
    reduce_scatter x18 -> x0, waiting for transfers between devices: 479 us -> none  [the longest x2 139 us: reduce_grads(): lax.psum_scatter(grad_outw.astype(jnp.bfloat16), 'ep', scatter_dimension=...]
    pallas_call x0 -> x4, Pallas kernels: none -> 296 us  [the longest x2 116 us: experts(): pl.pallas_call(functools.partial(experts_kernel, tile_rows=math.gcd(rows,...]
    all_gather x3 -> x0, blocking collectives: 244 us -> none  [the longest x1 162 us: on_device(): lax.all_gather(w_router, 'ep', axis=0, tiled=True)]
    reduce_sum x45 -> x8, other arithmetic: 157 us -> 4.56 us  [the longest x1 2.47 us: on_device_paired(): own_share = jnp.sum(shares.astype(jnp.float32), 0)]
    unnamed x32 -> x1, waiting for transfers between devices: 122 us -> 0.02 us
  transfers between devices with their start and end apart: 38 -> 49, of which waited for: 25 -> 23; matrix products, arithmetic and copies ran while one was open for 41% -> 9% of each run, Pallas kernels for 0% -> 10%
where the time goes in v1:
time: 1200 us; the launch traced here: 1190 us
  waiting for transfers between devices  584 us (49%)
  Pallas kernels  296 us (25%)
  other arithmetic  85.7 us (7%)
  local copies, waits for them, and re-layouts  84.6 us (7%)
  starting transfers between devices  71.9 us (6%)
  blocking collectives  30.1 us (3%)
  matrix products  18.7 us (2%)
  between operations  15.7 us (1%)
    ppermute x39, waiting for transfers between devices, flip(): lax.ppermute(values, 'ep', [(index, index ^ bits) for index in range(coun...  501 us
    pallas_call x2, Pallas kernels, experts(): pl.pallas_call(functools.partial(experts_kernel, tile_rows=math.gcd(rows,...  116 us
    pallas_call x1, Pallas kernels, attend_back(): pl.pallas_call(functools.partial(attend_back_kernel, query_block=query_bl...  113 us
    all_gather x1, waiting for transfers between devices, on_device_paired(): lax.all_gather(packed, ('ep', 'tp'), axis=0, tiled=False)  69.9 us
    pallas_call x1, Pallas kernels, attend(): pl.pallas_call(functools.partial(attend_kernel, query_block=query_block,...  67.2 us
    ppermute x39, starting transfers between devices, flip(): lax.ppermute(values, 'ep', [(index, index ^ bits) for index in range(coun...  44.2 us
    all_to_all x1, blocking collectives, every_device(): return lax.all_to_all(values, ('ep', 'tp'), 0, 0, tiled=True)  30.1 us
  transfers between devices with their start and end apart: 49, of which 23 were waited for; matrix products, arithmetic and copies ran while one was open for 9% of the time, Pallas kernels for 10%

profile of v1, /device:TPU:14, one launch (start us, length us, event | category | flops | bytes accessed | tf_op | source)
XLA Modules:
  0.0 1186.4 jit_solution(15729418739607466724)
XLA Ops:
  14.9 69.9 %all-gather.3.cloned.1.call-done = bf16[2048,1664]{1,0:T(8,128)(2,1)} async-done(((bf16[64,1664]{1,0:T(8,128)(2,1)}), bf16[2048,1664]{1,0:T(8,128)(2,1)}) %all-gather.3.cloned.1.call-update) | async-done | bytes 6815760 | tf_op jit(solution)/shard_map/all_gather | solution.py:986
  84.8 4.2 fusion.63
  90.2 4.0 copy.224
  108.6 5.0 all-to-all-start
  128.9 133.8 %collective-permute-done.12 = bf16[1536,512]{1,0:T(8,128)(2,1)S(1)} collective-permute-done((bf16[1536,512]{1,0:T(8,128)(2,1)}, bf16[1536,512]{1,0:T(8,128)(2,1)S(1)}, u32[]{:S(2)}, u32[]{:S(2)}) %collective-permute-start.12) | collective-permute-done | bytes 1572896 | tf_op jit(solution)/shard_map/ppermute | solution.py:894
  263.1 31.3 %collective-permute-done.11 = bf16[1536,512]{1,0:T(8,128)(2,1)} collective-permute-done((bf16[1536,512]{1,0:T(8,128)(2,1)}, bf16[1536,512]{1,0:T(8,128)(2,1)}, u32[]{:S(2)}, u32[]{:S(2)}) %collective-permute-start.11) | collective-permute-done | bytes 1572896 | tf_op jit(solution)/shard_map/ppermute | solution.py:894
  294.5 3.7 pad_maximum_fusion
  305.4 3.1 pad_maximum_fusion.9.dy_ref
  308.4 9.0 collective-permute-done.6
  317.4 9.6 collective-permute-done.5
  328.5 67.2 %attend.1 = (bf16[32,64,256]{2,1,0:T(8,128)(2,1)}, f32[32,64,256]{2,1,0:T(8,128)}, f32[1,8192]{1,0:T(1,128)}) custom-call(s32[1]{0:T(128)} %bitcast.tp_ref, bf16[32,128,256]{2,1,0:T(8,128)(2,1)} %all-to-all-done.own_ref, bf16[32,64,256]{2,1,0:T(8,128)(2,1)} %collective-permute-done.other_ref, s32[1,8192]{1,0:T(1,128)} %iota_maximum_fusion.limit_ref), custom_call_target="tpu_custom_call" | custom-call | flops 34359738368 | bytes 8388608 | tf_op jit(solution)/shard_map/attend/pallas_call | solution.py:598
  395.7 7.3 all-to-all-start.1
  403.0 6.3 broadcast_select_fusion.1
  414.0 4.7 fusion.64
  421.3 4.0 maximum_maximum_fusion.w_gate_ref
  431.3 3.1 fusion.62
  446.1 8.2 collective-permute-done.7
  455.8 21.3 %collective-permute-done.8 = f32[4,512]{1,0:T(4,128)S(1)} collective-permute-done((f32[4,512]{1,0:T(4,128)S(1)}, f32[4,512]{1,0:T(4,128)S(1)}, u32[]{:S(2)}, u32[]{:S(2)}) %collective-permute-start.8) | collective-permute-done | bytes 8224 | tf_op jit(solution)/shard_map/ppermute | solution.py:894
  479.0 3.3 reshape_squeeze.41.gate_ref
  482.3 3.3 reshape_squeeze.40.gate_ref
  487.1 3.7 collective-permute-done.2
  490.8 2.7 collective-permute-done.1
  493.5 3.0 pad_maximum_fusion.6.x_ref
  497.1 57.2 %experts.2 = (bf16[1024,1024]{1,0:T(8,128)(2,1)}, bf16[1024,1024]{1,0:T(8,128)(2,1)}, f32[4,1024,1]{2,1,0:T(8,128)}, bf16[4,3,512,512]{3,2,1,0:T(8,128)(2,1)}, bf16[4,3,512,512]{3,2,1,0:T(8,128)(2,1)}) custom-call(s32[1]{0:T(128)} %bitcast.tp_ref, bf16[1024,1024]{1,0:T(8,128)(2,1)} %pad_maximum_fusion.6.x_ref, bf16[1024,1024]{1,0:T(8,128)(2,1)} %pad_maximum_fusion.7.dy_ref, ...), custom_call_target="tpu_custom_call" | custom-call | flops 38654705664 | bytes 25165824 | tf_op jit(solution)/shard_map/experts/pallas_call | solution.py:849
  554.3 2.9 pad_maximum_fusion.8.x_ref
  557.2 58.5 %experts.3 = (bf16[1024,1024]{1,0:T(8,128)(2,1)}, bf16[1024,1024]{1,0:T(8,128)(2,1)}, f32[4,1024,1]{2,1,0:T(8,128)}, bf16[4,3,512,512]{3,2,1,0:T(8,128)(2,1)}, bf16[4,3,512,512]{3,2,1,0:T(8,128)(2,1)}) custom-call(s32[1]{0:T(128)} %bitcast.tp_ref, bf16[1024,1024]{1,0:T(8,128)(2,1)} %pad_maximum_fusion.8.x_ref, bf16[1024,1024]{1,0:T(8,128)(2,1)} %pad_maximum_fusion.9.dy_ref, ...), custom_call_target="tpu_custom_call" | custom-call | flops 38654705664 | bytes 25165824 | tf_op jit(solution)/shard_map/experts/pallas_call | solution.py:849
  634.8 9.9 collective-permute-done.31
  645.3 10.7 collective-permute-done.30
  657.4 9.8 collective-permute-done.28
  667.2 6.3 collective-permute-done.27
  679.0 30.1 %all_to_all.25.grad_ref = bf16[32,64,256]{2,1,0:T(8,128)(2,1)} all-to-all(bf16[32,64,256]{2,1,0:T(8,128)(2,1)S(1)} %bitcast.277), channel_id=1, replica_groups=mesh['ep'=16,'tp'=2] {'ep','tp'}, dimensions={0} | all-to-all | bytes 2097152 | tf_op jit(solution)/shard_map/all_to_all | solution.py:902
  709.1 113.3 %attend_back.1 = (bf16[32,64,256]{2,1,0:T(8,128)(2,1)}, f32[32,64,256]{2,1,0:T(8,128)}, bf16[32,64,256]{2,1,0:T(8,128)(2,1)}) custom-call(s32[1]{0:T(128)} %bitcast.tp_ref, bf16[32,128,256]{2,1,0:T(8,128)(2,1)} %all-to-all-done.own_ref, bf16[32,64,256]{2,1,0:T(8,128)(2,1)} %collective-permute-done.other_ref, s32[1,8192]{1,0:T(1,128)} %iota_maximum_fusion.limit_ref, ...), custom_call_target="tpu_custom_call" | custom-call | flops 68719476736 | bytes 12582912 | tf_op jit(solution)/shard_map/attend_back/pallas_call | solution.py:732
  822.4 2.9 collective-permute-done.38
  828.9 6.2 all-to-all-start.3
  844.6 26.1 %collective-permute-done.25 = bf16[256,1024]{1,0:T(8,128)(2,1)S(1)} collective-permute-done((bf16[256,1024]{1,0:T(8,128)(2,1)S(1)}, bf16[256,1024]{1,0:T(8,128)(2,1)S(1)}, u32[]{:S(2)}, u32[]{:S(2)}) %collective-permute-start.25) | collective-permute-done | bytes 524320 | tf_op jit(solution)/shard_map/ppermute | solution.py:894
  873.3 8.2 collective-permute-done.24
  886.3 8.9 collective-permute-done.16
  895.2 8.7 collective-permute-done.15
  925.8 9.6 collective-permute-done.39
  935.4 4.2 add_convert_fusion.1
  939.6 5.6 copy.245
  945.2 8.1 all-to-all-start.4
  953.3 9.3 add_convert_fusion
  962.6 4.7 slice_bitcast_fusion.2
  971.2 3.5 fusion.10
  974.7 156.2 %collective-permute-done.43 = bf16[3,512,512]{2,1,0:T(8,128)(2,1)} collective-permute-done((bf16[3,512,512]{2,1,0:T(8,128)(2,1)}, bf16[3,512,512]{2,1,0:T(8,128)(2,1)}, u32[]{:S(2)}, u32[]{:S(2)}) %collective-permute-start.43) | collective-permute-done | bytes 1572896 | tf_op jit(solution)/shard_map/ppermute | solution.py:894
  1130.8 32.5 %collective-permute-done.42 = bf16[3,512,512]{2,1,0:T(8,128)(2,1)} collective-permute-done((bf16[3,512,512]{2,1,0:T(8,128)(2,1)}, bf16[3,512,512]{2,1,0:T(8,128)(2,1)}, u32[]{:S(2)}, u32[]{:S(2)}) %collective-permute-start.42) | collective-permute-done | bytes 1572896 | tf_op jit(solution)/shard_map/ppermute | solution.py:894
  1163.4 3.7 fusion.1
  (345 shorter events, 162.3 us)
Async XLA Ops:
  7.2 77.6 %all-gather.3.cloned.1.call-start = ((), (), s32[]{:S(2)}) async-start(), calls=%async_computation.5 | async-start | bytes 7028736 | tf_op jit(solution)/shard_map/all_gather | solution.py:986
  108.6 189.7 %all-to-all-start = ((bf16[32,128,256]{2,1,0:T(8,128)(2,1)}), bf16[32,128,256]{2,1,0:T(8,128)(2,1)}, u32[]{:S(2)}, u32[]{:S(2)}) async-start(bf16[32,128,256]{2,1,0:T(8,128)(2,1)} %pad_maximum_fusion.3), calls=%async_computation | async-start | bytes 4194304 | tf_op jit(solution)/shard_map/all_to_all | solution.py:902
  121.8 140.9 %collective-permute-start.12 = (bf16[1536,512]{1,0:T(8,128)(2,1)}, bf16[1536,512]{1,0:T(8,128)(2,1)S(1)}, u32[]{:S(2)}, u32[]{:S(2)}) collective-permute-start(bf16[1536,512]{1,0:T(8,128)(2,1)} %maximum_select_fusion), channel_id=1, source_target_pairs={{0,24},{2,26},{4,28},{6,30},{8,16},{10,18},{12,20},{14,22},{16,8},... | collective-permute-start | bytes 4718600 | tf_op jit(solution)/shard_map/ppermute | solution.py:894
  123.3 171.2 %collective-permute-start.11 = (bf16[1536,512]{1,0:T(8,128)(2,1)}, bf16[1536,512]{1,0:T(8,128)(2,1)}, u32[]{:S(2)}, u32[]{:S(2)}) collective-permute-start(bf16[1536,512]{1,0:T(8,128)(2,1)} %maximum_select_fusion), channel_id=1, source_target_pairs={{0,16},{2,18},{4,20},{6,22},{8,24},{10,26},{12,28},{14,30},{16,0},... | collective-permute-start | bytes 4718600 | tf_op jit(solution)/shard_map/ppermute | solution.py:894
  124.6 169.8 %collective-permute-start.10 = (bf16[1536,512]{1,0:T(8,128)(2,1)}, bf16[1536,512]{1,0:T(8,128)(2,1)}, u32[]{:S(2)}, u32[]{:S(2)}) collective-permute-start(bf16[1536,512]{1,0:T(8,128)(2,1)} %maximum_select_fusion), channel_id=1, source_target_pairs={{0,8},{2,10},{4,12},{6,14},{8,0},{10,2},{12,4},{14,6},{16,24},{18,... | collective-permute-start | bytes 4718600 | tf_op jit(solution)/shard_map/ppermute | solution.py:894
  126.6 175.1 %collective-permute-start.22 = (bf16[256,1024]{1,0:T(8,128)(2,1)}, bf16[256,1024]{1,0:T(8,128)(2,1)}, u32[]{:S(2)}, u32[]{:S(2)}) collective-permute-start(bf16[256,1024]{1,0:T(8,128)(2,1)} %get-tuple-element.186), channel_id=1, source_target_pairs={{0,6},{2,4},{4,2},{6,0},{8,14},{10,12},{12,10},{14,8},{16,22},{18,... | collective-permute-start | bytes 1572872 | tf_op jit(solution)/shard_map/ppermute | solution.py:894
  127.1 175.1 %collective-permute-start.21 = (bf16[256,1024]{1,0:T(8,128)(2,1)}, bf16[256,1024]{1,0:T(8,128)(2,1)}, u32[]{:S(2)}, u32[]{:S(2)}) collective-permute-start(bf16[256,1024]{1,0:T(8,128)(2,1)} %get-tuple-element.186), channel_id=1, source_target_pairs={{0,4},{2,6},{4,0},{6,2},{8,12},{10,14},{12,8},{14,10},{16,20},{18,... | collective-permute-start | bytes 1572872 | tf_op jit(solution)/shard_map/ppermute | solution.py:894
  262.7 40.5 %collective-permute-start.20 = (bf16[256,1024]{1,0:T(8,128)(2,1)}, bf16[256,1024]{1,0:T(8,128)(2,1)}, u32[]{:S(2)}, u32[]{:S(2)}) collective-permute-start(bf16[256,1024]{1,0:T(8,128)(2,1)} %get-tuple-element.186), channel_id=1, source_target_pairs={{0,2},{2,0},{4,6},{6,4},{8,10},{10,8},{12,14},{14,12},{16,18},{18,... | collective-permute-start | bytes 1572872 | tf_op jit(solution)/shard_map/ppermute | solution.py:894
  298.2 104.8 %collective-permute-start.13 = (bf16[3,1536,512]{2,1,0:T(8,128)(2,1)}, bf16[3,1536,512]{2,1,0:T(8,128)(2,1)}, u32[]{:S(2)}, u32[]{:S(2)}) collective-permute-start(bf16[3,1536,512]{2,1,0:T(8,128)(2,1)} %pad_maximum_fusion), channel_id=1, source_target_pairs={{0,1},{1,0},{2,3},{3,2},{4,5},{5,4},{6,7},{7,6},{8,9},{9,8},{10,11... | collective-permute-start | bytes 14155784 | tf_op jit(solution)/shard_map/ppermute | solution.py:898
  300.6 27.9 %collective-permute-start = (bf16[32,64,256]{2,1,0:T(8,128)(2,1)}, bf16[32,64,256]{2,1,0:T(8,128)(2,1)}, u32[]{:S(2)}, u32[]{:S(2)}) collective-permute-start(bf16[32,64,256]{2,1,0:T(8,128)(2,1)} %slice.428), channel_id=1, source_target_pairs={{0,1},{1,0},{2,3},{3,2},{4,5},{5,4},{6,7},{7,6},{8,9},{9,8},{10,11... | collective-permute-start | bytes 3145736 | tf_op jit(solution)/shard_map/ppermute | solution.py:898
  301.7 15.7 %collective-permute-start.6 = (bf16[256,1024]{1,0:T(8,128)(2,1)S(1)}, bf16[256,1024]{1,0:T(8,128)(2,1)S(1)}, u32[]{:S(2)}, u32[]{:S(2)}) collective-permute-start(bf16[256,1024]{1,0:T(8,128)(2,1)S(1)} %get-tuple-element.185), channel_id=1, source_target_pairs={{0,6},{2,4},{4,2},{6,0},{8,14},{10,12},{12,10},{14,8},{16,22},{18,... | collective-permute-start | bytes 1572872 | tf_op jit(solution)/shard_map/ppermute | solution.py:894
  302.2 24.9 %collective-permute-start.5 = (bf16[256,1024]{1,0:T(8,128)(2,1)S(1)}, bf16[256,1024]{1,0:T(8,128)(2,1)S(1)}, u32[]{:S(2)}, u32[]{:S(2)}) collective-permute-start(bf16[256,1024]{1,0:T(8,128)(2,1)S(1)} %get-tuple-element.185), channel_id=1, source_target_pairs={{0,4},{2,6},{4,0},{6,2},{8,12},{10,14},{12,8},{14,10},{16,20},{18,... | collective-permute-start | bytes 1572872 | tf_op jit(solution)/shard_map/ppermute | solution.py:894
  303.1 23.9 %collective-permute-start.4 = (bf16[256,1024]{1,0:T(8,128)(2,1)S(1)}, bf16[256,1024]{1,0:T(8,128)(2,1)S(1)}, u32[]{:S(2)}, u32[]{:S(2)}) collective-permute-start(bf16[256,1024]{1,0:T(8,128)(2,1)S(1)} %get-tuple-element.185), channel_id=1, source_target_pairs={{0,2},{2,0},{4,6},{6,4},{8,10},{10,8},{12,14},{14,12},{16,18},{18,... | collective-permute-start | bytes 1572872 | tf_op jit(solution)/shard_map/ppermute | solution.py:894
  395.7 38.7 %all-to-all-start.1 = ((bf16[32,64,256]{2,1,0:T(8,128)(2,1)}), bf16[32,64,256]{2,1,0:T(8,128)(2,1)}, u32[]{:S(2)}, u32[]{:S(2)}) async-start(bf16[32,64,256]{2,1,0:T(8,128)(2,1)} %get-tuple-element.28), calls=%async_computation.1 | async-start | bytes 2097152 | tf_op jit(solution)/shard_map/all_to_all | solution.py:902
  439.8 114.5 %collective-permute-start.19 = (bf16[256,1024]{1,0:T(8,128)(2,1)}, bf16[256,1024]{1,0:T(8,128)(2,1)}, u32[]{:S(2)}, u32[]{:S(2)}) collective-permute-start(bf16[256,1024]{1,0:T(8,128)(2,1)} %get-tuple-element.188), channel_id=1, source_target_pairs={{0,6},{2,4},{4,2},{6,0},{8,14},{10,12},{12,10},{14,8},{16,22},{18,... | collective-permute-start | bytes 1572872 | tf_op jit(solution)/shard_map/ppermute | solution.py:894
  440.3 114.0 %collective-permute-start.18 = (bf16[256,1024]{1,0:T(8,128)(2,1)}, bf16[256,1024]{1,0:T(8,128)(2,1)}, u32[]{:S(2)}, u32[]{:S(2)}) collective-permute-start(bf16[256,1024]{1,0:T(8,128)(2,1)} %get-tuple-element.188), channel_id=1, source_target_pairs={{0,4},{2,6},{4,0},{6,2},{8,12},{10,14},{12,8},{14,10},{16,20},{18,... | collective-permute-start | bytes 1572872 | tf_op jit(solution)/shard_map/ppermute | solution.py:894
  442.6 11.7 collective-permute-start.7
  444.1 33.0 %collective-permute-start.8 = (f32[4,512]{1,0:T(4,128)S(1)}, f32[4,512]{1,0:T(4,128)S(1)}, u32[]{:S(2)}, u32[]{:S(2)}) collective-permute-start(f32[4,512]{1,0:T(4,128)S(1)} %get-tuple-element.208), channel_id=1, source_target_pairs={{0,4},{2,6},{4,0},{6,2},{8,12},{10,14},{12,8},{14,10},{16,20},{18,... | collective-permute-start | bytes 24584 | tf_op jit(solution)/shard_map/ppermute | solution.py:894
  444.6 33.7 %collective-permute-start.9 = (f32[4,512]{1,0:T(4,128)S(1)}, f32[4,512]{1,0:T(4,128)S(1)}, u32[]{:S(2)}, u32[]{:S(2)}) collective-permute-start(f32[4,512]{1,0:T(4,128)S(1)} %get-tuple-element.207), channel_id=1, source_target_pairs={{0,6},{2,4},{4,2},{6,0},{8,14},{10,12},{12,10},{14,8},{16,22},{18,... | collective-permute-start | bytes 24584 | tf_op jit(solution)/shard_map/ppermute | solution.py:894
  454.3 31.3 %collective-permute-start.3 = (bf16[256,1024]{1,0:T(8,128)(2,1)}, bf16[256,1024]{1,0:T(8,128)(2,1)}, u32[]{:S(2)}, u32[]{:S(2)}) collective-permute-start(bf16[256,1024]{1,0:T(8,128)(2,1)} %get-tuple-element.187), channel_id=1, source_target_pairs={{0,6},{2,4},{4,2},{6,0},{8,14},{10,12},{12,10},{14,8},{16,22},{18,... | collective-permute-start | bytes 1572872 | tf_op jit(solution)/shard_map/ppermute | solution.py:894
  477.1 13.7 %collective-permute-start.2 = (bf16[256,1024]{1,0:T(8,128)(2,1)}, bf16[256,1024]{1,0:T(8,128)(2,1)}, u32[]{:S(2)}, u32[]{:S(2)}) collective-permute-start(bf16[256,1024]{1,0:T(8,128)(2,1)} %get-tuple-element.187), channel_id=1, source_target_pairs={{0,4},{2,6},{4,0},{6,2},{8,12},{10,14},{12,8},{14,10},{16,20},{18,... | collective-permute-start | bytes 1572872 | tf_op jit(solution)/shard_map/ppermute | solution.py:894
  478.3 15.2 %collective-permute-start.1 = (bf16[256,1024]{1,0:T(8,128)(2,1)}, bf16[256,1024]{1,0:T(8,128)(2,1)}, u32[]{:S(2)}, u32[]{:S(2)}) collective-permute-start(bf16[256,1024]{1,0:T(8,128)(2,1)} %get-tuple-element.187), channel_id=1, source_target_pairs={{0,2},{2,0},{4,6},{6,4},{8,10},{10,8},{12,14},{14,12},{16,18},{18,... | collective-permute-start | bytes 1572872 | tf_op jit(solution)/shard_map/ppermute | solution.py:894
  485.6 68.7 %collective-permute-start.17 = (bf16[256,1024]{1,0:T(8,128)(2,1)}, bf16[256,1024]{1,0:T(8,128)(2,1)S(1)}, u32[]{:S(2)}, u32[]{:S(2)}) collective-permute-start(bf16[256,1024]{1,0:T(8,128)(2,1)} %get-tuple-element.188), channel_id=1, source_target_pairs={{0,2},{2,0},{4,6},{6,4},{8,10},{10,8},{12,14},{14,12},{16,18},{18,... | collective-permute-start | bytes 1572872 | tf_op jit(solution)/shard_map/ppermute | solution.py:894
  618.0 9.4 collective-permute-start.37
  619.5 9.4 collective-permute-start.36
  620.1 10.5 collective-permute-start.35
  623.8 7.4 collective-permute-start.34
  625.4 7.3 collective-permute-start.33
  627.4 6.7 collective-permute-start.32
  628.9 15.8 %collective-permute-start.31 = (bf16[256,1024]{1,0:T(8,128)(2,1)S(1)}, bf16[256,1024]{1,0:T(8,128)(2,1)S(1)}, u32[]{:S(2)}, u32[]{:S(2)}) collective-permute-start(bf16[256,1024]{1,0:T(8,128)(2,1)S(1)} %get-tuple-element.168), channel_id=1, source_target_pairs={{0,6},{2,4},{4,2},{6,0},{8,14},{10,12},{12,10},{14,8},{16,22},{18,... | collective-permute-start | bytes 1572872 | tf_op jit(solution)/shard_map/ppermute | solution.py:894
  630.6 25.4 %collective-permute-start.30 = (bf16[256,1024]{1,0:T(8,128)(2,1)S(1)}, bf16[256,1024]{1,0:T(8,128)(2,1)S(1)}, u32[]{:S(2)}, u32[]{:S(2)}) collective-permute-start(bf16[256,1024]{1,0:T(8,128)(2,1)S(1)} %get-tuple-element.169), channel_id=1, source_target_pairs={{0,4},{2,6},{4,0},{6,2},{8,12},{10,14},{12,8},{14,10},{16,20},{18,... | collective-permute-start | bytes 1572872 | tf_op jit(solution)/shard_map/ppermute | solution.py:894
  631.2 24.8 %collective-permute-start.29 = (bf16[256,1024]{1,0:T(8,128)(2,1)S(1)}, bf16[256,1024]{1,0:T(8,128)(2,1)S(1)}, u32[]{:S(2)}, u32[]{:S(2)}) collective-permute-start(bf16[256,1024]{1,0:T(8,128)(2,1)S(1)} %get-tuple-element.167), channel_id=1, source_target_pairs={{0,2},{2,0},{4,6},{6,4},{8,10},{10,8},{12,14},{14,12},{16,18},{18,... | collective-permute-start | bytes 1572872 | tf_op jit(solution)/shard_map/ppermute | solution.py:894
  632.7 34.6 %collective-permute-start.28 = (bf16[256,1024]{1,0:T(8,128)(2,1)S(1)}, bf16[256,1024]{1,0:T(8,128)(2,1)S(1)}, u32[]{:S(2)}, u32[]{:S(2)}) collective-permute-start(bf16[256,1024]{1,0:T(8,128)(2,1)S(1)} %get-tuple-element.165), channel_id=1, source_target_pairs={{0,6},{2,4},{4,2},{6,0},{8,14},{10,12},{12,10},{14,8},{16,22},{18,... | collective-permute-start | bytes 1572872 | tf_op jit(solution)/shard_map/ppermute | solution.py:894
  634.1 39.4 %collective-permute-start.27 = (bf16[256,1024]{1,0:T(8,128)(2,1)S(1)}, bf16[256,1024]{1,0:T(8,128)(2,1)S(1)}, u32[]{:S(2)}, u32[]{:S(2)}) collective-permute-start(bf16[256,1024]{1,0:T(8,128)(2,1)S(1)} %get-tuple-element.166), channel_id=1, source_target_pairs={{0,4},{2,6},{4,0},{6,2},{8,12},{10,14},{12,8},{14,10},{16,20},{18,... | collective-permute-start | bytes 1572872 | tf_op jit(solution)/shard_map/ppermute | solution.py:894
  644.7 28.8 %collective-permute-start.26 = (bf16[256,1024]{1,0:T(8,128)(2,1)S(1)}, bf16[256,1024]{1,0:T(8,128)(2,1)S(1)}, u32[]{:S(2)}, u32[]{:S(2)}) collective-permute-start(bf16[256,1024]{1,0:T(8,128)(2,1)S(1)} %get-tuple-element.164), channel_id=1, source_target_pairs={{0,2},{2,0},{4,6},{6,4},{8,10},{10,8},{12,14},{14,12},{16,18},{18,... | collective-permute-start | bytes 1572872 | tf_op jit(solution)/shard_map/ppermute | solution.py:894
  828.9 78.3 %all-to-all-start.3 = ((bf16[32,128,256]{2,1,0:T(8,128)(2,1)}), bf16[32,128,256]{2,1,0:T(8,128)(2,1)}, u32[]{:S(2)}, u32[]{:S(2)}) async-start(bf16[32,128,256]{2,1,0:T(8,128)(2,1)} %pad_maximum_fusion.11), calls=%async_computation.3 | async-start | bytes 4194304 | tf_op jit(solution)/shard_map/all_to_all | solution.py:902
  836.8 33.9 %collective-permute-start.25 = (bf16[256,1024]{1,0:T(8,128)(2,1)S(1)}, bf16[256,1024]{1,0:T(8,128)(2,1)S(1)}, u32[]{:S(2)}, u32[]{:S(2)}) collective-permute-start(bf16[256,1024]{1,0:T(8,128)(2,1)S(1)} %get-tuple-element.174), channel_id=1, source_target_pairs={{0,6},{2,4},{4,2},{6,0},{8,14},{10,12},{12,10},{14,8},{16,22},{18,... | collective-permute-start | bytes 1572872 | tf_op jit(solution)/shard_map/ppermute | solution.py:894
  837.4 44.1 %collective-permute-start.24 = (bf16[256,1024]{1,0:T(8,128)(2,1)S(1)}, bf16[256,1024]{1,0:T(8,128)(2,1)S(1)}, u32[]{:S(2)}, u32[]{:S(2)}) collective-permute-start(bf16[256,1024]{1,0:T(8,128)(2,1)S(1)} %get-tuple-element.175), channel_id=1, source_target_pairs={{0,4},{2,6},{4,0},{6,2},{8,12},{10,14},{12,8},{14,10},{16,20},{18,... | collective-permute-start | bytes 1572872 | tf_op jit(solution)/shard_map/ppermute | solution.py:894
  838.9 45.1 %collective-permute-start.23 = (bf16[256,1024]{1,0:T(8,128)(2,1)S(1)}, bf16[256,1024]{1,0:T(8,128)(2,1)S(1)}, u32[]{:S(2)}, u32[]{:S(2)}) collective-permute-start(bf16[256,1024]{1,0:T(8,128)(2,1)S(1)} %get-tuple-element.173), channel_id=1, source_target_pairs={{0,2},{2,0},{4,6},{6,4},{8,10},{10,8},{12,14},{14,12},{16,18},{18,... | collective-permute-start | bytes 1572872 | tf_op jit(solution)/shard_map/ppermute | solution.py:894
  840.5 54.8 %collective-permute-start.16 = (bf16[256,1024]{1,0:T(8,128)(2,1)S(1)}, bf16[256,1024]{1,0:T(8,128)(2,1)S(1)}, u32[]{:S(2)}, u32[]{:S(2)}) collective-permute-start(bf16[256,1024]{1,0:T(8,128)(2,1)S(1)} %get-tuple-element.171), channel_id=1, source_target_pairs={{0,6},{2,4},{4,2},{6,0},{8,14},{10,12},{12,10},{14,8},{16,22},{18,... | collective-permute-start | bytes 1572872 | tf_op jit(solution)/shard_map/ppermute | solution.py:894
  841.1 62.9 %collective-permute-start.15 = (bf16[256,1024]{1,0:T(8,128)(2,1)S(1)}, bf16[256,1024]{1,0:T(8,128)(2,1)S(1)}, u32[]{:S(2)}, u32[]{:S(2)}) collective-permute-start(bf16[256,1024]{1,0:T(8,128)(2,1)S(1)} %get-tuple-element.172), channel_id=1, source_target_pairs={{0,4},{2,6},{4,0},{6,2},{8,12},{10,14},{12,8},{14,10},{16,20},{18,... | collective-permute-start | bytes 1572872 | tf_op jit(solution)/shard_map/ppermute | solution.py:894
  870.7 35.2 %collective-permute-start.14 = (bf16[256,1024]{1,0:T(8,128)(2,1)S(1)}, bf16[256,1024]{1,0:T(8,128)(2,1)S(1)}, u32[]{:S(2)}, u32[]{:S(2)}) collective-permute-start(bf16[256,1024]{1,0:T(8,128)(2,1)S(1)} %get-tuple-element.170), channel_id=1, source_target_pairs={{0,2},{2,0},{4,6},{6,4},{8,10},{10,8},{12,14},{14,12},{16,18},{18,... | collective-permute-start | bytes 1572872 | tf_op jit(solution)/shard_map/ppermute | solution.py:894
  925.3 10.2 collective-permute-start.39
  925.3 28.0 %collective-permute-start.40 = (bf16[4,3,512,512]{3,2,1,0:T(8,128)(2,1)}, bf16[4,3,512,512]{3,2,1,0:T(8,128)(2,1)}, u32[]{:S(2)}, u32[]{:S(2)}) collective-permute-start(bf16[4,3,512,512]{3,2,1,0:T(8,128)(2,1)} %get-tuple-element.43), channel_id=1, source_target_pairs={{0,1},{1,0},{2,3},{3,2},{4,5},{5,4},{6,7},{7,6},{8,9},{9,8},{10,11... | collective-permute-start | bytes 18874376 | tf_op jit(solution)/shard_map/ppermute | solution.py:898
  945.2 224.8 %all-to-all-start.4 = ((bf16[16,64,1664]{2,1,0:T(8,128)(2,1)}), bf16[16,64,1664]{2,1,0:T(8,128)(2,1)}, u32[]{:S(2)}, u32[]{:S(2)}) async-start(bf16[16,64,1664]{2,1,0:T(8,128)(2,1)} %bitcast.267), calls=%async_computation.4 | async-start | bytes 6815744 | tf_op jit(solution)/shard_map/all_to_all | solution.py:1224
  967.3 163.5 %collective-permute-start.43 = (bf16[3,512,512]{2,1,0:T(8,128)(2,1)}, bf16[3,512,512]{2,1,0:T(8,128)(2,1)}, u32[]{:S(2)}, u32[]{:S(2)}) collective-permute-start(bf16[3,512,512]{2,1,0:T(8,128)(2,1)} %get-tuple-element.149), channel_id=1, source_target_pairs={{0,24},{2,26},{4,28},{6,30},{8,16},{10,18},{12,20},{14,22},{16,8},... | collective-permute-start | bytes 4718600 | tf_op jit(solution)/shard_map/ppermute | solution.py:894
  968.8 194.6 %collective-permute-start.42 = (bf16[3,512,512]{2,1,0:T(8,128)(2,1)}, bf16[3,512,512]{2,1,0:T(8,128)(2,1)}, u32[]{:S(2)}, u32[]{:S(2)}) collective-permute-start(bf16[3,512,512]{2,1,0:T(8,128)(2,1)} %get-tuple-element.150), channel_id=1, source_target_pairs={{0,16},{2,18},{4,20},{6,22},{8,24},{10,26},{12,28},{14,30},{16,0},... | collective-permute-start | bytes 4718600 | tf_op jit(solution)/shard_map/ppermute | solution.py:894
  970.3 193.1 %collective-permute-start.41 = (bf16[3,512,512]{2,1,0:T(8,128)(2,1)}, bf16[3,512,512]{2,1,0:T(8,128)(2,1)}, u32[]{:S(2)}, u32[]{:S(2)}) collective-permute-start(bf16[3,512,512]{2,1,0:T(8,128)(2,1)} %get-tuple-element.148), channel_id=1, source_target_pairs={{0,8},{2,10},{4,12},{6,14},{8,0},{10,2},{12,4},{14,6},{16,24},{18,... | collective-permute-start | bytes 4718600 | tf_op jit(solution)/shard_map/ppermute | solution.py:894
  (60 other events, 357.9 us)
Sparse Core Ops, SparseCore 0:
  13.1 71.6 all-gather.2

commit v2 on v0

--- a/solution.py
+++ b/solution.py
@@ -1,12 +1,18 @@
+import functools
 import math
 
 import jax
 import jax.numpy as jnp
 from jax import lax
+from jax.experimental import pallas as pl
+from jax.experimental.pallas import tpu as pltpu
 from jax.sharding import PartitionSpec as P
 
 HEAD_DIM = 64
 PIECE = 256
+PLANE = 4
+LANES = 128
+MIB = 1 << 20
 
 
 EPS = 1e-06
@@ -147,7 +153,7 @@
     )
 
 
-def on_device(
+def on_device_general(
     tokens,
     gain_attn,
     w_query,
@@ -489,6 +495,1002 @@
     )
 
 
+def dot_f32(left, right, left_dim, right_dim):
+    return lax.dot_general(
+        left, right, (((left_dim,), (right_dim,)), ((), ())), preferred_element_type=jnp.float32
+    )
+
+
+def at_rows(first_row, count):
+    return pl.ds(pl.multiple_of(first_row, count), count)
+
+
+def whole_vmem():
+    return pl.BlockSpec(memory_space=pltpu.VMEM)
+
+
+def attend_kernel(
+    tp_ref, own_ref, other_ref, limit_ref, out_ref, out_f_ref, log_ref,
+    keys, queries, values, highest, total,
+    *, query_block, key_block, diagonal_block, chains
+):
+    core = tp_ref[0]
+    blocks, _, rows = own_ref.shape
+    seq_len = blocks * rows
+    chain = query_block // chains
+
+    def fill(block, _):
+        cols = at_rows(block * rows, rows)
+        first, second = own_ref[block, HEAD_DIM:, :], other_ref[block]
+        key_rows = jnp.where(core == 0, first, second).astype(jnp.float32)
+        queries[:, cols] = own_ref[block, :HEAD_DIM, :]
+        values[:HEAD_DIM, cols] = jnp.where(core == 0, second, first)
+        values[HEAD_DIM:, cols] = jnp.ones((16, rows), jnp.bfloat16)
+        keys[cols, :] = (key_rows * HEAD_DIM ** (-0.5)).T.astype(jnp.bfloat16)
+        return 0
+
+    lax.fori_loop(0, blocks, fill, 0)
+
+    def update(scores, value_cols, here):
+        before = highest[:, here]
+        after = jnp.maximum(before, jnp.max(scores, 0, keepdims=True))
+        weights = jnp.exp(scores - after).astype(jnp.bfloat16)
+        highest[:, here] = after
+        total[:, here] = total[:, here] * jnp.exp(before - after) + dot_f32(
+            value_cols, weights, 1, 0
+        )
+
+    def near_diagonal(key_rows, key_first, query_cols, here):
+        scores = dot_f32(keys[key_rows, :], queries[:, query_cols], 1, 0)
+        key_pos = key_first + lax.broadcasted_iota(jnp.int32, scores.shape, 0)
+        allowed = key_pos <= limit_ref[:, query_cols]
+        update(jnp.where(allowed, scores, NEG), values[:, key_rows], here)
+
+    def query_step(index, _):
+        first = index * query_block
+        highest[...] = jnp.full_like(highest, NEG)
+        total[...] = jnp.zeros_like(total)
+
+        def full_step(step, _):
+            key_rows = at_rows(step * key_block, key_block)
+            scores = [
+                dot_f32(keys[key_rows, :], queries[:, at_rows(first + part * chain, chain)], 1, 0)
+                for part in range(chains)
+            ]
+            for part in range(chains):
+                update(scores[part], values[:, key_rows], slice(part * chain, (part + 1) * chain))
+            return 0
+
+        lax.fori_loop(0, first // key_block, full_step, 0)
+        for low in range(0, query_block, diagonal_block):
+            here = pl.multiple_of(first + low, diagonal_block)
+            if low:
+                near_diagonal(
+                    pl.ds(here, rows),
+                    here,
+                    pl.ds(pl.multiple_of(here - rows, rows), rows),
+                    slice(low - rows, low),
+                )
+            near_diagonal(
+                pl.ds(here, diagonal_block),
+                here,
+                pl.ds(here, query_block - low),
+                slice(low, query_block),
+            )
+        near_diagonal(
+            at_rows(jnp.minimum(first + query_block, seq_len - rows), rows),
+            first + query_block,
+            at_rows(first + query_block - rows, rows),
+            slice(query_block - rows, query_block),
+        )
+        for piece in range(query_block // rows):
+            here = slice(piece * rows, (piece + 1) * rows)
+            row_sum = total[HEAD_DIM : HEAD_DIM + 1, here]
+            result = total[:HEAD_DIM, here] / row_sum
+            block = index * (query_block // rows) + piece
+            out_ref[block] = result.astype(jnp.bfloat16)
+            out_f_ref[block] = result
+            log_ref[:, at_rows(first + piece * rows, rows)] = highest[:, here] + jnp.log(row_sum)
+        return 0
+
+    lax.fori_loop(0, seq_len // query_block, query_step, 0)
+
+
+def attend(core, own, other, limit):
+    blocks, _, rows = own.shape
+    seq_len = blocks * rows
+    query_block = math.gcd(seq_len, 2048)
+    key_block = math.gcd(query_block, 1024)
+    block_shape = (blocks, HEAD_DIM, rows)
+    return pl.pallas_call(
+        functools.partial(
+            attend_kernel,
+            query_block=query_block,
+            key_block=key_block,
+            diagonal_block=math.gcd(query_block, 512),
+            chains=query_block // math.gcd(query_block, 512),
+        ),
+        out_shape=(
+            jax.ShapeDtypeStruct(block_shape, jnp.bfloat16),
+            jax.ShapeDtypeStruct(block_shape, jnp.float32),
+            jax.ShapeDtypeStruct((1, seq_len), jnp.float32),
+        ),
+        in_specs=[pl.BlockSpec(memory_space=pltpu.SMEM)] + [whole_vmem()] * 3,
+        out_specs=(whole_vmem(),) * 3,
+        scratch_shapes=[
+            pltpu.VMEM((seq_len, HEAD_DIM), jnp.bfloat16),
+            pltpu.VMEM((HEAD_DIM, seq_len), jnp.bfloat16),
+            pltpu.VMEM((HEAD_DIM + 16, seq_len), jnp.bfloat16),
+            pltpu.VMEM((1, query_block), jnp.float32),
+            pltpu.VMEM((HEAD_DIM + 16, query_block), jnp.float32),
+        ],
+        cost_estimate=pl.CostEstimate(
+            flops=seq_len * seq_len * 512, bytes_accessed=8 * MIB, transcendentals=0
+        ),
+        compiler_params=pltpu.CompilerParams(vmem_limit_bytes=56 * MIB),
+        name="attend",
+    )(core, own, other, limit)
+
+
+def three_parts(values):
+    high = values.astype(jnp.bfloat16).astype(jnp.float32)
+    middle = (values - high).astype(jnp.bfloat16).astype(jnp.float32)
+    low = values - high - middle
+    row = lax.broadcasted_iota(jnp.int32, (16, values.shape[1]), 0)
+    parts = jnp.where(
+        row == 0, high, jnp.where(row == 1, middle, jnp.where(row == 2, low, 0.0))
+    )
+    return parts.astype(jnp.bfloat16)
+
+
+def attend_back_kernel(
+    tp_ref, own_ref, other_ref, limit_ref, out_f_ref, log_ref, grad_ref,
+    grad_q_ref, keep_ref, send_ref,
+    keys, keys_t, queries_t, queries, values, grads_t, grads, grad_k, grad_v, grad_q,
+    *, query_block, key_block, diagonal_block
+):
+    core = tp_ref[0]
+    blocks, _, rows = own_ref.shape
+    seq_len = blocks * rows
+
+    def fill(block, _):
+        cols = at_rows(block * rows, rows)
+        first, second = own_ref[block, HEAD_DIM:, :], other_ref[block]
+        key_rows = jnp.where(core == 0, first, second).astype(jnp.float32)
+        key_rows = key_rows * HEAD_DIM ** (-0.5)
+        value_rows = jnp.where(core == 0, second, first).astype(jnp.float32)
+        query, grad = own_ref[block, :HEAD_DIM, :], grad_ref[block]
+        grad_f = grad.astype(jnp.float32)
+        delta = jnp.sum(grad_f * out_f_ref[block], 0, keepdims=True)
+        ones = jnp.ones((16, rows), jnp.float32)
+        queries_t[:HEAD_DIM, cols] = query
+        queries_t[HEAD_DIM:, cols] = three_parts(-log_ref[:, cols])
+        queries[cols, :] = query.astype(jnp.float32).T.astype(jnp.bfloat16)
+        keys_t[:, cols] = key_rows.astype(jnp.bfloat16)
+        keys[cols, :] = jnp.concatenate([key_rows, ones], 0).T.astype(jnp.bfloat16)
+        values[cols, :] = jnp.concatenate([value_rows, ones], 0).T.astype(jnp.bfloat16)
+        grads_t[:HEAD_DIM, cols] = grad
+        grads_t[HEAD_DIM:, cols] = three_parts(-delta)
+        grads[cols, :] = grad_f.T.astype(jnp.bfloat16)
+        grad_k[cols, :] = jnp.zeros((rows, HEAD_DIM), jnp.float32)
+        grad_v[cols, :] = jnp.zeros((rows, HEAD_DIM), jnp.float32)
+        return 0
+
+    lax.fori_loop(0, blocks, fill, 0)
+
+    def tile(key_rows, key_first, query_cols, here):
+        probs = jnp.exp(dot_f32(keys[key_rows, :], queries_t[:, query_cols], 1, 0))
+        if key_first is not None:
+            key_pos = key_first + lax.broadcasted_iota(jnp.int32, probs.shape, 0)
+            probs = jnp.where(key_pos <= limit_ref[:, query_cols], probs, 0.0)
+        grad_probs = dot_f32(values[key_rows, :], grads_t[:, query_cols], 1, 0)
+        grad_scores = (probs * grad_probs).astype(jnp.bfloat16)
+        grad_v[key_rows, :] += dot_f32(probs.astype(jnp.bfloat16), grads[query_cols, :], 1, 0)
+        grad_k[key_rows, :] += dot_f32(grad_scores, queries[query_cols, :], 1, 0)
+        grad_q[:, here] += dot_f32(keys_t[:, key_rows], grad_scores, 1, 0)
+
+    def query_step(index, _):
+        first = index * query_block
+        whole = slice(0, query_block)
+        grad_q[...] = jnp.zeros_like(grad_q)
+
+        def full_step(step, _):
+            tile(at_rows(step * key_block, key_block), None, at_rows(first, query_block), whole)
+            return 0
+
+        lax.fori_loop(0, first // key_block, full_step, 0)
+        for low in range(0, query_block, diagonal_block):
+            here = pl.multiple_of(first + low, diagonal_block)
+            if low:
+                tile(
+                    pl.ds(here, rows),
+                    here,
+                    pl.ds(pl.multiple_of(here - rows, rows), rows),
+                    slice(low - rows, low),
+                )
+            tile(
+                pl.ds(here, diagonal_block),
+                here,
+                pl.ds(here, query_block - low),
+                slice(low, query_block),
+            )
+        tile(
+            at_rows(jnp.minimum(first + query_block, seq_len - rows), rows),
+            first + query_block,
+            at_rows(first + query_block - rows, rows),
+            slice(query_block - rows, query_block),
+        )
+        for piece in range(query_block // rows):
+            here = slice(piece * rows, (piece + 1) * rows)
+            grad_q_ref[index * (query_block // rows) + piece] = grad_q[:, here].astype(
+                jnp.bfloat16
+            )
+        return 0
+
+    lax.fori_loop(0, seq_len // query_block, query_step, 0)
+
+    def finish(block, _):
+        cols = at_rows(block * rows, rows)
+        key_part = (grad_k[cols, :] * HEAD_DIM ** (-0.5)).T
+        value_part = grad_v[cols, :].T
+        keep_ref[block] = jnp.where(core == 0, key_part, value_part)
+        send_ref[block] = jnp.where(core == 0, value_part, key_part).astype(jnp.bfloat16)
+        return 0
+
+    lax.fori_loop(0, blocks, finish, 0)
+
+
+def attend_back(core, own, other, limit, out_f, log_total, grad):
+    blocks, _, rows = own.shape
+    seq_len = blocks * rows
+    query_block = math.gcd(seq_len, 1024)
+    key_block = math.gcd(query_block, 1024)
+    block_shape = (blocks, HEAD_DIM, rows)
+    wide = HEAD_DIM + 16
+    return pl.pallas_call(
+        functools.partial(
+            attend_back_kernel,
+            query_block=query_block,
+            key_block=key_block,
+            diagonal_block=math.gcd(query_block, 512),
+        ),
+        out_shape=(
+            jax.ShapeDtypeStruct(block_shape, jnp.bfloat16),
+            jax.ShapeDtypeStruct(block_shape, jnp.float32),
+            jax.ShapeDtypeStruct(block_shape, jnp.bfloat16),
+        ),
+        in_specs=[pl.BlockSpec(memory_space=pltpu.SMEM)] + [whole_vmem()] * 6,
+        out_specs=(whole_vmem(),) * 3,
+        scratch_shapes=[
+            pltpu.VMEM((seq_len, wide), jnp.bfloat16),
+            pltpu.VMEM((HEAD_DIM, seq_len), jnp.bfloat16),
+            pltpu.VMEM((wide, seq_len), jnp.bfloat16),
+            pltpu.VMEM((seq_len, HEAD_DIM), jnp.bfloat16),
+            pltpu.VMEM((seq_len, wide), jnp.bfloat16),
+            pltpu.VMEM((wide, seq_len), jnp.bfloat16),
+            pltpu.VMEM((seq_len, HEAD_DIM), jnp.bfloat16),
+            pltpu.VMEM((seq_len, HEAD_DIM), jnp.float32),
+            pltpu.VMEM((seq_len, HEAD_DIM), jnp.float32),
+            pltpu.VMEM((HEAD_DIM, query_block), jnp.float32),
+        ],
+        cost_estimate=pl.CostEstimate(
+            flops=seq_len * seq_len * 1024, bytes_accessed=12 * MIB, transcendentals=0
+        ),
+        compiler_params=pltpu.CompilerParams(vmem_limit_bytes=60 * MIB),
+        name="attend_back",
+    )(core, own, other, limit, out_f, log_total, grad)
+
+
+def project_kernel(*refs, count):
+    place_ref, x_ref, cosine_ref, sine_ref = refs[:4]
+    mine_refs, other_refs = refs[4 : 4 + count], refs[4 + count : 4 + 2 * count]
+    normed_ref, sent_ref, heads_ref, small_ref = refs[4 + 2 * count :]
+    core, level, spot = place_ref[0], place_ref[1], place_ref[2]
+    micro_count, rows, width = x_ref.shape
+    columns, shard, _ = mine_refs[0].shape
+    half_cols = heads_ref.shape[2]
+    half_dim = HEAD_DIM // 2
+    units = half_cols // (2 * HEAD_DIM)
+    for step in range(count):
+        for up in range(columns):
+            here = at_rows(((level ^ up) * count + (spot ^ step)) * shard, shard)
+            heads_ref[core, here, :] = mine_refs[step][up, :, :half_cols]
+            heads_ref[1 - core, here, :] = other_refs[step][up, :, :half_cols]
+            small_ref[here, :] = mine_refs[step][up, :, half_cols:]
+    cosine, sine = cosine_ref[...], sine_ref[...]
+    gain_row = small_ref.shape[1] // 2
+    gain = small_ref[...].astype(jnp.float32).T[gain_row : gain_row + 1]
+
+    def rotated(heads):
+        first, second = heads[:half_dim], heads[half_dim:]
+        return jnp.concatenate(
+            [first * cosine - second * sine, second * cosine + first * sine], 0
+        ).astype(jnp.bfloat16)
+
+    for micro in range(micro_count):
+        x = x_ref[micro].astype(jnp.float32)
+        scale = lax.rsqrt(jnp.mean(x * x, -1, keepdims=True) + EPS)
+        normed = (x * scale * gain).astype(jnp.bfloat16)
+        normed_ref[micro * rows : (micro + 1) * rows, :] = normed
+        for part in range(2):
+            heads = dot_f32(normed, heads_ref[part], 1, 0).T
+            for unit in range(units):
+                first = unit * 2 * HEAD_DIM
+                block = (micro * 2 + part) * units + unit
+                second = heads[first + HEAD_DIM : first + 2 * HEAD_DIM]
+                sent_ref[block, :HEAD_DIM, :] = rotated(heads[first : first + HEAD_DIM])
+                sent_ref[block, HEAD_DIM:, :] = (
+                    rotated(second) if unit % 2 == 0 else second.astype(jnp.bfloat16)
+                )
+
+
+def project(place, x, cosine, sine, mine, other, devices):
+    micro_count, rows, width = x.shape
+    half_cols = mine[0].shape[2] - LANES
+    return pl.pallas_call(
+        functools.partial(project_kernel, count=len(mine)),
+        out_shape=(
+            jax.ShapeDtypeStruct((micro_count * rows, width), jnp.bfloat16),
+            jax.ShapeDtypeStruct((devices, 2 * HEAD_DIM, rows), jnp.bfloat16),
+            jax.ShapeDtypeStruct((2, width, half_cols), jnp.bfloat16),
+            jax.ShapeDtypeStruct((width, LANES), jnp.bfloat16),
+        ),
+        in_specs=[pl.BlockSpec(memory_space=pltpu.SMEM)]
+        + [whole_vmem()] * (3 + len(mine) + len(other)),
+        out_specs=(whole_vmem(),) * 4,
+        compiler_params=pltpu.CompilerParams(vmem_limit_bytes=48 * MIB),
+        name="project",
+    )(place, x, cosine, sine, *mine, *other)
+
+
+def project_back_kernel(
+    tp_ref, grad_ref, heads_ref, normed_ref, x_ref, grad_resid_ref, gain_ref, cosine_ref,
+    sine_ref, grad_x_ref, kept_ref, given_ref, grad_rows
+):
+    core = tp_ref[0]
+    micro_count, rows, width = x_ref.shape
+    half_cols = heads_ref.shape[2]
+    half_dim = HEAD_DIM // 2
+    units = half_cols // (2 * HEAD_DIM)
+    cosine, sine = cosine_ref[...], sine_ref[...]
+
+    def turned_back(heads):
+        first, second = heads[:half_dim].astype(jnp.float32), heads[half_dim:].astype(jnp.float32)
+        return [first * cosine + second * sine, second * cosine - first * sine]
+
+    for micro in range(micro_count):
+        for part in range(2):
+            pieces = []
+            for unit in range(units):
+                block = (micro * 2 + part) * units + unit
+                second = grad_ref[block, HEAD_DIM:, :]
+                pieces += turned_back(grad_ref[block, :HEAD_DIM, :])
+                pieces += turned_back(second) if unit % 2 == 0 else [second.astype(jnp.float32)]
+            grad_rows[part, micro * rows : (micro + 1) * rows, :] = (
+                jnp.concatenate(pieces, 0).T.astype(jnp.bfloat16)
+            )
+    gain = gain_ref[...]
+    grad_gain = jnp.zeros((1, width), jnp.float32)
+    for micro in range(micro_count):
+        here = slice(micro * rows, (micro + 1) * rows)
+        grad_normed = dot_f32(grad_rows[0, here, :], heads_ref[0], 1, 1) + dot_f32(
+            grad_rows[1, here, :], heads_ref[1], 1, 1
+        )
+        x = x_ref[micro].astype(jnp.float32)
+        scale = lax.rsqrt(jnp.mean(x * x, -1, keepdims=True) + EPS)
+        gained = grad_normed * gain
+        grad_gain = grad_gain + jnp.sum(grad_normed * x * scale, 0, keepdims=True)
+        grad_x_ref[micro] = (
+            grad_resid_ref[here, :]
+            + scale * gained
+            - x * scale**3 * jnp.mean(x * gained, -1, keepdims=True)
+        )
+    normed_t = normed_ref[...].T
+    gain_cols = jnp.broadcast_to(grad_gain, (LANES, width)).T.astype(jnp.bfloat16)
+    for ref, part in ((kept_ref, core), (given_ref, 1 - core)):
+        ref[:, :half_cols] = dot_f32(normed_t, grad_rows[part], 1, 0).astype(jnp.bfloat16)
+        ref[:, half_cols:] = gain_cols
+
+
+def project_back(core, grad_own, heads, normed, x, grad_resid, gain, cosine, sine):
+    micro_count, rows, width = x.shape
+    half_cols = heads.shape[2]
+    share = jax.ShapeDtypeStruct((width, half_cols + LANES), jnp.bfloat16)
+    return pl.pallas_call(
+        project_back_kernel,
+        out_shape=(jax.ShapeDtypeStruct(x.shape, jnp.float32), share, share),
+        in_specs=[pl.BlockSpec(memory_space=pltpu.SMEM)] + [whole_vmem()] * 8,
+        out_specs=(whole_vmem(),) * 3,
+        scratch_shapes=[pltpu.VMEM((2, micro_count * rows, half_cols), jnp.bfloat16)],
+        compiler_params=pltpu.CompilerParams(vmem_limit_bytes=56 * MIB),
+        name="project_back",
+    )(core, grad_own, heads, normed, x, grad_resid, gain, cosine, sine)
+
+
+def experts_kernel(*refs, slots, first_call, pieces, piece_count):
+    place_ref, refs = refs[0], refs[1:]
+    x_refs, dy_refs = refs[:slots], refs[slots : 2 * slots]
+    w_route_ref, weight_refs = refs[2 * slots], refs[2 * slots + 1 : 2 * slots + 1 + piece_count]
+    refs = refs[2 * slots + 1 + piece_count :]
+    if not first_call:
+        keep_in_ref, send_in_ref = refs[:2]
+        refs = refs[2:]
+    mix_refs, grad_x_refs = refs[:slots], refs[slots : 2 * slots]
+    grad_gate_ref, keep_ref, send_ref = refs[2 * slots : 2 * slots + 3]
+    (
+        x_all, x_t, dy_all, dy_t, gates, grad_gates, mix_sum, grad_x_sum, grad_w, weights, sems
+    ) = refs[2 * slots + 3 :]
+    expert, expert_count = pl.program_id(0), pl.num_programs(0)
+    rows, width = x_refs[0].shape
+    total = slots * rows
+    half = width // 2
+    core = place_ref[0]
+
+    def moves(index):
+        copies = []
+        for number, (array, whose, first, last) in enumerate(pieces[index]):
+            target = weights.at[index % 2, pl.ds(first, last - first)]
+            if whose is not None:
+                part = core if whose == 0 else 1 - core
+                target = weights.at[
+                    index % 2, pl.ds(first, last - first), pl.ds(pl.multiple_of(part * half, half), half)
+                ]
+            copies.append(
+                pltpu.make_async_copy(weight_refs[array], target, sems.at[index, number])
+            )
+        return copies
+
+    @pl.when(expert == 0)
+    def _():
+        for copy in moves(0) + moves(1):
+            copy.start()
+        for slot in range(slots):
+            here = slice(slot * rows, (slot + 1) * rows)
+            x, dy = x_refs[slot][...], dy_refs[slot][:, :width]
+            x_all[here, :] = x
+            x_t[:, here] = x.T
+            dy_all[here, :] = dy
+            dy_t[:, here] = dy.T
+            chosen = dy_refs[slot][:, width:].astype(jnp.float32)
+            logits = jnp.where(chosen > 0.0, dot_f32(x, w_route_ref[...], 1, 0), NEG)
+            raised = jnp.exp(logits - jnp.max(logits, 1, keepdims=True)) * chosen
+            gates[here, :] = raised / jnp.sum(raised, 1, keepdims=True)
+        mix_sum[...] = jnp.zeros_like(mix_sum)
+        grad_x_sum[...] = jnp.zeros_like(grad_x_sum)
+
+    for index in range(len(pieces)):
+
+        @pl.when(expert == index)
+        def _():
+            if 1 <= index < len(pieces) - 1:
+                for copy in moves(index + 1):
+                    copy.start()
+            for copy in moves(index):
+                copy.wait()
+
+    if first_call:
+        grad_w[...] = jnp.zeros_like(grad_w)
+    else:
+        for part in range(2):
+            grad_w[part] = jnp.where(core == part, keep_in_ref[0], send_in_ref[0]).astype(
+                jnp.float32
+            )
+    buffer = lax.rem(expert, 2)
+    w_gate, w_up, w_down_t = weights[buffer, 0], weights[buffer, 1], weights[buffer, 2]
+    x = x_all[...]
+    dy = dy_all[...].astype(jnp.float32)
+    lane = lax.broadcasted_iota(jnp.int32, (total, LANES), 1)
+    gate = jnp.sum(jnp.where(lane == place_ref[1 + expert], gates[...], 0.0), 1, keepdims=True)
+    gate_row = jnp.broadcast_to(gate, (total, LANES)).T[:1]
+    gate_pre = dot_f32(x, w_gate, 1, 0)
+    up_pre = dot_f32(x, w_up, 1, 0)
+    sigmoid_val = 1.0 / (1.0 + jnp.exp(-gate_pre))
+    silu_val = gate_pre * sigmoid_val
+    hidden = (silu_val * up_pre).astype(jnp.bfloat16)
+    out = dot_f32(hidden, w_down_t, 1, 1).astype(jnp.bfloat16).astype(jnp.float32)
+    grad_gate = jnp.sum(out * dy, 1, keepdims=True)
+    grad_gates[pl.ds(expert, 1), :] = jnp.broadcast_to(grad_gate, (total, LANES)).T[:1]
+    mix_sum[...] += gate * out
+    grad_out = (gate * dy).astype(jnp.bfloat16)
+    grad_hidden = dot_f32(grad_out, w_down_t, 1, 0)
+    slope = sigmoid_val * (1.0 + gate_pre * (1.0 - sigmoid_val))
+    grad_gate_pre = (grad_hidden * up_pre * slope).astype(jnp.bfloat16)
+    grad_up_pre = (grad_hidden * silu_val).astype(jnp.bfloat16)
+    grad_copy = dot_f32(grad_gate_pre, w_gate, 1, 1) + dot_f32(grad_up_pre, w_up, 1, 1)
+    grad_x_sum[...] += grad_copy.astype(jnp.bfloat16).astype(jnp.float32)
+    grad_out_t = (dy_t[...].astype(jnp.float32) * gate_row).astype(jnp.bfloat16)
+    terms = (
+        dot_f32(x_t[...], grad_gate_pre, 1, 0),
+        dot_f32(x_t[...], grad_up_pre, 1, 0),
+        dot_f32(grad_out_t, hidden, 1, 0),
+    )
+    for part in range(2):
+        for matrix, term in enumerate(terms):
+            grad_w[part, matrix] += term[part * half : (part + 1) * half]
+    keep_ref[0] = grad_w[core].astype(jnp.bfloat16)
+    send_ref[0] = grad_w[1 - core].astype(jnp.bfloat16)
+
+    @pl.when(expert == expert_count - 1)
+    def _():
+        for slot in range(slots):
+            here = slice(slot * rows, (slot + 1) * rows)
+            mix_refs[slot][...] = mix_sum[here, :].astype(jnp.bfloat16)
+            grad_x_refs[slot][...] = grad_x_sum[here, :].astype(jnp.bfloat16)
+            grad_gate_ref[slot] = grad_gates[: grad_gate_ref.shape[1], here]
+
+
+def experts(place, x_parts, dy_parts, w_route, weights, pieces, before):
+    rows = dy_parts[0][0].shape[1]
+    width, hidden_width = weights[0].shape[-2:]
+    count, slots = len(pieces), len(x_parts)
+    total = slots * rows
+    half = width // 2
+    first_call = before is None
+    before = () if first_call else tuple(before)
+
+    def at_block(shape, index):
+        return pl.BlockSpec(
+            shape,
+            lambda expert: (index,) + (0,) * (len(shape) - 1),
+            pipeline_mode=pl.Buffered(1),
+        )
+
+    row_spec = pl.BlockSpec((rows, width), lambda expert: (0, 0))
+    grad_spec = pl.BlockSpec((1, 3, half, hidden_width), lambda expert: (expert, 0, 0, 0))
+    grad_shape = jax.ShapeDtypeStruct((count, 3, half, hidden_width), jnp.bfloat16)
+    row_shape = jax.ShapeDtypeStruct((rows, width), jnp.bfloat16)
+    outs = pl.pallas_call(
+        functools.partial(
+            experts_kernel,
+            slots=slots,
+            first_call=first_call,
+            pieces=pieces,
+            piece_count=len(weights),
+        ),
+        grid=(count,),
+        out_shape=(row_shape,) * (2 * slots)
+        + (jax.ShapeDtypeStruct((slots, count, rows), jnp.float32), grad_shape, grad_shape),
+        in_specs=[pl.BlockSpec(memory_space=pltpu.SMEM)]
+        + [at_block((rows, width), index) for _, index in x_parts]
+        + [at_block((None, rows, width + LANES), index) for _, index in dy_parts]
+        + [at_block((width, LANES), 0)]
+        + [pl.BlockSpec(memory_space=pl.ANY)] * len(weights)
+        + [grad_spec] * len(before),
+        out_specs=(row_spec,) * (2 * slots)
+        + (pl.BlockSpec((slots, count, rows), lambda expert: (0, 0, 0)), grad_spec, grad_spec),
+        scratch_shapes=[
+            pltpu.VMEM((total, width), jnp.bfloat16),
+            pltpu.VMEM((width, total), jnp.bfloat16),
+            pltpu.VMEM((total, width), jnp.bfloat16),
+            pltpu.VMEM((width, total), jnp.bfloat16),
+            pltpu.VMEM((total, LANES), jnp.float32),
+            pltpu.VMEM((8, total), jnp.float32),
+            pltpu.VMEM((total, width), jnp.float32),
+            pltpu.VMEM((total, width), jnp.float32),
+            pltpu.VMEM((2, 3, half, hidden_width), jnp.float32),
+            pltpu.VMEM((2, 3, width, hidden_width), jnp.bfloat16),
+            pltpu.SemaphoreType.DMA((count, max(len(group) for group in pieces))),
+        ],
+        cost_estimate=pl.CostEstimate(
+            flops=count * total * width * hidden_width * 18,
+            bytes_accessed=count * width * hidden_width * 12,
+            transcendentals=0,
+        ),
+        compiler_params=pltpu.CompilerParams(
+            vmem_limit_bytes=62 * MIB, dimension_semantics=("arbitrary",)
+        ),
+        name="experts",
+    )(
+        place,
+        *[array for array, _ in (*x_parts, *dy_parts)],
+        w_route,
+        *weights,
+        *before,
+    )
+    return outs[:slots], outs[slots : 2 * slots], outs[2 * slots], outs[2 * slots + 1 :]
+
+
+def together(*values):
+    return lax.optimization_barrier(values)
+
+
+def flip(values, bits):
+    count = lax.axis_size("ep")
+    return lax.ppermute(values, "ep", [(index, index ^ bits) for index in range(count)])
+
+
+def swap_cores(values):
+    return lax.ppermute(values, "tp", [(0, 1), (1, 0)])
+
+
+def after(values, *earlier):
+    return together(values, *earlier)[0]
+
+
+def every_device(values):
+    return lax.all_to_all(values, ("ep", "tp"), 0, 0, tiled=True)
+
+
+def head_tables(first_pos, rows):
+    positions = first_pos + jnp.arange(rows, dtype=jnp.int32)
+    halves = jnp.arange(HEAD_DIM // 2, dtype=jnp.float32)
+    freqs = THETA ** (-2.0 * halves / HEAD_DIM)
+    angles = freqs[:, None] * positions.astype(jnp.float32)[None, :]
+    return jnp.cos(angles), jnp.sin(angles)
+
+
+def paired_layout(ep_count, tp_count, micro_count, slice_rows, width, q_cols, kv_cols, experts_here):
+    group = q_cols // kv_cols
+    kv_heads = kv_cols * tp_count // HEAD_DIM
+    return (
+        tp_count == 2
+        and group == 2
+        and ep_count == micro_count * kv_heads
+        and ep_count == PLANE * PLANE
+        and experts_here == 1
+        and slice_rows >= PIECE
+        and slice_rows % PIECE == 0
+        and width % (2 * LANES) == 0
+    )
+
+
+def on_device_paired(
+    tokens,
+    gain_attn,
+    w_query,
+    w_key,
+    w_value,
+    w_output,
+    gain_moe,
+    w_router,
+    w_gate,
+    w_up,
+    w_down,
+    routes,
+    piece_starts,
+    cotangent,
+):
+    ep_count = lax.axis_size("ep")
+    tp_count = lax.axis_size("tp")
+    ep_index, tp_index = lax.axis_index("ep"), lax.axis_index("tp")
+    micro_count, rows, width = tokens.shape
+    devices = ep_count * tp_count
+    seq_len = rows * devices
+    all_rows = micro_count * rows
+    shard = gain_attn.shape[0]
+    q_cols, kv_cols = w_query.shape[1], w_key.shape[1]
+    kv_here = kv_cols // HEAD_DIM
+    half_cols = q_cols + 2 * kv_cols
+    out_cols = w_output.shape[0]
+    columns = ep_count // PLANE
+    experts_all = ep_count
+    core = tp_index.astype(jnp.int32).reshape(1)
+
+    level, spot = ep_index // PLANE, ep_index % PLANE
+    half = width // 2
+    micros = range(micro_count)
+
+    head_cols = jnp.stack(
+        [
+            w_query.reshape(shard, kv_here, 2, HEAD_DIM),
+            jnp.stack(
+                [
+                    w_key.reshape(shard, kv_here, HEAD_DIM),
+                    w_value.reshape(shard, kv_here, HEAD_DIM),
+                ],
+                2,
+            ),
+        ],
+        3,
+    ).reshape(shard, half_cols)
+    small = jnp.concatenate([w_router, jnp.zeros((shard, LANES - experts_all), w_router.dtype)], 1)
+    lanes = jnp.arange(LANES, dtype=jnp.int32)
+    small = jnp.where(lanes == LANES // 2, gain_attn[:, None], small)
+    small = jnp.where(lanes == LANES // 2 + 1, gain_moe[:, None], small)
+    packed = jnp.concatenate([head_cols, small], 1)
+    levels = [packed] + [flip(packed, PLANE * step) for step in range(1, columns)]
+    mine = jnp.stack(levels)
+    mine = [mine] + [flip(mine, step) for step in range(1, PLANE)]
+
+    w_down_t = w_down[0].T
+    first_half = tp_index * half
+    expert_half = jnp.stack(
+        [
+            lax.dynamic_slice_in_dim(whole, first_half, half, 0)
+            for whole in (w_gate[0], w_up[0], w_down_t)
+        ]
+    )
+    expert_half, levels = together(expert_half, levels)
+    far_out = flip(expert_half[2:], 2 * PLANE)
+    mine, far_out = together(mine, far_out)
+    other = [swap_cores(part) for part in mine]
+    near_all = flip(expert_half, PLANE)
+
+    x_rows = tokens.reshape(all_rows, width).astype(jnp.float32)
+    device_index = ep_index * tp_count + tp_index
+    cosine, sine = head_tables(device_index * rows, rows)
+    spot_here = jnp.stack([tp_index, level, spot]).astype(jnp.int32)
+    normed, sent, w_heads, small_all = project(
+        spot_here, tokens, cosine, sine, mine, other, devices
+    )
+    w_route_full = small_all[:, :experts_all]
+    gain_one = small_all[:, LANES // 2].astype(jnp.float32)
+    gain_two = small_all[:, LANES // 2 + 1].astype(jnp.float32)
+    own = every_device(sent)
+    other = swap_cores(own[:, HEAD_DIM:, :])
+
+    chosen = jnp.any(routes[:, :, :, None] == lanes, 2).astype(jnp.bfloat16)
+    own_dy = jnp.concatenate([cotangent, chosen], 2)
+    last_dy = flip(after(own_dy, sent), PLANE - 1)
+    other, last_dy = together(other, last_dy)
+    w_output_t, expert_late, far_out, dy_late, other = together(
+        w_output.T, expert_half, far_out, own_dy, other
+    )
+    far_in = flip(expert_late[:2], 2 * PLANE)
+    plane_dy = [flip(dy_late, step) for step in range(1, PLANE - 1)] + [last_dy]
+    nearfar_out = flip(far_out, PLANE)
+    gathered_out = lax.all_gather(w_output_t, ("ep", "tp"), axis=0, tiled=False)
+
+    micro_here = ep_index // (ep_count // micro_count)
+    starts = lax.dynamic_index_in_dim(piece_starts, micro_here, 0, keepdims=False)
+    all_pos = jnp.arange(seq_len, dtype=jnp.int32)[None, :]
+    inside = (all_pos >= starts[:, None]) & (all_pos < starts[:, None] + PIECE)
+    piece_last = jnp.max(jnp.where(inside, starts[:, None] + (PIECE - 1), -1), 0, keepdims=True)
+    limit = jnp.maximum(all_pos, piece_last).astype(jnp.int32)
+    out_b, out_f, log_total = attend(core, own, other, limit)
+    out_b, far_in, plane_dy, nearfar_out, near_all = together(
+        out_b, far_in, plane_dy, nearfar_out, near_all
+    )
+    nearfar_in = flip(far_in, PLANE)
+    attended_t = every_device(out_b).reshape(micro_count, out_cols * tp_count, rows)
+    gathered_out = gathered_out.reshape(ep_count, tp_count, shard, out_cols)
+    w_out_t = jnp.concatenate(
+        [gathered_out[:, part].reshape(width, out_cols) for part in range(2)], 1
+    )
+
+    attn_rows = jnp.concatenate(
+        [dot_f32(attended_t[micro], w_out_t, 0, 1) for micro in micros], 0
+    )
+    resid = x_rows + attn_rows
+    scale_two = rms_scale(resid)
+    normed_two = (resid * scale_two * gain_two).astype(jnp.bfloat16)
+    normed_parts = [normed_two[micro * rows : (micro + 1) * rows] for micro in micros]
+    plane_x = [[flip(normed_parts[0], step) for step in range(1, PLANE)]]
+
+    column_weights = [w_gate, w_up, w_down_t[None]]
+    for piece in (near_all, far_in, far_out, after(nearfar_in, normed_two), nearfar_out):
+        column_weights += [piece, swap_cores(piece)]
+    pieces = [[(0, None, 0, 1), (1, None, 1, 2), (2, None, 2, 3)]]
+    pieces.append([(5, 0, 0, 2), (6, 1, 0, 2), (7, 0, 2, 3), (8, 1, 2, 3)])
+    pieces.append([(3, 0, 0, 3), (4, 1, 0, 3)])
+    pieces.append([(9, 0, 0, 2), (10, 1, 0, 2), (11, 0, 2, 3), (12, 1, 2, 3)])
+
+    logits = jnp.dot(normed_two, w_route_full, preferred_element_type=jnp.float32)
+    route_rows = routes.reshape(all_rows, -1)
+    expert_ids = jnp.arange(experts_all, dtype=jnp.int32)
+    route_hot = (route_rows[:, :, None] == expert_ids[None, None, :]).astype(jnp.float32)
+    picked = jnp.sum(route_hot * logits[:, None, :], -1)
+    highest = jnp.max(picked, -1, keepdims=True)
+    raised = jnp.exp(picked - highest)
+    gates = raised / jnp.sum(raised, -1, keepdims=True)
+
+    slot_ids = jnp.stack(
+        [
+            jnp.stack([(level ^ up) * PLANE + (spot ^ step) for up in (0, 2, 1, 3)])
+            for step in range(PLANE)
+        ]
+    )
+    slot_hot = (route_rows[None, None, :, :] == slot_ids[:, :, None, None]).astype(jnp.float32)
+
+    place = jnp.concatenate([core, slot_ids[0]])
+    own_mix, own_grad_x, own_grad_gate, before = experts(
+        place,
+        [(normed_two, micro) for micro in micros],
+        [(own_dy, micro) for micro in micros],
+        small_all,
+        column_weights,
+        pieces,
+        None,
+    )
+    leaving = normed_parts[1:]
+    leaving, own_grad_gate = together(leaving, own_grad_gate)
+    plane_x += [[flip(part, step) for step in range(1, PLANE)] for part in leaving]
+    far_mix, late_mix, far_grad_x, far_grad_gate = [], [], [], []
+    for micro in micros:
+        mix, grad_x, grad_gate, before = experts(
+            place,
+            [(part, 0) for part in plane_x[micro]],
+            [(part, micro) for part in plane_dy],
+            small_all,
+            column_weights,
+            pieces,
+            before,
+        )
+        if micro:
+            grad_x, mix, grad_gate, before, far_grad_x, far_mix = together(
+                grad_x, mix, grad_gate, before, far_grad_x, far_mix
+            )
+        far_grad_x.append([flip(grad_x[step - 1], step) for step in range(1, PLANE)])
+        far_grad_gate.append(grad_gate)
+        early = PLANE - 2 if micro < micro_count - 1 else 0
+        far_mix.append([flip(mix[step - 1], step) for step in range(1, early + 1)])
+        late_mix.append([(mix[step - 1], step) for step in range(early + 1, PLANE)])
+    far_grad_gate = jnp.concatenate(far_grad_gate, 2)
+    far_grad_gate = [flip(far_grad_gate[step - 1], step) for step in range(1, PLANE)]
+    keep_w, send_w = before
+    given_w = swap_cores(send_w)
+
+    def column_sum(first, last, low, high):
+        kept = keep_w[first:last, low:high].astype(jnp.float32)
+        return (kept + given_w[first:last, low:high].astype(jnp.float32)).astype(jnp.bfloat16)
+
+    own_w = keep_w[0].astype(jnp.float32) + given_w[0].astype(jnp.float32)
+    far_in_w, near_in_w, last_in_w = [column_sum(slot, slot + 1, 0, 2) for slot in (1, 2, 3)]
+    far_out_w, near_out_w = column_sum(1, 2, 2, 3), column_sum(2, 4, 2, 3)
+    near_out_w, far_grad_x[-1] = together(near_out_w, far_grad_x[-1])
+    near_out_w = flip(near_out_w, PLANE)
+
+    def at_home(own_parts, far_parts):
+        return jnp.concatenate(
+            [
+                own_parts[micro].astype(jnp.float32)
+                + sum(part.astype(jnp.float32) for part in far_parts[micro])
+                for micro in micros
+            ],
+            0,
+        )
+
+    grad_out = cotangent.reshape(all_rows, width).astype(jnp.float32)
+    slot_grads = jnp.stack(
+        [jnp.concatenate([own_grad_gate[micro] for micro in micros], 1)]
+        + far_grad_gate
+    )
+    grad_gates = jnp.sum(slot_hot * slot_grads[:, :, :, None], (0, 1))
+    grad_spread = gates * (grad_gates - jnp.sum(gates * grad_gates, -1, keepdims=True))
+    grad_logits = jnp.sum(grad_spread[:, :, None] * route_hot, 1).astype(jnp.bfloat16)
+    grad_normed_two = at_home(own_grad_x, far_grad_x) + dot_f32(
+        grad_logits, w_route_full, 1, 1
+    )
+    grad_route = dot_f32(normed_two, grad_logits, 0, 0)
+    gained_two = grad_normed_two * gain_two
+    grad_gain_two = jnp.sum(grad_normed_two * resid * scale_two, 0)
+    grad_resid = (
+        grad_out
+        + scale_two * gained_two
+        - resid * scale_two**3 * jnp.mean(resid * gained_two, -1, keepdims=True)
+    )
+    grad_branch = grad_resid.astype(jnp.bfloat16)
+    grad_att = jnp.concatenate(
+        [
+            dot_f32(w_out_t, grad_branch[micro * rows : (micro + 1) * rows], 0, 1).astype(
+                jnp.bfloat16
+            )
+            for micro in micros
+        ],
+        0,
+    ).reshape(devices, HEAD_DIM, rows)
+    grad_outw = sum(
+        dot_f32(grad_branch[micro * rows : (micro + 1) * rows], attended_t[micro], 0, 1)
+        for micro in micros
+    )
+    grad_att, near_out_w = together(grad_att, near_out_w)
+    near_out_w = near_out_w.astype(jnp.float32)
+    grad_heads = every_device(grad_att)
+    grad_heads, near_out_w, far_in_w, near_in_w, last_in_w, far_out_w = together(
+        grad_heads, near_out_w, far_in_w, near_in_w, last_in_w, far_out_w
+    )
+    far_in_w = flip(far_in_w, 2 * PLANE)
+    near_in_w = flip(near_in_w, PLANE)
+    last_in_w = flip(last_in_w, 3 * PLANE)
+    far_out_w = flip(
+        (far_out_w[0].astype(jnp.float32) + near_out_w[1]).astype(jnp.bfloat16), 2 * PLANE
+    )
+
+    def to_shards(kept, given):
+        core_sum = kept.astype(jnp.float32) + swap_cores(given).astype(jnp.float32)
+        shares = lax.all_to_all(
+            core_sum.astype(jnp.bfloat16).reshape(ep_count, shard, -1), "ep", 0, 0, tiled=True
+        )
+        return jnp.sum(shares.astype(jnp.float32), 0)
+
+    def in_lanes(columns_f):
+        small = jnp.concatenate(columns_f, 1)
+        return jnp.pad(small, ((0, 0), (0, LANES - small.shape[1]))).astype(jnp.bfloat16)
+
+    def own_rows(values):
+        return lax.dynamic_slice_in_dim(values, tp_index * (shard // 2), shard // 2, 0)
+
+    grad_heads, grad_outw, grad_route, grad_gain_two = together(
+        grad_heads, grad_outw.astype(jnp.bfloat16), grad_route, grad_gain_two
+    )
+    late_small = in_lanes([grad_route, grad_gain_two[:, None]])
+    out_parts = [
+        jnp.concatenate([grad_outw[:, part * out_cols : (part + 1) * out_cols], late_small], 1)
+        for part in range(2)
+    ]
+    out_kept = jnp.where(tp_index == 0, out_parts[0], out_parts[1])
+    out_given = jnp.where(tp_index == 0, out_parts[1], out_parts[0])
+    out_sum = out_kept.astype(jnp.float32) + swap_cores(out_given).astype(jnp.float32)
+    plane_groups = [
+        [up * PLANE + step for step in range(PLANE)] for up in range(columns)
+    ]
+    column_groups = [
+        [up * PLANE + step for up in range(columns)] for step in range(PLANE)
+    ]
+    out_spots = lax.all_to_all(
+        jnp.swapaxes(
+            out_sum.astype(jnp.bfloat16).reshape(columns, PLANE, shard, -1), 0, 1
+        ),
+        "ep",
+        0,
+        0,
+        tiled=True,
+        axis_index_groups=plane_groups,
+    )
+
+    grad_q, keep_kv, send_kv = attend_back(
+        core, own, other, limit, out_f, log_total, grad_heads
+    )
+    grad_q, keep_kv, send_kv, far_in_w, near_in_w, last_in_w, far_out_w, out_spots = together(
+        grad_q, keep_kv, send_kv, far_in_w, near_in_w, last_in_w, far_out_w, out_spots
+    )
+    for micro in micros:
+        far_mix[micro] = far_mix[micro] + [
+            flip(after(part, grad_q), step) for part, step in late_mix[micro]
+        ]
+    grad_kv = (keep_kv + swap_cores(send_kv).astype(jnp.float32)).astype(jnp.bfloat16)
+    grad_own = every_device(jnp.concatenate([grad_q, grad_kv], 1))
+    grad_own, far_mix = together(grad_own, far_mix)
+
+    out_levels = jnp.sum(out_spots.astype(jnp.float32), 0).astype(jnp.bfloat16)
+    out_levels = lax.all_to_all(
+        out_levels, "ep", 0, 0, tiled=True, axis_index_groups=column_groups
+    )
+    out_share = jnp.sum(out_levels.astype(jnp.float32), 0)
+    out_small = own_rows(out_share[:, out_cols:])
+    grad_tokens, kept, given = project_back(
+        core, grad_own, w_heads, normed, tokens, grad_resid, gain_one[None, :], cosine, sine
+    )
+    kept, given, far_in_w, near_in_w, last_in_w, far_out_w = together(
+        kept, given, far_in_w, near_in_w, last_in_w, far_out_w
+    )
+    grad_in_w = own_w[:2] + sum(
+        part[0].astype(jnp.float32) for part in (far_in_w, near_in_w, last_in_w)
+    )
+    grad_out_w = own_w[2] + near_out_w[0, 0] + far_out_w[0].astype(jnp.float32)
+    mixed = (resid + at_home(own_mix, far_mix)).astype(jnp.bfloat16)
+
+    own_share = to_shards(kept, given)
+    head_grads = own_share[:, :half_cols].reshape(shard, kv_here, 2, 2, HEAD_DIM)
+    return (
+        mixed.reshape(micro_count, rows, width),
+        grad_tokens,
+        own_rows(own_share[:, half_cols:])[:, 0],
+        head_grads[:, :, :, 0].reshape(shard, q_cols),
+        head_grads[:, :, 0, 1].reshape(shard, kv_cols),
+        head_grads[:, :, 1, 1].reshape(shard, kv_cols),
+        out_share[:, :out_cols].T,
+        out_small[:, experts_all],
+        out_small[:, :experts_all],
+        grad_in_w[0][None],
+        grad_in_w[1][None],
+        grad_out_w.T[None],
+    )
+
+
+def on_device(*args):
+    tokens, w_query, w_key, w_gate = args[0], args[2], args[3], args[8]
+    paired = paired_layout(
+        lax.axis_size("ep"),
+        lax.axis_size("tp"),
+        *tokens.shape,
+        w_query.shape[1],
+        w_key.shape[1],
+        w_gate.shape[0],
+    )
+    return (on_device_paired if paired else on_device_general)(*args)
+
+
 def solution(mesh):
     in_specs = (
         P(None, ("ep", "tp"), None),

time: 3500 us -> 781 us (0.22)
  waiting for transfers between devices: 1520 us -> 265 us
  matrix products: 964 us -> 7.48 us
  blocking collectives: 305 us -> 0 us
  Pallas kernels: 0 us -> 300 us
  other arithmetic: 346 us -> 50 us
  local copies, waits for them, and re-layouts: 268 us -> 43.2 us
  starting transfers between devices: 50.2 us -> 92.2 us
    dot_general x272 -> x9, matrix products: 964 us -> 7.48 us  [the longest x8 5.81 us: dot_f32(): lax.dot_general(left, right, (((left_dim,), (right_dim,)), ((), ())), pre...]
    all_to_all x8 -> x7, waiting for transfers between devices: 778 us -> 118 us  [the longest x4 81.3 us: every_device(): return lax.all_to_all(values, ('ep', 'tp'), 0, 0, tiled=True)]
    reduce_scatter x18 -> x0, waiting for transfers between devices: 479 us -> none  [the longest x2 139 us: reduce_grads(): lax.psum_scatter(grad_outw.astype(jnp.bfloat16), 'ep', scatter_dimension=...]
    pallas_call x0 -> x7, Pallas kernels: none -> 300 us  [the longest x3 114 us: experts(): pl.pallas_call(functools.partial(experts_kernel, slots=slots, first_call=...]
    all_gather x3 -> x0, blocking collectives: 244 us -> none  [the longest x1 162 us: on_device(): lax.all_gather(w_router, 'ep', axis=0, tiled=True)]
    reduce_sum x45 -> x8, other arithmetic: 157 us -> 3.31 us  [the longest x1 2.01 us: to_shards(): return jnp.sum(shares.astype(jnp.float32), 0)]
    ppermute x0 -> x54, waiting for transfers between devices: none -> 147 us  [the longest x40 142 us: flip(): lax.ppermute(values, 'ep', [(index, index ^ bits) for index in range(coun...]
    all_gather x10 -> x1, waiting for transfers between devices: 141 us -> 0.02 us  [on_device_paired(): gathered_out = lax.all_gather(w_output_t, ('ep', 'tp'), axis=0, tiled=False)]
  transfers between devices with their start and end apart: 38 -> 62, of which waited for: 25 -> 24; matrix products, arithmetic and copies ran while one was open for 41% -> 8% of each run, Pallas kernels for 0% -> 37%
where the time goes in v2:
time: 781 us; the launch traced here: 774 us
  Pallas kernels  300 us (38%)
  waiting for transfers between devices  265 us (34%)
  starting transfers between devices  92.2 us (12%)
  other arithmetic  50 us (6%)
  local copies, waits for them, and re-layouts  43.2 us (6%)
  between operations  15.7 us (2%)
    ppermute x40, waiting for transfers between devices, flip(): lax.ppermute(values, 'ep', [(index, index ^ bits) for index in range(coun...  142 us
    pallas_call x3, Pallas kernels, experts(): pl.pallas_call(functools.partial(experts_kernel, slots=slots, first_call=...  114 us
    pallas_call x1, Pallas kernels, attend_back(): pl.pallas_call(functools.partial(attend_back_kernel, query_block=query_bl...  109 us
    all_to_all x4, waiting for transfers between devices, every_device(): return lax.all_to_all(values, ('ep', 'tp'), 0, 0, tiled=True)  81.3 us
    pallas_call x1, Pallas kernels, attend(): pl.pallas_call(functools.partial(attend_kernel, query_block=query_block,...  59.8 us
    ppermute x40, starting transfers between devices, flip(): lax.ppermute(values, 'ep', [(index, index ^ bits) for index in range(coun...  47.4 us
    all_to_all x1, waiting for transfers between devices, to_shards(): lax.all_to_all(core_sum.astype(jnp.bfloat16).reshape(ep_count, shard, -1)...  32.2 us
    all_to_all x4, starting transfers between devices, every_device(): return lax.all_to_all(values, ('ep', 'tp'), 0, 0, tiled=True)  22.7 us
  transfers between devices with their start and end apart: 62, of which 24 were waited for; matrix products, arithmetic and copies ran while one was open for 8% of the time, Pallas kernels for 37%

profile of v2, /device:TPU:14, one launch (start us, length us, event | category | flops | bytes accessed | tf_op | source)
XLA Modules:
  0.0 774.0 jit_solution(6532991751299875729)
XLA Ops:
  13.5 2.6 collective-permute-start.1
  19.8 7.0 collective-permute-done.1
  26.8 2.9 collective-permute-done.2
  31.9 2.4 collective-permute-start.5
  35.2 20.2 %collective-permute-done.6.refs_13_.refs_15_ = bf16[1,512,512]{2,1,0:T(8,128)(2,1)S(1)} collective-permute-done((bf16[1,512,512]{2,1,0:T(8,128)(2,1)S(1)}, bf16[1,512,512]{2,1,0:T(8,128)(2,1)S(1)}, u32[]{:S(2)}, u32[]{:S(2)}) %collective-permute-start.6) | collective-permute-done | bytes 524320 | tf_op jit(solution)/shard_map/ppermute | solution.py:1099
  55.4 2.3 collective-permute-done.4.refs_6_
  63.4 5.9 project.1
  71.6 5.2 all-to-all-start
  77.5 2.9 fusion.2
  82.5 40.5 %all-to-all-done.own_ref = bf16[32,128,256]{2,1,0:T(8,128)(2,1)} async-done(((bf16[32,128,256]{2,1,0:T(8,128)(2,1)}), bf16[32,128,256]{2,1,0:T(8,128)(2,1)}, u32[]{:S(2)}, u32[]{:S(2)}) %all-to-all-start) | async-done | bytes 2097184 | tf_op jit(solution)/shard_map/all_to_all | solution.py:1111
  125.1 2.8 collective-permute-start.17
  136.9 59.8 %attend.1 = (bf16[32,64,256]{2,1,0:T(8,128)(2,1)}, f32[32,64,256]{2,1,0:T(8,128)}, f32[1,8192]{1,0:T(1,128)}) custom-call(s32[1]{0:T(128)} %bitcast.tp_ref, bf16[32,128,256]{2,1,0:T(8,128)(2,1)} %all-to-all-done.own_ref, bf16[32,64,256]{2,1,0:T(8,128)(2,1)} %copy-done.60, s32[1,8192]{1,0:T(1,128)} %iota_maximum_fusion.limit_ref), custom_call_target="tpu_custom_call" | custom-call | flops 34359738368 | bytes 8388608 | tf_op jit(solution)/shard_map/attend/pallas_call | solution.py:605
  196.8 2.7 collective-permute-done.16.refs_17_.refs_19_
  199.5 5.8 all-to-all-start.1
  207.2 27.8 %all-to-all-done.1 = bf16[32,64,256]{2,1,0:T(8,128)(2,1)S(1)} async-done(((bf16[32,64,256]{2,1,0:T(8,128)(2,1)}), bf16[32,64,256]{2,1,0:T(8,128)(2,1)S(1)}, u32[]{:S(2)}, u32[]{:S(2)}) %all-to-all-start.1) | async-done | bytes 1048608 | tf_op jit(solution)/shard_map/all_to_all | solution.py:1111
  241.9 10.1 %collective-permute-done.21.refs_15_.refs_17_ = bf16[2,512,512]{2,1,0:T(8,128)(2,1)} collective-permute-done((bf16[2,512,512]{2,1,0:T(8,128)(2,1)}, bf16[2,512,512]{2,1,0:T(8,128)(2,1)}, u32[]{:S(2)}, u32[]{:S(2)}) %collective-permute-start.21) | collective-permute-done | bytes 1048608 | tf_op jit(solution)/shard_map/ppermute | solution.py:1099
  252.5 2.3 copy.117
  257.3 2.6 collective-permute-start.29
  259.8 29.1 %experts.3 = (bf16[256,1024]{1,0:T(8,128)(2,1)}, bf16[256,1024]{1,0:T(8,128)(2,1)}, bf16[256,1024]{1,0:T(8,128)(2,1)}, bf16[256,1024]{1,0:T(8,128)(2,1)}, f32[2,...) custom-call(s32[5]{0:T(128)} %concatenate.57.refs_0_, ...), custom_call_target="tpu_custom_call" | custom-call | flops 19327352832 | bytes 25165824 | tf_op jit(solution)/shard_map/experts/pallas_call | solution.py:1042
  289.9 2.6 collective-permute-start.26
  292.5 41.7 %experts.4 = (bf16[256,1024]{1,0:T(8,128)(2,1)}, bf16[256,1024]{1,0:T(8,128)(2,1)}, bf16[256,1024]{1,0:T(8,128)(2,1)}, bf16[256,1024]{1,0:T(8,128)(2,1)}, bf16[2...) custom-call(s32[5]{0:T(128)} %concatenate.57.refs_0_, ...), custom_call_target="tpu_custom_call" | custom-call | flops 28991029248 | bytes 25165824 | tf_op jit(solution)/shard_map/experts/pallas_call | solution.py:1042
  335.2 2.6 collective-permute-start.32
  338.8 42.7 %experts.5 = (bf16[256,1024]{1,0:T(8,128)(2,1)}, bf16[256,1024]{1,0:T(8,128)(2,1)}, bf16[256,1024]{1,0:T(8,128)(2,1)}, bf16[256,1024]{1,0:T(8,128)(2,1)}, bf16[2...) custom-call(s32[5]{0:T(128)} %concatenate.57.refs_0_, ...), custom_call_target="tpu_custom_call" | custom-call | flops 28991029248 | bytes 25165824 | tf_op jit(solution)/shard_map/experts/pallas_call | solution.py:1042
  395.5 7.5 collective-permute-done.36
  403.0 13.1 %collective-permute-done.37 = bf16[256,1024]{1,0:T(8,128)(2,1)S(1)} collective-permute-done((bf16[256,1024]{1,0:T(8,128)(2,1)S(1)}, bf16[256,1024]{1,0:T(8,128)(2,1)S(1)}, u32[]{:S(2)}, u32[]{:S(2)}) %collective-permute-start.37) | collective-permute-done | bytes 524320 | tf_op jit(solution)/shard_map/ppermute | solution.py:1099
  423.8 17.2 %collective-permute-done.42 = bf16[2,1,512,512]{3,2,1,0:T(8,128)(2,1)S(1)} collective-permute-done((bf16[2,1,512,512]{3,2,1,0:T(8,128)(2,1)S(1)}, bf16[2,1,512,512]{3,2,1,0:T(8,128)(2,1)S(1)}, u32[]{:S(2)}, u32[]{:S(2)}) %collective-permute-start.42) | collective-permute-done | bytes 1048608 | tf_op jit(solution)/shard_map/ppermute | solution.py:1099
  441.9 5.9 all-to-all-start.2
  451.0 5.1 add_convert_fusion.5
  459.0 13.0 %all-to-all-done.2.grad_ref = bf16[32,64,256]{2,1,0:T(8,128)(2,1)} async-done(((bf16[32,64,256]{2,1,0:T(8,128)(2,1)}), bf16[32,64,256]{2,1,0:T(8,128)(2,1)}, u32[]{:S(2)}, u32[]{:S(2)}) %all-to-all-start.2) | async-done | bytes 1048608 | tf_op jit(solution)/shard_map/all_to_all | solution.py:1111
  475.0 2.4 collective-permute-start.46
  477.9 2.4 collective-permute-start.44
  482.7 4.4 all-to-all-start.3
  487.1 109.3 %attend_back.1 = (bf16[32,64,256]{2,1,0:T(8,128)(2,1)}, f32[32,64,256]{2,1,0:T(8,128)}, bf16[32,64,256]{2,1,0:T(8,128)(2,1)}) custom-call(s32[1]{0:T(128)} %bitcast.tp_ref, bf16[32,128,256]{2,1,0:T(8,128)(2,1)} %all-to-all-done.own_ref, bf16[32,64,256]{2,1,0:T(8,128)(2,1)} %copy-done.60, s32[1,8192]{1,0:T(1,128)} %iota_maximum_fusion.limit_ref, ...), custom_call_target="tpu_custom_call" | custom-call | flops 68719476736 | bytes 12582912 | tf_op jit(solution)/shard_map/attend_back/pallas_call | solution.py:750
  596.6 2.9 collective-permute-done.48
  603.0 5.8 all-to-all-start.4
  612.9 31.5 %collective-permute-done.52 = bf16[256,1024]{1,0:T(8,128)(2,1)S(1)} collective-permute-done((bf16[256,1024]{1,0:T(8,128)(2,1)}, bf16[256,1024]{1,0:T(8,128)(2,1)S(1)}, u32[]{:S(2)}, u32[]{:S(2)}) %collective-permute-start.52) | collective-permute-done | bytes 524320 | tf_op jit(solution)/shard_map/ppermute | solution.py:1099
  644.4 11.0 %collective-permute-done.51 = bf16[256,1024]{1,0:T(8,128)(2,1)S(1)} collective-permute-done((bf16[256,1024]{1,0:T(8,128)(2,1)}, bf16[256,1024]{1,0:T(8,128)(2,1)S(1)}, u32[]{:S(2)}, u32[]{:S(2)}) %collective-permute-start.51) | collective-permute-done | bytes 524320 | tf_op jit(solution)/shard_map/ppermute | solution.py:1099
  655.4 2.4 collective-permute-done.50
  658.6 10.1 %collective-permute-done.49 = bf16[256,1024]{1,0:T(8,128)(2,1)} collective-permute-done((bf16[256,1024]{1,0:T(8,128)(2,1)}, bf16[256,1024]{1,0:T(8,128)(2,1)}, u32[]{:S(2)}, u32[]{:S(2)}) %collective-permute-start.49) | collective-permute-done | bytes 524320 | tf_op jit(solution)/shard_map/ppermute | solution.py:1099
  670.1 11.7 %project_back.1 = (f32[2,256,1024]{2,1,0:T(8,128)}, bf16[1024,1152]{1,0:T(8,128)(2,1)}, bf16[1024,1152]{1,0:T(8,128)(2,1)}) custom-call(s32[1]{0:T(128)} %bitcast.tp_ref, bf16[32,128,256]{2,1,0:T(8,128)(2,1)} %copy-done.17, bf16[2,1024,1024]{2,1,0:T(8,128)(2,1)} %get-tuple-element.230.heads_ref, bf16[512,1024]{1,0:T(8,128)(2,1)} %copy-done.2, ...), custom_call_target="tpu_custom_call" | custom-call | tf_op jit(solution)/shard_map/project_back/pallas_call | solution.py:899
  682.7 5.5 all-to-all-start.6
  688.2 4.4 add_convert_fusion
  692.5 4.2 all-to-all-done.6
  696.8 9.3 %all-to-all-start.5 = ((bf16[16,64,1152]{2,1,0:T(8,128)(2,1)}), bf16[16,64,1152]{2,1,0:T(8,128)(2,1)}, u32[]{:S(2)}, u32[]{:S(2)}) async-start(bf16[16,64,1152]{2,1,0:T(8,128)(2,1)} %bitcast.62), calls=%async_computation.5 | async-start | bytes 4718592 | tf_op jit(solution)/shard_map/all_to_all | solution.py:1391
  706.1 2.4 convert_add_fusion
  712.1 2.6 fusion.7
  714.7 2.5 copy.121
  727.3 32.2 %all-to-all-done.5 = bf16[16,64,1152]{2,1,0:T(8,128)(2,1)} async-done(((bf16[16,64,1152]{2,1,0:T(8,128)(2,1)}), bf16[16,64,1152]{2,1,0:T(8,128)(2,1)}, u32[]{:S(2)}, u32[]{:S(2)}) %all-to-all-start.5) | async-done | bytes 2359328 | tf_op jit(solution)/shard_map/all_to_all | solution.py:1391
  (329 shorter events, 115.2 us)
Async XLA Ops:
  13.5 13.3 %collective-permute-start.1 = (bf16[64,1152]{1,0:T(8,128)(2,1)}, bf16[64,1152]{1,0:T(8,128)(2,1)}, u32[]{:S(2)}, u32[]{:S(2)}) collective-permute-start(bf16[64,1152]{1,0:T(8,128)(2,1)} %get-tuple-element.354), channel_id=1, source_target_pairs={{0,16},{2,18},{4,20},{6,22},{8,24},{10,26},{12,28},{14,30},{16,0},... | collective-permute-start | bytes 442376 | tf_op jit(solution)/shard_map/ppermute | solution.py:1099
  16.1 13.6 %collective-permute-start.2 = (bf16[64,1152]{1,0:T(8,128)(2,1)}, bf16[64,1152]{1,0:T(8,128)(2,1)}, u32[]{:S(2)}, u32[]{:S(2)}) collective-permute-start(bf16[64,1152]{1,0:T(8,128)(2,1)} %get-tuple-element.354), channel_id=1, source_target_pairs={{0,24},{2,26},{4,28},{6,30},{8,16},{10,18},{12,20},{14,22},{16,8},... | collective-permute-start | bytes 442376 | tf_op jit(solution)/shard_map/ppermute | solution.py:1099
  30.8 24.6 %collective-permute-start.3 = (bf16[4,64,1152]{2,1,0:T(8,128)(2,1)S(1)}, bf16[4,64,1152]{2,1,0:T(8,128)(2,1)S(1)}, u32[]{:S(2)}, u32[]{:S(2)}) collective-permute-start(bf16[4,64,1152]{2,1,0:T(8,128)(2,1)S(1)} %pad_maximum_fusion.7.refs_4_), channel_id=1, source_target_pairs={{0,2},{2,0},{4,6},{6,4},{8,10},{10,8},{12,14},{14,12},{16,18},{18,... | collective-permute-start | bytes 1769480 | tf_op jit(solution)/shard_map/ppermute | solution.py:1099
  31.4 26.3 %collective-permute-start.4 = (bf16[4,64,1152]{2,1,0:T(8,128)(2,1)S(1)}, bf16[4,64,1152]{2,1,0:T(8,128)(2,1)S(1)}, u32[]{:S(2)}, u32[]{:S(2)}) collective-permute-start(bf16[4,64,1152]{2,1,0:T(8,128)(2,1)S(1)} %pad_maximum_fusion.7.refs_4_), channel_id=1, source_target_pairs={{0,4},{2,6},{4,0},{6,2},{8,12},{10,14},{12,8},{14,10},{16,20},{18,... | collective-permute-start | bytes 1769480 | tf_op jit(solution)/shard_map/ppermute | solution.py:1099
  31.9 25.8 %collective-permute-start.5 = (bf16[4,64,1152]{2,1,0:T(8,128)(2,1)S(1)}, bf16[4,64,1152]{2,1,0:T(8,128)(2,1)S(1)}, u32[]{:S(2)}, u32[]{:S(2)}) collective-permute-start(bf16[4,64,1152]{2,1,0:T(8,128)(2,1)S(1)} %pad_maximum_fusion.7.refs_4_), channel_id=1, source_target_pairs={{0,6},{2,4},{4,2},{6,0},{8,14},{10,12},{12,10},{14,8},{16,22},{18,... | collective-permute-start | bytes 1769480 | tf_op jit(solution)/shard_map/ppermute | solution.py:1099
  34.6 20.8 %collective-permute-start.6 = (bf16[1,512,512]{2,1,0:T(8,128)(2,1)S(1)}, bf16[1,512,512]{2,1,0:T(8,128)(2,1)S(1)}, u32[]{:S(2)}, u32[]{:S(2)}) collective-permute-start(bf16[1,512,512]{2,1,0:T(8,128)(2,1)S(1)} %slice.161), channel_id=1, source_target_pairs={{0,16},{2,18},{4,20},{6,22},{8,24},{10,26},{12,28},{14,30},{16,0},... | collective-permute-start | bytes 1572872 | tf_op jit(solution)/shard_map/ppermute | solution.py:1099
  71.6 51.5 %all-to-all-start = ((bf16[32,128,256]{2,1,0:T(8,128)(2,1)}), bf16[32,128,256]{2,1,0:T(8,128)(2,1)}, u32[]{:S(2)}, u32[]{:S(2)}) async-start(bf16[32,128,256]{2,1,0:T(8,128)(2,1)} %get-tuple-element.134), calls=%async_computation | async-start | bytes 4194304 | tf_op jit(solution)/shard_map/all_to_all | solution.py:1111
  76.8 158.4 %all-gather.3.cloned.1.call-start = ((), (), s32[]{:S(2)}) async-start(), calls=%async_computation.7 | async-start | bytes 2162688 | tf_op jit(solution)/shard_map/all_gather | solution.py:1232
  82.0 48.1 %collective-permute-start.12 = (bf16[2,256,1152]{2,1,0:T(8,128)(2,1)}, bf16[2,256,1152]{2,1,0:T(8,128)(2,1)S(1)}, u32[]{:S(2)}, u32[]{:S(2)}) collective-permute-start(bf16[2,256,1152]{2,1,0:T(8,128)(2,1)} %pad_maximum_fusion.5.refs_3_.refs_4_), channel_id=1, source_target_pairs={{0,6},{2,4},{4,2},{6,0},{8,14},{10,12},{12,10},{14,8},{16,22},{18,... | collective-permute-start | bytes 3538952 | tf_op jit(solution)/shard_map/ppermute | solution.py:1099
  125.1 71.6 %collective-permute-start.17 = (bf16[3,512,512]{2,1,0:T(8,128)(2,1)S(1)}, bf16[3,512,512]{2,1,0:T(8,128)(2,1)}, u32[]{:S(2)}, u32[]{:S(2)}) collective-permute-start(bf16[3,512,512]{2,1,0:T(8,128)(2,1)S(1)} %copy-done.20), channel_id=1, source_target_pairs={{0,8},{2,10},{4,12},{6,14},{8,0},{10,2},{12,4},{14,6},{16,24},{18,... | collective-permute-start | bytes 4718600 | tf_op jit(solution)/shard_map/ppermute | solution.py:1099
  131.1 68.4 %collective-permute-start.14 = (bf16[2,256,1152]{2,1,0:T(8,128)(2,1)}, bf16[2,256,1152]{2,1,0:T(8,128)(2,1)}, u32[]{:S(2)}, u32[]{:S(2)}) collective-permute-start(bf16[2,256,1152]{2,1,0:T(8,128)(2,1)} %pad_maximum_fusion.5.refs_3_.refs_4_), channel_id=1, source_target_pairs={{0,2},{2,0},{4,6},{6,4},{8,10},{10,8},{12,14},{14,12},{16,18},{18,... | collective-permute-start | bytes 3538952 | tf_op jit(solution)/shard_map/ppermute | solution.py:1099
  132.5 67.0 %collective-permute-start.15 = (bf16[2,256,1152]{2,1,0:T(8,128)(2,1)}, bf16[2,256,1152]{2,1,0:T(8,128)(2,1)}, u32[]{:S(2)}, u32[]{:S(2)}) collective-permute-start(bf16[2,256,1152]{2,1,0:T(8,128)(2,1)} %pad_maximum_fusion.5.refs_3_.refs_4_), channel_id=1, source_target_pairs={{0,4},{2,6},{4,0},{6,2},{8,12},{10,14},{12,8},{14,10},{16,20},{18,... | collective-permute-start | bytes 3538952 | tf_op jit(solution)/shard_map/ppermute | solution.py:1099
  133.4 66.0 %collective-permute-start.13 = (bf16[2,512,512]{2,1,0:T(8,128)(2,1)S(1)}, bf16[2,512,512]{2,1,0:T(8,128)(2,1)}, u32[]{:S(2)}, u32[]{:S(2)}) collective-permute-start(bf16[2,512,512]{2,1,0:T(8,128)(2,1)S(1)} %slice.163), channel_id=1, source_target_pairs={{0,16},{2,18},{4,20},{6,22},{8,24},{10,26},{12,28},{14,30},{16,0},... | collective-permute-start | bytes 3145736 | tf_op jit(solution)/shard_map/ppermute | solution.py:1099
  135.5 64.0 %collective-permute-start.16 = (bf16[1,512,512]{2,1,0:T(8,128)(2,1)}, bf16[1,512,512]{2,1,0:T(8,128)(2,1)}, u32[]{:S(2)}, u32[]{:S(2)}) collective-permute-start(bf16[1,512,512]{2,1,0:T(8,128)(2,1)} %copy-done.61), channel_id=1, source_target_pairs={{0,8},{2,10},{4,12},{6,14},{8,0},{10,2},{12,4},{14,6},{16,24},{18,... | collective-permute-start | bytes 1572872 | tf_op jit(solution)/shard_map/ppermute | solution.py:1099
  199.5 35.6 %all-to-all-start.1 = ((bf16[32,64,256]{2,1,0:T(8,128)(2,1)}), bf16[32,64,256]{2,1,0:T(8,128)(2,1)S(1)}, u32[]{:S(2)}, u32[]{:S(2)}) async-start(bf16[32,64,256]{2,1,0:T(8,128)(2,1)} %get-tuple-element.144), calls=%async_computation.1 | async-start | bytes 2097152 | tf_op jit(solution)/shard_map/all_to_all | solution.py:1111
  206.2 45.8 %collective-permute-start.21 = (bf16[2,512,512]{2,1,0:T(8,128)(2,1)}, bf16[2,512,512]{2,1,0:T(8,128)(2,1)}, u32[]{:S(2)}, u32[]{:S(2)}) collective-permute-start(bf16[2,512,512]{2,1,0:T(8,128)(2,1)} %collective-permute-done.13.refs_11_.refs_13_), channel_id=1, source_target_pairs={{0,8},{2,10},{4,12},{6,14},{8,0},{10,2},{12,4},{14,6},{16,24},{18,... | collective-permute-start | bytes 3145736 | tf_op jit(solution)/shard_map/ppermute | solution.py:1099
  206.7 50.5 %collective-permute-start.19 = (bf16[2,512,512]{2,1,0:T(8,128)(2,1)}, bf16[2,512,512]{2,1,0:T(8,128)(2,1)}, u32[]{:S(2)}, u32[]{:S(2)}) collective-permute-start(bf16[2,512,512]{2,1,0:T(8,128)(2,1)} %collective-permute-done.13.refs_11_.refs_13_), channel_id=1, source_target_pairs={{0,1},{1,0},{2,3},{3,2},{4,5},{5,4},{6,7},{7,6},{8,9},{9,8},{10,11... | collective-permute-start | bytes 3145736 | tf_op jit(solution)/shard_map/ppermute | solution.py:1103
  206.7 53.1 %collective-permute-start.18 = (bf16[3,512,512]{2,1,0:T(8,128)(2,1)}, bf16[3,512,512]{2,1,0:T(8,128)(2,1)}, u32[]{:S(2)}, u32[]{:S(2)}) collective-permute-start(bf16[3,512,512]{2,1,0:T(8,128)(2,1)} %collective-permute-done.17.refs_9_.refs_11_), channel_id=1, source_target_pairs={{0,1},{1,0},{2,3},{3,2},{4,5},{5,4},{6,7},{7,6},{8,9},{9,8},{10,11... | collective-permute-start | bytes 4718600 | tf_op jit(solution)/shard_map/ppermute | solution.py:1103
  256.3 33.6 %collective-permute-start.27 = (bf16[256,1024]{1,0:T(8,128)(2,1)S(1)}, bf16[256,1024]{1,0:T(8,128)(2,1)}, u32[]{:S(2)}, u32[]{:S(2)}) collective-permute-start(bf16[256,1024]{1,0:T(8,128)(2,1)S(1)} %get-tuple-element.349), channel_id=1, source_target_pairs={{0,2},{2,0},{4,6},{6,4},{8,10},{10,8},{12,14},{14,12},{16,18},{18,... | collective-permute-start | bytes 1572872 | tf_op jit(solution)/shard_map/ppermute | solution.py:1099
  256.9 35.6 %collective-permute-start.28 = (bf16[256,1024]{1,0:T(8,128)(2,1)S(1)}, bf16[256,1024]{1,0:T(8,128)(2,1)}, u32[]{:S(2)}, u32[]{:S(2)}) collective-permute-start(bf16[256,1024]{1,0:T(8,128)(2,1)S(1)} %get-tuple-element.349), channel_id=1, source_target_pairs={{0,4},{2,6},{4,0},{6,2},{8,12},{10,14},{12,8},{14,10},{16,20},{18,... | collective-permute-start | bytes 1572872 | tf_op jit(solution)/shard_map/ppermute | solution.py:1099
  257.3 35.3 %collective-permute-start.29 = (bf16[256,1024]{1,0:T(8,128)(2,1)S(1)}, bf16[256,1024]{1,0:T(8,128)(2,1)}, u32[]{:S(2)}, u32[]{:S(2)}) collective-permute-start(bf16[256,1024]{1,0:T(8,128)(2,1)S(1)} %get-tuple-element.349), channel_id=1, source_target_pairs={{0,6},{2,4},{4,2},{6,0},{8,14},{10,12},{12,10},{14,8},{16,22},{18,... | collective-permute-start | bytes 1572872 | tf_op jit(solution)/shard_map/ppermute | solution.py:1099
  289.0 46.3 %collective-permute-start.24 = (bf16[256,1024]{1,0:T(8,128)(2,1)}, bf16[256,1024]{1,0:T(8,128)(2,1)}, u32[]{:S(2)}, u32[]{:S(2)}) collective-permute-start(bf16[256,1024]{1,0:T(8,128)(2,1)} %get-tuple-element.156), channel_id=1, source_target_pairs={{0,2},{2,0},{4,6},{6,4},{8,10},{10,8},{12,14},{14,12},{16,18},{18,... | collective-permute-start | bytes 1572872 | tf_op jit(solution)/shard_map/ppermute | solution.py:1099
  289.6 48.2 %collective-permute-start.25 = (bf16[256,1024]{1,0:T(8,128)(2,1)}, bf16[256,1024]{1,0:T(8,128)(2,1)}, u32[]{:S(2)}, u32[]{:S(2)}) collective-permute-start(bf16[256,1024]{1,0:T(8,128)(2,1)} %get-tuple-element.156), channel_id=1, source_target_pairs={{0,4},{2,6},{4,0},{6,2},{8,12},{10,14},{12,8},{14,10},{16,20},{18,... | collective-permute-start | bytes 1572872 | tf_op jit(solution)/shard_map/ppermute | solution.py:1099
  289.9 48.4 %collective-permute-start.26 = (bf16[256,1024]{1,0:T(8,128)(2,1)}, bf16[256,1024]{1,0:T(8,128)(2,1)}, u32[]{:S(2)}, u32[]{:S(2)}) collective-permute-start(bf16[256,1024]{1,0:T(8,128)(2,1)} %get-tuple-element.156), channel_id=1, source_target_pairs={{0,6},{2,4},{4,2},{6,0},{8,14},{10,12},{12,10},{14,8},{16,22},{18,... | collective-permute-start | bytes 1572872 | tf_op jit(solution)/shard_map/ppermute | solution.py:1099
  334.3 47.2 %collective-permute-start.30 = (bf16[256,1024]{1,0:T(8,128)(2,1)}, bf16[256,1024]{1,0:T(8,128)(2,1)}, u32[]{:S(2)}, u32[]{:S(2)}) collective-permute-start(bf16[256,1024]{1,0:T(8,128)(2,1)} %get-tuple-element.173), channel_id=1, source_target_pairs={{0,2},{2,0},{4,6},{6,4},{8,10},{10,8},{12,14},{14,12},{16,18},{18,... | collective-permute-start | bytes 1572872 | tf_op jit(solution)/shard_map/ppermute | solution.py:1099
  334.9 46.6 %collective-permute-start.31 = (bf16[256,1024]{1,0:T(8,128)(2,1)}, bf16[256,1024]{1,0:T(8,128)(2,1)}, u32[]{:S(2)}, u32[]{:S(2)}) collective-permute-start(bf16[256,1024]{1,0:T(8,128)(2,1)} %get-tuple-element.174), channel_id=1, source_target_pairs={{0,4},{2,6},{4,0},{6,2},{8,12},{10,14},{12,8},{14,10},{16,20},{18,... | collective-permute-start | bytes 1572872 | tf_op jit(solution)/shard_map/ppermute | solution.py:1099
  335.2 46.2 %collective-permute-start.32 = (bf16[256,1024]{1,0:T(8,128)(2,1)}, bf16[256,1024]{1,0:T(8,128)(2,1)}, u32[]{:S(2)}, u32[]{:S(2)}) collective-permute-start(bf16[256,1024]{1,0:T(8,128)(2,1)} %get-tuple-element.175), channel_id=1, source_target_pairs={{0,6},{2,4},{4,2},{6,0},{8,14},{10,12},{12,10},{14,8},{16,22},{18,... | collective-permute-start | bytes 1572872 | tf_op jit(solution)/shard_map/ppermute | solution.py:1099
  337.8 43.7 %collective-permute-start.33 = (bf16[256,1024]{1,0:T(8,128)(2,1)}, bf16[256,1024]{1,0:T(8,128)(2,1)S(1)}, u32[]{:S(2)}, u32[]{:S(2)}) collective-permute-start(bf16[256,1024]{1,0:T(8,128)(2,1)} %get-tuple-element.176), channel_id=1, source_target_pairs={{0,2},{2,0},{4,6},{6,4},{8,10},{10,8},{12,14},{14,12},{16,18},{18,... | collective-permute-start | bytes 1572872 | tf_op jit(solution)/shard_map/ppermute | solution.py:1099
  338.4 43.1 %collective-permute-start.34 = (bf16[256,1024]{1,0:T(8,128)(2,1)}, bf16[256,1024]{1,0:T(8,128)(2,1)}, u32[]{:S(2)}, u32[]{:S(2)}) collective-permute-start(bf16[256,1024]{1,0:T(8,128)(2,1)} %get-tuple-element.177), channel_id=1, source_target_pairs={{0,4},{2,6},{4,0},{6,2},{8,12},{10,14},{12,8},{14,10},{16,20},{18,... | collective-permute-start | bytes 1572872 | tf_op jit(solution)/shard_map/ppermute | solution.py:1099
  381.5 12.0 %collective-permute-start.35 = (bf16[4,3,512,512]{3,2,1,0:T(8,128)(2,1)}, bf16[4,3,512,512]{3,2,1,0:T(8,128)(2,1)}, u32[]{:S(2)}, u32[]{:S(2)}) collective-permute-start(bf16[4,3,512,512]{3,2,1,0:T(8,128)(2,1)} %get-tuple-element.183), channel_id=1, source_target_pairs={{0,1},{1,0},{2,3},{3,2},{4,5},{5,4},{6,7},{7,6},{8,9},{9,8},{10,11... | collective-permute-start | bytes 18874376 | tf_op jit(solution)/shard_map/ppermute | solution.py:1103
  387.9 15.0 %collective-permute-start.36 = (bf16[256,1024]{1,0:T(8,128)(2,1)}, bf16[256,1024]{1,0:T(8,128)(2,1)S(1)}, u32[]{:S(2)}, u32[]{:S(2)}) collective-permute-start(bf16[256,1024]{1,0:T(8,128)(2,1)} %get-tuple-element.184), channel_id=1, source_target_pairs={{0,2},{2,0},{4,6},{6,4},{8,10},{10,8},{12,14},{14,12},{16,18},{18,... | collective-permute-start | bytes 1572872 | tf_op jit(solution)/shard_map/ppermute | solution.py:1099
  391.5 24.5 %collective-permute-start.37 = (bf16[256,1024]{1,0:T(8,128)(2,1)S(1)}, bf16[256,1024]{1,0:T(8,128)(2,1)S(1)}, u32[]{:S(2)}, u32[]{:S(2)}) collective-permute-start(bf16[256,1024]{1,0:T(8,128)(2,1)S(1)} %copy-done.64), channel_id=1, source_target_pairs={{0,4},{2,6},{4,0},{6,2},{8,12},{10,14},{12,8},{14,10},{16,20},{18,... | collective-permute-start | bytes 1572872 | tf_op jit(solution)/shard_map/ppermute | solution.py:1099
  393.0 23.0 %collective-permute-start.38 = (bf16[256,1024]{1,0:T(8,128)(2,1)S(1)}, bf16[256,1024]{1,0:T(8,128)(2,1)S(1)}, u32[]{:S(2)}, u32[]{:S(2)}) collective-permute-start(bf16[256,1024]{1,0:T(8,128)(2,1)S(1)} %copy-done.63), channel_id=1, source_target_pairs={{0,6},{2,4},{4,2},{6,0},{8,14},{10,12},{12,10},{14,8},{16,22},{18,... | collective-permute-start | bytes 1572872 | tf_op jit(solution)/shard_map/ppermute | solution.py:1099
  417.4 23.6 %collective-permute-start.42 = (bf16[2,1,512,512]{3,2,1,0:T(8,128)(2,1)S(1)}, bf16[2,1,512,512]{3,2,1,0:T(8,128)(2,1)S(1)}, u32[]{:S(2)}, u32[]{:S(2)}) collective-permute-start(bf16[2,1,512,512]{3,2,1,0:T(8,128)(2,1)S(1)} %add_convert_fusion.8), channel_id=1, source_target_pairs={{0,8},{2,10},{4,12},{6,14},{8,0},{10,2},{12,4},{14,6},{16,24},{18,... | collective-permute-start | bytes 3145736 | tf_op jit(solution)/shard_map/ppermute | solution.py:1099
  441.9 30.1 %all-to-all-start.2 = ((bf16[32,64,256]{2,1,0:T(8,128)(2,1)}), bf16[32,64,256]{2,1,0:T(8,128)(2,1)}, u32[]{:S(2)}, u32[]{:S(2)}) async-start(bf16[32,64,256]{2,1,0:T(8,128)(2,1)} %bitcast.57), calls=%async_computation.2 | async-start | bytes 2097152 | tf_op jit(solution)/shard_map/all_to_all | solution.py:1111
  472.8 8.1 %collective-permute-start.47 = (bf16[1024,640]{1,0:T(8,128)(2,1)S(1)}, bf16[1024,640]{1,0:T(8,128)(2,1)S(1)}, u32[]{:S(2)}, u32[]{:S(2)}) collective-permute-start(bf16[1024,640]{1,0:T(8,128)(2,1)S(1)} %broadcast_select_fusion), channel_id=1, source_target_pairs={{0,1},{1,0},{2,3},{3,2},{4,5},{5,4},{6,7},{7,6},{8,9},{9,8},{10,11... | collective-permute-start | bytes 3932168 | tf_op jit(solution)/shard_map/ppermute | solution.py:1103
  475.0 121.4 %collective-permute-start.46 = (bf16[1,512,512]{2,1,0:T(8,128)(2,1)}, bf16[1,512,512]{2,1,0:T(8,128)(2,1)}, u32[]{:S(2)}, u32[]{:S(2)}) collective-permute-start(bf16[1,512,512]{2,1,0:T(8,128)(2,1)} %fusion.8), channel_id=1, source_target_pairs={{0,16},{2,18},{4,20},{6,22},{8,24},{10,26},{12,28},{14,30},{16,0},... | collective-permute-start | bytes 1572872 | tf_op jit(solution)/shard_map/ppermute | solution.py:1099
  477.4 119.0 %collective-permute-start.43 = (bf16[1,2,512,512]{3,2,1,0:T(8,128)(2,1)}, bf16[1,2,512,512]{3,2,1,0:T(8,128)(2,1)S(1)}, u32[]{:S(2)}, u32[]{:S(2)}) collective-permute-start(bf16[1,2,512,512]{3,2,1,0:T(8,128)(2,1)} %get-tuple-element.201), channel_id=1, source_target_pairs={{0,16},{2,18},{4,20},{6,22},{8,24},{10,26},{12,28},{14,30},{16,0},... | collective-permute-start | bytes 3145736 | tf_op jit(solution)/shard_map/ppermute | solution.py:1099
  477.9 118.5 %collective-permute-start.44 = (bf16[1,2,512,512]{3,2,1,0:T(8,128)(2,1)}, bf16[1,2,512,512]{3,2,1,0:T(8,128)(2,1)S(1)}, u32[]{:S(2)}, u32[]{:S(2)}) collective-permute-start(bf16[1,2,512,512]{3,2,1,0:T(8,128)(2,1)} %get-tuple-element.202), channel_id=1, source_target_pairs={{0,8},{2,10},{4,12},{6,14},{8,0},{10,2},{12,4},{14,6},{16,24},{18,... | collective-permute-start | bytes 3145736 | tf_op jit(solution)/shard_map/ppermute | solution.py:1099
  480.4 116.1 %collective-permute-start.45 = (bf16[1,2,512,512]{3,2,1,0:T(8,128)(2,1)}, bf16[1,2,512,512]{3,2,1,0:T(8,128)(2,1)}, u32[]{:S(2)}, u32[]{:S(2)}) collective-permute-start(bf16[1,2,512,512]{3,2,1,0:T(8,128)(2,1)} %get-tuple-element.203), channel_id=1, source_target_pairs={{0,24},{2,26},{4,28},{6,30},{8,16},{10,18},{12,20},{14,22},{16,8},... | collective-permute-start | bytes 3145736 | tf_op jit(solution)/shard_map/ppermute | solution.py:1099
  482.7 113.8 %all-to-all-start.3 = ((bf16[4,4,64,640]{3,2,1,0:T(8,128)(2,1)}), bf16[4,4,64,640]{3,2,1,0:T(8,128)(2,1)S(1)}, u32[]{:S(2)}, u32[]{:S(2)}) async-start(bf16[4,4,64,640]{3,2,1,0:T(8,128)(2,1)} %bitcast.126), calls=%async_computation.3 | async-start | bytes 2621440 | tf_op jit(solution)/shard_map/all_to_all | solution.py:1420
  603.0 65.7 %all-to-all-start.4 = ((bf16[32,128,256]{2,1,0:T(8,128)(2,1)}), bf16[32,128,256]{2,1,0:T(8,128)(2,1)S(1)}, u32[]{:S(2)}, u32[]{:S(2)}) async-start(bf16[32,128,256]{2,1,0:T(8,128)(2,1)} %pad_maximum_fusion.2), calls=%async_computation.4 | async-start | bytes 4194304 | tf_op jit(solution)/shard_map/all_to_all | solution.py:1111
  608.8 35.6 %collective-permute-start.52 = (bf16[256,1024]{1,0:T(8,128)(2,1)}, bf16[256,1024]{1,0:T(8,128)(2,1)S(1)}, u32[]{:S(2)}, u32[]{:S(2)}) collective-permute-start(bf16[256,1024]{1,0:T(8,128)(2,1)} %get-tuple-element.221), channel_id=1, source_target_pairs={{0,6},{2,4},{4,2},{6,0},{8,14},{10,12},{12,10},{14,8},{16,22},{18,... | collective-permute-start | bytes 1572872 | tf_op jit(solution)/shard_map/ppermute | solution.py:1099
  609.4 46.0 %collective-permute-start.51 = (bf16[256,1024]{1,0:T(8,128)(2,1)}, bf16[256,1024]{1,0:T(8,128)(2,1)S(1)}, u32[]{:S(2)}, u32[]{:S(2)}) collective-permute-start(bf16[256,1024]{1,0:T(8,128)(2,1)} %get-tuple-element.219), channel_id=1, source_target_pairs={{0,4},{2,6},{4,0},{6,2},{8,12},{10,14},{12,8},{14,10},{16,20},{18,... | collective-permute-start | bytes 1572872 | tf_op jit(solution)/shard_map/ppermute | solution.py:1099
  610.9 46.9 %collective-permute-start.50 = (bf16[256,1024]{1,0:T(8,128)(2,1)}, bf16[256,1024]{1,0:T(8,128)(2,1)S(1)}, u32[]{:S(2)}, u32[]{:S(2)}) collective-permute-start(bf16[256,1024]{1,0:T(8,128)(2,1)} %get-tuple-element.217), channel_id=1, source_target_pairs={{0,2},{2,0},{4,6},{6,4},{8,10},{10,8},{12,14},{14,12},{16,18},{18,... | collective-permute-start | bytes 1572872 | tf_op jit(solution)/shard_map/ppermute | solution.py:1099
  612.4 56.3 %collective-permute-start.49 = (bf16[256,1024]{1,0:T(8,128)(2,1)}, bf16[256,1024]{1,0:T(8,128)(2,1)}, u32[]{:S(2)}, u32[]{:S(2)}) collective-permute-start(bf16[256,1024]{1,0:T(8,128)(2,1)} %get-tuple-element.215), channel_id=1, source_target_pairs={{0,6},{2,4},{4,2},{6,0},{8,14},{10,12},{12,10},{14,8},{16,22},{18,... | collective-permute-start | bytes 1572872 | tf_op jit(solution)/shard_map/ppermute | solution.py:1099
  682.7 14.0 %all-to-all-start.6 = ((bf16[4,64,640]{2,1,0:T(8,128)(2,1)}), bf16[4,64,640]{2,1,0:T(8,128)(2,1)S(1)}, u32[]{:S(2)}, u32[]{:S(2)}) async-start(bf16[4,64,640]{2,1,0:T(8,128)(2,1)} %reduce_sum.111), calls=%async_computation.6 | async-start | bytes 655360 | tf_op jit(solution)/shard_map/all_to_all | solution.py:1446
  696.8 62.8 %all-to-all-start.5 = ((bf16[16,64,1152]{2,1,0:T(8,128)(2,1)}), bf16[16,64,1152]{2,1,0:T(8,128)(2,1)}, u32[]{:S(2)}, u32[]{:S(2)}) async-start(bf16[16,64,1152]{2,1,0:T(8,128)(2,1)} %bitcast.62), calls=%async_computation.5 | async-start | bytes 4718592 | tf_op jit(solution)/shard_map/all_to_all | solution.py:1391
  (79 other events, 713.9 us)
Sparse Core Ops, SparseCore 0:
  137.1 90.6 all-gather.2

commit v3 on v2

--- a/solution.py
+++ b/solution.py
@@ -495,6 +495,9 @@
     )
 
 
+RAISE_AT = 40.0
+
+
 def dot_f32(left, right, left_dim, right_dim):
     return lax.dot_general(
         left, right, (((left_dim,), (right_dim,)), ((), ())), preferred_element_type=jnp.float32
@@ -512,12 +515,12 @@
 def attend_kernel(
     tp_ref, own_ref, other_ref, limit_ref, out_ref, out_f_ref, log_ref,
     keys, queries, values, highest, total,
-    *, query_block, key_block, diagonal_block, chains
+    *, query_block, key_block, chain
 ):
     core = tp_ref[0]
     blocks, _, rows = own_ref.shape
     seq_len = blocks * rows
-    chain = query_block // chains
+    chains = query_block // chain
 
     def fill(block, _):
         cols = at_rows(block * rows, rows)
@@ -530,67 +533,77 @@
         return 0
 
     lax.fori_loop(0, blocks, fill, 0)
-
-    def update(scores, value_cols, here):
-        before = highest[:, here]
-        after = jnp.maximum(before, jnp.max(scores, 0, keepdims=True))
-        weights = jnp.exp(scores - after).astype(jnp.bfloat16)
-        highest[:, here] = after
-        total[:, here] = total[:, here] * jnp.exp(before - after) + dot_f32(
-            value_cols, weights, 1, 0
-        )
-
-    def near_diagonal(key_rows, key_first, query_cols, here):
-        scores = dot_f32(keys[key_rows, :], queries[:, query_cols], 1, 0)
-        key_pos = key_first + lax.broadcasted_iota(jnp.int32, scores.shape, 0)
-        allowed = key_pos <= limit_ref[:, query_cols]
-        update(jnp.where(allowed, scores, NEG), values[:, key_rows], here)
+    keys[seq_len:, :] = jnp.zeros((rows, HEAD_DIM), jnp.bfloat16)
+    values[:, seq_len:] = jnp.zeros((HEAD_DIM + 16, rows), jnp.bfloat16)
+
+    def diagonal_step(index, _):
+        firsts = [pl.multiple_of((index * chains + part) * chain, chain) for part in range(chains)]
+        spans = [pl.ds(first, chain + rows) for first in firsts]
+        scores = [
+            dot_f32(keys[span, :], queries[:, pl.ds(first, chain)], 1, 0)
+            for first, span in zip(firsts, spans)
+        ]
+        for first, span, score in zip(firsts, spans, scores):
+            here = pl.ds(first, chain)
+            key_pos = first + lax.broadcasted_iota(jnp.int32, score.shape, 0)
+            score = jnp.where(key_pos <= limit_ref[:, here], score, NEG)
+            most = jnp.max(score, 0, keepdims=True)
+            highest[:, here] = most
+            total[:, here] = dot_f32(
+                values[:, span], jnp.exp(score - most).astype(jnp.bfloat16), 1, 0
+            )
+        return 0
+
+    lax.fori_loop(0, seq_len // query_block, diagonal_step, 0)
+
+    def earlier_keys(span, firsts):
+        terms, over = [], []
+        for first in firsts:
+            here = pl.ds(first, chain)
+            score = dot_f32(keys[span, :], queries[:, here], 1, 0)
+            most = highest[:, here]
+            over.append(jnp.max(score, 0, keepdims=True) - most)
+            weights = jnp.exp(score - most).astype(jnp.bfloat16)
+            terms.append(dot_f32(values[:, span], weights, 1, 0))
+        most_over = jnp.max(functools.reduce(jnp.maximum, over))
+
+        @pl.when(most_over <= RAISE_AT)
+        def _():
+            for first, term in zip(firsts, terms):
+                total[:, pl.ds(first, chain)] += term
+
+        @pl.when(most_over > RAISE_AT)
+        def _():
+            for first in firsts:
+                here = pl.ds(first, chain)
+                score = dot_f32(keys[span, :], queries[:, here], 1, 0)
+                before = highest[:, here]
+                after_all = jnp.maximum(before, jnp.max(score, 0, keepdims=True))
+                weights = jnp.exp(score - after_all).astype(jnp.bfloat16)
+                highest[:, here] = after_all
+                total[:, here] = total[:, here] * jnp.exp(before - after_all) + dot_f32(
+                    values[:, span], weights, 1, 0
+                )
 
     def query_step(index, _):
         first = index * query_block
-        highest[...] = jnp.full_like(highest, NEG)
-        total[...] = jnp.zeros_like(total)
+        firsts = [pl.multiple_of(first + part * chain, chain) for part in range(chains)]
 
         def full_step(step, _):
-            key_rows = at_rows(step * key_block, key_block)
-            scores = [
-                dot_f32(keys[key_rows, :], queries[:, at_rows(first + part * chain, chain)], 1, 0)
-                for part in range(chains)
-            ]
-            for part in range(chains):
-                update(scores[part], values[:, key_rows], slice(part * chain, (part + 1) * chain))
+            earlier_keys(at_rows(step * key_block, key_block), firsts)
             return 0
 
         lax.fori_loop(0, first // key_block, full_step, 0)
-        for low in range(0, query_block, diagonal_block):
-            here = pl.multiple_of(first + low, diagonal_block)
-            if low:
-                near_diagonal(
-                    pl.ds(here, rows),
-                    here,
-                    pl.ds(pl.multiple_of(here - rows, rows), rows),
-                    slice(low - rows, low),
-                )
-            near_diagonal(
-                pl.ds(here, diagonal_block),
-                here,
-                pl.ds(here, query_block - low),
-                slice(low, query_block),
-            )
-        near_diagonal(
-            at_rows(jnp.minimum(first + query_block, seq_len - rows), rows),
-            first + query_block,
-            at_rows(first + query_block - rows, rows),
-            slice(query_block - rows, query_block),
-        )
+        for part in range(1, chains):
+            earlier_keys(pl.ds(firsts[part - 1], chain), firsts[part:])
         for piece in range(query_block // rows):
-            here = slice(piece * rows, (piece + 1) * rows)
+            here = at_rows(first + piece * rows, rows)
             row_sum = total[HEAD_DIM : HEAD_DIM + 1, here]
             result = total[:HEAD_DIM, here] / row_sum
             block = index * (query_block // rows) + piece
             out_ref[block] = result.astype(jnp.bfloat16)
             out_f_ref[block] = result
-            log_ref[:, at_rows(first + piece * rows, rows)] = highest[:, here] + jnp.log(row_sum)
+            log_ref[:, here] = highest[:, here] + jnp.log(row_sum)
         return 0
 
     lax.fori_loop(0, seq_len // query_block, query_step, 0)
@@ -600,15 +613,14 @@
     blocks, _, rows = own.shape
     seq_len = blocks * rows
     query_block = math.gcd(seq_len, 2048)
-    key_block = math.gcd(query_block, 1024)
+    key_block = math.gcd(query_block, 2048)
     block_shape = (blocks, HEAD_DIM, rows)
     return pl.pallas_call(
         functools.partial(
             attend_kernel,
             query_block=query_block,
             key_block=key_block,
-            diagonal_block=math.gcd(query_block, 512),
-            chains=query_block // math.gcd(query_block, 512),
+            chain=math.gcd(query_block, 512),
         ),
         out_shape=(
             jax.ShapeDtypeStruct(block_shape, jnp.bfloat16),
@@ -618,11 +630,11 @@
         in_specs=[pl.BlockSpec(memory_space=pltpu.SMEM)] + [whole_vmem()] * 3,
         out_specs=(whole_vmem(),) * 3,
         scratch_shapes=[
-            pltpu.VMEM((seq_len, HEAD_DIM), jnp.bfloat16),
+            pltpu.VMEM((seq_len + rows, HEAD_DIM), jnp.bfloat16),
             pltpu.VMEM((HEAD_DIM, seq_len), jnp.bfloat16),
-            pltpu.VMEM((HEAD_DIM + 16, seq_len), jnp.bfloat16),
-            pltpu.VMEM((1, query_block), jnp.float32),
-            pltpu.VMEM((HEAD_DIM + 16, query_block), jnp.float32),
+            pltpu.VMEM((HEAD_DIM + 16, seq_len + rows), jnp.bfloat16),
+            pltpu.VMEM((1, seq_len), jnp.float32),
+            pltpu.VMEM((HEAD_DIM + 16, seq_len), jnp.float32),
         ],
         cost_estimate=pl.CostEstimate(
             flops=seq_len * seq_len * 512, bytes_accessed=8 * MIB, transcendentals=0
@@ -632,107 +644,109 @@
     )(core, own, other, limit)
 
 
-def three_parts(values):
+def split_three(values):
     high = values.astype(jnp.bfloat16).astype(jnp.float32)
     middle = (values - high).astype(jnp.bfloat16).astype(jnp.float32)
-    low = values - high - middle
+    return high, middle, values - high - middle
+
+
+def three_parts(values):
+    high, middle, low = split_three(values)
     row = lax.broadcasted_iota(jnp.int32, (16, values.shape[1]), 0)
-    parts = jnp.where(
+    return jnp.where(
         row == 0, high, jnp.where(row == 1, middle, jnp.where(row == 2, low, 0.0))
     )
-    return parts.astype(jnp.bfloat16)
 
 
 def attend_back_kernel(
     tp_ref, own_ref, other_ref, limit_ref, out_f_ref, log_ref, grad_ref,
     grad_q_ref, keep_ref, send_ref,
-    keys, keys_t, queries_t, queries, values, grads_t, grads, grad_k, grad_v, grad_q,
-    *, query_block, key_block, diagonal_block
+    queries, queries_t, keys_t, values_t, grads, grads_t, grad_k, grad_v, grad_q,
+    *, query_block, key_block, chain
 ):
     core = tp_ref[0]
     blocks, _, rows = own_ref.shape
     seq_len = blocks * rows
+    chains = query_block // chain
 
     def fill(block, _):
         cols = at_rows(block * rows, rows)
         first, second = own_ref[block, HEAD_DIM:, :], other_ref[block]
         key_rows = jnp.where(core == 0, first, second).astype(jnp.float32)
         key_rows = key_rows * HEAD_DIM ** (-0.5)
-        value_rows = jnp.where(core == 0, second, first).astype(jnp.float32)
         query, grad = own_ref[block, :HEAD_DIM, :], grad_ref[block]
         grad_f = grad.astype(jnp.float32)
         delta = jnp.sum(grad_f * out_f_ref[block], 0, keepdims=True)
-        ones = jnp.ones((16, rows), jnp.float32)
-        queries_t[:HEAD_DIM, cols] = query
-        queries_t[HEAD_DIM:, cols] = three_parts(-log_ref[:, cols])
-        queries[cols, :] = query.astype(jnp.float32).T.astype(jnp.bfloat16)
-        keys_t[:, cols] = key_rows.astype(jnp.bfloat16)
-        keys[cols, :] = jnp.concatenate([key_rows, ones], 0).T.astype(jnp.bfloat16)
-        values[cols, :] = jnp.concatenate([value_rows, ones], 0).T.astype(jnp.bfloat16)
-        grads_t[:HEAD_DIM, cols] = grad
-        grads_t[HEAD_DIM:, cols] = three_parts(-delta)
-        grads[cols, :] = grad_f.T.astype(jnp.bfloat16)
-        grad_k[cols, :] = jnp.zeros((rows, HEAD_DIM), jnp.float32)
-        grad_v[cols, :] = jnp.zeros((rows, HEAD_DIM), jnp.float32)
+        ones = jnp.ones((16, rows), jnp.bfloat16)
+        query_parts = [query.astype(jnp.float32), three_parts(-log_ref[:, cols])]
+        queries[cols, :] = jnp.concatenate(query_parts, 0).T.astype(jnp.bfloat16)
+        queries_t[:, cols] = query
+        keys_t[:HEAD_DIM, cols] = key_rows.astype(jnp.bfloat16)
+        keys_t[HEAD_DIM:, cols] = ones
+        values_t[:HEAD_DIM, cols] = jnp.where(core == 0, second, first)
+        values_t[HEAD_DIM:, cols] = ones
+        grads[cols, :] = jnp.concatenate([grad_f, three_parts(-delta)], 0).T.astype(jnp.bfloat16)
+        grads_t[:, cols] = grad
+        grad_k[:, cols] = jnp.zeros((HEAD_DIM, rows), jnp.float32)
+        grad_v[:, cols] = jnp.zeros((HEAD_DIM, rows), jnp.float32)
         return 0
 
     lax.fori_loop(0, blocks, fill, 0)
 
-    def tile(key_rows, key_first, query_cols, here):
-        probs = jnp.exp(dot_f32(keys[key_rows, :], queries_t[:, query_cols], 1, 0))
+    def tile(query_rows, here, key_cols, key_first):
+        probs = jnp.exp(dot_f32(queries[query_rows, :], keys_t[:, key_cols], 1, 0))
         if key_first is not None:
-            key_pos = key_first + lax.broadcasted_iota(jnp.int32, probs.shape, 0)
-            probs = jnp.where(key_pos <= limit_ref[:, query_cols], probs, 0.0)
-        grad_probs = dot_f32(values[key_rows, :], grads_t[:, query_cols], 1, 0)
+            limit = limit_ref[:, query_rows].astype(jnp.float32)
+            limit = jnp.broadcast_to(limit, (8, limit.shape[1])).T[:, :1]
+            key_pos = key_first + lax.broadcasted_iota(jnp.int32, probs.shape, 1)
+            probs = jnp.where(key_pos.astype(jnp.float32) <= limit, probs, 0.0)
+        grad_probs = dot_f32(grads[query_rows, :], values_t[:, key_cols], 1, 0)
         grad_scores = (probs * grad_probs).astype(jnp.bfloat16)
-        grad_v[key_rows, :] += dot_f32(probs.astype(jnp.bfloat16), grads[query_cols, :], 1, 0)
-        grad_k[key_rows, :] += dot_f32(grad_scores, queries[query_cols, :], 1, 0)
-        grad_q[:, here] += dot_f32(keys_t[:, key_rows], grad_scores, 1, 0)
+        grad_v[:, key_cols] += dot_f32(grads_t[:, query_rows], probs.astype(jnp.bfloat16), 1, 0)
+        grad_k[:, key_cols] += dot_f32(queries_t[:, query_rows], grad_scores, 1, 0)
+        grad_q[:, here] += dot_f32(keys_t[:HEAD_DIM, key_cols], grad_scores, 1, 1)
 
     def query_step(index, _):
         first = index * query_block
-        whole = slice(0, query_block)
         grad_q[...] = jnp.zeros_like(grad_q)
 
         def full_step(step, _):
-            tile(at_rows(step * key_block, key_block), None, at_rows(first, query_block), whole)
+            tile(
+                at_rows(first, query_block),
+                slice(0, query_block),
+                at_rows(step * key_block, key_block),
+                None,
+            )
             return 0
 
         lax.fori_loop(0, first // key_block, full_step, 0)
-        for low in range(0, query_block, diagonal_block):
-            here = pl.multiple_of(first + low, diagonal_block)
+        for low in range(0, query_block, chain):
+            here = pl.multiple_of(first + low, chain)
             if low:
                 tile(
-                    pl.ds(here, rows),
-                    here,
-                    pl.ds(pl.multiple_of(here - rows, rows), rows),
-                    slice(low - rows, low),
+                    pl.ds(here, query_block - low),
+                    slice(low, query_block),
+                    pl.ds(pl.multiple_of(here - chain, chain), chain),
+                    None,
                 )
+            tile(pl.ds(here, chain), slice(low, low + chain), pl.ds(here, chain), here)
             tile(
-                pl.ds(here, diagonal_block),
-                here,
-                pl.ds(here, query_block - low),
-                slice(low, query_block),
+                at_rows(here + chain - rows, rows),
+                slice(low + chain - rows, low + chain),
+                at_rows(jnp.minimum(here + chain, seq_len - rows), rows),
+                here + chain,
             )
-        tile(
-            at_rows(jnp.minimum(first + query_block, seq_len - rows), rows),
-            first + query_block,
-            at_rows(first + query_block - rows, rows),
-            slice(query_block - rows, query_block),
-        )
         for piece in range(query_block // rows):
-            here = slice(piece * rows, (piece + 1) * rows)
-            grad_q_ref[index * (query_block // rows) + piece] = grad_q[:, here].astype(
-                jnp.bfloat16
-            )
+            here = grad_q[:, piece * rows : (piece + 1) * rows]
+            grad_q_ref[index * (query_block // rows) + piece] = here.astype(jnp.bfloat16)
         return 0
 
     lax.fori_loop(0, seq_len // query_block, query_step, 0)
 
     def finish(block, _):
         cols = at_rows(block * rows, rows)
-        key_part = (grad_k[cols, :] * HEAD_DIM ** (-0.5)).T
-        value_part = grad_v[cols, :].T
+        key_part = grad_k[:, cols] * HEAD_DIM ** (-0.5)
+        value_part = grad_v[:, cols]
         keep_ref[block] = jnp.where(core == 0, key_part, value_part)
         send_ref[block] = jnp.where(core == 0, value_part, key_part).astype(jnp.bfloat16)
         return 0
@@ -743,7 +757,7 @@
 def attend_back(core, own, other, limit, out_f, log_total, grad):
     blocks, _, rows = own.shape
     seq_len = blocks * rows
-    query_block = math.gcd(seq_len, 1024)
+    query_block = math.gcd(seq_len, 2048)
     key_block = math.gcd(query_block, 1024)
     block_shape = (blocks, HEAD_DIM, rows)
     wide = HEAD_DIM + 16
@@ -752,7 +766,7 @@
             attend_back_kernel,
             query_block=query_block,
             key_block=key_block,
-            diagonal_block=math.gcd(query_block, 512),
+            chain=math.gcd(query_block, 512),
         ),
         out_shape=(
             jax.ShapeDtypeStruct(block_shape, jnp.bfloat16),
@@ -765,12 +779,11 @@
             pltpu.VMEM((seq_len, wide), jnp.bfloat16),
             pltpu.VMEM((HEAD_DIM, seq_len), jnp.bfloat16),
             pltpu.VMEM((wide, seq_len), jnp.bfloat16),
-            pltpu.VMEM((seq_len, HEAD_DIM), jnp.bfloat16),
+            pltpu.VMEM((wide, seq_len), jnp.bfloat16),
             pltpu.VMEM((seq_len, wide), jnp.bfloat16),
-            pltpu.VMEM((wide, seq_len), jnp.bfloat16),
-            pltpu.VMEM((seq_len, HEAD_DIM), jnp.bfloat16),
-            pltpu.VMEM((seq_len, HEAD_DIM), jnp.float32),
-            pltpu.VMEM((seq_len, HEAD_DIM), jnp.float32),
+            pltpu.VMEM((HEAD_DIM, seq_len), jnp.bfloat16),
+            pltpu.VMEM((HEAD_DIM, seq_len), jnp.float32),
+            pltpu.VMEM((HEAD_DIM, seq_len), jnp.float32),
             pltpu.VMEM((HEAD_DIM, query_block), jnp.float32),
         ],
         cost_estimate=pl.CostEstimate(
@@ -791,6 +804,7 @@
     half_cols = heads_ref.shape[2]
     half_dim = HEAD_DIM // 2
     units = half_cols // (2 * HEAD_DIM)
+    kv_heads = units // 2
     for step in range(count):
         for up in range(columns):
             here = at_rows(((level ^ up) * count + (spot ^ step)) * shard, shard)
@@ -815,9 +829,10 @@
         for part in range(2):
             heads = dot_f32(normed, heads_ref[part], 1, 0).T
             for unit in range(units):
-                first = unit * 2 * HEAD_DIM
+                first = unit * HEAD_DIM
+                paired = (units + unit // 2 + unit % 2 * kv_heads) * HEAD_DIM
                 block = (micro * 2 + part) * units + unit
-                second = heads[first + HEAD_DIM : first + 2 * HEAD_DIM]
+                second = heads[paired : paired + HEAD_DIM]
                 sent_ref[block, :HEAD_DIM, :] = rotated(heads[first : first + HEAD_DIM])
                 sent_ref[block, HEAD_DIM:, :] = (
                     rotated(second) if unit % 2 == 0 else second.astype(jnp.bfloat16)
@@ -860,12 +875,14 @@
 
     for micro in range(micro_count):
         for part in range(2):
+            first_block = (micro * 2 + part) * units
             pieces = []
-            for unit in range(units):
-                block = (micro * 2 + part) * units + unit
-                second = grad_ref[block, HEAD_DIM:, :]
+            for block in range(first_block, first_block + units):
                 pieces += turned_back(grad_ref[block, :HEAD_DIM, :])
-                pieces += turned_back(second) if unit % 2 == 0 else [second.astype(jnp.float32)]
+            for block in range(first_block, first_block + units, 2):
+                pieces += turned_back(grad_ref[block, HEAD_DIM:, :])
+            for block in range(first_block + 1, first_block + units, 2):
+                pieces.append(grad_ref[block, HEAD_DIM:, :].astype(jnp.float32))
             grad_rows[part, micro * rows : (micro + 1) * rows, :] = (
                 jnp.concatenate(pieces, 0).T.astype(jnp.bfloat16)
             )
@@ -907,19 +924,19 @@
     )(core, grad_own, heads, normed, x, grad_resid, gain, cosine, sine)
 
 
-def experts_kernel(*refs, slots, first_call, pieces, piece_count):
+def experts_kernel(*refs, slots, first_call, pieces, piece_count, spread):
     place_ref, refs = refs[0], refs[1:]
     x_refs, dy_refs = refs[:slots], refs[slots : 2 * slots]
     w_route_ref, weight_refs = refs[2 * slots], refs[2 * slots + 1 : 2 * slots + 1 + piece_count]
     refs = refs[2 * slots + 1 + piece_count :]
     if not first_call:
-        keep_in_ref, send_in_ref = refs[:2]
-        refs = refs[2:]
-    mix_refs, grad_x_refs = refs[:slots], refs[slots : 2 * slots]
-    grad_gate_ref, keep_ref, send_ref = refs[2 * slots : 2 * slots + 3]
+        before_refs, refs = refs[:3], refs[3:]
+    mix_ref, grad_x_refs, refs = refs[0], refs[1 : 1 + slots], refs[1 + slots :]
+    keep_ref, send_in_ref, send_out_ref = refs[:3]
     (
-        x_all, x_t, dy_all, dy_t, gates, grad_gates, mix_sum, grad_x_sum, grad_w, weights, sems
-    ) = refs[2 * slots + 3 :]
+        x_all, x_t, dy_all, dy_t, gates, grad_gates, mix_sum, grad_x_sum, grad_w, weights, sems,
+        hidden, grad_gate_pre, grad_up_pre,
+    ) = refs[3:]
     expert, expert_count = pl.program_id(0), pl.num_programs(0)
     rows, width = x_refs[0].shape
     total = slots * rows
@@ -955,6 +972,7 @@
             logits = jnp.where(chosen > 0.0, dot_f32(x, w_route_ref[...], 1, 0), NEG)
             raised = jnp.exp(logits - jnp.max(logits, 1, keepdims=True)) * chosen
             gates[here, :] = raised / jnp.sum(raised, 1, keepdims=True)
+        grad_gates[...] = jnp.zeros_like(grad_gates)
         mix_sum[...] = jnp.zeros_like(mix_sum)
         grad_x_sum[...] = jnp.zeros_like(grad_x_sum)
 
@@ -971,60 +989,71 @@
     if first_call:
         grad_w[...] = jnp.zeros_like(grad_w)
     else:
-        for part in range(2):
-            grad_w[part] = jnp.where(core == part, keep_in_ref[0], send_in_ref[0]).astype(
-                jnp.float32
-            )
+        keep_before, in_before, out_before = before_refs
+        grad_w[core] = keep_before[0].astype(jnp.float32)
+        grad_w[1 - core, :2] = in_before[0].astype(jnp.float32)
+        grad_w[1 - core, 2:] = out_before[0].astype(jnp.float32)
     buffer = lax.rem(expert, 2)
     w_gate, w_up, w_down_t = weights[buffer, 0], weights[buffer, 1], weights[buffer, 2]
-    x = x_all[...]
-    dy = dy_all[...].astype(jnp.float32)
     lane = lax.broadcasted_iota(jnp.int32, (total, LANES), 1)
     gate = jnp.sum(jnp.where(lane == place_ref[1 + expert], gates[...], 0.0), 1, keepdims=True)
     gate_row = jnp.broadcast_to(gate, (total, LANES)).T[:1]
+    x = x_all[...]
+    dy = dy_all[...].astype(jnp.float32)
     gate_pre = dot_f32(x, w_gate, 1, 0)
     up_pre = dot_f32(x, w_up, 1, 0)
-    sigmoid_val = 1.0 / (1.0 + jnp.exp(-gate_pre))
+    sigmoid_val = 0.5 + 0.5 * jnp.tanh(0.5 * gate_pre)
     silu_val = gate_pre * sigmoid_val
-    hidden = (silu_val * up_pre).astype(jnp.bfloat16)
-    out = dot_f32(hidden, w_down_t, 1, 1).astype(jnp.bfloat16).astype(jnp.float32)
+    up_slope = up_pre * (sigmoid_val * (1.0 + gate_pre * (1.0 - sigmoid_val)))
+    hidden[...] = (silu_val * up_pre).astype(jnp.bfloat16)
+    grad_hidden = dot_f32((gate * dy).astype(jnp.bfloat16), w_down_t, 1, 0)
+    grad_gate_pre[...] = (grad_hidden * up_slope).astype(jnp.bfloat16)
+    grad_up_pre[...] = (grad_hidden * silu_val).astype(jnp.bfloat16)
+    out = dot_f32(hidden[...], w_down_t, 1, 1).astype(jnp.bfloat16).astype(jnp.float32)
     grad_gate = jnp.sum(out * dy, 1, keepdims=True)
     grad_gates[pl.ds(expert, 1), :] = jnp.broadcast_to(grad_gate, (total, LANES)).T[:1]
     mix_sum[...] += gate * out
-    grad_out = (gate * dy).astype(jnp.bfloat16)
-    grad_hidden = dot_f32(grad_out, w_down_t, 1, 0)
-    slope = sigmoid_val * (1.0 + gate_pre * (1.0 - sigmoid_val))
-    grad_gate_pre = (grad_hidden * up_pre * slope).astype(jnp.bfloat16)
-    grad_up_pre = (grad_hidden * silu_val).astype(jnp.bfloat16)
-    grad_copy = dot_f32(grad_gate_pre, w_gate, 1, 1) + dot_f32(grad_up_pre, w_up, 1, 1)
+    grad_copy = dot_f32(grad_gate_pre[...], w_gate, 1, 1) + dot_f32(
+        grad_up_pre[...], w_up, 1, 1
+    )
     grad_x_sum[...] += grad_copy.astype(jnp.bfloat16).astype(jnp.float32)
     grad_out_t = (dy_t[...].astype(jnp.float32) * gate_row).astype(jnp.bfloat16)
     terms = (
-        dot_f32(x_t[...], grad_gate_pre, 1, 0),
-        dot_f32(x_t[...], grad_up_pre, 1, 0),
-        dot_f32(grad_out_t, hidden, 1, 0),
+        dot_f32(x_t[...], grad_gate_pre[...], 1, 0),
+        dot_f32(x_t[...], grad_up_pre[...], 1, 0),
+        dot_f32(grad_out_t, hidden[...], 1, 0),
     )
     for part in range(2):
         for matrix, term in enumerate(terms):
             grad_w[part, matrix] += term[part * half : (part + 1) * half]
     keep_ref[0] = grad_w[core].astype(jnp.bfloat16)
-    send_ref[0] = grad_w[1 - core].astype(jnp.bfloat16)
+    send_in_ref[0] = grad_w[1 - core, :2].astype(jnp.bfloat16)
+    send_out_ref[0] = grad_w[1 - core, 2:].astype(jnp.bfloat16)
 
     @pl.when(expert == expert_count - 1)
     def _():
         for slot in range(slots):
             here = slice(slot * rows, (slot + 1) * rows)
-            mix_refs[slot][...] = mix_sum[here, :].astype(jnp.bfloat16)
-            grad_x_refs[slot][...] = grad_x_sum[here, :].astype(jnp.bfloat16)
-            grad_gate_ref[slot] = grad_gates[: grad_gate_ref.shape[1], here]
-
-
-def experts(place, x_parts, dy_parts, w_route, weights, pieces, before):
+            block = (place_ref[place_ref.shape[0] - 1] ^ (slot + 1)) if spread else slot
+            mix_ref[block] = mix_sum[here, :].astype(jnp.bfloat16)
+            grad_x_refs[slot][:, :width] = grad_x_sum[here, :].astype(jnp.bfloat16)
+            parts = split_three(grad_gates[:, here])
+            rest = jnp.zeros((LANES - 3 * parts[0].shape[0], rows), jnp.float32)
+            grad_x_refs[slot][:, width:] = (
+                jnp.concatenate([*parts, rest], 0).T.astype(jnp.bfloat16)
+            )
+        if spread:
+            own_block = place_ref[place_ref.shape[0] - 1]
+            mix_ref[own_block] = jnp.zeros((rows, width), jnp.bfloat16)
+
+
+def experts(place, x_parts, dy_parts, w_route, weights, pieces, before, spread):
     rows = dy_parts[0][0].shape[1]
-    width, hidden_width = weights[0].shape[-2:]
+    width, hidden_width = x_parts[0][0].shape[1], weights[0].shape[-1]
     count, slots = len(pieces), len(x_parts)
     total = slots * rows
     half = width // 2
+    mix_slots = slots + 1 if spread else slots
     first_call = before is None
     before = () if first_call else tuple(before)
 
@@ -1035,10 +1064,15 @@
             pipeline_mode=pl.Buffered(1),
         )
 
-    row_spec = pl.BlockSpec((rows, width), lambda expert: (0, 0))
-    grad_spec = pl.BlockSpec((1, 3, half, hidden_width), lambda expert: (expert, 0, 0, 0))
-    grad_shape = jax.ShapeDtypeStruct((count, 3, half, hidden_width), jnp.bfloat16)
-    row_shape = jax.ShapeDtypeStruct((rows, width), jnp.bfloat16)
+    row_spec = pl.BlockSpec((rows, width + LANES), lambda expert: (0, 0))
+    grad_specs = [
+        pl.BlockSpec((1, size, half, hidden_width), lambda expert: (expert, 0, 0, 0))
+        for size in (3, 2, 1)
+    ]
+    grad_shapes = tuple(
+        jax.ShapeDtypeStruct((count, size, half, hidden_width), jnp.bfloat16) for size in (3, 2, 1)
+    )
+    row_shape = jax.ShapeDtypeStruct((rows, width + LANES), jnp.bfloat16)
     outs = pl.pallas_call(
         functools.partial(
             experts_kernel,
@@ -1046,18 +1080,21 @@
             first_call=first_call,
             pieces=pieces,
             piece_count=len(weights),
+            spread=spread,
         ),
         grid=(count,),
-        out_shape=(row_shape,) * (2 * slots)
-        + (jax.ShapeDtypeStruct((slots, count, rows), jnp.float32), grad_shape, grad_shape),
+        out_shape=(jax.ShapeDtypeStruct((mix_slots, rows, width), jnp.bfloat16),)
+        + (row_shape,) * slots
+        + grad_shapes,
         in_specs=[pl.BlockSpec(memory_space=pltpu.SMEM)]
         + [at_block((rows, width), index) for _, index in x_parts]
         + [at_block((None, rows, width + LANES), index) for _, index in dy_parts]
         + [at_block((width, LANES), 0)]
         + [pl.BlockSpec(memory_space=pl.ANY)] * len(weights)
-        + [grad_spec] * len(before),
-        out_specs=(row_spec,) * (2 * slots)
-        + (pl.BlockSpec((slots, count, rows), lambda expert: (0, 0, 0)), grad_spec, grad_spec),
+        + grad_specs[: len(before)],
+        out_specs=(pl.BlockSpec((mix_slots, rows, width), lambda expert: (0, 0, 0)),)
+        + (row_spec,) * slots
+        + tuple(grad_specs),
         scratch_shapes=[
             pltpu.VMEM((total, width), jnp.bfloat16),
             pltpu.VMEM((width, total), jnp.bfloat16),
@@ -1070,7 +1107,8 @@
             pltpu.VMEM((2, 3, half, hidden_width), jnp.float32),
             pltpu.VMEM((2, 3, width, hidden_width), jnp.bfloat16),
             pltpu.SemaphoreType.DMA((count, max(len(group) for group in pieces))),
-        ],
+        ]
+        + [pltpu.VMEM((total, hidden_width), jnp.bfloat16)] * 3,
         cost_estimate=pl.CostEstimate(
             flops=count * total * width * hidden_width * 18,
             bytes_accessed=count * width * hidden_width * 12,
@@ -1087,7 +1125,7 @@
         *weights,
         *before,
     )
-    return outs[:slots], outs[slots : 2 * slots], outs[2 * slots], outs[2 * slots + 1 :]
+    return outs[0], outs[1 : 1 + slots], outs[1 + slots :]
 
 
 def together(*values):
@@ -1101,10 +1139,6 @@
 
 def swap_cores(values):
     return lax.ppermute(values, "tp", [(0, 1), (1, 0)])
-
-
-def after(values, *earlier):
-    return together(values, *earlier)[0]
 
 
 def every_device(values):
@@ -1170,24 +1204,11 @@
     half = width // 2
     micros = range(micro_count)
 
-    head_cols = jnp.stack(
-        [
-            w_query.reshape(shard, kv_here, 2, HEAD_DIM),
-            jnp.stack(
-                [
-                    w_key.reshape(shard, kv_here, HEAD_DIM),
-                    w_value.reshape(shard, kv_here, HEAD_DIM),
-                ],
-                2,
-            ),
-        ],
-        3,
-    ).reshape(shard, half_cols)
     small = jnp.concatenate([w_router, jnp.zeros((shard, LANES - experts_all), w_router.dtype)], 1)
     lanes = jnp.arange(LANES, dtype=jnp.int32)
     small = jnp.where(lanes == LANES // 2, gain_attn[:, None], small)
     small = jnp.where(lanes == LANES // 2 + 1, gain_moe[:, None], small)
-    packed = jnp.concatenate([head_cols, small], 1)
+    packed = jnp.concatenate([w_query, w_key, w_value, small], 1)
     levels = [packed] + [flip(packed, PLANE * step) for step in range(1, columns)]
     mine = jnp.stack(levels)
     mine = [mine] + [flip(mine, step) for step in range(1, PLANE)]
@@ -1202,9 +1223,9 @@
     )
     expert_half, levels = together(expert_half, levels)
     far_out = flip(expert_half[2:], 2 * PLANE)
-    mine, far_out = together(mine, far_out)
+    near_out = flip(expert_half[2:], PLANE)
+    mine, far_out, near_out = together(mine, far_out, near_out)
     other = [swap_cores(part) for part in mine]
-    near_all = flip(expert_half, PLANE)
 
     x_rows = tokens.reshape(all_rows, width).astype(jnp.float32)
     device_index = ep_index * tp_count + tp_index
@@ -1216,19 +1237,19 @@
     w_route_full = small_all[:, :experts_all]
     gain_one = small_all[:, LANES // 2].astype(jnp.float32)
     gain_two = small_all[:, LANES // 2 + 1].astype(jnp.float32)
+    nearfar_out = flip(far_out, PLANE)
+    sent, nearfar_out = together(sent, nearfar_out)
     own = every_device(sent)
     other = swap_cores(own[:, HEAD_DIM:, :])
 
     chosen = jnp.any(routes[:, :, :, None] == lanes, 2).astype(jnp.bfloat16)
     own_dy = jnp.concatenate([cotangent, chosen], 2)
-    last_dy = flip(after(own_dy, sent), PLANE - 1)
-    other, last_dy = together(other, last_dy)
     w_output_t, expert_late, far_out, dy_late, other = together(
         w_output.T, expert_half, far_out, own_dy, other
     )
     far_in = flip(expert_late[:2], 2 * PLANE)
-    plane_dy = [flip(dy_late, step) for step in range(1, PLANE - 1)] + [last_dy]
-    nearfar_out = flip(far_out, PLANE)
+    near_in = flip(expert_late[:2], PLANE)
+    plane_dy = [flip(dy_late, step) for step in range(1, PLANE)]
     gathered_out = lax.all_gather(w_output_t, ("ep", "tp"), axis=0, tiled=False)
 
     micro_here = ep_index // (ep_count // micro_count)
@@ -1238,9 +1259,7 @@
     piece_last = jnp.max(jnp.where(inside, starts[:, None] + (PIECE - 1), -1), 0, keepdims=True)
     limit = jnp.maximum(all_pos, piece_last).astype(jnp.int32)
     out_b, out_f, log_total = attend(core, own, other, limit)
-    out_b, far_in, plane_dy, nearfar_out, near_all = together(
-        out_b, far_in, plane_dy, nearfar_out, near_all
-    )
+    out_b, near_in, far_in, plane_dy = together(out_b, near_in, far_in, plane_dy)
     nearfar_in = flip(far_in, PLANE)
     attended_t = every_device(out_b).reshape(micro_count, out_cols * tp_count, rows)
     gathered_out = gathered_out.reshape(ep_count, tp_count, shard, out_cols)
@@ -1257,13 +1276,15 @@
     normed_parts = [normed_two[micro * rows : (micro + 1) * rows] for micro in micros]
     plane_x = [[flip(normed_parts[0], step) for step in range(1, PLANE)]]
 
-    column_weights = [w_gate, w_up, w_down_t[None]]
-    for piece in (near_all, far_in, far_out, after(nearfar_in, normed_two), nearfar_out):
-        column_weights += [piece, swap_cores(piece)]
+    weights = [w_gate, w_up, w_down_t[None]]
+    nearfar_in, normed_late = together(nearfar_in, normed_two)
+    for piece in (near_in, near_out, far_in, far_out, nearfar_in, nearfar_out):
+        weights += [piece, swap_cores(piece)]
     pieces = [[(0, None, 0, 1), (1, None, 1, 2), (2, None, 2, 3)]]
-    pieces.append([(5, 0, 0, 2), (6, 1, 0, 2), (7, 0, 2, 3), (8, 1, 2, 3)])
-    pieces.append([(3, 0, 0, 3), (4, 1, 0, 3)])
-    pieces.append([(9, 0, 0, 2), (10, 1, 0, 2), (11, 0, 2, 3), (12, 1, 2, 3)])
+    for first in (3, 7, 11):
+        pieces.append(
+            [(first, 0, 0, 2), (first + 1, 1, 0, 2), (first + 2, 0, 2, 3), (first + 3, 1, 2, 3)]
+        )
 
     logits = jnp.dot(normed_two, w_route_full, preferred_element_type=jnp.float32)
     route_rows = routes.reshape(all_rows, -1)
@@ -1276,82 +1297,94 @@
 
     slot_ids = jnp.stack(
         [
-            jnp.stack([(level ^ up) * PLANE + (spot ^ step) for up in (0, 2, 1, 3)])
+            jnp.stack([(level ^ up) * PLANE + (spot ^ step) for up in range(columns)])
             for step in range(PLANE)
         ]
     )
     slot_hot = (route_rows[None, None, :, :] == slot_ids[:, :, None, None]).astype(jnp.float32)
 
-    place = jnp.concatenate([core, slot_ids[0]])
-    own_mix, own_grad_x, own_grad_gate, before = experts(
+    spot_here = spot.astype(jnp.int32).reshape(1)
+    column_ids = jnp.stack([(level ^ up) * PLANE + spot for up in range(columns)])
+    place = jnp.concatenate([core, column_ids.astype(jnp.int32), spot_here])
+    own_mix, own_grad_x, before = experts(
         place,
         [(normed_two, micro) for micro in micros],
         [(own_dy, micro) for micro in micros],
         small_all,
-        column_weights,
+        weights,
         pieces,
         None,
+        False,
     )
     leaving = normed_parts[1:]
-    leaving, own_grad_gate = together(leaving, own_grad_gate)
+    leaving, own_mix = together(leaving, own_mix)
     plane_x += [[flip(part, step) for step in range(1, PLANE)] for part in leaving]
-    far_mix, late_mix, far_grad_x, far_grad_gate = [], [], [], []
+    plane_groups = [[up * PLANE + step for step in range(PLANE)] for up in range(columns)]
+    column_groups = [[up * PLANE + step for up in range(columns)] for step in range(PLANE)]
+
+    def within_plane(parts):
+        return lax.all_to_all(parts, "ep", 0, 0, tiled=True, axis_index_groups=plane_groups)
+
+    far_mix, far_grad_x = [], []
     for micro in micros:
-        mix, grad_x, grad_gate, before = experts(
+        mix, grad_x, before = experts(
             place,
             [(part, 0) for part in plane_x[micro]],
             [(part, micro) for part in plane_dy],
             small_all,
-            column_weights,
+            weights,
             pieces,
             before,
+            True,
         )
         if micro:
-            grad_x, mix, grad_gate, before, far_grad_x, far_mix = together(
-                grad_x, mix, grad_gate, before, far_grad_x, far_mix
-            )
+            grad_x, before, far_grad_x, far_mix = together(grad_x, before, far_grad_x, far_mix)
         far_grad_x.append([flip(grad_x[step - 1], step) for step in range(1, PLANE)])
-        far_grad_gate.append(grad_gate)
-        early = PLANE - 2 if micro < micro_count - 1 else 0
-        far_mix.append([flip(mix[step - 1], step) for step in range(1, early + 1)])
-        late_mix.append([(mix[step - 1], step) for step in range(early + 1, PLANE)])
-    far_grad_gate = jnp.concatenate(far_grad_gate, 2)
-    far_grad_gate = [flip(far_grad_gate[step - 1], step) for step in range(1, PLANE)]
-    keep_w, send_w = before
-    given_w = swap_cores(send_w)
-
-    def column_sum(first, last, low, high):
-        kept = keep_w[first:last, low:high].astype(jnp.float32)
-        return (kept + given_w[first:last, low:high].astype(jnp.float32)).astype(jnp.bfloat16)
-
-    own_w = keep_w[0].astype(jnp.float32) + given_w[0].astype(jnp.float32)
-    far_in_w, near_in_w, last_in_w = [column_sum(slot, slot + 1, 0, 2) for slot in (1, 2, 3)]
-    far_out_w, near_out_w = column_sum(1, 2, 2, 3), column_sum(2, 4, 2, 3)
-    near_out_w, far_grad_x[-1] = together(near_out_w, far_grad_x[-1])
-    near_out_w = flip(near_out_w, PLANE)
+        if micro < micro_count - 1:
+            far_mix.append(within_plane(mix))
+    last_mix = mix
+    keep_w, send_in_w, send_out_w = before
+    given_out = swap_cores(send_out_w)[:, 0]
+    out_w = keep_w[:, 2].astype(jnp.float32) + given_out.astype(jnp.float32)
+    near_out_w = flip(out_w[1::2].astype(jnp.bfloat16), PLANE)
+    far_grad_x[-1], near_out_w = together(far_grad_x[-1], near_out_w)
+    near_out_w = near_out_w.astype(jnp.float32)
 
     def at_home(own_parts, far_parts):
         return jnp.concatenate(
             [
-                own_parts[micro].astype(jnp.float32)
-                + sum(part.astype(jnp.float32) for part in far_parts[micro])
+                sum(part.astype(jnp.float32) for part in (own_parts[micro], *far_parts[micro]))
                 for micro in micros
             ],
             0,
         )
 
     grad_out = cotangent.reshape(all_rows, width).astype(jnp.float32)
-    slot_grads = jnp.stack(
-        [jnp.concatenate([own_grad_gate[micro] for micro in micros], 1)]
-        + far_grad_gate
+    home_grad_x = [
+        [own_grad_x[micro], *far_grad_x[micro]] for micro in micros
+    ]
+    slot_grads = jnp.concatenate(
+        [
+            jnp.stack(
+                [
+                    sum(
+                        part[:, width + low : width + low + columns].astype(jnp.float32)
+                        for low in (0, 8, 16)
+                    ).T
+                    for part in parts
+                ]
+            )
+            for parts in home_grad_x
+        ],
+        2,
     )
     grad_gates = jnp.sum(slot_hot * slot_grads[:, :, :, None], (0, 1))
     grad_spread = gates * (grad_gates - jnp.sum(gates * grad_gates, -1, keepdims=True))
     grad_logits = jnp.sum(grad_spread[:, :, None] * route_hot, 1).astype(jnp.bfloat16)
-    grad_normed_two = at_home(own_grad_x, far_grad_x) + dot_f32(
-        grad_logits, w_route_full, 1, 1
-    )
-    grad_route = dot_f32(normed_two, grad_logits, 0, 0)
+    grad_normed_two = jnp.concatenate(
+        [sum(part[:, :width].astype(jnp.float32) for part in parts) for parts in home_grad_x], 0
+    ) + dot_f32(grad_logits, w_route_full, 1, 1)
+    grad_route = dot_f32(normed_late, grad_logits, 0, 0)
     gained_two = grad_normed_two * gain_two
     grad_gain_two = jnp.sum(grad_normed_two * resid * scale_two, 0)
     grad_resid = (
@@ -1372,19 +1405,25 @@
     grad_outw = sum(
         dot_f32(grad_branch[micro * rows : (micro + 1) * rows], attended_t[micro], 0, 1)
         for micro in micros
-    )
-    grad_att, near_out_w = together(grad_att, near_out_w)
-    near_out_w = near_out_w.astype(jnp.float32)
+    ).astype(jnp.bfloat16)
     grad_heads = every_device(grad_att)
-    grad_heads, near_out_w, far_in_w, near_in_w, last_in_w, far_out_w = together(
-        grad_heads, near_out_w, far_in_w, near_in_w, last_in_w, far_out_w
-    )
-    far_in_w = flip(far_in_w, 2 * PLANE)
+    far_out_w = (out_w[2] + near_out_w[1]).astype(jnp.bfloat16)
+    given_in = swap_cores(send_in_w)
+
+    def column_sum(slot):
+        kept = keep_w[slot, :2].astype(jnp.float32)
+        return (kept + given_in[slot].astype(jnp.float32)).astype(jnp.bfloat16)
+
+    own_w = keep_w[0, :2].astype(jnp.float32) + given_in[0].astype(jnp.float32)
+    near_in_w, far_in_w, last_in_w = column_sum(1), column_sum(2), column_sum(3)
+    grad_heads, near_in_w, last_in_w, far_in_w, far_out_w, own_w = together(
+        grad_heads, near_in_w, last_in_w, far_in_w, far_out_w, own_w
+    )
+    last_mix = within_plane(last_mix)
     near_in_w = flip(near_in_w, PLANE)
     last_in_w = flip(last_in_w, 3 * PLANE)
-    far_out_w = flip(
-        (far_out_w[0].astype(jnp.float32) + near_out_w[1]).astype(jnp.bfloat16), 2 * PLANE
-    )
+    far_in_w = flip(far_in_w, 2 * PLANE)
+    far_out_w = flip(far_out_w, 2 * PLANE)
 
     def to_shards(kept, given):
         core_sum = kept.astype(jnp.float32) + swap_cores(given).astype(jnp.float32)
@@ -1400,9 +1439,6 @@
     def own_rows(values):
         return lax.dynamic_slice_in_dim(values, tp_index * (shard // 2), shard // 2, 0)
 
-    grad_heads, grad_outw, grad_route, grad_gain_two = together(
-        grad_heads, grad_outw.astype(jnp.bfloat16), grad_route, grad_gain_two
-    )
     late_small = in_lanes([grad_route, grad_gain_two[:, None]])
     out_parts = [
         jnp.concatenate([grad_outw[:, part * out_cols : (part + 1) * out_cols], late_small], 1)
@@ -1410,71 +1446,60 @@
     ]
     out_kept = jnp.where(tp_index == 0, out_parts[0], out_parts[1])
     out_given = jnp.where(tp_index == 0, out_parts[1], out_parts[0])
-    out_sum = out_kept.astype(jnp.float32) + swap_cores(out_given).astype(jnp.float32)
-    plane_groups = [
-        [up * PLANE + step for step in range(PLANE)] for up in range(columns)
-    ]
-    column_groups = [
-        [up * PLANE + step for up in range(columns)] for step in range(PLANE)
-    ]
-    out_spots = lax.all_to_all(
-        jnp.swapaxes(
-            out_sum.astype(jnp.bfloat16).reshape(columns, PLANE, shard, -1), 0, 1
-        ),
-        "ep",
-        0,
-        0,
-        tiled=True,
-        axis_index_groups=plane_groups,
-    )
-
     grad_q, keep_kv, send_kv = attend_back(
         core, own, other, limit, out_f, log_total, grad_heads
     )
-    grad_q, keep_kv, send_kv, far_in_w, near_in_w, last_in_w, far_out_w, out_spots = together(
-        grad_q, keep_kv, send_kv, far_in_w, near_in_w, last_in_w, far_out_w, out_spots
-    )
-    for micro in micros:
-        far_mix[micro] = far_mix[micro] + [
-            flip(after(part, grad_q), step) for part, step in late_mix[micro]
+    grad_q, keep_kv, send_kv, near_in_w, last_in_w, far_in_w, far_out_w, last_mix = together(
+        grad_q, keep_kv, send_kv, near_in_w, last_in_w, far_in_w, far_out_w, last_mix
+    )
+    far_mix.append(last_mix)
+    grad_kv = (keep_kv + swap_cores(send_kv).astype(jnp.float32)).astype(jnp.bfloat16)
+    sent_back = jnp.concatenate([grad_q, grad_kv], 1)
+    grad_own = every_device(sent_back)
+    out_sum = out_kept.astype(jnp.float32) + swap_cores(out_given).astype(jnp.float32)
+    out_sum = out_sum.astype(jnp.bfloat16).reshape(columns, PLANE, shard, -1)
+
+    def summed(values, axis, place_here, stride):
+        own_part = lax.dynamic_index_in_dim(values, place_here, axis, False).astype(jnp.float32)
+        return own_part, [
+            flip(lax.dynamic_index_in_dim(values, place_here ^ step, axis, False), stride * step)
+            for step in range(1, values.shape[axis])
         ]
-    grad_kv = (keep_kv + swap_cores(send_kv).astype(jnp.float32)).astype(jnp.bfloat16)
-    grad_own = every_device(jnp.concatenate([grad_q, grad_kv], 1))
-    grad_own, far_mix = together(grad_own, far_mix)
-
-    out_levels = jnp.sum(out_spots.astype(jnp.float32), 0).astype(jnp.bfloat16)
-    out_levels = lax.all_to_all(
-        out_levels, "ep", 0, 0, tiled=True, axis_index_groups=column_groups
-    )
-    out_share = jnp.sum(out_levels.astype(jnp.float32), 0)
+
+    out_own, out_far = summed(out_sum, 1, spot, 1)
+    out_levels = out_own + sum(part.astype(jnp.float32) for part in out_far)
+    out_own, out_far = summed(out_levels.astype(jnp.bfloat16), 0, level, PLANE)
+    grad_own, out_far = together(grad_own, out_far)
+    out_share = out_own + sum(part.astype(jnp.float32) for part in out_far)
     out_small = own_rows(out_share[:, out_cols:])
     grad_tokens, kept, given = project_back(
         core, grad_own, w_heads, normed, tokens, grad_resid, gain_one[None, :], cosine, sine
     )
-    kept, given, far_in_w, near_in_w, last_in_w, far_out_w = together(
-        kept, given, far_in_w, near_in_w, last_in_w, far_out_w
-    )
-    grad_in_w = own_w[:2] + sum(
-        part[0].astype(jnp.float32) for part in (far_in_w, near_in_w, last_in_w)
-    )
-    grad_out_w = own_w[2] + near_out_w[0, 0] + far_out_w[0].astype(jnp.float32)
+    kept, given, near_in_w, last_in_w, far_in_w, far_out_w = together(
+        kept, given, near_in_w, last_in_w, far_in_w, far_out_w
+    )
+    grad_w = [
+        own_w[matrix]
+        + sum(part[matrix].astype(jnp.float32) for part in (near_in_w, last_in_w, far_in_w))
+        for matrix in range(2)
+    ]
+    grad_w.append(out_w[0] + near_out_w[0] + far_out_w.astype(jnp.float32))
     mixed = (resid + at_home(own_mix, far_mix)).astype(jnp.bfloat16)
 
     own_share = to_shards(kept, given)
-    head_grads = own_share[:, :half_cols].reshape(shard, kv_here, 2, 2, HEAD_DIM)
     return (
         mixed.reshape(micro_count, rows, width),
         grad_tokens,
         own_rows(own_share[:, half_cols:])[:, 0],
-        head_grads[:, :, :, 0].reshape(shard, q_cols),
-        head_grads[:, :, 0, 1].reshape(shard, kv_cols),
-        head_grads[:, :, 1, 1].reshape(shard, kv_cols),
+        own_share[:, :q_cols],
+        own_share[:, q_cols : q_cols + kv_cols],
+        own_share[:, q_cols + kv_cols : half_cols],
         out_share[:, :out_cols].T,
         out_small[:, experts_all],
         out_small[:, :experts_all],
-        grad_in_w[0][None],
-        grad_in_w[1][None],
-        grad_out_w.T[None],
+        grad_w[0][None],
+        grad_w[1][None],
+        grad_w[2].T[None],
     )
 
 

time: 781 us -> 745 us (0.954)
  waiting for transfers between devices: 265 us -> 245 us
  Pallas kernels: 300 us -> 285 us
  other arithmetic: 50 us -> 61.6 us
  local copies, waits for them, and re-layouts: 43.2 us -> 32.5 us
    ppermute x40 -> x38, waiting for transfers between devices: 142 us -> 109 us  [flip(): lax.ppermute(values, 'ep', [(index, index ^ bits) for index in range(coun...]
    add x6 -> x7, other arithmetic: 8.71 us -> 24.8 us  [the longest x1 6.73 us: on_device_paired(): own_w = keep_w[0, :2].astype(jnp.float32) + given_in[0].astype(jnp.float32)]
    ppermute x14 -> x16, waiting for transfers between devices: 5.41 us -> 16 us  [swap_cores(): return lax.ppermute(values, 'tp', [(0, 1), (1, 0)])]
    pallas_call x1, Pallas kernels: 109 us -> 100 us  [attend_back(): pl.pallas_call(functools.partial(attend_back_kernel, query_block=query_bl...]
    pallas_call x1, Pallas kernels: 59.8 us -> 51.2 us  [attend(): pl.pallas_call(functools.partial(attend_kernel, query_block=query_block,...]
    unnamed x137 -> x112, local copies, waits for them, and re-layouts: 21.9 us -> 17.8 us
    ppermute x40 -> x38, starting transfers between devices: 47.4 us -> 44 us  [flip(): lax.ppermute(values, 'ep', [(index, index ^ bits) for index in range(coun...]
  transfers between devices with their start and end apart: 62 -> 62, of which waited for: 24 -> 28; matrix products, arithmetic and copies ran while one was open for 8% -> 9% of each run, Pallas kernels for 37% -> 37%
where the time goes in v3:
time: 745 us; the launch traced here: 737 us
  Pallas kernels  285 us (38%)
  waiting for transfers between devices  245 us (33%)
  starting transfers between devices  88.4 us (12%)
  other arithmetic  61.6 us (8%)
  local copies, waits for them, and re-layouts  32.5 us (4%)
  between operations  15.4 us (2%)
  matrix products  8.9 us (1%)
    pallas_call x3, Pallas kernels, experts(): pl.pallas_call(functools.partial(experts_kernel, slots=slots, first_call=...  116 us
    ppermute x38, waiting for transfers between devices, flip(): lax.ppermute(values, 'ep', [(index, index ^ bits) for index in range(coun...  109 us
    pallas_call x1, Pallas kernels, attend_back(): pl.pallas_call(functools.partial(attend_back_kernel, query_block=query_bl...  100 us
    all_to_all x4, waiting for transfers between devices, every_device(): return lax.all_to_all(values, ('ep', 'tp'), 0, 0, tiled=True)  83.1 us
    pallas_call x1, Pallas kernels, attend(): pl.pallas_call(functools.partial(attend_kernel, query_block=query_block,...  51.2 us
    ppermute x38, starting transfers between devices, flip(): lax.ppermute(values, 'ep', [(index, index ^ bits) for index in range(coun...  44 us
    all_to_all x1, waiting for transfers between devices, to_shards(): lax.all_to_all(core_sum.astype(jnp.bfloat16).reshape(ep_count, shard, -1)...  36.8 us
    all_to_all x4, starting transfers between devices, every_device(): return lax.all_to_all(values, ('ep', 'tp'), 0, 0, tiled=True)  22.7 us
  transfers between devices with their start and end apart: 62, of which 28 were waited for; matrix products, arithmetic and copies ran while one was open for 9% of the time, Pallas kernels for 37%

profile of v3, /device:TPU:14, one launch (start us, length us, event | category | flops | bytes accessed | tf_op | source)
XLA Modules:
  0.0 736.7 jit_solution(12717855962365576471)
XLA Ops:
  10.3 2.6 collective-permute-start.1
  16.2 7.0 collective-permute-done.1
  23.3 2.8 collective-permute-done.2
  33.1 17.7 %collective-permute-done.6.refs_15_.refs_17_ = bf16[1,512,512]{2,1,0:T(8,128)(2,1)S(1)} collective-permute-done((bf16[1,512,512]{2,1,0:T(8,128)(2,1)S(1)}, bf16[1,512,512]{2,1,0:T(8,128)(2,1)S(1)}, u32[]{:S(2)}, u32[]{:S(2)}) %collective-permute-start.6) | collective-permute-done | bytes 524320 | tf_op jit(solution)/shard_map/ppermute | solution.py:1137
  50.8 3.4 collective-permute-done.7.refs_11_.refs_13_
  60.0 5.9 project.1
  69.7 4.0 all-to-all-start
  73.9 2.9 fusion.2
  78.3 41.6 %all-to-all-done.own_ref = bf16[32,128,256]{2,1,0:T(8,128)(2,1)} async-done(((bf16[32,128,256]{2,1,0:T(8,128)(2,1)}), bf16[32,128,256]{2,1,0:T(8,128)(2,1)}, u32[]{:S(2)}, u32[]{:S(2)}) %all-to-all-start) | async-done | bytes 2097184 | tf_op jit(solution)/shard_map/all_to_all | solution.py:1145
  125.9 2.9 collective-permute-start.14
  132.8 51.2 %attend.1 = (bf16[32,64,256]{2,1,0:T(8,128)(2,1)}, f32[32,64,256]{2,1,0:T(8,128)}, f32[1,8192]{1,0:T(1,128)}) custom-call(s32[1]{0:T(128)} %bitcast.tp_ref, bf16[32,128,256]{2,1,0:T(8,128)(2,1)} %all-to-all-done.own_ref, bf16[32,64,256]{2,1,0:T(8,128)(2,1)} %copy-done.49, s32[1,8192]{1,0:T(1,128)} %iota_maximum_fusion.limit_ref), custom_call_target="tpu_custom_call" | custom-call | flops 34359738368 | bytes 8388608 | tf_op jit(solution)/shard_map/attend/pallas_call | solution.py:618
  184.1 5.8 all-to-all-start.1
  192.1 28.0 %all-to-all-done.1 = bf16[32,64,256]{2,1,0:T(8,128)(2,1)S(1)} async-done(((bf16[32,64,256]{2,1,0:T(8,128)(2,1)}), bf16[32,64,256]{2,1,0:T(8,128)(2,1)S(1)}, u32[]{:S(2)}, u32[]{:S(2)}) %all-to-all-start.1) | async-done | bytes 1048608 | tf_op jit(solution)/shard_map/all_to_all | solution.py:1145
  226.9 10.4 %collective-permute-done.23.refs_17_.refs_19_ = bf16[2,512,512]{2,1,0:T(8,128)(2,1)} collective-permute-done((bf16[2,512,512]{2,1,0:T(8,128)(2,1)}, bf16[2,512,512]{2,1,0:T(8,128)(2,1)}, u32[]{:S(2)}, u32[]{:S(2)}) %collective-permute-start.23) | collective-permute-done | bytes 1048608 | tf_op jit(solution)/shard_map/ppermute | solution.py:1137
  242.8 2.5 collective-permute-start.31
  245.3 28.7 %experts.3 = (bf16[2,256,1024]{2,1,0:T(8,128)(2,1)}, bf16[256,1152]{1,0:T(8,128)(2,1)}, bf16[256,1152]{1,0:T(8,128)(2,1)}, bf16[4,3,512,512]{3,2,1,0:T(8,128)(2,...) custom-call(s32[6]{0:T(128)} %concatenate.53.refs_0_, bf16[512,1024]{1,0:T(8,128)(2,1)} %copy-done.9, ...), custom_call_target="tpu_custom_call" | custom-call | flops 19327352832 | bytes 25165824 | tf_op jit(solution)/shard_map/experts/pallas_call | solution.py:1076
  275.0 2.5 collective-permute-start.28
  277.5 43.5 %experts.4 = (bf16[4,256,1024]{2,1,0:T(8,128)(2,1)}, bf16[256,1152]{1,0:T(8,128)(2,1)}, bf16[256,1152]{1,0:T(8,128)(2,1)}, bf16[256,1152]{1,0:T(8,128)(2,1)}, bf...) custom-call(s32[6]{0:T(128)} %concatenate.53.refs_0_, ...), custom_call_target="tpu_custom_call" | custom-call | flops 28991029248 | bytes 25165824 | tf_op jit(solution)/shard_map/experts/pallas_call | solution.py:1076
  322.1 7.1 all-to-all-start.2
  329.3 43.7 %experts.5 = (bf16[4,256,1024]{2,1,0:T(8,128)(2,1)}, bf16[256,1152]{1,0:T(8,128)(2,1)}, bf16[256,1152]{1,0:T(8,128)(2,1)}, bf16[256,1152]{1,0:T(8,128)(2,1)}, bf...) custom-call(s32[6]{0:T(128)} %concatenate.53.refs_0_, ...), custom_call_target="tpu_custom_call" | custom-call | flops 28991029248 | bytes 25165824 | tf_op jit(solution)/shard_map/experts/pallas_call | solution.py:1076
  377.7 5.0 convert_add_fusion
  392.5 2.8 convert_add_fusion.3
  395.3 6.6 collective-permute-done.35
  401.9 13.3 %collective-permute-done.36 = bf16[256,1152]{1,0:T(8,128)(2,1)} collective-permute-done((bf16[256,1152]{1,0:T(8,128)(2,1)}, bf16[256,1152]{1,0:T(8,128)(2,1)}, u32[]{:S(2)}, u32[]{:S(2)}) %collective-permute-start.36) | collective-permute-done | bytes 589856 | tf_op jit(solution)/shard_map/ppermute | solution.py:1137
  420.7 2.6 multiply_reduce_fusion
  428.3 5.8 all-to-all-start.3
  437.9 6.7 add_bitcast_fusion
  444.7 13.5 %all-to-all-done.3.grad_ref = bf16[32,64,256]{2,1,0:T(8,128)(2,1)S(1)} async-done(((bf16[32,64,256]{2,1,0:T(8,128)(2,1)}), bf16[32,64,256]{2,1,0:T(8,128)(2,1)S(1)}, u32[]{:S(2)}, u32[]{:S(2)}) %all-to-all-start.3) | async-done | bytes 1048608 | tf_op jit(solution)/shard_map/all_to_all | solution.py:1145
  459.1 5.7 all-to-all-start.4
  466.7 2.5 collective-permute-start.43
  469.7 100.1 %attend_back.1 = (bf16[32,64,256]{2,1,0:T(8,128)(2,1)}, f32[32,64,256]{2,1,0:T(8,128)}, bf16[32,64,256]{2,1,0:T(8,128)(2,1)}) custom-call(s32[1]{0:T(128)} %bitcast.tp_ref, bf16[32,128,256]{2,1,0:T(8,128)(2,1)} %all-to-all-done.own_ref, bf16[32,64,256]{2,1,0:T(8,128)(2,1)} %copy-done.49, s32[1,8192]{1,0:T(1,128)} %iota_maximum_fusion.limit_ref, ...), custom_call_target="tpu_custom_call" | custom-call | flops 68719476736 | bytes 12582912 | tf_op jit(solution)/shard_map/attend_back/pallas_call | solution.py:764
  569.8 9.0 %collective-permute-done.44 = bf16[512,512]{1,0:T(8,128)(2,1)} collective-permute-done((bf16[512,512]{1,0:T(8,128)(2,1)}, bf16[512,512]{1,0:T(8,128)(2,1)}, u32[]{:S(2)}, u32[]{:S(2)}) %collective-permute-start.44) | collective-permute-done | bytes 524320 | tf_op jit(solution)/shard_map/ppermute | solution.py:1137
  578.9 3.0 collective-permute-done.45
  585.6 7.2 all-to-all-start.5
  595.9 3.0 collective-permute-done.46
  605.4 13.4 %collective-permute-done.47 = bf16[4,64,640]{2,1,0:T(8,128)(2,1)S(1)} collective-permute-done((bf16[4,64,640]{2,1,0:T(8,128)(2,1)S(1)}, bf16[4,64,640]{2,1,0:T(8,128)(2,1)S(1)}, u32[]{:S(2)}, u32[]{:S(2)}) %collective-permute-start.47) | collective-permute-done | bytes 327712 | tf_op jit(solution)/shard_map/ppermute | solution.py:1137
  618.8 4.3 collective-permute-done.48
  623.1 6.6 collective-permute-done.49
  630.9 3.8 collective-permute-start.51
  635.2 8.9 %collective-permute-done.51 = bf16[64,640]{1,0:T(8,128)(2,1)} collective-permute-done((bf16[64,640]{1,0:T(8,128)(2,1)S(1)}, bf16[64,640]{1,0:T(8,128)(2,1)}, u32[]{:S(2)}, u32[]{:S(2)}) %collective-permute-start.51) | collective-permute-done | bytes 81952 | tf_op jit(solution)/shard_map/ppermute | solution.py:1137
  644.1 3.2 collective-permute-done.52
  647.3 11.7 %project_back.1 = (f32[2,256,1024]{2,1,0:T(8,128)}, bf16[1024,1152]{1,0:T(8,128)(2,1)}, bf16[1024,1152]{1,0:T(8,128)(2,1)}) custom-call(s32[1]{0:T(128)} %bitcast.tp_ref, bf16[32,128,256]{2,1,0:T(8,128)(2,1)} %all-to-all-done.5.grad_ref, bf16[2,1024,1024]{2,1,0:T(8,128)(2,1)} %get-tuple-element.183.heads_ref, bf16[512,1024]{1,0:T(8,128)(2,1)} %copy-done.2, ...), custom_call_target="tpu_custom_call" | custom-call | tf_op jit(solution)/shard_map/project_back/pallas_call | solution.py:916
  659.0 4.7 collective-permute-done.53
  663.8 3.6 add_convert_fusion
  667.4 6.1 all-to-all-start.6
  673.5 3.3 add_bitcast_fusion.2
  686.2 4.3 add_add_fusion
  690.5 36.8 %all-to-all-done.6 = bf16[16,64,1152]{2,1,0:T(8,128)(2,1)S(1)} async-done(((bf16[16,64,1152]{2,1,0:T(8,128)(2,1)}), bf16[16,64,1152]{2,1,0:T(8,128)(2,1)S(1)}, u32[]{:S(2)}, u32[]{:S(2)}) %all-to-all-start.6) | async-done | bytes 2359328 | tf_op jit(solution)/shard_map/all_to_all | solution.py:1430
  (301 shorter events, 109.6 us)
Async XLA Ops:
  10.3 13.0 %collective-permute-start.1 = (bf16[64,1152]{1,0:T(8,128)(2,1)S(1)}, bf16[64,1152]{1,0:T(8,128)(2,1)S(1)}, u32[]{:S(2)}, u32[]{:S(2)}) collective-permute-start(bf16[64,1152]{1,0:T(8,128)(2,1)S(1)} %get-tuple-element.309), channel_id=1, source_target_pairs={{0,16},{2,18},{4,20},{6,22},{8,24},{10,26},{12,28},{14,30},{16,0},... | collective-permute-start | bytes 442376 | tf_op jit(solution)/shard_map/ppermute | solution.py:1137
  12.8 13.3 %collective-permute-start.2 = (bf16[64,1152]{1,0:T(8,128)(2,1)S(1)}, bf16[64,1152]{1,0:T(8,128)(2,1)S(1)}, u32[]{:S(2)}, u32[]{:S(2)}) collective-permute-start(bf16[64,1152]{1,0:T(8,128)(2,1)S(1)} %get-tuple-element.309), channel_id=1, source_target_pairs={{0,24},{2,26},{4,28},{6,30},{8,16},{10,18},{12,20},{14,22},{16,8},... | collective-permute-start | bytes 442376 | tf_op jit(solution)/shard_map/ppermute | solution.py:1137
  26.2 28.0 %collective-permute-start.3 = (bf16[4,64,1152]{2,1,0:T(8,128)(2,1)S(1)}, bf16[4,64,1152]{2,1,0:T(8,128)(2,1)S(1)}, u32[]{:S(2)}, u32[]{:S(2)}) collective-permute-start(bf16[4,64,1152]{2,1,0:T(8,128)(2,1)S(1)} %pad_maximum_fusion.9.refs_4_), channel_id=1, source_target_pairs={{0,2},{2,0},{4,6},{6,4},{8,10},{10,8},{12,14},{14,12},{16,18},{18,... | collective-permute-start | bytes 1769480 | tf_op jit(solution)/shard_map/ppermute | solution.py:1137
  26.8 27.4 %collective-permute-start.4 = (bf16[4,64,1152]{2,1,0:T(8,128)(2,1)S(1)}, bf16[4,64,1152]{2,1,0:T(8,128)(2,1)S(1)}, u32[]{:S(2)}, u32[]{:S(2)}) collective-permute-start(bf16[4,64,1152]{2,1,0:T(8,128)(2,1)S(1)} %pad_maximum_fusion.9.refs_4_), channel_id=1, source_target_pairs={{0,4},{2,6},{4,0},{6,2},{8,12},{10,14},{12,8},{14,10},{16,20},{18,... | collective-permute-start | bytes 1769480 | tf_op jit(solution)/shard_map/ppermute | solution.py:1137
  27.3 26.9 %collective-permute-start.5 = (bf16[4,64,1152]{2,1,0:T(8,128)(2,1)S(1)}, bf16[4,64,1152]{2,1,0:T(8,128)(2,1)S(1)}, u32[]{:S(2)}, u32[]{:S(2)}) collective-permute-start(bf16[4,64,1152]{2,1,0:T(8,128)(2,1)S(1)} %pad_maximum_fusion.9.refs_4_), channel_id=1, source_target_pairs={{0,6},{2,4},{4,2},{6,0},{8,14},{10,12},{12,10},{14,8},{16,22},{18,... | collective-permute-start | bytes 1769480 | tf_op jit(solution)/shard_map/ppermute | solution.py:1137
  30.0 20.8 %collective-permute-start.6 = (bf16[1,512,512]{2,1,0:T(8,128)(2,1)S(1)}, bf16[1,512,512]{2,1,0:T(8,128)(2,1)S(1)}, u32[]{:S(2)}, u32[]{:S(2)}) collective-permute-start(bf16[1,512,512]{2,1,0:T(8,128)(2,1)S(1)} %slice.258), channel_id=1, source_target_pairs={{0,16},{2,18},{4,20},{6,22},{8,24},{10,26},{12,28},{14,30},{16,0},... | collective-permute-start | bytes 1572872 | tf_op jit(solution)/shard_map/ppermute | solution.py:1137
  30.6 23.6 %collective-permute-start.7 = (bf16[1,512,512]{2,1,0:T(8,128)(2,1)S(1)}, bf16[1,512,512]{2,1,0:T(8,128)(2,1)S(1)}, u32[]{:S(2)}, u32[]{:S(2)}) collective-permute-start(bf16[1,512,512]{2,1,0:T(8,128)(2,1)S(1)} %slice.258), channel_id=1, source_target_pairs={{0,8},{2,10},{4,12},{6,14},{8,0},{10,2},{12,4},{14,6},{16,24},{18,... | collective-permute-start | bytes 1572872 | tf_op jit(solution)/shard_map/ppermute | solution.py:1137
  55.3 14.3 %collective-permute-start.12 = (bf16[1,512,512]{2,1,0:T(8,128)(2,1)}, bf16[1,512,512]{2,1,0:T(8,128)(2,1)}, u32[]{:S(2)}, u32[]{:S(2)}) collective-permute-start(bf16[1,512,512]{2,1,0:T(8,128)(2,1)} %copy-done.50), channel_id=1, source_target_pairs={{0,8},{2,10},{4,12},{6,14},{8,0},{10,2},{12,4},{14,6},{16,24},{18,... | collective-permute-start | bytes 1572872 | tf_op jit(solution)/shard_map/ppermute | solution.py:1137
  69.7 50.2 %all-to-all-start = ((bf16[32,128,256]{2,1,0:T(8,128)(2,1)}), bf16[32,128,256]{2,1,0:T(8,128)(2,1)}, u32[]{:S(2)}, u32[]{:S(2)}) async-start(bf16[32,128,256]{2,1,0:T(8,128)(2,1)} %get-tuple-element.114), calls=%async_computation | async-start | bytes 4194304 | tf_op jit(solution)/shard_map/all_to_all | solution.py:1145
  73.7 146.6 %all-gather.3.cloned.1.call-start = ((), (), s32[]{:S(2)}) async-start(), calls=%async_computation.7 | async-start | bytes 2162688 | tf_op jit(solution)/shard_map/all_gather | solution.py:1253
  125.9 58.1 %collective-permute-start.14 = (bf16[2,512,512]{2,1,0:T(8,128)(2,1)}, bf16[2,512,512]{2,1,0:T(8,128)(2,1)}, u32[]{:S(2)}, u32[]{:S(2)}) collective-permute-start(bf16[2,512,512]{2,1,0:T(8,128)(2,1)} %slice.260), channel_id=1, source_target_pairs={{0,8},{2,10},{4,12},{6,14},{8,0},{10,2},{12,4},{14,6},{16,24},{18,... | collective-permute-start | bytes 3145736 | tf_op jit(solution)/shard_map/ppermute | solution.py:1137
  128.8 55.2 %collective-permute-start.15 = (bf16[2,512,512]{2,1,0:T(8,128)(2,1)}, bf16[2,512,512]{2,1,0:T(8,128)(2,1)}, u32[]{:S(2)}, u32[]{:S(2)}) collective-permute-start(bf16[2,512,512]{2,1,0:T(8,128)(2,1)} %slice.260), channel_id=1, source_target_pairs={{0,16},{2,18},{4,20},{6,22},{8,24},{10,26},{12,28},{14,30},{16,0},... | collective-permute-start | bytes 3145736 | tf_op jit(solution)/shard_map/ppermute | solution.py:1137
  129.3 54.7 %collective-permute-start.16 = (bf16[2,256,1152]{2,1,0:T(8,128)(2,1)S(1)}, bf16[2,256,1152]{2,1,0:T(8,128)(2,1)S(1)}, u32[]{:S(2)}, u32[]{:S(2)}) collective-permute-start(bf16[2,256,1152]{2,1,0:T(8,128)(2,1)S(1)} %copy-done.32), channel_id=1, source_target_pairs={{0,2},{2,0},{4,6},{6,4},{8,10},{10,8},{12,14},{14,12},{16,18},{18,... | collective-permute-start | bytes 3538952 | tf_op jit(solution)/shard_map/ppermute | solution.py:1137
  129.3 54.7 %collective-permute-start.17 = (bf16[2,256,1152]{2,1,0:T(8,128)(2,1)S(1)}, bf16[2,256,1152]{2,1,0:T(8,128)(2,1)}, u32[]{:S(2)}, u32[]{:S(2)}) collective-permute-start(bf16[2,256,1152]{2,1,0:T(8,128)(2,1)S(1)} %copy-done.32), channel_id=1, source_target_pairs={{0,4},{2,6},{4,0},{6,2},{8,12},{10,14},{12,8},{14,10},{16,20},{18,... | collective-permute-start | bytes 3538952 | tf_op jit(solution)/shard_map/ppermute | solution.py:1137
  130.9 53.2 %collective-permute-start.18 = (bf16[2,256,1152]{2,1,0:T(8,128)(2,1)S(1)}, bf16[2,256,1152]{2,1,0:T(8,128)(2,1)}, u32[]{:S(2)}, u32[]{:S(2)}) collective-permute-start(bf16[2,256,1152]{2,1,0:T(8,128)(2,1)S(1)} %copy-done.32), channel_id=1, source_target_pairs={{0,6},{2,4},{4,2},{6,0},{8,14},{10,12},{12,10},{14,8},{16,22},{18,... | collective-permute-start | bytes 3538952 | tf_op jit(solution)/shard_map/ppermute | solution.py:1137
  184.1 36.0 %all-to-all-start.1 = ((bf16[32,64,256]{2,1,0:T(8,128)(2,1)}), bf16[32,64,256]{2,1,0:T(8,128)(2,1)S(1)}, u32[]{:S(2)}, u32[]{:S(2)}) async-start(bf16[32,64,256]{2,1,0:T(8,128)(2,1)} %get-tuple-element.119), calls=%async_computation.1 | async-start | bytes 2097152 | tf_op jit(solution)/shard_map/all_to_all | solution.py:1145
  189.8 47.9 %collective-permute-start.20 = (bf16[1,512,512]{2,1,0:T(8,128)(2,1)}, bf16[1,512,512]{2,1,0:T(8,128)(2,1)}, u32[]{:S(2)}, u32[]{:S(2)}) collective-permute-start(bf16[1,512,512]{2,1,0:T(8,128)(2,1)} %copy-done.52), channel_id=1, source_target_pairs={{0,1},{1,0},{2,3},{3,2},{4,5},{5,4},{6,7},{7,6},{8,9},{9,8},{10,11... | collective-permute-start | bytes 1572872 | tf_op jit(solution)/shard_map/ppermute | solution.py:1141
  191.0 46.3 %collective-permute-start.23 = (bf16[2,512,512]{2,1,0:T(8,128)(2,1)}, bf16[2,512,512]{2,1,0:T(8,128)(2,1)}, u32[]{:S(2)}, u32[]{:S(2)}) collective-permute-start(bf16[2,512,512]{2,1,0:T(8,128)(2,1)} %collective-permute-done.15.refs_13_.refs_15_), channel_id=1, source_target_pairs={{0,8},{2,10},{4,12},{6,14},{8,0},{10,2},{12,4},{14,6},{16,24},{18,... | collective-permute-start | bytes 3145736 | tf_op jit(solution)/shard_map/ppermute | solution.py:1137
  191.5 53.8 %collective-permute-start.21 = (bf16[2,512,512]{2,1,0:T(8,128)(2,1)}, bf16[2,512,512]{2,1,0:T(8,128)(2,1)}, u32[]{:S(2)}, u32[]{:S(2)}) collective-permute-start(bf16[2,512,512]{2,1,0:T(8,128)(2,1)} %collective-permute-done.15.refs_13_.refs_15_), channel_id=1, source_target_pairs={{0,1},{1,0},{2,3},{3,2},{4,5},{5,4},{6,7},{7,6},{8,9},{9,8},{10,11... | collective-permute-start | bytes 3145736 | tf_op jit(solution)/shard_map/ppermute | solution.py:1141
  191.6 51.2 %collective-permute-start.19 = (bf16[2,512,512]{2,1,0:T(8,128)(2,1)}, bf16[2,512,512]{2,1,0:T(8,128)(2,1)}, u32[]{:S(2)}, u32[]{:S(2)}) collective-permute-start(bf16[2,512,512]{2,1,0:T(8,128)(2,1)} %collective-permute-done.14.refs_9_.refs_11_), channel_id=1, source_target_pairs={{0,1},{1,0},{2,3},{3,2},{4,5},{5,4},{6,7},{7,6},{8,9},{9,8},{10,11... | collective-permute-start | bytes 3145736 | tf_op jit(solution)/shard_map/ppermute | solution.py:1141
  241.8 33.3 %collective-permute-start.29 = (bf16[256,1024]{1,0:T(8,128)(2,1)S(1)}, bf16[256,1024]{1,0:T(8,128)(2,1)}, u32[]{:S(2)}, u32[]{:S(2)}) collective-permute-start(bf16[256,1024]{1,0:T(8,128)(2,1)S(1)} %get-tuple-element.299), channel_id=1, source_target_pairs={{0,2},{2,0},{4,6},{6,4},{8,10},{10,8},{12,14},{14,12},{16,18},{18,... | collective-permute-start | bytes 1572872 | tf_op jit(solution)/shard_map/ppermute | solution.py:1137
  242.4 35.1 %collective-permute-start.30 = (bf16[256,1024]{1,0:T(8,128)(2,1)S(1)}, bf16[256,1024]{1,0:T(8,128)(2,1)}, u32[]{:S(2)}, u32[]{:S(2)}) collective-permute-start(bf16[256,1024]{1,0:T(8,128)(2,1)S(1)} %get-tuple-element.299), channel_id=1, source_target_pairs={{0,4},{2,6},{4,0},{6,2},{8,12},{10,14},{12,8},{14,10},{16,20},{18,... | collective-permute-start | bytes 1572872 | tf_op jit(solution)/shard_map/ppermute | solution.py:1137
  242.8 34.7 %collective-permute-start.31 = (bf16[256,1024]{1,0:T(8,128)(2,1)S(1)}, bf16[256,1024]{1,0:T(8,128)(2,1)}, u32[]{:S(2)}, u32[]{:S(2)}) collective-permute-start(bf16[256,1024]{1,0:T(8,128)(2,1)S(1)} %get-tuple-element.299), channel_id=1, source_target_pairs={{0,6},{2,4},{4,2},{6,0},{8,14},{10,12},{12,10},{14,8},{16,22},{18,... | collective-permute-start | bytes 1572872 | tf_op jit(solution)/shard_map/ppermute | solution.py:1137
  274.0 55.2 %collective-permute-start.26 = (bf16[256,1024]{1,0:T(8,128)(2,1)}, bf16[256,1024]{1,0:T(8,128)(2,1)}, u32[]{:S(2)}, u32[]{:S(2)}) collective-permute-start(bf16[256,1024]{1,0:T(8,128)(2,1)} %get-tuple-element.130), channel_id=1, source_target_pairs={{0,2},{2,0},{4,6},{6,4},{8,10},{10,8},{12,14},{14,12},{16,18},{18,... | collective-permute-start | bytes 1572872 | tf_op jit(solution)/shard_map/ppermute | solution.py:1137
  274.7 54.7 %collective-permute-start.27 = (bf16[256,1024]{1,0:T(8,128)(2,1)}, bf16[256,1024]{1,0:T(8,128)(2,1)}, u32[]{:S(2)}, u32[]{:S(2)}) collective-permute-start(bf16[256,1024]{1,0:T(8,128)(2,1)} %get-tuple-element.130), channel_id=1, source_target_pairs={{0,4},{2,6},{4,0},{6,2},{8,12},{10,14},{12,8},{14,10},{16,20},{18,... | collective-permute-start | bytes 1572872 | tf_op jit(solution)/shard_map/ppermute | solution.py:1137
  275.0 54.3 %collective-permute-start.28 = (bf16[256,1024]{1,0:T(8,128)(2,1)}, bf16[256,1024]{1,0:T(8,128)(2,1)}, u32[]{:S(2)}, u32[]{:S(2)}) collective-permute-start(bf16[256,1024]{1,0:T(8,128)(2,1)} %get-tuple-element.130), channel_id=1, source_target_pairs={{0,6},{2,4},{4,2},{6,0},{8,14},{10,12},{12,10},{14,8},{16,22},{18,... | collective-permute-start | bytes 1572872 | tf_op jit(solution)/shard_map/ppermute | solution.py:1137
  321.1 52.0 %collective-permute-start.32 = (bf16[256,1152]{1,0:T(8,128)(2,1)}, bf16[256,1152]{1,0:T(8,128)(2,1)S(1)}, u32[]{:S(2)}, u32[]{:S(2)}) collective-permute-start(bf16[256,1152]{1,0:T(8,128)(2,1)} %get-tuple-element.146), channel_id=1, source_target_pairs={{0,2},{2,0},{4,6},{6,4},{8,10},{10,8},{12,14},{14,12},{16,18},{18,... | collective-permute-start | bytes 1769480 | tf_op jit(solution)/shard_map/ppermute | solution.py:1137
  321.8 51.3 %collective-permute-start.33 = (bf16[256,1152]{1,0:T(8,128)(2,1)}, bf16[256,1152]{1,0:T(8,128)(2,1)}, u32[]{:S(2)}, u32[]{:S(2)}) collective-permute-start(bf16[256,1152]{1,0:T(8,128)(2,1)} %get-tuple-element.147), channel_id=1, source_target_pairs={{0,4},{2,6},{4,0},{6,2},{8,12},{10,14},{12,8},{14,10},{16,20},{18,... | collective-permute-start | bytes 1769480 | tf_op jit(solution)/shard_map/ppermute | solution.py:1137
  322.1 51.0 %all-to-all-start.2 = ((bf16[4,256,1024]{2,1,0:T(8,128)(2,1)}), bf16[4,256,1024]{2,1,0:T(8,128)(2,1)}, u32[]{:S(2)}, u32[]{:S(2)}) async-start(bf16[4,256,1024]{2,1,0:T(8,128)(2,1)} %get-tuple-element.149), calls=%async_computation.2 | async-start | bytes 4194304 | tf_op jit(solution)/shard_map/all_to_all | solution.py:1326
  329.2 43.8 %collective-permute-start.34 = (bf16[256,1152]{1,0:T(8,128)(2,1)}, bf16[256,1152]{1,0:T(8,128)(2,1)}, u32[]{:S(2)}, u32[]{:S(2)}) collective-permute-start(bf16[256,1152]{1,0:T(8,128)(2,1)} %get-tuple-element.148), channel_id=1, source_target_pairs={{0,6},{2,4},{4,2},{6,0},{8,14},{10,12},{12,10},{14,8},{16,22},{18,... | collective-permute-start | bytes 1769480 | tf_op jit(solution)/shard_map/ppermute | solution.py:1137
  383.8 31.4 %collective-permute-start.39 = (bf16[2,512,512]{2,1,0:T(8,128)(2,1)}, bf16[2,512,512]{2,1,0:T(8,128)(2,1)S(1)}, u32[]{:S(2)}, u32[]{:S(2)}) collective-permute-start(bf16[2,512,512]{2,1,0:T(8,128)(2,1)} %slice.276), channel_id=1, source_target_pairs={{0,8},{2,10},{4,12},{6,14},{8,0},{10,2},{12,4},{14,6},{16,24},{18,... | collective-permute-start | bytes 3145736 | tf_op jit(solution)/shard_map/ppermute | solution.py:1137
  385.4 16.5 %collective-permute-start.35 = (bf16[256,1152]{1,0:T(8,128)(2,1)}, bf16[256,1152]{1,0:T(8,128)(2,1)}, u32[]{:S(2)}, u32[]{:S(2)}) collective-permute-start(bf16[256,1152]{1,0:T(8,128)(2,1)} %get-tuple-element.158), channel_id=1, source_target_pairs={{0,2},{2,0},{4,6},{6,4},{8,10},{10,8},{12,14},{14,12},{16,18},{18,... | collective-permute-start | bytes 1769480 | tf_op jit(solution)/shard_map/ppermute | solution.py:1137
  387.4 27.8 %collective-permute-start.36 = (bf16[256,1152]{1,0:T(8,128)(2,1)}, bf16[256,1152]{1,0:T(8,128)(2,1)}, u32[]{:S(2)}, u32[]{:S(2)}) collective-permute-start(bf16[256,1152]{1,0:T(8,128)(2,1)} %get-tuple-element.159), channel_id=1, source_target_pairs={{0,4},{2,6},{4,0},{6,2},{8,12},{10,14},{12,8},{14,10},{16,20},{18,... | collective-permute-start | bytes 1769480 | tf_op jit(solution)/shard_map/ppermute | solution.py:1137
  388.9 26.3 %collective-permute-start.37 = (bf16[256,1152]{1,0:T(8,128)(2,1)}, bf16[256,1152]{1,0:T(8,128)(2,1)}, u32[]{:S(2)}, u32[]{:S(2)}) collective-permute-start(bf16[256,1152]{1,0:T(8,128)(2,1)} %get-tuple-element.160), channel_id=1, source_target_pairs={{0,6},{2,4},{4,2},{6,0},{8,14},{10,12},{12,10},{14,8},{16,22},{18,... | collective-permute-start | bytes 1769480 | tf_op jit(solution)/shard_map/ppermute | solution.py:1137
  392.4 45.5 %collective-permute-start.40 = (bf16[4,2,512,512]{3,2,1,0:T(8,128)(2,1)}, bf16[4,2,512,512]{3,2,1,0:T(8,128)(2,1)}, u32[]{:S(2)}, u32[]{:S(2)}) collective-permute-start(bf16[4,2,512,512]{3,2,1,0:T(8,128)(2,1)} %get-tuple-element.166), channel_id=1, source_target_pairs={{0,1},{1,0},{2,3},{3,2},{4,5},{5,4},{6,7},{7,6},{8,9},{9,8},{10,11... | collective-permute-start | bytes 12582920 | tf_op jit(solution)/shard_map/ppermute | solution.py:1141
  428.3 29.9 %all-to-all-start.3 = ((bf16[32,64,256]{2,1,0:T(8,128)(2,1)}), bf16[32,64,256]{2,1,0:T(8,128)(2,1)S(1)}, u32[]{:S(2)}, u32[]{:S(2)}) async-start(bf16[32,64,256]{2,1,0:T(8,128)(2,1)} %bitcast.66), calls=%async_computation.3 | async-start | bytes 2097152 | tf_op jit(solution)/shard_map/all_to_all | solution.py:1145
  459.1 110.6 %all-to-all-start.4 = ((bf16[4,256,1024]{2,1,0:T(8,128)(2,1)}), bf16[4,256,1024]{2,1,0:T(8,128)(2,1)S(1)}, u32[]{:S(2)}, u32[]{:S(2)}) async-start(bf16[4,256,1024]{2,1,0:T(8,128)(2,1)} %get-tuple-element.176), calls=%async_computation.4 | async-start | bytes 4194304 | tf_op jit(solution)/shard_map/all_to_all | solution.py:1326
  464.8 114.0 %collective-permute-start.41 = (bf16[2,512,512]{2,1,0:T(8,128)(2,1)}, bf16[2,512,512]{2,1,0:T(8,128)(2,1)S(1)}, u32[]{:S(2)}, u32[]{:S(2)}) collective-permute-start(bf16[2,512,512]{2,1,0:T(8,128)(2,1)} %get-tuple-element.172), channel_id=1, source_target_pairs={{0,8},{2,10},{4,12},{6,14},{8,0},{10,2},{12,4},{14,6},{16,24},{18,... | collective-permute-start | bytes 3145736 | tf_op jit(solution)/shard_map/ppermute | solution.py:1137
  466.2 112.6 %collective-permute-start.42 = (bf16[2,512,512]{2,1,0:T(8,128)(2,1)}, bf16[2,512,512]{2,1,0:T(8,128)(2,1)}, u32[]{:S(2)}, u32[]{:S(2)}) collective-permute-start(bf16[2,512,512]{2,1,0:T(8,128)(2,1)} %get-tuple-element.173), channel_id=1, source_target_pairs={{0,24},{2,26},{4,28},{6,30},{8,16},{10,18},{12,20},{14,22},{16,8},... | collective-permute-start | bytes 3145736 | tf_op jit(solution)/shard_map/ppermute | solution.py:1137
  466.7 112.0 %collective-permute-start.43 = (bf16[2,512,512]{2,1,0:T(8,128)(2,1)}, bf16[2,512,512]{2,1,0:T(8,128)(2,1)}, u32[]{:S(2)}, u32[]{:S(2)}) collective-permute-start(bf16[2,512,512]{2,1,0:T(8,128)(2,1)} %get-tuple-element.174), channel_id=1, source_target_pairs={{0,16},{2,18},{4,20},{6,22},{8,24},{10,26},{12,28},{14,30},{16,0},... | collective-permute-start | bytes 3145736 | tf_op jit(solution)/shard_map/ppermute | solution.py:1137
  469.2 109.5 %collective-permute-start.44 = (bf16[512,512]{1,0:T(8,128)(2,1)}, bf16[512,512]{1,0:T(8,128)(2,1)}, u32[]{:S(2)}, u32[]{:S(2)}) collective-permute-start(bf16[512,512]{1,0:T(8,128)(2,1)} %fusion.11), channel_id=1, source_target_pairs={{0,16},{2,18},{4,20},{6,22},{8,24},{10,26},{12,28},{14,30},{16,0},... | collective-permute-start | bytes 1572872 | tf_op jit(solution)/shard_map/ppermute | solution.py:1137
  585.6 61.7 %all-to-all-start.5 = ((bf16[32,128,256]{2,1,0:T(8,128)(2,1)}), bf16[32,128,256]{2,1,0:T(8,128)(2,1)}, u32[]{:S(2)}, u32[]{:S(2)}) async-start(bf16[32,128,256]{2,1,0:T(8,128)(2,1)} %pad_maximum_fusion.3), calls=%async_computation.5 | async-start | bytes 4194304 | tf_op jit(solution)/shard_map/all_to_all | solution.py:1145
  601.9 16.9 %collective-permute-start.47 = (bf16[4,64,640]{2,1,0:T(8,128)(2,1)S(1)}, bf16[4,64,640]{2,1,0:T(8,128)(2,1)S(1)}, u32[]{:S(2)}, u32[]{:S(2)}) collective-permute-start(bf16[4,64,640]{2,1,0:T(8,128)(2,1)S(1)} %get-tuple-element.294), channel_id=1, source_target_pairs={{0,2},{2,0},{4,6},{6,4},{8,10},{10,8},{12,14},{14,12},{16,18},{18,... | collective-permute-start | bytes 983048 | tf_op jit(solution)/shard_map/ppermute | solution.py:1137
  602.5 20.6 %collective-permute-start.48 = (bf16[4,64,640]{2,1,0:T(8,128)(2,1)S(1)}, bf16[4,64,640]{2,1,0:T(8,128)(2,1)S(1)}, u32[]{:S(2)}, u32[]{:S(2)}) collective-permute-start(bf16[4,64,640]{2,1,0:T(8,128)(2,1)S(1)} %get-tuple-element.296), channel_id=1, source_target_pairs={{0,4},{2,6},{4,0},{6,2},{8,12},{10,14},{12,8},{14,10},{16,20},{18,... | collective-permute-start | bytes 983048 | tf_op jit(solution)/shard_map/ppermute | solution.py:1137
  603.1 26.7 %collective-permute-start.49 = (bf16[4,64,640]{2,1,0:T(8,128)(2,1)S(1)}, bf16[4,64,640]{2,1,0:T(8,128)(2,1)S(1)}, u32[]{:S(2)}, u32[]{:S(2)}) collective-permute-start(bf16[4,64,640]{2,1,0:T(8,128)(2,1)S(1)} %get-tuple-element.295), channel_id=1, source_target_pairs={{0,6},{2,4},{4,2},{6,0},{8,14},{10,12},{12,10},{14,8},{16,22},{18,... | collective-permute-start | bytes 983048 | tf_op jit(solution)/shard_map/ppermute | solution.py:1137
  630.9 13.2 %collective-permute-start.51 = (bf16[64,640]{1,0:T(8,128)(2,1)S(1)}, bf16[64,640]{1,0:T(8,128)(2,1)}, u32[]{:S(2)}, u32[]{:S(2)}) collective-permute-start(bf16[64,640]{1,0:T(8,128)(2,1)S(1)} %get-tuple-element.304), channel_id=1, source_target_pairs={{0,16},{2,18},{4,20},{6,22},{8,24},{10,26},{12,28},{14,30},{16,0},... | collective-permute-start | bytes 245768 | tf_op jit(solution)/shard_map/ppermute | solution.py:1137
  634.7 12.6 %collective-permute-start.52 = (bf16[64,640]{1,0:T(8,128)(2,1)S(1)}, bf16[64,640]{1,0:T(8,128)(2,1)}, u32[]{:S(2)}, u32[]{:S(2)}) collective-permute-start(bf16[64,640]{1,0:T(8,128)(2,1)S(1)} %get-tuple-element.303), channel_id=1, source_target_pairs={{0,24},{2,26},{4,28},{6,30},{8,16},{10,18},{12,20},{14,22},{16,8},... | collective-permute-start | bytes 245768 | tf_op jit(solution)/shard_map/ppermute | solution.py:1137
  667.4 60.0 %all-to-all-start.6 = ((bf16[16,64,1152]{2,1,0:T(8,128)(2,1)}), bf16[16,64,1152]{2,1,0:T(8,128)(2,1)S(1)}, u32[]{:S(2)}, u32[]{:S(2)}) async-start(bf16[16,64,1152]{2,1,0:T(8,128)(2,1)} %bitcast.83), calls=%async_computation.6 | async-start | bytes 4718592 | tf_op jit(solution)/shard_map/all_to_all | solution.py:1430
  (67 other events, 529.4 us)
Sparse Core Ops, SparseCore 0:
  132.9 85.6 all-gather.2

commit v4 on v3

--- a/solution.py
+++ b/solution.py
@@ -924,14 +924,15 @@
     )(core, grad_own, heads, normed, x, grad_resid, gain, cosine, sine)
 
 
-def experts_kernel(*refs, slots, first_call, pieces, piece_count, spread):
+def experts_kernel(*refs, slots, first_call, pieces, piece_count, spread, spread_x):
     place_ref, refs = refs[0], refs[1:]
     x_refs, dy_refs = refs[:slots], refs[slots : 2 * slots]
     w_route_ref, weight_refs = refs[2 * slots], refs[2 * slots + 1 : 2 * slots + 1 + piece_count]
     refs = refs[2 * slots + 1 + piece_count :]
     if not first_call:
         before_refs, refs = refs[:3], refs[3:]
-    mix_ref, grad_x_refs, refs = refs[0], refs[1 : 1 + slots], refs[1 + slots :]
+    x_outs = 1 if spread_x else slots
+    mix_ref, grad_x_refs, refs = refs[0], refs[1 : 1 + x_outs], refs[1 + x_outs :]
     keep_ref, send_in_ref, send_out_ref = refs[:3]
     (
         x_all, x_t, dy_all, dy_t, gates, grad_gates, mix_sum, grad_x_sum, grad_w, weights, sems,
@@ -969,9 +970,7 @@
             dy_all[here, :] = dy
             dy_t[:, here] = dy.T
             chosen = dy_refs[slot][:, width:].astype(jnp.float32)
-            logits = jnp.where(chosen > 0.0, dot_f32(x, w_route_ref[...], 1, 0), NEG)
-            raised = jnp.exp(logits - jnp.max(logits, 1, keepdims=True)) * chosen
-            gates[here, :] = raised / jnp.sum(raised, 1, keepdims=True)
+            gates[here, :] = chosen_gates(x, w_route_ref[...], chosen)
         grad_gates[...] = jnp.zeros_like(grad_gates)
         mix_sum[...] = jnp.zeros_like(mix_sum)
         grad_x_sum[...] = jnp.zeros_like(grad_x_sum)
@@ -1036,18 +1035,21 @@
             here = slice(slot * rows, (slot + 1) * rows)
             block = (place_ref[place_ref.shape[0] - 1] ^ (slot + 1)) if spread else slot
             mix_ref[block] = mix_sum[here, :].astype(jnp.bfloat16)
-            grad_x_refs[slot][:, :width] = grad_x_sum[here, :].astype(jnp.bfloat16)
+            grad_x_ref = grad_x_refs[0].at[block] if spread_x else grad_x_refs[slot]
+            grad_x_ref[:, :width] = grad_x_sum[here, :].astype(jnp.bfloat16)
             parts = split_three(grad_gates[:, here])
             rest = jnp.zeros((LANES - 3 * parts[0].shape[0], rows), jnp.float32)
-            grad_x_refs[slot][:, width:] = (
+            grad_x_ref[:, width:] = (
                 jnp.concatenate([*parts, rest], 0).T.astype(jnp.bfloat16)
             )
         if spread:
             own_block = place_ref[place_ref.shape[0] - 1]
             mix_ref[own_block] = jnp.zeros((rows, width), jnp.bfloat16)
-
-
-def experts(place, x_parts, dy_parts, w_route, weights, pieces, before, spread):
+        if spread_x:
+            grad_x_refs[0][own_block] = jnp.zeros((rows, width + LANES), jnp.bfloat16)
+
+
+def experts(place, x_parts, dy_parts, w_route, weights, pieces, before, spread, spread_x):
     rows = dy_parts[0][0].shape[1]
     width, hidden_width = x_parts[0][0].shape[1], weights[0].shape[-1]
     count, slots = len(pieces), len(x_parts)
@@ -1064,7 +1066,9 @@
             pipeline_mode=pl.Buffered(1),
         )
 
-    row_spec = pl.BlockSpec((rows, width + LANES), lambda expert: (0, 0))
+    row_specs = (pl.BlockSpec((rows, width + LANES), lambda expert: (0, 0)),) * slots
+    if spread_x:
+        row_specs = (pl.BlockSpec((mix_slots, rows, width + LANES), lambda expert: (0, 0, 0)),)
     grad_specs = [
         pl.BlockSpec((1, size, half, hidden_width), lambda expert: (expert, 0, 0, 0))
         for size in (3, 2, 1)
@@ -1072,7 +1076,9 @@
     grad_shapes = tuple(
         jax.ShapeDtypeStruct((count, size, half, hidden_width), jnp.bfloat16) for size in (3, 2, 1)
     )
-    row_shape = jax.ShapeDtypeStruct((rows, width + LANES), jnp.bfloat16)
+    row_shapes = (jax.ShapeDtypeStruct((rows, width + LANES), jnp.bfloat16),) * slots
+    if spread_x:
+        row_shapes = (jax.ShapeDtypeStruct((mix_slots, rows, width + LANES), jnp.bfloat16),)
     outs = pl.pallas_call(
         functools.partial(
             experts_kernel,
@@ -1081,10 +1087,11 @@
             pieces=pieces,
             piece_count=len(weights),
             spread=spread,
+            spread_x=spread_x,
         ),
         grid=(count,),
         out_shape=(jax.ShapeDtypeStruct((mix_slots, rows, width), jnp.bfloat16),)
-        + (row_shape,) * slots
+        + row_shapes
         + grad_shapes,
         in_specs=[pl.BlockSpec(memory_space=pltpu.SMEM)]
         + [at_block((rows, width), index) for _, index in x_parts]
@@ -1093,7 +1100,7 @@
         + [pl.BlockSpec(memory_space=pl.ANY)] * len(weights)
         + grad_specs[: len(before)],
         out_specs=(pl.BlockSpec((mix_slots, rows, width), lambda expert: (0, 0, 0)),)
-        + (row_spec,) * slots
+        + row_specs
         + tuple(grad_specs),
         scratch_shapes=[
             pltpu.VMEM((total, width), jnp.bfloat16),
@@ -1125,11 +1132,91 @@
         *weights,
         *before,
     )
-    return outs[0], outs[1 : 1 + slots], outs[1 + slots :]
+    return outs[0], outs[1 : 1 + len(row_shapes)], outs[1 + len(row_shapes) :]
 
 
 def together(*values):
     return lax.optimization_barrier(values)
+
+
+def chosen_gates(x, w_route, chosen):
+    logits = jnp.where(chosen > 0.0, dot_f32(x, w_route, 1, 0), NEG)
+    raised = jnp.exp(logits - jnp.max(logits, 1, keepdims=True)) * chosen
+    return raised / jnp.sum(raised, 1, keepdims=True)
+
+
+def resid_back_kernel(*refs, counts):
+    ids_ref, resid_ref, normed_ref, dy_ref, gain_ref, w_route_ref, w_out_ref = refs[:7]
+    part_refs, refs = refs[7 : 7 + sum(counts)], refs[7 + sum(counts) :]
+    grad_resid_ref, grad_branch_ref, grad_att_ref, grad_logits_ref, grad_gain_ref = refs
+    micro_count, rows, width = dy_ref.shape[0], dy_ref.shape[1], resid_ref.shape[1]
+    columns = ids_ref.shape[0] // (2 * PLANE)
+    heads = w_out_ref.shape[1] // HEAD_DIM
+    lane = lax.broadcasted_iota(jnp.int32, (rows, LANES), 1)
+    gain = gain_ref[...]
+    grad_gain = jnp.zeros((1, width), jnp.float32)
+    for micro in range(micro_count):
+        here = slice(micro * rows, (micro + 1) * rows)
+        grad_normed = jnp.zeros((rows, width), jnp.float32)
+        grad_gates = jnp.zeros((rows, LANES), jnp.float32)
+        group = part_refs[sum(counts[:micro]) : sum(counts[: micro + 1])]
+        if counts[micro] == 2:
+            sources = [(group[1].at[place], PLANE + place) for place in range(PLANE)]
+            sources.append((group[0], 0))
+        else:
+            sources = [(part_ref, step) for step, part_ref in enumerate(group)]
+        for part_ref, step in sources:
+            grad_normed = grad_normed + part_ref[:, :width].astype(jnp.float32)
+            three = part_ref[:, width:].astype(jnp.float32)
+            for up in range(columns):
+                column = three[:, up : up + 1] + three[:, 8 + up : 9 + up]
+                column = column + three[:, 16 + up : 17 + up]
+                grad_gates = jnp.where(lane == ids_ref[step * columns + up], column, grad_gates)
+        chosen = dy_ref[micro, :, width:].astype(jnp.float32)
+        gates = chosen_gates(normed_ref[here, :], w_route_ref[...], chosen)
+        weighted = jnp.sum(gates * grad_gates, 1, keepdims=True)
+        grad_logits = (gates * (grad_gates - weighted)).astype(jnp.bfloat16)
+        grad_logits_ref[here, :] = grad_logits
+        grad_normed = grad_normed + dot_f32(grad_logits, w_route_ref[...], 1, 1)
+        resid = resid_ref[here, :]
+        scale = lax.rsqrt(jnp.mean(resid * resid, -1, keepdims=True) + EPS)
+        gained = grad_normed * gain
+        grad_gain = grad_gain + jnp.sum(grad_normed * resid * scale, 0, keepdims=True)
+        grad_resid = (
+            dy_ref[micro, :, :width].astype(jnp.float32)
+            + scale * gained
+            - resid * scale**3 * jnp.mean(resid * gained, -1, keepdims=True)
+        )
+        grad_resid_ref[here, :] = grad_resid
+        grad_branch = grad_resid.astype(jnp.bfloat16)
+        grad_branch_ref[here, :] = grad_branch
+        turned = dot_f32(grad_branch, w_out_ref[...], 1, 0).T
+        for head in range(heads):
+            grad_att_ref[micro * heads + head] = turned[
+                head * HEAD_DIM : (head + 1) * HEAD_DIM
+            ].astype(jnp.bfloat16)
+    grad_gain_ref[...] = jnp.broadcast_to(grad_gain, grad_gain_ref.shape)
+
+
+def resid_back(ids, resid, normed, dy, gain, w_route, w_out_t, parts):
+    total, width = resid.shape
+    rows = dy.shape[1]
+    heads = dy.shape[0] * w_out_t.shape[1] // HEAD_DIM
+    flat = [part for group in parts for part in group]
+    return pl.pallas_call(
+        functools.partial(resid_back_kernel, counts=tuple(len(group) for group in parts)),
+        out_shape=(
+            jax.ShapeDtypeStruct((total, width), jnp.float32),
+            jax.ShapeDtypeStruct((total, width), jnp.bfloat16),
+            jax.ShapeDtypeStruct((heads, HEAD_DIM, rows), jnp.bfloat16),
+            jax.ShapeDtypeStruct((total, LANES), jnp.bfloat16),
+            jax.ShapeDtypeStruct((8, width), jnp.float32),
+        ),
+        in_specs=[pl.BlockSpec(memory_space=pltpu.SMEM)] + [whole_vmem()] * (6 + len(flat)),
+        out_specs=(whole_vmem(),) * 5,
+        compiler_params=pltpu.CompilerParams(vmem_limit_bytes=48 * MIB),
+        name="resid_back",
+    )(ids, resid, normed, dy, gain, w_route, w_out_t, *flat)
 
 
 def flip(values, bits):
@@ -1286,23 +1373,6 @@
             [(first, 0, 0, 2), (first + 1, 1, 0, 2), (first + 2, 0, 2, 3), (first + 3, 1, 2, 3)]
         )
 
-    logits = jnp.dot(normed_two, w_route_full, preferred_element_type=jnp.float32)
-    route_rows = routes.reshape(all_rows, -1)
-    expert_ids = jnp.arange(experts_all, dtype=jnp.int32)
-    route_hot = (route_rows[:, :, None] == expert_ids[None, None, :]).astype(jnp.float32)
-    picked = jnp.sum(route_hot * logits[:, None, :], -1)
-    highest = jnp.max(picked, -1, keepdims=True)
-    raised = jnp.exp(picked - highest)
-    gates = raised / jnp.sum(raised, -1, keepdims=True)
-
-    slot_ids = jnp.stack(
-        [
-            jnp.stack([(level ^ up) * PLANE + (spot ^ step) for up in range(columns)])
-            for step in range(PLANE)
-        ]
-    )
-    slot_hot = (route_rows[None, None, :, :] == slot_ids[:, :, None, None]).astype(jnp.float32)
-
     spot_here = spot.astype(jnp.int32).reshape(1)
     column_ids = jnp.stack([(level ^ up) * PLANE + spot for up in range(columns)])
     place = jnp.concatenate([core, column_ids.astype(jnp.int32), spot_here])
@@ -1315,6 +1385,7 @@
         pieces,
         None,
         False,
+        False,
     )
     leaving = normed_parts[1:]
     leaving, own_mix = together(leaving, own_mix)
@@ -1336,78 +1407,53 @@
             pieces,
             before,
             True,
+            micro == micro_count - 1,
         )
         if micro:
-            grad_x, before, far_grad_x, far_mix = together(grad_x, before, far_grad_x, far_mix)
-        far_grad_x.append([flip(grad_x[step - 1], step) for step in range(1, PLANE)])
+            grad_x, before, far_grad_x = together(grad_x, before, far_grad_x)
         if micro < micro_count - 1:
-            far_mix.append(within_plane(mix))
-    last_mix = mix
+            far_grad_x.append([flip(grad_x[step - 1], step) for step in range(1, PLANE)])
+        else:
+            far_grad_x.append([within_plane(grad_x[0])])
+        far_mix.append(mix)
     keep_w, send_in_w, send_out_w = before
-    given_out = swap_cores(send_out_w)[:, 0]
-    out_w = keep_w[:, 2].astype(jnp.float32) + given_out.astype(jnp.float32)
-    near_out_w = flip(out_w[1::2].astype(jnp.bfloat16), PLANE)
-    far_grad_x[-1], near_out_w = together(far_grad_x[-1], near_out_w)
+    given_out = swap_cores(send_out_w)
+
+    def out_sum_of(slot):
+        return keep_w[slot, 2].astype(jnp.float32) + given_out[slot, 0].astype(jnp.float32)
+
+    near_out_w = jnp.stack([out_sum_of(slot).astype(jnp.bfloat16) for slot in (1, 3)])
+    near_out_w = flip(near_out_w, PLANE)
+    far_grad_x[-1], near_out_w, given_out = together(far_grad_x[-1], near_out_w, given_out)
     near_out_w = near_out_w.astype(jnp.float32)
 
-    def at_home(own_parts, far_parts):
-        return jnp.concatenate(
-            [
-                sum(part.astype(jnp.float32) for part in (own_parts[micro], *far_parts[micro]))
-                for micro in micros
-            ],
-            0,
-        )
-
-    grad_out = cotangent.reshape(all_rows, width).astype(jnp.float32)
-    home_grad_x = [
-        [own_grad_x[micro], *far_grad_x[micro]] for micro in micros
-    ]
-    slot_grads = jnp.concatenate(
+    plane_ids = jnp.stack(
         [
-            jnp.stack(
-                [
-                    sum(
-                        part[:, width + low : width + low + columns].astype(jnp.float32)
-                        for low in (0, 8, 16)
-                    ).T
-                    for part in parts
-                ]
-            )
-            for parts in home_grad_x
-        ],
-        2,
-    )
-    grad_gates = jnp.sum(slot_hot * slot_grads[:, :, :, None], (0, 1))
-    grad_spread = gates * (grad_gates - jnp.sum(gates * grad_gates, -1, keepdims=True))
-    grad_logits = jnp.sum(grad_spread[:, :, None] * route_hot, 1).astype(jnp.bfloat16)
-    grad_normed_two = jnp.concatenate(
-        [sum(part[:, :width].astype(jnp.float32) for part in parts) for parts in home_grad_x], 0
-    ) + dot_f32(grad_logits, w_route_full, 1, 1)
-    grad_route = dot_f32(normed_late, grad_logits, 0, 0)
-    gained_two = grad_normed_two * gain_two
-    grad_gain_two = jnp.sum(grad_normed_two * resid * scale_two, 0)
-    grad_resid = (
-        grad_out
-        + scale_two * gained_two
-        - resid * scale_two**3 * jnp.mean(resid * gained_two, -1, keepdims=True)
-    )
-    grad_branch = grad_resid.astype(jnp.bfloat16)
-    grad_att = jnp.concatenate(
-        [
-            dot_f32(w_out_t, grad_branch[micro * rows : (micro + 1) * rows], 0, 1).astype(
-                jnp.bfloat16
-            )
-            for micro in micros
-        ],
-        0,
-    ).reshape(devices, HEAD_DIM, rows)
+            (level ^ up) * PLANE + (spot ^ step)
+            for step in range(PLANE)
+            for up in range(columns)
+        ]
+        + [(level ^ up) * PLANE + place for place in range(PLANE) for up in range(columns)]
+    )
+    grad_resid, grad_branch, grad_att, grad_logits, grad_gain_two = resid_back(
+        plane_ids.astype(jnp.int32),
+        resid,
+        normed_two,
+        own_dy,
+        gain_two[None, :],
+        small_all,
+        w_out_t,
+        [[own_grad_x[micro], *far_grad_x[micro]] for micro in micros],
+    )
+    grad_route = dot_f32(normed_late, grad_logits, 0, 0)[:, :experts_all]
+    grad_gain_two = grad_gain_two[0]
     grad_outw = sum(
         dot_f32(grad_branch[micro * rows : (micro + 1) * rows], attended_t[micro], 0, 1)
         for micro in micros
     ).astype(jnp.bfloat16)
     grad_heads = every_device(grad_att)
-    far_out_w = (out_w[2] + near_out_w[1]).astype(jnp.bfloat16)
+    far_out_w = (out_sum_of(2) + near_out_w[1]).astype(jnp.bfloat16)
+    own_out_w = out_sum_of(0)
     given_in = swap_cores(send_in_w)
 
     def column_sum(slot):
@@ -1416,10 +1462,11 @@
 
     own_w = keep_w[0, :2].astype(jnp.float32) + given_in[0].astype(jnp.float32)
     near_in_w, far_in_w, last_in_w = column_sum(1), column_sum(2), column_sum(3)
-    grad_heads, near_in_w, last_in_w, far_in_w, far_out_w, own_w = together(
-        grad_heads, near_in_w, last_in_w, far_in_w, far_out_w, own_w
-    )
-    last_mix = within_plane(last_mix)
+    all_mix = jnp.concatenate(far_mix, 1)
+    grad_heads, near_in_w, last_in_w, far_in_w, far_out_w, own_w, all_mix = together(
+        grad_heads, near_in_w, last_in_w, far_in_w, far_out_w, own_w, all_mix
+    )
+    all_mix = within_plane(all_mix)
     near_in_w = flip(near_in_w, PLANE)
     last_in_w = flip(last_in_w, 3 * PLANE)
     far_in_w = flip(far_in_w, 2 * PLANE)
@@ -1449,10 +1496,9 @@
     grad_q, keep_kv, send_kv = attend_back(
         core, own, other, limit, out_f, log_total, grad_heads
     )
-    grad_q, keep_kv, send_kv, near_in_w, last_in_w, far_in_w, far_out_w, last_mix = together(
-        grad_q, keep_kv, send_kv, near_in_w, last_in_w, far_in_w, far_out_w, last_mix
-    )
-    far_mix.append(last_mix)
+    grad_q, keep_kv, send_kv, near_in_w, last_in_w, far_in_w, far_out_w, all_mix = together(
+        grad_q, keep_kv, send_kv, near_in_w, last_in_w, far_in_w, far_out_w, all_mix
+    )
     grad_kv = (keep_kv + swap_cores(send_kv).astype(jnp.float32)).astype(jnp.bfloat16)
     sent_back = jnp.concatenate([grad_q, grad_kv], 1)
     grad_own = every_device(sent_back)
@@ -1483,8 +1529,9 @@
         + sum(part[matrix].astype(jnp.float32) for part in (near_in_w, last_in_w, far_in_w))
         for matrix in range(2)
     ]
-    grad_w.append(out_w[0] + near_out_w[0] + far_out_w.astype(jnp.float32))
-    mixed = (resid + at_home(own_mix, far_mix)).astype(jnp.bfloat16)
+    grad_w.append(own_out_w + near_out_w[0] + far_out_w.astype(jnp.float32))
+    mixed = resid + own_mix.reshape(all_rows, width).astype(jnp.float32)
+    mixed = (mixed + jnp.sum(all_mix.astype(jnp.float32), 0)).astype(jnp.bfloat16)
 
     own_share = to_shards(kept, given)
     return (

time: 745 us -> 726 us (0.974)
  waiting for transfers between devices: 245 us -> 228 us
  Pallas kernels: 285 us -> 296 us
    ppermute x38 -> x35, waiting for transfers between devices: 109 us -> 80.9 us  [flip(): lax.ppermute(values, 'ep', [(index, index ^ bits) for index in range(coun...]
    all_to_all x2, waiting for transfers between devices: 0.01 us -> 19 us  [within_plane(): lax.all_to_all(parts, 'ep', 0, 0, tiled=True, axis_index_groups=plane_gro...]
    add x4 -> x0, other arithmetic: 12.7 us -> none  [the longest x1 5.02 us: on_device_paired(): out_w = keep_w[:, 2].astype(jnp.float32) + given_out.astype(jnp.float32)]
    pallas_call x0 -> x1, Pallas kernels: none -> 10.7 us  [resid_back(): pl.pallas_call(functools.partial(resid_back_kernel, counts=tuple((len(gro...]
    ppermute x38 -> x35, starting transfers between devices: 44 us -> 48.8 us  [flip(): lax.ppermute(values, 'ep', [(index, index ^ bits) for index in range(coun...]
    unnamed x112 -> x98, local copies, waits for them, and re-layouts: 17.8 us -> 15.7 us
  transfers between devices with their start and end apart: 62 -> 59, of which waited for: 28 -> 24; matrix products, arithmetic and copies ran while one was open for 9% -> 8% of each run, Pallas kernels for 37% -> 40%
where the time goes in v4:
time: 726 us; the launch traced here: 719 us
  Pallas kernels  296 us (41%)
  waiting for transfers between devices  228 us (31%)
  starting transfers between devices  92.6 us (13%)
  other arithmetic  54.2 us (7%)
  local copies, waits for them, and re-layouts  29.4 us (4%)
  between operations  15.6 us (2%)
    pallas_call x3, Pallas kernels, experts(): pl.pallas_call(functools.partial(experts_kernel, slots=slots, first_call=...  116 us
    pallas_call x1, Pallas kernels, attend_back(): pl.pallas_call(functools.partial(attend_back_kernel, query_block=query_bl...  100 us
    ppermute x35, waiting for transfers between devices, flip(): lax.ppermute(values, 'ep', [(index, index ^ bits) for index in range(coun...  80.9 us
    all_to_all x4, waiting for transfers between devices, every_device(): return lax.all_to_all(values, ('ep', 'tp'), 0, 0, tiled=True)  77.5 us
    pallas_call x1, Pallas kernels, attend(): pl.pallas_call(functools.partial(attend_kernel, query_block=query_block,...  51.5 us
    ppermute x35, starting transfers between devices, flip(): lax.ppermute(values, 'ep', [(index, index ^ bits) for index in range(coun...  48.8 us
    all_to_all x1, waiting for transfers between devices, to_shards(): lax.all_to_all(core_sum.astype(jnp.bfloat16).reshape(ep_count, shard, -1)...  37.3 us
    all_to_all x4, starting transfers between devices, every_device(): return lax.all_to_all(values, ('ep', 'tp'), 0, 0, tiled=True)  23.7 us
  transfers between devices with their start and end apart: 59, of which 24 were waited for; matrix products, arithmetic and copies ran while one was open for 8% of the time, Pallas kernels for 40%

profile of v4, /device:TPU:14, one launch (start us, length us, event | category | flops | bytes accessed | tf_op | source)
XLA Modules:
  0.0 718.6 jit_solution(639550326485535586)
XLA Ops:
  16.3 6.4 collective-permute-done.2
  25.2 2.4 collective-permute-start.5
  27.9 3.4 collective-permute-start.6
  31.3 19.6 %collective-permute-done.6.refs_15_.refs_17_ = bf16[1,512,512]{2,1,0:T(8,128)(2,1)} collective-permute-done((bf16[1,512,512]{2,1,0:T(8,128)(2,1)S(1)}, bf16[1,512,512]{2,1,0:T(8,128)(2,1)}, u32[]{:S(2)}, u32[]{:S(2)}) %collective-permute-start.6) | collective-permute-done | bytes 524320 | tf_op jit(solution)/shard_map/ppermute | solution.py:1224
  53.2 2.6 collective-permute-start.12
  57.9 5.9 project.1
  68.2 5.2 all-to-all-start
  73.7 2.9 fusion
  78.4 41.3 %all-to-all-done.own_ref = bf16[32,128,256]{2,1,0:T(8,128)(2,1)} async-done(((bf16[32,128,256]{2,1,0:T(8,128)(2,1)}), bf16[32,128,256]{2,1,0:T(8,128)(2,1)}, u32[]{:S(2)}, u32[]{:S(2)}) %all-to-all-start) | async-done | bytes 2097184 | tf_op jit(solution)/shard_map/all_to_all | solution.py:1232
  125.7 2.9 collective-permute-start.14
  132.6 51.5 %attend.1 = (bf16[32,64,256]{2,1,0:T(8,128)(2,1)}, f32[32,64,256]{2,1,0:T(8,128)}, f32[1,8192]{1,0:T(1,128)}) custom-call(s32[1]{0:T(128)} %bitcast.tp_ref, bf16[32,128,256]{2,1,0:T(8,128)(2,1)} %all-to-all-done.own_ref, bf16[32,64,256]{2,1,0:T(8,128)(2,1)} %copy-done.41, s32[1,8192]{1,0:T(1,128)} %iota_maximum_fusion.limit_ref), custom_call_target="tpu_custom_call" | custom-call | flops 34359738368 | bytes 8388608 | tf_op jit(solution)/shard_map/attend/pallas_call | solution.py:618
  185.2 5.8 all-to-all-start.1
  193.0 27.9 %all-to-all-done.1 = bf16[32,64,256]{2,1,0:T(8,128)(2,1)S(1)} async-done(((bf16[32,64,256]{2,1,0:T(8,128)(2,1)}), bf16[32,64,256]{2,1,0:T(8,128)(2,1)S(1)}, u32[]{:S(2)}, u32[]{:S(2)}) %all-to-all-start.1) | async-done | bytes 1048608 | tf_op jit(solution)/shard_map/all_to_all | solution.py:1232
  228.9 9.3 %collective-permute-done.23.refs_17_.refs_19_ = bf16[2,512,512]{2,1,0:T(8,128)(2,1)} collective-permute-done((bf16[2,512,512]{2,1,0:T(8,128)(2,1)}, bf16[2,512,512]{2,1,0:T(8,128)(2,1)}, u32[]{:S(2)}, u32[]{:S(2)}) %collective-permute-start.23) | collective-permute-done | bytes 1048608 | tf_op jit(solution)/shard_map/ppermute | solution.py:1224
  243.2 2.2 collective-permute-start.31
  245.5 28.7 %experts.3 = (bf16[2,256,1024]{2,1,0:T(8,128)(2,1)}, bf16[256,1152]{1,0:T(8,128)(2,1)}, bf16[256,1152]{1,0:T(8,128)(2,1)}, bf16[4,3,512,512]{3,2,1,0:T(8,128)(2,...) custom-call(s32[6]{0:T(128)} %concatenate.42.refs_0_, bf16[512,1024]{1,0:T(8,128)(2,1)} %copy-done.13, ...), custom_call_target="tpu_custom_call" | custom-call | flops 19327352832 | bytes 25165824 | tf_op jit(solution)/shard_map/experts/pallas_call | solution.py:1082
  278.5 43.4 %experts.4 = (bf16[4,256,1024]{2,1,0:T(8,128)(2,1)}, bf16[256,1152]{1,0:T(8,128)(2,1)}, bf16[256,1152]{1,0:T(8,128)(2,1)}, bf16[256,1152]{1,0:T(8,128)(2,1)}, bf...) custom-call(s32[6]{0:T(128)} %concatenate.42.refs_0_, ...), custom_call_target="tpu_custom_call" | custom-call | flops 28991029248 | bytes 25165824 | tf_op jit(solution)/shard_map/experts/pallas_call | solution.py:1082
  323.2 2.2 collective-permute-start.34
  325.4 43.9 %experts.5 = (bf16[4,256,1024]{2,1,0:T(8,128)(2,1)}, bf16[4,256,1152]{2,1,0:T(8,128)(2,1)}, bf16[4,3,512,512]{3,2,1,0:T(8,128)(2,1)}, bf16[4,2,512,512]{3,2,1,0:T(8,128)(2,1)}, bf16[4,1,512,512]{3,2,1,0:T(8,128)(2,1)}) custom-call(s32[6]{0:T(128)} %concatenate.42.refs_0_, bf16[256,1024]{1,0:T(8,128)(2,1)} %collective-permute-done.26.refs_1_, ...), custom_call_target="tpu_custom_call" | custom-call | flops 28991029248 | bytes 25165824 | tf_op jit(solution)/shard_map/experts/pallas_call | solution.py:1082
  370.2 5.4 all-to-all-start.2
  380.2 2.9 pad_maximum_fusion.1.refs_6_
  383.1 19.0 %all-to-all-done.2.refs_12_ = bf16[4,256,1152]{2,1,0:T(8,128)(2,1)} async-done(((bf16[4,256,1152]{2,1,0:T(8,128)(2,1)}), bf16[4,256,1152]{2,1,0:T(8,128)(2,1)}, u32[]{:S(2)}, u32[]{:S(2)}) %all-to-all-start.2) | async-done | bytes 2359328 | tf_op jit(solution)/shard_map/all_to_all | solution.py:1397
  404.5 10.7 %resid_back.1 = (f32[512,1024]{1,0:T(8,128)}, bf16[512,1024]{1,0:T(8,128)(2,1)S(1)}, bf16[32,64,256]{2,1,0:T(8,128)(2,1)}, bf16[512,128]{1,0:T(8,128)(2,1)S(1)}, f32[8,1024]{1,0:T(8,128)S(1)}) custom-call(s32[32]{0:T(128)S(1)} %stack.183.refs_0_, f32[512,1024]{1,0:T(8,128)} %get-tuple-element.253.refs_1_, bf16[512,1024]{1,0:T(8,128)(2,1)} %copy-done.13, ...), custom_call_target="tpu_custom_call" | custom-call | tf_op jit(solution)/shard_map/resid_back/pallas_call | solution.py:1206
  415.2 5.6 all-to-all-start.3
  420.8 4.9 pad_maximum_fusion
  425.7 2.8 convert_element_type.334
  428.5 2.5 fusion.8
  431.1 5.5 add_bitcast_fusion
  436.5 8.4 %all-to-all-done.3.grad_ref = bf16[32,64,256]{2,1,0:T(8,128)(2,1)S(1)} async-done(((bf16[32,64,256]{2,1,0:T(8,128)(2,1)}), bf16[32,64,256]{2,1,0:T(8,128)(2,1)S(1)}, u32[]{:S(2)}, u32[]{:S(2)}) %all-to-all-start.3) | async-done | bytes 1048608 | tf_op jit(solution)/shard_map/all_to_all | solution.py:1232
  444.9 2.4 collective-permute-start.38
  450.8 5.5 all-to-all-start.4
  456.3 100.1 %attend_back.1 = (bf16[32,64,256]{2,1,0:T(8,128)(2,1)}, f32[32,64,256]{2,1,0:T(8,128)}, bf16[32,64,256]{2,1,0:T(8,128)(2,1)}) custom-call(s32[1]{0:T(128)} %bitcast.tp_ref, bf16[32,128,256]{2,1,0:T(8,128)(2,1)} %all-to-all-done.own_ref, bf16[32,64,256]{2,1,0:T(8,128)(2,1)} %copy-done.41, s32[1,8192]{1,0:T(1,128)} %iota_maximum_fusion.limit_ref, ...), custom_call_target="tpu_custom_call" | custom-call | flops 68719476736 | bytes 12582912 | tf_op jit(solution)/shard_map/attend_back/pallas_call | solution.py:764
  556.3 4.1 collective-permute-done.41
  560.9 2.6 collective-permute-done.42
  567.2 7.1 all-to-all-start.5
  577.2 3.0 collective-permute-done.43
  586.7 18.9 %collective-permute-done.46 = bf16[4,64,640]{2,1,0:T(8,128)(2,1)S(1)} collective-permute-done((bf16[4,64,640]{2,1,0:T(8,128)(2,1)S(1)}, bf16[4,64,640]{2,1,0:T(8,128)(2,1)S(1)}, u32[]{:S(2)}, u32[]{:S(2)}) %collective-permute-start.46) | collective-permute-done | bytes 327712 | tf_op jit(solution)/shard_map/ppermute | solution.py:1224
  605.6 5.2 collective-permute-done.45
  611.5 6.1 collective-permute-start.48
  617.7 8.0 %collective-permute-done.48 = bf16[64,640]{1,0:T(8,128)(2,1)S(1)} collective-permute-done((bf16[64,640]{1,0:T(8,128)(2,1)S(1)}, bf16[64,640]{1,0:T(8,128)(2,1)S(1)}, u32[]{:S(2)}, u32[]{:S(2)}) %collective-permute-start.48) | collective-permute-done | bytes 81952 | tf_op jit(solution)/shard_map/ppermute | solution.py:1224
  625.7 3.1 collective-permute-done.49
  628.8 11.8 %project_back.1 = (f32[2,256,1024]{2,1,0:T(8,128)}, bf16[1024,1152]{1,0:T(8,128)(2,1)}, bf16[1024,1152]{1,0:T(8,128)(2,1)}) custom-call(s32[1]{0:T(128)} %bitcast.tp_ref, bf16[32,128,256]{2,1,0:T(8,128)(2,1)} %all-to-all-done.5.grad_ref, bf16[2,1024,1024]{2,1,0:T(8,128)(2,1)} %get-tuple-element.182.heads_ref, bf16[512,1024]{1,0:T(8,128)(2,1)} %copy-done.2, ...), custom_call_target="tpu_custom_call" | custom-call | tf_op jit(solution)/shard_map/project_back/pallas_call | solution.py:916
  640.6 4.7 collective-permute-done.50
  645.3 3.7 add_convert_fusion
  649.0 6.0 all-to-all-start.6
  655.1 3.6 convert_reduce_fusion
  667.3 4.3 add_add_fusion
  671.6 37.3 %all-to-all-done.6 = bf16[16,64,1152]{2,1,0:T(8,128)(2,1)S(1)} async-done(((bf16[16,64,1152]{2,1,0:T(8,128)(2,1)}), bf16[16,64,1152]{2,1,0:T(8,128)(2,1)S(1)}, u32[]{:S(2)}, u32[]{:S(2)}) %all-to-all-start.6) | async-done | bytes 2359328 | tf_op jit(solution)/shard_map/all_to_all | solution.py:1477
  (250 shorter events, 90.4 us)
Async XLA Ops:
  9.7 12.9 %collective-permute-start.2 = (bf16[64,1152]{1,0:T(8,128)(2,1)S(1)}, bf16[64,1152]{1,0:T(8,128)(2,1)S(1)}, u32[]{:S(2)}, u32[]{:S(2)}) collective-permute-start(bf16[64,1152]{1,0:T(8,128)(2,1)S(1)} %get-tuple-element.281), channel_id=1, source_target_pairs={{0,24},{2,26},{4,28},{6,30},{8,16},{10,18},{12,20},{14,22},{16,8},... | collective-permute-start | bytes 442376 | tf_op jit(solution)/shard_map/ppermute | solution.py:1224
  11.4 12.6 %collective-permute-start.1 = (bf16[64,1152]{1,0:T(8,128)(2,1)S(1)}, bf16[64,1152]{1,0:T(8,128)(2,1)S(1)}, u32[]{:S(2)}, u32[]{:S(2)}) collective-permute-start(bf16[64,1152]{1,0:T(8,128)(2,1)S(1)} %get-tuple-element.281), channel_id=1, source_target_pairs={{0,16},{2,18},{4,20},{6,22},{8,24},{10,26},{12,28},{14,30},{16,0},... | collective-permute-start | bytes 442376 | tf_op jit(solution)/shard_map/ppermute | solution.py:1224
  12.6 11.4 %collective-permute-start = (bf16[64,1152]{1,0:T(8,128)(2,1)S(1)}, bf16[64,1152]{1,0:T(8,128)(2,1)S(1)}, u32[]{:S(2)}, u32[]{:S(2)}) collective-permute-start(bf16[64,1152]{1,0:T(8,128)(2,1)S(1)} %get-tuple-element.281), channel_id=1, source_target_pairs={{0,8},{2,10},{4,12},{6,14},{8,0},{10,2},{12,4},{14,6},{16,24},{18,... | collective-permute-start | bytes 442376 | tf_op jit(solution)/shard_map/ppermute | solution.py:1224
  24.1 28.0 %collective-permute-start.3 = (bf16[4,64,1152]{2,1,0:T(8,128)(2,1)S(1)}, bf16[4,64,1152]{2,1,0:T(8,128)(2,1)S(1)}, u32[]{:S(2)}, u32[]{:S(2)}) collective-permute-start(bf16[4,64,1152]{2,1,0:T(8,128)(2,1)S(1)} %pad_maximum_fusion.9.refs_4_), channel_id=1, source_target_pairs={{0,2},{2,0},{4,6},{6,4},{8,10},{10,8},{12,14},{14,12},{16,18},{18,... | collective-permute-start | bytes 1769480 | tf_op jit(solution)/shard_map/ppermute | solution.py:1224
  24.7 27.4 %collective-permute-start.4 = (bf16[4,64,1152]{2,1,0:T(8,128)(2,1)S(1)}, bf16[4,64,1152]{2,1,0:T(8,128)(2,1)S(1)}, u32[]{:S(2)}, u32[]{:S(2)}) collective-permute-start(bf16[4,64,1152]{2,1,0:T(8,128)(2,1)S(1)} %pad_maximum_fusion.9.refs_4_), channel_id=1, source_target_pairs={{0,4},{2,6},{4,0},{6,2},{8,12},{10,14},{12,8},{14,10},{16,20},{18,... | collective-permute-start | bytes 1769480 | tf_op jit(solution)/shard_map/ppermute | solution.py:1224
  25.2 26.9 %collective-permute-start.5 = (bf16[4,64,1152]{2,1,0:T(8,128)(2,1)S(1)}, bf16[4,64,1152]{2,1,0:T(8,128)(2,1)S(1)}, u32[]{:S(2)}, u32[]{:S(2)}) collective-permute-start(bf16[4,64,1152]{2,1,0:T(8,128)(2,1)S(1)} %pad_maximum_fusion.9.refs_4_), channel_id=1, source_target_pairs={{0,6},{2,4},{4,2},{6,0},{8,14},{10,12},{12,10},{14,8},{16,22},{18,... | collective-permute-start | bytes 1769480 | tf_op jit(solution)/shard_map/ppermute | solution.py:1224
  27.9 23.1 %collective-permute-start.6 = (bf16[1,512,512]{2,1,0:T(8,128)(2,1)S(1)}, bf16[1,512,512]{2,1,0:T(8,128)(2,1)}, u32[]{:S(2)}, u32[]{:S(2)}) collective-permute-start(bf16[1,512,512]{2,1,0:T(8,128)(2,1)S(1)} %slice.164), channel_id=1, source_target_pairs={{0,16},{2,18},{4,20},{6,22},{8,24},{10,26},{12,28},{14,30},{16,0},... | collective-permute-start | bytes 1572872 | tf_op jit(solution)/shard_map/ppermute | solution.py:1224
  31.3 20.7 %collective-permute-start.7 = (bf16[1,512,512]{2,1,0:T(8,128)(2,1)S(1)}, bf16[1,512,512]{2,1,0:T(8,128)(2,1)}, u32[]{:S(2)}, u32[]{:S(2)}) collective-permute-start(bf16[1,512,512]{2,1,0:T(8,128)(2,1)S(1)} %slice.164), channel_id=1, source_target_pairs={{0,8},{2,10},{4,12},{6,14},{8,0},{10,2},{12,4},{14,6},{16,24},{18,... | collective-permute-start | bytes 1572872 | tf_op jit(solution)/shard_map/ppermute | solution.py:1224
  53.2 15.0 %collective-permute-start.12 = (bf16[1,512,512]{2,1,0:T(8,128)(2,1)}, bf16[1,512,512]{2,1,0:T(8,128)(2,1)}, u32[]{:S(2)}, u32[]{:S(2)}) collective-permute-start(bf16[1,512,512]{2,1,0:T(8,128)(2,1)} %collective-permute-done.6.refs_15_.refs_17_), channel_id=1, source_target_pairs={{0,8},{2,10},{4,12},{6,14},{8,0},{10,2},{12,4},{14,6},{16,24},{18,... | collective-permute-start | bytes 1572872 | tf_op jit(solution)/shard_map/ppermute | solution.py:1224
  68.2 51.5 %all-to-all-start = ((bf16[32,128,256]{2,1,0:T(8,128)(2,1)}), bf16[32,128,256]{2,1,0:T(8,128)(2,1)}, u32[]{:S(2)}, u32[]{:S(2)}) async-start(bf16[32,128,256]{2,1,0:T(8,128)(2,1)} %get-tuple-element.114), calls=%async_computation | async-start | bytes 4194304 | tf_op jit(solution)/shard_map/all_to_all | solution.py:1232
  73.5 147.5 %all-gather.3.cloned.1.call-start = ((), (), s32[]{:S(2)}) async-start(), calls=%async_computation.7 | async-start | bytes 2162688 | tf_op jit(solution)/shard_map/all_gather | solution.py:1340
  125.7 58.4 %collective-permute-start.14 = (bf16[2,512,512]{2,1,0:T(8,128)(2,1)}, bf16[2,512,512]{2,1,0:T(8,128)(2,1)}, u32[]{:S(2)}, u32[]{:S(2)}) collective-permute-start(bf16[2,512,512]{2,1,0:T(8,128)(2,1)} %slice.166), channel_id=1, source_target_pairs={{0,8},{2,10},{4,12},{6,14},{8,0},{10,2},{12,4},{14,6},{16,24},{18,... | collective-permute-start | bytes 3145736 | tf_op jit(solution)/shard_map/ppermute | solution.py:1224
  128.6 55.5 %collective-permute-start.15 = (bf16[2,512,512]{2,1,0:T(8,128)(2,1)}, bf16[2,512,512]{2,1,0:T(8,128)(2,1)}, u32[]{:S(2)}, u32[]{:S(2)}) collective-permute-start(bf16[2,512,512]{2,1,0:T(8,128)(2,1)} %slice.166), channel_id=1, source_target_pairs={{0,16},{2,18},{4,20},{6,22},{8,24},{10,26},{12,28},{14,30},{16,0},... | collective-permute-start | bytes 3145736 | tf_op jit(solution)/shard_map/ppermute | solution.py:1224
  129.1 55.0 %collective-permute-start.16 = (bf16[2,256,1152]{2,1,0:T(8,128)(2,1)S(1)}, bf16[2,256,1152]{2,1,0:T(8,128)(2,1)S(1)}, u32[]{:S(2)}, u32[]{:S(2)}) collective-permute-start(bf16[2,256,1152]{2,1,0:T(8,128)(2,1)S(1)} %pad_maximum_fusion.7.refs_3_.refs_4_), channel_id=1, source_target_pairs={{0,2},{2,0},{4,6},{6,4},{8,10},{10,8},{12,14},{14,12},{16,18},{18,... | collective-permute-start | bytes 3538952 | tf_op jit(solution)/shard_map/ppermute | solution.py:1224
  129.1 55.0 %collective-permute-start.17 = (bf16[2,256,1152]{2,1,0:T(8,128)(2,1)S(1)}, bf16[2,256,1152]{2,1,0:T(8,128)(2,1)}, u32[]{:S(2)}, u32[]{:S(2)}) collective-permute-start(bf16[2,256,1152]{2,1,0:T(8,128)(2,1)S(1)} %pad_maximum_fusion.7.refs_3_.refs_4_), channel_id=1, source_target_pairs={{0,4},{2,6},{4,0},{6,2},{8,12},{10,14},{12,8},{14,10},{16,20},{18,... | collective-permute-start | bytes 3538952 | tf_op jit(solution)/shard_map/ppermute | solution.py:1224
  130.7 53.5 %collective-permute-start.18 = (bf16[2,256,1152]{2,1,0:T(8,128)(2,1)S(1)}, bf16[2,256,1152]{2,1,0:T(8,128)(2,1)}, u32[]{:S(2)}, u32[]{:S(2)}) collective-permute-start(bf16[2,256,1152]{2,1,0:T(8,128)(2,1)S(1)} %pad_maximum_fusion.7.refs_3_.refs_4_), channel_id=1, source_target_pairs={{0,6},{2,4},{4,2},{6,0},{8,14},{10,12},{12,10},{14,8},{16,22},{18,... | collective-permute-start | bytes 3538952 | tf_op jit(solution)/shard_map/ppermute | solution.py:1224
  185.2 35.7 %all-to-all-start.1 = ((bf16[32,64,256]{2,1,0:T(8,128)(2,1)}), bf16[32,64,256]{2,1,0:T(8,128)(2,1)S(1)}, u32[]{:S(2)}, u32[]{:S(2)}) async-start(bf16[32,64,256]{2,1,0:T(8,128)(2,1)} %get-tuple-element.119), calls=%async_computation.1 | async-start | bytes 2097152 | tf_op jit(solution)/shard_map/all_to_all | solution.py:1232
  190.9 47.8 %collective-permute-start.20 = (bf16[1,512,512]{2,1,0:T(8,128)(2,1)}, bf16[1,512,512]{2,1,0:T(8,128)(2,1)}, u32[]{:S(2)}, u32[]{:S(2)}) collective-permute-start(bf16[1,512,512]{2,1,0:T(8,128)(2,1)} %collective-permute-done.7.refs_11_.refs_13_), channel_id=1, source_target_pairs={{0,1},{1,0},{2,3},{3,2},{4,5},{5,4},{6,7},{7,6},{8,9},{9,8},{10,11... | collective-permute-start | bytes 1572872 | tf_op jit(solution)/shard_map/ppermute | solution.py:1228
  192.1 53.4 %collective-permute-start.21 = (bf16[2,512,512]{2,1,0:T(8,128)(2,1)}, bf16[2,512,512]{2,1,0:T(8,128)(2,1)}, u32[]{:S(2)}, u32[]{:S(2)}) collective-permute-start(bf16[2,512,512]{2,1,0:T(8,128)(2,1)} %collective-permute-done.15.refs_13_.refs_15_), channel_id=1, source_target_pairs={{0,1},{1,0},{2,3},{3,2},{4,5},{5,4},{6,7},{7,6},{8,9},{9,8},{10,11... | collective-permute-start | bytes 3145736 | tf_op jit(solution)/shard_map/ppermute | solution.py:1228
  192.4 45.8 %collective-permute-start.23 = (bf16[2,512,512]{2,1,0:T(8,128)(2,1)}, bf16[2,512,512]{2,1,0:T(8,128)(2,1)}, u32[]{:S(2)}, u32[]{:S(2)}) collective-permute-start(bf16[2,512,512]{2,1,0:T(8,128)(2,1)} %collective-permute-done.15.refs_13_.refs_15_), channel_id=1, source_target_pairs={{0,8},{2,10},{4,12},{6,14},{8,0},{10,2},{12,4},{14,6},{16,24},{18,... | collective-permute-start | bytes 3145736 | tf_op jit(solution)/shard_map/ppermute | solution.py:1224
  193.0 50.2 %collective-permute-start.19 = (bf16[2,512,512]{2,1,0:T(8,128)(2,1)}, bf16[2,512,512]{2,1,0:T(8,128)(2,1)}, u32[]{:S(2)}, u32[]{:S(2)}) collective-permute-start(bf16[2,512,512]{2,1,0:T(8,128)(2,1)} %collective-permute-done.14.refs_9_.refs_11_), channel_id=1, source_target_pairs={{0,1},{1,0},{2,3},{3,2},{4,5},{5,4},{6,7},{7,6},{8,9},{9,8},{10,11... | collective-permute-start | bytes 3145736 | tf_op jit(solution)/shard_map/ppermute | solution.py:1228
  238.2 7.3 %collective-permute-start.24 = (bf16[2,512,512]{2,1,0:T(8,128)(2,1)}, bf16[2,512,512]{2,1,0:T(8,128)(2,1)}, u32[]{:S(2)}, u32[]{:S(2)}) collective-permute-start(bf16[2,512,512]{2,1,0:T(8,128)(2,1)} %collective-permute-done.23.refs_17_.refs_19_), channel_id=1, source_target_pairs={{0,1},{1,0},{2,3},{3,2},{4,5},{5,4},{6,7},{7,6},{8,9},{9,8},{10,11... | collective-permute-start | bytes 3145736 | tf_op jit(solution)/shard_map/ppermute | solution.py:1228
  241.9 33.5 %collective-permute-start.29 = (bf16[256,1024]{1,0:T(8,128)(2,1)S(1)}, bf16[256,1024]{1,0:T(8,128)(2,1)S(1)}, u32[]{:S(2)}, u32[]{:S(2)}) collective-permute-start(bf16[256,1024]{1,0:T(8,128)(2,1)S(1)} %get-tuple-element.271), channel_id=1, source_target_pairs={{0,2},{2,0},{4,6},{6,4},{8,10},{10,8},{12,14},{14,12},{16,18},{18,... | collective-permute-start | bytes 1572872 | tf_op jit(solution)/shard_map/ppermute | solution.py:1224
  242.7 35.0 %collective-permute-start.30 = (bf16[256,1024]{1,0:T(8,128)(2,1)S(1)}, bf16[256,1024]{1,0:T(8,128)(2,1)S(1)}, u32[]{:S(2)}, u32[]{:S(2)}) collective-permute-start(bf16[256,1024]{1,0:T(8,128)(2,1)S(1)} %get-tuple-element.271), channel_id=1, source_target_pairs={{0,4},{2,6},{4,0},{6,2},{8,12},{10,14},{12,8},{14,10},{16,20},{18,... | collective-permute-start | bytes 1572872 | tf_op jit(solution)/shard_map/ppermute | solution.py:1224
  243.2 34.5 %collective-permute-start.31 = (bf16[256,1024]{1,0:T(8,128)(2,1)S(1)}, bf16[256,1024]{1,0:T(8,128)(2,1)}, u32[]{:S(2)}, u32[]{:S(2)}) collective-permute-start(bf16[256,1024]{1,0:T(8,128)(2,1)S(1)} %get-tuple-element.271), channel_id=1, source_target_pairs={{0,6},{2,4},{4,2},{6,0},{8,14},{10,12},{12,10},{14,8},{16,22},{18,... | collective-permute-start | bytes 1572872 | tf_op jit(solution)/shard_map/ppermute | solution.py:1224
  274.1 49.0 %collective-permute-start.26 = (bf16[256,1024]{1,0:T(8,128)(2,1)}, bf16[256,1024]{1,0:T(8,128)(2,1)}, u32[]{:S(2)}, u32[]{:S(2)}) collective-permute-start(bf16[256,1024]{1,0:T(8,128)(2,1)} %get-tuple-element.133), channel_id=1, source_target_pairs={{0,2},{2,0},{4,6},{6,4},{8,10},{10,8},{12,14},{14,12},{16,18},{18,... | collective-permute-start | bytes 1572872 | tf_op jit(solution)/shard_map/ppermute | solution.py:1224
  274.9 50.5 %collective-permute-start.27 = (bf16[256,1024]{1,0:T(8,128)(2,1)}, bf16[256,1024]{1,0:T(8,128)(2,1)}, u32[]{:S(2)}, u32[]{:S(2)}) collective-permute-start(bf16[256,1024]{1,0:T(8,128)(2,1)} %get-tuple-element.133), channel_id=1, source_target_pairs={{0,4},{2,6},{4,0},{6,2},{8,12},{10,14},{12,8},{14,10},{16,20},{18,... | collective-permute-start | bytes 1572872 | tf_op jit(solution)/shard_map/ppermute | solution.py:1224
  275.5 49.9 %collective-permute-start.28 = (bf16[256,1024]{1,0:T(8,128)(2,1)}, bf16[256,1024]{1,0:T(8,128)(2,1)}, u32[]{:S(2)}, u32[]{:S(2)}) collective-permute-start(bf16[256,1024]{1,0:T(8,128)(2,1)} %get-tuple-element.133), channel_id=1, source_target_pairs={{0,6},{2,4},{4,2},{6,0},{8,14},{10,12},{12,10},{14,8},{16,22},{18,... | collective-permute-start | bytes 1572872 | tf_op jit(solution)/shard_map/ppermute | solution.py:1224
  321.8 47.5 %collective-permute-start.32 = (bf16[256,1152]{1,0:T(8,128)(2,1)}, bf16[256,1152]{1,0:T(8,128)(2,1)S(1)}, u32[]{:S(2)}, u32[]{:S(2)}) collective-permute-start(bf16[256,1152]{1,0:T(8,128)(2,1)} %get-tuple-element.147), channel_id=1, source_target_pairs={{0,2},{2,0},{4,6},{6,4},{8,10},{10,8},{12,14},{14,12},{16,18},{18,... | collective-permute-start | bytes 1769480 | tf_op jit(solution)/shard_map/ppermute | solution.py:1224
  322.6 46.6 %collective-permute-start.33 = (bf16[256,1152]{1,0:T(8,128)(2,1)}, bf16[256,1152]{1,0:T(8,128)(2,1)S(1)}, u32[]{:S(2)}, u32[]{:S(2)}) collective-permute-start(bf16[256,1152]{1,0:T(8,128)(2,1)} %get-tuple-element.148), channel_id=1, source_target_pairs={{0,4},{2,6},{4,0},{6,2},{8,12},{10,14},{12,8},{14,10},{16,20},{18,... | collective-permute-start | bytes 1769480 | tf_op jit(solution)/shard_map/ppermute | solution.py:1224
  323.2 46.2 %collective-permute-start.34 = (bf16[256,1152]{1,0:T(8,128)(2,1)}, bf16[256,1152]{1,0:T(8,128)(2,1)}, u32[]{:S(2)}, u32[]{:S(2)}) collective-permute-start(bf16[256,1152]{1,0:T(8,128)(2,1)} %get-tuple-element.149), channel_id=1, source_target_pairs={{0,6},{2,4},{4,2},{6,0},{8,14},{10,12},{12,10},{14,8},{16,22},{18,... | collective-permute-start | bytes 1769480 | tf_op jit(solution)/shard_map/ppermute | solution.py:1224
  369.4 61.6 %collective-permute-start.37 = (bf16[4,2,512,512]{3,2,1,0:T(8,128)(2,1)}, bf16[4,2,512,512]{3,2,1,0:T(8,128)(2,1)}, u32[]{:S(2)}, u32[]{:S(2)}) collective-permute-start(bf16[4,2,512,512]{3,2,1,0:T(8,128)(2,1)} %get-tuple-element.159), channel_id=1, source_target_pairs={{0,1},{1,0},{2,3},{3,2},{4,5},{5,4},{6,7},{7,6},{8,9},{9,8},{10,11... | collective-permute-start | bytes 12582920 | tf_op jit(solution)/shard_map/ppermute | solution.py:1228
  370.2 31.9 %all-to-all-start.2 = ((bf16[4,256,1152]{2,1,0:T(8,128)(2,1)}), bf16[4,256,1152]{2,1,0:T(8,128)(2,1)}, u32[]{:S(2)}, u32[]{:S(2)}) async-start(bf16[4,256,1152]{2,1,0:T(8,128)(2,1)} %get-tuple-element.154), calls=%async_computation.2 | async-start | bytes 4718592 | tf_op jit(solution)/shard_map/all_to_all | solution.py:1397
  378.5 24.9 %collective-permute-start.36 = (bf16[2,512,512]{2,1,0:T(8,128)(2,1)}, bf16[2,512,512]{2,1,0:T(8,128)(2,1)}, u32[]{:S(2)}, u32[]{:S(2)}) collective-permute-start(bf16[2,512,512]{2,1,0:T(8,128)(2,1)} %pad_maximum_fusion.8), channel_id=1, source_target_pairs={{0,8},{2,10},{4,12},{6,14},{8,0},{10,2},{12,4},{14,6},{16,24},{18,... | collective-permute-start | bytes 3145736 | tf_op jit(solution)/shard_map/ppermute | solution.py:1224
  415.2 29.7 %all-to-all-start.3 = ((bf16[32,64,256]{2,1,0:T(8,128)(2,1)}), bf16[32,64,256]{2,1,0:T(8,128)(2,1)S(1)}, u32[]{:S(2)}, u32[]{:S(2)}) async-start(bf16[32,64,256]{2,1,0:T(8,128)(2,1)} %get-tuple-element.158), calls=%async_computation.3 | async-start | bytes 2097152 | tf_op jit(solution)/shard_map/all_to_all | solution.py:1232
  444.9 115.5 %collective-permute-start.38 = (bf16[2,512,512]{2,1,0:T(8,128)(2,1)}, bf16[2,512,512]{2,1,0:T(8,128)(2,1)}, u32[]{:S(2)}, u32[]{:S(2)}) collective-permute-start(bf16[2,512,512]{2,1,0:T(8,128)(2,1)} %get-tuple-element.168), channel_id=1, source_target_pairs={{0,8},{2,10},{4,12},{6,14},{8,0},{10,2},{12,4},{14,6},{16,24},{18,... | collective-permute-start | bytes 3145736 | tf_op jit(solution)/shard_map/ppermute | solution.py:1224
  447.3 113.1 %collective-permute-start.39 = (bf16[2,512,512]{2,1,0:T(8,128)(2,1)}, bf16[2,512,512]{2,1,0:T(8,128)(2,1)}, u32[]{:S(2)}, u32[]{:S(2)}) collective-permute-start(bf16[2,512,512]{2,1,0:T(8,128)(2,1)} %get-tuple-element.169), channel_id=1, source_target_pairs={{0,24},{2,26},{4,28},{6,30},{8,16},{10,18},{12,20},{14,22},{16,8},... | collective-permute-start | bytes 3145736 | tf_op jit(solution)/shard_map/ppermute | solution.py:1224
  447.8 112.6 %collective-permute-start.40 = (bf16[2,512,512]{2,1,0:T(8,128)(2,1)}, bf16[2,512,512]{2,1,0:T(8,128)(2,1)}, u32[]{:S(2)}, u32[]{:S(2)}) collective-permute-start(bf16[2,512,512]{2,1,0:T(8,128)(2,1)} %get-tuple-element.170), channel_id=1, source_target_pairs={{0,16},{2,18},{4,20},{6,22},{8,24},{10,26},{12,28},{14,30},{16,0},... | collective-permute-start | bytes 3145736 | tf_op jit(solution)/shard_map/ppermute | solution.py:1224
  449.7 110.7 %collective-permute-start.41 = (bf16[512,512]{1,0:T(8,128)(2,1)}, bf16[512,512]{1,0:T(8,128)(2,1)S(1)}, u32[]{:S(2)}, u32[]{:S(2)}) collective-permute-start(bf16[512,512]{1,0:T(8,128)(2,1)} %fusion.8), channel_id=1, source_target_pairs={{0,16},{2,18},{4,20},{6,22},{8,24},{10,26},{12,28},{14,30},{16,0},... | collective-permute-start | bytes 1572872 | tf_op jit(solution)/shard_map/ppermute | solution.py:1224
  450.8 109.7 %all-to-all-start.4 = ((bf16[4,512,1024]{2,1,0:T(8,128)(2,1)}), bf16[4,512,1024]{2,1,0:T(8,128)(2,1)}, u32[]{:S(2)}, u32[]{:S(2)}) async-start(bf16[4,512,1024]{2,1,0:T(8,128)(2,1)} %pad_maximum_fusion), calls=%async_computation.4 | async-start | bytes 8388608 | tf_op jit(solution)/shard_map/all_to_all | solution.py:1397
  567.2 61.6 %all-to-all-start.5 = ((bf16[32,128,256]{2,1,0:T(8,128)(2,1)}), bf16[32,128,256]{2,1,0:T(8,128)(2,1)}, u32[]{:S(2)}, u32[]{:S(2)}) async-start(bf16[32,128,256]{2,1,0:T(8,128)(2,1)} %pad_maximum_fusion.3), calls=%async_computation.5 | async-start | bytes 4194304 | tf_op jit(solution)/shard_map/all_to_all | solution.py:1232
  583.2 22.5 %collective-permute-start.46 = (bf16[4,64,640]{2,1,0:T(8,128)(2,1)S(1)}, bf16[4,64,640]{2,1,0:T(8,128)(2,1)S(1)}, u32[]{:S(2)}, u32[]{:S(2)}) collective-permute-start(bf16[4,64,640]{2,1,0:T(8,128)(2,1)S(1)} %get-tuple-element.269), channel_id=1, source_target_pairs={{0,6},{2,4},{4,2},{6,0},{8,14},{10,12},{12,10},{14,8},{16,22},{18,... | collective-permute-start | bytes 983048 | tf_op jit(solution)/shard_map/ppermute | solution.py:1224
  583.8 27.0 %collective-permute-start.45 = (bf16[4,64,640]{2,1,0:T(8,128)(2,1)S(1)}, bf16[4,64,640]{2,1,0:T(8,128)(2,1)S(1)}, u32[]{:S(2)}, u32[]{:S(2)}) collective-permute-start(bf16[4,64,640]{2,1,0:T(8,128)(2,1)S(1)} %get-tuple-element.270), channel_id=1, source_target_pairs={{0,4},{2,6},{4,0},{6,2},{8,12},{10,14},{12,8},{14,10},{16,20},{18,... | collective-permute-start | bytes 983048 | tf_op jit(solution)/shard_map/ppermute | solution.py:1224
  585.3 25.8 %collective-permute-start.44 = (bf16[4,64,640]{2,1,0:T(8,128)(2,1)S(1)}, bf16[4,64,640]{2,1,0:T(8,128)(2,1)S(1)}, u32[]{:S(2)}, u32[]{:S(2)}) collective-permute-start(bf16[4,64,640]{2,1,0:T(8,128)(2,1)S(1)} %get-tuple-element.268), channel_id=1, source_target_pairs={{0,2},{2,0},{4,6},{6,4},{8,10},{10,8},{12,14},{14,12},{16,18},{18,... | collective-permute-start | bytes 983048 | tf_op jit(solution)/shard_map/ppermute | solution.py:1224
  611.3 6.4 collective-permute-start.47
  611.5 14.2 %collective-permute-start.48 = (bf16[64,640]{1,0:T(8,128)(2,1)S(1)}, bf16[64,640]{1,0:T(8,128)(2,1)S(1)}, u32[]{:S(2)}, u32[]{:S(2)}) collective-permute-start(bf16[64,640]{1,0:T(8,128)(2,1)S(1)} %get-tuple-element.276), channel_id=1, source_target_pairs={{0,16},{2,18},{4,20},{6,22},{8,24},{10,26},{12,28},{14,30},{16,0},... | collective-permute-start | bytes 245768 | tf_op jit(solution)/shard_map/ppermute | solution.py:1224
  617.6 11.1 %collective-permute-start.49 = (bf16[64,640]{1,0:T(8,128)(2,1)S(1)}, bf16[64,640]{1,0:T(8,128)(2,1)S(1)}, u32[]{:S(2)}, u32[]{:S(2)}) collective-permute-start(bf16[64,640]{1,0:T(8,128)(2,1)S(1)} %get-tuple-element.275), channel_id=1, source_target_pairs={{0,24},{2,26},{4,28},{6,30},{8,16},{10,18},{12,20},{14,22},{16,8},... | collective-permute-start | bytes 245768 | tf_op jit(solution)/shard_map/ppermute | solution.py:1224
  649.0 59.9 %all-to-all-start.6 = ((bf16[16,64,1152]{2,1,0:T(8,128)(2,1)}), bf16[16,64,1152]{2,1,0:T(8,128)(2,1)S(1)}, u32[]{:S(2)}, u32[]{:S(2)}) async-start(bf16[16,64,1152]{2,1,0:T(8,128)(2,1)} %bitcast.75), calls=%async_computation.6 | async-start | bytes 4718592 | tf_op jit(solution)/shard_map/all_to_all | solution.py:1477
  (58 other events, 618.0 us)
Sparse Core Ops, SparseCore 0:
  132.7 84.9 all-gather.2

commit v5 on v4

--- a/solution.py
+++ b/solution.py
@@ -1321,7 +1321,6 @@
     normed, sent, w_heads, small_all = project(
         spot_here, tokens, cosine, sine, mine, other, devices
     )
-    w_route_full = small_all[:, :experts_all]
     gain_one = small_all[:, LANES // 2].astype(jnp.float32)
     gain_two = small_all[:, LANES // 2 + 1].astype(jnp.float32)
     nearfar_out = flip(far_out, PLANE)
@@ -1331,12 +1330,15 @@
 
     chosen = jnp.any(routes[:, :, :, None] == lanes, 2).astype(jnp.bfloat16)
     own_dy = jnp.concatenate([cotangent, chosen], 2)
-    w_output_t, expert_late, far_out, dy_late, other = together(
-        w_output.T, expert_half, far_out, own_dy, other
+    early_dy, small_all = together(own_dy, small_all)
+    plane_dy = [flip(early_dy, step) for step in range(1, PLANE - 1)]
+    other, plane_dy = together(other, plane_dy)
+    w_output_t, expert_late, dy_late, other = together(
+        w_output.T, expert_half, own_dy, other
     )
     far_in = flip(expert_late[:2], 2 * PLANE)
     near_in = flip(expert_late[:2], PLANE)
-    plane_dy = [flip(dy_late, step) for step in range(1, PLANE)]
+    plane_dy = plane_dy + [flip(dy_late, PLANE - 1)]
     gathered_out = lax.all_gather(w_output_t, ("ep", "tp"), axis=0, tiled=False)
 
     micro_here = ep_index // (ep_count // micro_count)

time: 726 us -> 724 us (level)
  transfers between devices with their start and end apart: 59 -> 59, of which waited for: 24 -> 25; matrix products, arithmetic and copies ran while one was open for 8% -> 9% of each run, Pallas kernels for 40% -> 40%
where the time goes in v5:
time: 724 us; the launch traced here: 716 us
  Pallas kernels  295 us (41%)
  waiting for transfers between devices  227 us (31%)
  starting transfers between devices  91.5 us (13%)
  other arithmetic  54.2 us (7%)
  local copies, waits for them, and re-layouts  29.5 us (4%)
  between operations  15.3 us (2%)
    pallas_call x3, Pallas kernels, experts(): pl.pallas_call(functools.partial(experts_kernel, slots=slots, first_call=...  116 us
    pallas_call x1, Pallas kernels, attend_back(): pl.pallas_call(functools.partial(attend_back_kernel, query_block=query_bl...  100 us
    ppermute x35, waiting for transfers between devices, flip(): lax.ppermute(values, 'ep', [(index, index ^ bits) for index in range(coun...  81.5 us
    all_to_all x4, waiting for transfers between devices, every_device(): return lax.all_to_all(values, ('ep', 'tp'), 0, 0, tiled=True)  77.3 us
    pallas_call x1, Pallas kernels, attend(): pl.pallas_call(functools.partial(attend_kernel, query_block=query_block,...  51.2 us
    ppermute x35, starting transfers between devices, flip(): lax.ppermute(values, 'ep', [(index, index ^ bits) for index in range(coun...  47.5 us
    all_to_all x1, waiting for transfers between devices, to_shards(): lax.all_to_all(core_sum.astype(jnp.bfloat16).reshape(ep_count, shard, -1)...  37.3 us
    all_to_all x4, starting transfers between devices, every_device(): return lax.all_to_all(values, ('ep', 'tp'), 0, 0, tiled=True)  23.8 us
  transfers between devices with their start and end apart: 59, of which 25 were waited for; matrix products, arithmetic and copies ran while one was open for 9% of the time, Pallas kernels for 40%

profile of v5, /device:TPU:14, one launch (start us, length us, event | category | flops | bytes accessed | tf_op | source)
XLA Modules:
  0.0 716.1 jit_solution(12237834887779289418)
XLA Ops:
  16.3 6.4 collective-permute-done.2
  25.2 2.4 collective-permute-start.5
  27.9 3.4 collective-permute-start.6
  31.3 19.6 %collective-permute-done.6.refs_15_.refs_17_ = bf16[1,512,512]{2,1,0:T(8,128)(2,1)} collective-permute-done((bf16[1,512,512]{2,1,0:T(8,128)(2,1)S(1)}, bf16[1,512,512]{2,1,0:T(8,128)(2,1)}, u32[]{:S(2)}, u32[]{:S(2)}) %collective-permute-start.6) | collective-permute-done | bytes 524320 | tf_op jit(solution)/shard_map/ppermute | solution.py:1224
  53.2 2.6 collective-permute-start.12
  57.9 5.9 project.1
  68.2 5.2 all-to-all-start
  73.7 2.9 fusion
  79.6 40.1 %all-to-all-done.own_ref = bf16[32,128,256]{2,1,0:T(8,128)(2,1)} async-done(((bf16[32,128,256]{2,1,0:T(8,128)(2,1)}), bf16[32,128,256]{2,1,0:T(8,128)(2,1)}, u32[]{:S(2)}, u32[]{:S(2)}) %all-to-all-start) | async-done | bytes 2097184 | tf_op jit(solution)/shard_map/all_to_all | solution.py:1232
  125.8 2.9 collective-permute-start.16
  130.2 51.2 %attend.1 = (bf16[32,64,256]{2,1,0:T(8,128)(2,1)}, f32[32,64,256]{2,1,0:T(8,128)}, f32[1,8192]{1,0:T(1,128)}) custom-call(s32[1]{0:T(128)} %bitcast.tp_ref, bf16[32,128,256]{2,1,0:T(8,128)(2,1)} %all-to-all-done.own_ref, bf16[32,64,256]{2,1,0:T(8,128)(2,1)} %copy-done.41, s32[1,8192]{1,0:T(1,128)} %iota_maximum_fusion.limit_ref), custom_call_target="tpu_custom_call" | custom-call | flops 34359738368 | bytes 8388608 | tf_op jit(solution)/shard_map/attend/pallas_call | solution.py:618
  182.4 5.7 all-to-all-start.1
  190.1 28.8 %all-to-all-done.1 = bf16[32,64,256]{2,1,0:T(8,128)(2,1)S(1)} async-done(((bf16[32,64,256]{2,1,0:T(8,128)(2,1)}), bf16[32,64,256]{2,1,0:T(8,128)(2,1)S(1)}, u32[]{:S(2)}, u32[]{:S(2)}) %all-to-all-start.1) | async-done | bytes 1048608 | tf_op jit(solution)/shard_map/all_to_all | solution.py:1232
  226.9 9.0 %collective-permute-done.23.refs_17_.refs_19_ = bf16[2,512,512]{2,1,0:T(8,128)(2,1)} collective-permute-done((bf16[2,512,512]{2,1,0:T(8,128)(2,1)}, bf16[2,512,512]{2,1,0:T(8,128)(2,1)}, u32[]{:S(2)}, u32[]{:S(2)}) %collective-permute-start.23) | collective-permute-done | bytes 1048608 | tf_op jit(solution)/shard_map/ppermute | solution.py:1224
  240.9 2.3 collective-permute-start.31
  243.2 28.7 %experts.3 = (bf16[2,256,1024]{2,1,0:T(8,128)(2,1)}, bf16[256,1152]{1,0:T(8,128)(2,1)}, bf16[256,1152]{1,0:T(8,128)(2,1)}, bf16[4,3,512,512]{3,2,1,0:T(8,128)(2,...) custom-call(s32[6]{0:T(128)} %concatenate.42.refs_0_, bf16[512,1024]{1,0:T(8,128)(2,1)} %copy-done.13, ...), custom_call_target="tpu_custom_call" | custom-call | flops 19327352832 | bytes 25165824 | tf_op jit(solution)/shard_map/experts/pallas_call | solution.py:1082
  273.1 2.3 collective-permute-start.28
  276.2 43.5 %experts.4 = (bf16[4,256,1024]{2,1,0:T(8,128)(2,1)}, bf16[256,1152]{1,0:T(8,128)(2,1)}, bf16[256,1152]{1,0:T(8,128)(2,1)}, bf16[256,1152]{1,0:T(8,128)(2,1)}, bf...) custom-call(s32[6]{0:T(128)} %concatenate.42.refs_0_, ...), custom_call_target="tpu_custom_call" | custom-call | flops 28991029248 | bytes 25165824 | tf_op jit(solution)/shard_map/experts/pallas_call | solution.py:1082
  323.3 43.7 %experts.5 = (bf16[4,256,1024]{2,1,0:T(8,128)(2,1)}, bf16[4,256,1152]{2,1,0:T(8,128)(2,1)}, bf16[4,3,512,512]{3,2,1,0:T(8,128)(2,1)}, bf16[4,2,512,512]{3,2,1,0:T(8,128)(2,1)}, bf16[4,1,512,512]{3,2,1,0:T(8,128)(2,1)}) custom-call(s32[6]{0:T(128)} %concatenate.42.refs_0_, bf16[256,1024]{1,0:T(8,128)(2,1)} %collective-permute-done.26.refs_1_, ...), custom_call_target="tpu_custom_call" | custom-call | flops 28991029248 | bytes 25165824 | tf_op jit(solution)/shard_map/experts/pallas_call | solution.py:1082
  367.9 5.4 all-to-all-start.2
  377.9 2.9 pad_maximum_fusion.1.refs_6_
  380.8 18.9 %all-to-all-done.2.refs_12_ = bf16[4,256,1152]{2,1,0:T(8,128)(2,1)} async-done(((bf16[4,256,1152]{2,1,0:T(8,128)(2,1)}), bf16[4,256,1152]{2,1,0:T(8,128)(2,1)}, u32[]{:S(2)}, u32[]{:S(2)}) %all-to-all-start.2) | async-done | bytes 2359328 | tf_op jit(solution)/shard_map/all_to_all | solution.py:1399
  402.2 10.7 %resid_back.1 = (f32[512,1024]{1,0:T(8,128)}, bf16[512,1024]{1,0:T(8,128)(2,1)S(1)}, bf16[32,64,256]{2,1,0:T(8,128)(2,1)}, bf16[512,128]{1,0:T(8,128)(2,1)S(1)}, f32[8,1024]{1,0:T(8,128)S(1)}) custom-call(s32[32]{0:T(128)S(1)} %stack.183.refs_0_, f32[512,1024]{1,0:T(8,128)} %get-tuple-element.261.refs_1_, bf16[512,1024]{1,0:T(8,128)(2,1)} %copy-done.13, ...), custom_call_target="tpu_custom_call" | custom-call | tf_op jit(solution)/shard_map/resid_back/pallas_call | solution.py:1206
  412.9 5.8 all-to-all-start.3
  418.7 4.9 pad_maximum_fusion
  423.6 2.8 convert_element_type.334
  426.4 2.5 fusion.8
  429.0 5.5 add_bitcast_fusion
  434.4 8.4 %all-to-all-done.3.grad_ref = bf16[32,64,256]{2,1,0:T(8,128)(2,1)S(1)} async-done(((bf16[32,64,256]{2,1,0:T(8,128)(2,1)}), bf16[32,64,256]{2,1,0:T(8,128)(2,1)S(1)}, u32[]{:S(2)}, u32[]{:S(2)}) %all-to-all-start.3) | async-done | bytes 1048608 | tf_op jit(solution)/shard_map/all_to_all | solution.py:1232
  442.8 2.4 collective-permute-start.38
  448.7 5.7 all-to-all-start.4
  454.4 100.1 %attend_back.1 = (bf16[32,64,256]{2,1,0:T(8,128)(2,1)}, f32[32,64,256]{2,1,0:T(8,128)}, bf16[32,64,256]{2,1,0:T(8,128)(2,1)}) custom-call(s32[1]{0:T(128)} %bitcast.tp_ref, bf16[32,128,256]{2,1,0:T(8,128)(2,1)} %all-to-all-done.own_ref, bf16[32,64,256]{2,1,0:T(8,128)(2,1)} %copy-done.41, s32[1,8192]{1,0:T(1,128)} %iota_maximum_fusion.limit_ref, ...), custom_call_target="tpu_custom_call" | custom-call | flops 68719476736 | bytes 12582912 | tf_op jit(solution)/shard_map/attend_back/pallas_call | solution.py:764
  554.5 3.9 collective-permute-done.41
  558.8 2.6 collective-permute-done.42
  565.2 7.1 all-to-all-start.5
  575.0 3.0 collective-permute-done.43
  584.6 18.9 %collective-permute-done.46 = bf16[4,64,640]{2,1,0:T(8,128)(2,1)S(1)} collective-permute-done((bf16[4,64,640]{2,1,0:T(8,128)(2,1)S(1)}, bf16[4,64,640]{2,1,0:T(8,128)(2,1)S(1)}, u32[]{:S(2)}, u32[]{:S(2)}) %collective-permute-start.46) | collective-permute-done | bytes 327712 | tf_op jit(solution)/shard_map/ppermute | solution.py:1224
  603.5 5.2 collective-permute-done.45
  609.4 6.1 collective-permute-start.48
  615.5 8.0 %collective-permute-done.48 = bf16[64,640]{1,0:T(8,128)(2,1)S(1)} collective-permute-done((bf16[64,640]{1,0:T(8,128)(2,1)S(1)}, bf16[64,640]{1,0:T(8,128)(2,1)S(1)}, u32[]{:S(2)}, u32[]{:S(2)}) %collective-permute-start.48) | collective-permute-done | bytes 81952 | tf_op jit(solution)/shard_map/ppermute | solution.py:1224
  623.5 3.1 collective-permute-done.49
  626.6 11.8 %project_back.1 = (f32[2,256,1024]{2,1,0:T(8,128)}, bf16[1024,1152]{1,0:T(8,128)(2,1)}, bf16[1024,1152]{1,0:T(8,128)(2,1)}) custom-call(s32[1]{0:T(128)} %bitcast.tp_ref, bf16[32,128,256]{2,1,0:T(8,128)(2,1)} %all-to-all-done.5.grad_ref, bf16[2,1024,1024]{2,1,0:T(8,128)(2,1)} %get-tuple-element.190.heads_ref, bf16[512,1024]{1,0:T(8,128)(2,1)} %copy-done.2, ...), custom_call_target="tpu_custom_call" | custom-call | tf_op jit(solution)/shard_map/project_back/pallas_call | solution.py:916
  638.4 4.7 collective-permute-done.50
  643.2 3.7 add_convert_fusion
  646.9 6.0 all-to-all-start.6
  652.9 3.6 convert_reduce_fusion
  665.1 4.3 add_add_fusion
  669.4 37.3 %all-to-all-done.6 = bf16[16,64,1152]{2,1,0:T(8,128)(2,1)S(1)} async-done(((bf16[16,64,1152]{2,1,0:T(8,128)(2,1)}), bf16[16,64,1152]{2,1,0:T(8,128)(2,1)S(1)}, u32[]{:S(2)}, u32[]{:S(2)}) %all-to-all-start.6) | async-done | bytes 2359328 | tf_op jit(solution)/shard_map/all_to_all | solution.py:1479
  (250 shorter events, 89.1 us)
Async XLA Ops:
  9.7 12.9 %collective-permute-start.2 = (bf16[64,1152]{1,0:T(8,128)(2,1)S(1)}, bf16[64,1152]{1,0:T(8,128)(2,1)S(1)}, u32[]{:S(2)}, u32[]{:S(2)}) collective-permute-start(bf16[64,1152]{1,0:T(8,128)(2,1)S(1)} %get-tuple-element.289), channel_id=1, source_target_pairs={{0,24},{2,26},{4,28},{6,30},{8,16},{10,18},{12,20},{14,22},{16,8},... | collective-permute-start | bytes 442376 | tf_op jit(solution)/shard_map/ppermute | solution.py:1224
  11.4 12.6 %collective-permute-start.1 = (bf16[64,1152]{1,0:T(8,128)(2,1)S(1)}, bf16[64,1152]{1,0:T(8,128)(2,1)S(1)}, u32[]{:S(2)}, u32[]{:S(2)}) collective-permute-start(bf16[64,1152]{1,0:T(8,128)(2,1)S(1)} %get-tuple-element.289), channel_id=1, source_target_pairs={{0,16},{2,18},{4,20},{6,22},{8,24},{10,26},{12,28},{14,30},{16,0},... | collective-permute-start | bytes 442376 | tf_op jit(solution)/shard_map/ppermute | solution.py:1224
  12.6 11.4 %collective-permute-start = (bf16[64,1152]{1,0:T(8,128)(2,1)S(1)}, bf16[64,1152]{1,0:T(8,128)(2,1)S(1)}, u32[]{:S(2)}, u32[]{:S(2)}) collective-permute-start(bf16[64,1152]{1,0:T(8,128)(2,1)S(1)} %get-tuple-element.289), channel_id=1, source_target_pairs={{0,8},{2,10},{4,12},{6,14},{8,0},{10,2},{12,4},{14,6},{16,24},{18,... | collective-permute-start | bytes 442376 | tf_op jit(solution)/shard_map/ppermute | solution.py:1224
  24.1 28.0 %collective-permute-start.3 = (bf16[4,64,1152]{2,1,0:T(8,128)(2,1)S(1)}, bf16[4,64,1152]{2,1,0:T(8,128)(2,1)S(1)}, u32[]{:S(2)}, u32[]{:S(2)}) collective-permute-start(bf16[4,64,1152]{2,1,0:T(8,128)(2,1)S(1)} %pad_maximum_fusion.9.refs_4_), channel_id=1, source_target_pairs={{0,2},{2,0},{4,6},{6,4},{8,10},{10,8},{12,14},{14,12},{16,18},{18,... | collective-permute-start | bytes 1769480 | tf_op jit(solution)/shard_map/ppermute | solution.py:1224
  24.7 27.4 %collective-permute-start.4 = (bf16[4,64,1152]{2,1,0:T(8,128)(2,1)S(1)}, bf16[4,64,1152]{2,1,0:T(8,128)(2,1)S(1)}, u32[]{:S(2)}, u32[]{:S(2)}) collective-permute-start(bf16[4,64,1152]{2,1,0:T(8,128)(2,1)S(1)} %pad_maximum_fusion.9.refs_4_), channel_id=1, source_target_pairs={{0,4},{2,6},{4,0},{6,2},{8,12},{10,14},{12,8},{14,10},{16,20},{18,... | collective-permute-start | bytes 1769480 | tf_op jit(solution)/shard_map/ppermute | solution.py:1224
  25.2 26.9 %collective-permute-start.5 = (bf16[4,64,1152]{2,1,0:T(8,128)(2,1)S(1)}, bf16[4,64,1152]{2,1,0:T(8,128)(2,1)S(1)}, u32[]{:S(2)}, u32[]{:S(2)}) collective-permute-start(bf16[4,64,1152]{2,1,0:T(8,128)(2,1)S(1)} %pad_maximum_fusion.9.refs_4_), channel_id=1, source_target_pairs={{0,6},{2,4},{4,2},{6,0},{8,14},{10,12},{12,10},{14,8},{16,22},{18,... | collective-permute-start | bytes 1769480 | tf_op jit(solution)/shard_map/ppermute | solution.py:1224
  27.9 23.1 %collective-permute-start.6 = (bf16[1,512,512]{2,1,0:T(8,128)(2,1)S(1)}, bf16[1,512,512]{2,1,0:T(8,128)(2,1)}, u32[]{:S(2)}, u32[]{:S(2)}) collective-permute-start(bf16[1,512,512]{2,1,0:T(8,128)(2,1)S(1)} %slice.164), channel_id=1, source_target_pairs={{0,16},{2,18},{4,20},{6,22},{8,24},{10,26},{12,28},{14,30},{16,0},... | collective-permute-start | bytes 1572872 | tf_op jit(solution)/shard_map/ppermute | solution.py:1224
  31.3 20.7 %collective-permute-start.7 = (bf16[1,512,512]{2,1,0:T(8,128)(2,1)S(1)}, bf16[1,512,512]{2,1,0:T(8,128)(2,1)}, u32[]{:S(2)}, u32[]{:S(2)}) collective-permute-start(bf16[1,512,512]{2,1,0:T(8,128)(2,1)S(1)} %slice.164), channel_id=1, source_target_pairs={{0,8},{2,10},{4,12},{6,14},{8,0},{10,2},{12,4},{14,6},{16,24},{18,... | collective-permute-start | bytes 1572872 | tf_op jit(solution)/shard_map/ppermute | solution.py:1224
  53.2 15.0 %collective-permute-start.12 = (bf16[1,512,512]{2,1,0:T(8,128)(2,1)}, bf16[1,512,512]{2,1,0:T(8,128)(2,1)}, u32[]{:S(2)}, u32[]{:S(2)}) collective-permute-start(bf16[1,512,512]{2,1,0:T(8,128)(2,1)} %collective-permute-done.6.refs_15_.refs_17_), channel_id=1, source_target_pairs={{0,8},{2,10},{4,12},{6,14},{8,0},{10,2},{12,4},{14,6},{16,24},{18,... | collective-permute-start | bytes 1572872 | tf_op jit(solution)/shard_map/ppermute | solution.py:1224
  68.2 51.5 %all-to-all-start = ((bf16[32,128,256]{2,1,0:T(8,128)(2,1)}), bf16[32,128,256]{2,1,0:T(8,128)(2,1)}, u32[]{:S(2)}, u32[]{:S(2)}) async-start(bf16[32,128,256]{2,1,0:T(8,128)(2,1)} %get-tuple-element.118), calls=%async_computation | async-start | bytes 4194304 | tf_op jit(solution)/shard_map/all_to_all | solution.py:1232
  73.5 145.5 %all-gather.3.cloned.1.call-start = ((), (), s32[]{:S(2)}) async-start(), calls=%async_computation.7 | async-start | bytes 2162688 | tf_op jit(solution)/shard_map/all_gather | solution.py:1342
  78.4 44.5 %collective-permute-start.14 = (bf16[2,256,1152]{2,1,0:T(8,128)(2,1)S(1)}, bf16[2,256,1152]{2,1,0:T(8,128)(2,1)}, u32[]{:S(2)}, u32[]{:S(2)}) collective-permute-start(bf16[2,256,1152]{2,1,0:T(8,128)(2,1)S(1)} %pad_maximum_fusion.7.refs_3_.refs_4_), channel_id=1, source_target_pairs={{0,2},{2,0},{4,6},{6,4},{8,10},{10,8},{12,14},{14,12},{16,18},{18,... | collective-permute-start | bytes 3538952 | tf_op jit(solution)/shard_map/ppermute | solution.py:1224
  79.0 43.9 %collective-permute-start.15 = (bf16[2,256,1152]{2,1,0:T(8,128)(2,1)S(1)}, bf16[2,256,1152]{2,1,0:T(8,128)(2,1)}, u32[]{:S(2)}, u32[]{:S(2)}) collective-permute-start(bf16[2,256,1152]{2,1,0:T(8,128)(2,1)S(1)} %pad_maximum_fusion.7.refs_3_.refs_4_), channel_id=1, source_target_pairs={{0,4},{2,6},{4,0},{6,2},{8,12},{10,14},{12,8},{14,10},{16,20},{18,... | collective-permute-start | bytes 3538952 | tf_op jit(solution)/shard_map/ppermute | solution.py:1224
  125.8 55.6 %collective-permute-start.16 = (bf16[2,512,512]{2,1,0:T(8,128)(2,1)}, bf16[2,512,512]{2,1,0:T(8,128)(2,1)}, u32[]{:S(2)}, u32[]{:S(2)}) collective-permute-start(bf16[2,512,512]{2,1,0:T(8,128)(2,1)} %slice.166), channel_id=1, source_target_pairs={{0,8},{2,10},{4,12},{6,14},{8,0},{10,2},{12,4},{14,6},{16,24},{18,... | collective-permute-start | bytes 3145736 | tf_op jit(solution)/shard_map/ppermute | solution.py:1224
  128.7 52.7 %collective-permute-start.17 = (bf16[2,512,512]{2,1,0:T(8,128)(2,1)}, bf16[2,512,512]{2,1,0:T(8,128)(2,1)}, u32[]{:S(2)}, u32[]{:S(2)}) collective-permute-start(bf16[2,512,512]{2,1,0:T(8,128)(2,1)} %slice.166), channel_id=1, source_target_pairs={{0,16},{2,18},{4,20},{6,22},{8,24},{10,26},{12,28},{14,30},{16,0},... | collective-permute-start | bytes 3145736 | tf_op jit(solution)/shard_map/ppermute | solution.py:1224
  129.1 52.3 %collective-permute-start.18 = (bf16[2,256,1152]{2,1,0:T(8,128)(2,1)S(1)}, bf16[2,256,1152]{2,1,0:T(8,128)(2,1)S(1)}, u32[]{:S(2)}, u32[]{:S(2)}) collective-permute-start(bf16[2,256,1152]{2,1,0:T(8,128)(2,1)S(1)} %pad_maximum_fusion.7.refs_3_.refs_4_), channel_id=1, source_target_pairs={{0,6},{2,4},{4,2},{6,0},{8,14},{10,12},{12,10},{14,8},{16,22},{18,... | collective-permute-start | bytes 3538952 | tf_op jit(solution)/shard_map/ppermute | solution.py:1224
  182.4 36.4 %all-to-all-start.1 = ((bf16[32,64,256]{2,1,0:T(8,128)(2,1)}), bf16[32,64,256]{2,1,0:T(8,128)(2,1)S(1)}, u32[]{:S(2)}, u32[]{:S(2)}) async-start(bf16[32,64,256]{2,1,0:T(8,128)(2,1)} %get-tuple-element.128), calls=%async_computation.1 | async-start | bytes 2097152 | tf_op jit(solution)/shard_map/all_to_all | solution.py:1232
  188.1 48.3 %collective-permute-start.20 = (bf16[1,512,512]{2,1,0:T(8,128)(2,1)}, bf16[1,512,512]{2,1,0:T(8,128)(2,1)}, u32[]{:S(2)}, u32[]{:S(2)}) collective-permute-start(bf16[1,512,512]{2,1,0:T(8,128)(2,1)} %collective-permute-done.7.refs_11_.refs_13_), channel_id=1, source_target_pairs={{0,1},{1,0},{2,3},{3,2},{4,5},{5,4},{6,7},{7,6},{8,9},{9,8},{10,11... | collective-permute-start | bytes 1572872 | tf_op jit(solution)/shard_map/ppermute | solution.py:1228
  189.3 53.9 %collective-permute-start.21 = (bf16[2,512,512]{2,1,0:T(8,128)(2,1)}, bf16[2,512,512]{2,1,0:T(8,128)(2,1)}, u32[]{:S(2)}, u32[]{:S(2)}) collective-permute-start(bf16[2,512,512]{2,1,0:T(8,128)(2,1)} %collective-permute-done.17.refs_13_.refs_15_), channel_id=1, source_target_pairs={{0,1},{1,0},{2,3},{3,2},{4,5},{5,4},{6,7},{7,6},{8,9},{9,8},{10,11... | collective-permute-start | bytes 3145736 | tf_op jit(solution)/shard_map/ppermute | solution.py:1228
  189.6 46.3 %collective-permute-start.23 = (bf16[2,512,512]{2,1,0:T(8,128)(2,1)}, bf16[2,512,512]{2,1,0:T(8,128)(2,1)}, u32[]{:S(2)}, u32[]{:S(2)}) collective-permute-start(bf16[2,512,512]{2,1,0:T(8,128)(2,1)} %collective-permute-done.17.refs_13_.refs_15_), channel_id=1, source_target_pairs={{0,8},{2,10},{4,12},{6,14},{8,0},{10,2},{12,4},{14,6},{16,24},{18,... | collective-permute-start | bytes 3145736 | tf_op jit(solution)/shard_map/ppermute | solution.py:1224
  190.1 50.8 %collective-permute-start.19 = (bf16[2,512,512]{2,1,0:T(8,128)(2,1)}, bf16[2,512,512]{2,1,0:T(8,128)(2,1)}, u32[]{:S(2)}, u32[]{:S(2)}) collective-permute-start(bf16[2,512,512]{2,1,0:T(8,128)(2,1)} %collective-permute-done.16.refs_9_.refs_11_), channel_id=1, source_target_pairs={{0,1},{1,0},{2,3},{3,2},{4,5},{5,4},{6,7},{7,6},{8,9},{9,8},{10,11... | collective-permute-start | bytes 3145736 | tf_op jit(solution)/shard_map/ppermute | solution.py:1228
  235.9 7.3 %collective-permute-start.24 = (bf16[2,512,512]{2,1,0:T(8,128)(2,1)}, bf16[2,512,512]{2,1,0:T(8,128)(2,1)}, u32[]{:S(2)}, u32[]{:S(2)}) collective-permute-start(bf16[2,512,512]{2,1,0:T(8,128)(2,1)} %collective-permute-done.23.refs_17_.refs_19_), channel_id=1, source_target_pairs={{0,1},{1,0},{2,3},{3,2},{4,5},{5,4},{6,7},{7,6},{8,9},{9,8},{10,11... | collective-permute-start | bytes 3145736 | tf_op jit(solution)/shard_map/ppermute | solution.py:1228
  239.7 33.5 %collective-permute-start.29 = (bf16[256,1024]{1,0:T(8,128)(2,1)S(1)}, bf16[256,1024]{1,0:T(8,128)(2,1)S(1)}, u32[]{:S(2)}, u32[]{:S(2)}) collective-permute-start(bf16[256,1024]{1,0:T(8,128)(2,1)S(1)} %get-tuple-element.279), channel_id=1, source_target_pairs={{0,2},{2,0},{4,6},{6,4},{8,10},{10,8},{12,14},{14,12},{16,18},{18,... | collective-permute-start | bytes 1572872 | tf_op jit(solution)/shard_map/ppermute | solution.py:1224
  240.4 35.0 %collective-permute-start.30 = (bf16[256,1024]{1,0:T(8,128)(2,1)S(1)}, bf16[256,1024]{1,0:T(8,128)(2,1)S(1)}, u32[]{:S(2)}, u32[]{:S(2)}) collective-permute-start(bf16[256,1024]{1,0:T(8,128)(2,1)S(1)} %get-tuple-element.279), channel_id=1, source_target_pairs={{0,4},{2,6},{4,0},{6,2},{8,12},{10,14},{12,8},{14,10},{16,20},{18,... | collective-permute-start | bytes 1572872 | tf_op jit(solution)/shard_map/ppermute | solution.py:1224
  240.9 34.5 %collective-permute-start.31 = (bf16[256,1024]{1,0:T(8,128)(2,1)S(1)}, bf16[256,1024]{1,0:T(8,128)(2,1)}, u32[]{:S(2)}, u32[]{:S(2)}) collective-permute-start(bf16[256,1024]{1,0:T(8,128)(2,1)S(1)} %get-tuple-element.279), channel_id=1, source_target_pairs={{0,6},{2,4},{4,2},{6,0},{8,14},{10,12},{12,10},{14,8},{16,22},{18,... | collective-permute-start | bytes 1572872 | tf_op jit(solution)/shard_map/ppermute | solution.py:1224
  271.8 49.2 %collective-permute-start.26 = (bf16[256,1024]{1,0:T(8,128)(2,1)}, bf16[256,1024]{1,0:T(8,128)(2,1)}, u32[]{:S(2)}, u32[]{:S(2)}) collective-permute-start(bf16[256,1024]{1,0:T(8,128)(2,1)} %get-tuple-element.141), channel_id=1, source_target_pairs={{0,2},{2,0},{4,6},{6,4},{8,10},{10,8},{12,14},{14,12},{16,18},{18,... | collective-permute-start | bytes 1572872 | tf_op jit(solution)/shard_map/ppermute | solution.py:1224
  272.6 50.7 %collective-permute-start.27 = (bf16[256,1024]{1,0:T(8,128)(2,1)}, bf16[256,1024]{1,0:T(8,128)(2,1)}, u32[]{:S(2)}, u32[]{:S(2)}) collective-permute-start(bf16[256,1024]{1,0:T(8,128)(2,1)} %get-tuple-element.141), channel_id=1, source_target_pairs={{0,4},{2,6},{4,0},{6,2},{8,12},{10,14},{12,8},{14,10},{16,20},{18,... | collective-permute-start | bytes 1572872 | tf_op jit(solution)/shard_map/ppermute | solution.py:1224
  273.1 50.2 %collective-permute-start.28 = (bf16[256,1024]{1,0:T(8,128)(2,1)}, bf16[256,1024]{1,0:T(8,128)(2,1)}, u32[]{:S(2)}, u32[]{:S(2)}) collective-permute-start(bf16[256,1024]{1,0:T(8,128)(2,1)} %get-tuple-element.141), channel_id=1, source_target_pairs={{0,6},{2,4},{4,2},{6,0},{8,14},{10,12},{12,10},{14,8},{16,22},{18,... | collective-permute-start | bytes 1572872 | tf_op jit(solution)/shard_map/ppermute | solution.py:1224
  319.7 47.2 %collective-permute-start.32 = (bf16[256,1152]{1,0:T(8,128)(2,1)}, bf16[256,1152]{1,0:T(8,128)(2,1)S(1)}, u32[]{:S(2)}, u32[]{:S(2)}) collective-permute-start(bf16[256,1152]{1,0:T(8,128)(2,1)} %get-tuple-element.155), channel_id=1, source_target_pairs={{0,2},{2,0},{4,6},{6,4},{8,10},{10,8},{12,14},{14,12},{16,18},{18,... | collective-permute-start | bytes 1769480 | tf_op jit(solution)/shard_map/ppermute | solution.py:1224
  320.6 46.4 %collective-permute-start.33 = (bf16[256,1152]{1,0:T(8,128)(2,1)}, bf16[256,1152]{1,0:T(8,128)(2,1)S(1)}, u32[]{:S(2)}, u32[]{:S(2)}) collective-permute-start(bf16[256,1152]{1,0:T(8,128)(2,1)} %get-tuple-element.156), channel_id=1, source_target_pairs={{0,4},{2,6},{4,0},{6,2},{8,12},{10,14},{12,8},{14,10},{16,20},{18,... | collective-permute-start | bytes 1769480 | tf_op jit(solution)/shard_map/ppermute | solution.py:1224
  321.0 46.0 %collective-permute-start.34 = (bf16[256,1152]{1,0:T(8,128)(2,1)}, bf16[256,1152]{1,0:T(8,128)(2,1)}, u32[]{:S(2)}, u32[]{:S(2)}) collective-permute-start(bf16[256,1152]{1,0:T(8,128)(2,1)} %get-tuple-element.157), channel_id=1, source_target_pairs={{0,6},{2,4},{4,2},{6,0},{8,14},{10,12},{12,10},{14,8},{16,22},{18,... | collective-permute-start | bytes 1769480 | tf_op jit(solution)/shard_map/ppermute | solution.py:1224
  367.1 61.9 %collective-permute-start.37 = (bf16[4,2,512,512]{3,2,1,0:T(8,128)(2,1)}, bf16[4,2,512,512]{3,2,1,0:T(8,128)(2,1)}, u32[]{:S(2)}, u32[]{:S(2)}) collective-permute-start(bf16[4,2,512,512]{3,2,1,0:T(8,128)(2,1)} %get-tuple-element.167), channel_id=1, source_target_pairs={{0,1},{1,0},{2,3},{3,2},{4,5},{5,4},{6,7},{7,6},{8,9},{9,8},{10,11... | collective-permute-start | bytes 12582920 | tf_op jit(solution)/shard_map/ppermute | solution.py:1228
  367.9 31.9 %all-to-all-start.2 = ((bf16[4,256,1152]{2,1,0:T(8,128)(2,1)}), bf16[4,256,1152]{2,1,0:T(8,128)(2,1)}, u32[]{:S(2)}, u32[]{:S(2)}) async-start(bf16[4,256,1152]{2,1,0:T(8,128)(2,1)} %get-tuple-element.162), calls=%async_computation.2 | async-start | bytes 4718592 | tf_op jit(solution)/shard_map/all_to_all | solution.py:1399
  376.2 24.9 %collective-permute-start.36 = (bf16[2,512,512]{2,1,0:T(8,128)(2,1)}, bf16[2,512,512]{2,1,0:T(8,128)(2,1)}, u32[]{:S(2)}, u32[]{:S(2)}) collective-permute-start(bf16[2,512,512]{2,1,0:T(8,128)(2,1)} %pad_maximum_fusion.8), channel_id=1, source_target_pairs={{0,8},{2,10},{4,12},{6,14},{8,0},{10,2},{12,4},{14,6},{16,24},{18,... | collective-permute-start | bytes 3145736 | tf_op jit(solution)/shard_map/ppermute | solution.py:1224
  412.9 29.9 %all-to-all-start.3 = ((bf16[32,64,256]{2,1,0:T(8,128)(2,1)}), bf16[32,64,256]{2,1,0:T(8,128)(2,1)S(1)}, u32[]{:S(2)}, u32[]{:S(2)}) async-start(bf16[32,64,256]{2,1,0:T(8,128)(2,1)} %get-tuple-element.166), calls=%async_computation.3 | async-start | bytes 2097152 | tf_op jit(solution)/shard_map/all_to_all | solution.py:1232
  442.8 115.5 %collective-permute-start.38 = (bf16[2,512,512]{2,1,0:T(8,128)(2,1)}, bf16[2,512,512]{2,1,0:T(8,128)(2,1)}, u32[]{:S(2)}, u32[]{:S(2)}) collective-permute-start(bf16[2,512,512]{2,1,0:T(8,128)(2,1)} %get-tuple-element.176), channel_id=1, source_target_pairs={{0,8},{2,10},{4,12},{6,14},{8,0},{10,2},{12,4},{14,6},{16,24},{18,... | collective-permute-start | bytes 3145736 | tf_op jit(solution)/shard_map/ppermute | solution.py:1224
  445.2 113.1 %collective-permute-start.39 = (bf16[2,512,512]{2,1,0:T(8,128)(2,1)}, bf16[2,512,512]{2,1,0:T(8,128)(2,1)}, u32[]{:S(2)}, u32[]{:S(2)}) collective-permute-start(bf16[2,512,512]{2,1,0:T(8,128)(2,1)} %get-tuple-element.177), channel_id=1, source_target_pairs={{0,24},{2,26},{4,28},{6,30},{8,16},{10,18},{12,20},{14,22},{16,8},... | collective-permute-start | bytes 3145736 | tf_op jit(solution)/shard_map/ppermute | solution.py:1224
  445.8 112.6 %collective-permute-start.40 = (bf16[2,512,512]{2,1,0:T(8,128)(2,1)}, bf16[2,512,512]{2,1,0:T(8,128)(2,1)}, u32[]{:S(2)}, u32[]{:S(2)}) collective-permute-start(bf16[2,512,512]{2,1,0:T(8,128)(2,1)} %get-tuple-element.178), channel_id=1, source_target_pairs={{0,16},{2,18},{4,20},{6,22},{8,24},{10,26},{12,28},{14,30},{16,0},... | collective-permute-start | bytes 3145736 | tf_op jit(solution)/shard_map/ppermute | solution.py:1224
  447.6 110.7 %collective-permute-start.41 = (bf16[512,512]{1,0:T(8,128)(2,1)}, bf16[512,512]{1,0:T(8,128)(2,1)S(1)}, u32[]{:S(2)}, u32[]{:S(2)}) collective-permute-start(bf16[512,512]{1,0:T(8,128)(2,1)} %fusion.8), channel_id=1, source_target_pairs={{0,16},{2,18},{4,20},{6,22},{8,24},{10,26},{12,28},{14,30},{16,0},... | collective-permute-start | bytes 1572872 | tf_op jit(solution)/shard_map/ppermute | solution.py:1224
  448.7 109.7 %all-to-all-start.4 = ((bf16[4,512,1024]{2,1,0:T(8,128)(2,1)}), bf16[4,512,1024]{2,1,0:T(8,128)(2,1)}, u32[]{:S(2)}, u32[]{:S(2)}) async-start(bf16[4,512,1024]{2,1,0:T(8,128)(2,1)} %pad_maximum_fusion), calls=%async_computation.4 | async-start | bytes 8388608 | tf_op jit(solution)/shard_map/all_to_all | solution.py:1399
  565.2 61.5 %all-to-all-start.5 = ((bf16[32,128,256]{2,1,0:T(8,128)(2,1)}), bf16[32,128,256]{2,1,0:T(8,128)(2,1)}, u32[]{:S(2)}, u32[]{:S(2)}) async-start(bf16[32,128,256]{2,1,0:T(8,128)(2,1)} %pad_maximum_fusion.3), calls=%async_computation.5 | async-start | bytes 4194304 | tf_op jit(solution)/shard_map/all_to_all | solution.py:1232
  581.0 22.5 %collective-permute-start.46 = (bf16[4,64,640]{2,1,0:T(8,128)(2,1)S(1)}, bf16[4,64,640]{2,1,0:T(8,128)(2,1)S(1)}, u32[]{:S(2)}, u32[]{:S(2)}) collective-permute-start(bf16[4,64,640]{2,1,0:T(8,128)(2,1)S(1)} %get-tuple-element.277), channel_id=1, source_target_pairs={{0,6},{2,4},{4,2},{6,0},{8,14},{10,12},{12,10},{14,8},{16,22},{18,... | collective-permute-start | bytes 983048 | tf_op jit(solution)/shard_map/ppermute | solution.py:1224
  581.6 27.0 %collective-permute-start.45 = (bf16[4,64,640]{2,1,0:T(8,128)(2,1)S(1)}, bf16[4,64,640]{2,1,0:T(8,128)(2,1)S(1)}, u32[]{:S(2)}, u32[]{:S(2)}) collective-permute-start(bf16[4,64,640]{2,1,0:T(8,128)(2,1)S(1)} %get-tuple-element.278), channel_id=1, source_target_pairs={{0,4},{2,6},{4,0},{6,2},{8,12},{10,14},{12,8},{14,10},{16,20},{18,... | collective-permute-start | bytes 983048 | tf_op jit(solution)/shard_map/ppermute | solution.py:1224
  583.1 25.8 %collective-permute-start.44 = (bf16[4,64,640]{2,1,0:T(8,128)(2,1)S(1)}, bf16[4,64,640]{2,1,0:T(8,128)(2,1)S(1)}, u32[]{:S(2)}, u32[]{:S(2)}) collective-permute-start(bf16[4,64,640]{2,1,0:T(8,128)(2,1)S(1)} %get-tuple-element.276), channel_id=1, source_target_pairs={{0,2},{2,0},{4,6},{6,4},{8,10},{10,8},{12,14},{14,12},{16,18},{18,... | collective-permute-start | bytes 983048 | tf_op jit(solution)/shard_map/ppermute | solution.py:1224
  609.1 6.4 collective-permute-start.47
  609.4 14.2 %collective-permute-start.48 = (bf16[64,640]{1,0:T(8,128)(2,1)S(1)}, bf16[64,640]{1,0:T(8,128)(2,1)S(1)}, u32[]{:S(2)}, u32[]{:S(2)}) collective-permute-start(bf16[64,640]{1,0:T(8,128)(2,1)S(1)} %get-tuple-element.284), channel_id=1, source_target_pairs={{0,16},{2,18},{4,20},{6,22},{8,24},{10,26},{12,28},{14,30},{16,0},... | collective-permute-start | bytes 245768 | tf_op jit(solution)/shard_map/ppermute | solution.py:1224
  615.5 11.1 %collective-permute-start.49 = (bf16[64,640]{1,0:T(8,128)(2,1)S(1)}, bf16[64,640]{1,0:T(8,128)(2,1)S(1)}, u32[]{:S(2)}, u32[]{:S(2)}) collective-permute-start(bf16[64,640]{1,0:T(8,128)(2,1)S(1)} %get-tuple-element.283), channel_id=1, source_target_pairs={{0,24},{2,26},{4,28},{6,30},{8,16},{10,18},{12,20},{14,22},{16,8},... | collective-permute-start | bytes 245768 | tf_op jit(solution)/shard_map/ppermute | solution.py:1224
  646.9 59.8 %all-to-all-start.6 = ((bf16[16,64,1152]{2,1,0:T(8,128)(2,1)}), bf16[16,64,1152]{2,1,0:T(8,128)(2,1)S(1)}, u32[]{:S(2)}, u32[]{:S(2)}) async-start(bf16[16,64,1152]{2,1,0:T(8,128)(2,1)} %bitcast.75), calls=%async_computation.6 | async-start | bytes 4718592 | tf_op jit(solution)/shard_map/all_to_all | solution.py:1479
  (58 other events, 612.6 us)
Sparse Core Ops, SparseCore 0:
  130.3 88.1 all-gather.2
